TPU v7x, 32 devices: a whole 2x2x4 slice. The times are simulated.
32 devices in a mesh: fsdp: 4 (over z), tensor: 8 (over y, x, core).
Axes of the slice: x: 2, y: 2, z: 4, core: 2. Of those that a mesh axis runs over, the one named last changes fastest.
Arguments:
- momentum: float32 [4, 1152, 7168], P(None, 'fsdp', 'tensor'), may hold values from -600 to 600
- gradient: float32 [4, 1152, 7168], P(None, 'fsdp', 'tensor'), may hold values from -600 to 600
- live_ranks: int32 [4], replicated, may hold values from 0 to 1, as said below
- owner_group: int32 [4], replicated, may hold values from 0 to 3, each once
- row_counts: int32 [4, 4], replicated, may hold values from 1 to 288, as said below
- row_offsets: int32 [4, 4], replicated, may hold values from 0 to 575, as said below
Outputs:
- new_momentum: float32 [4, 1152, 7168], P(None, 'fsdp', 'tensor')
- update_shards: float32 [4, 1152, 7168], P(None, 'fsdp', 'tensor')
- owned_update: float32 [4, 576, 7168], P('fsdp', None, 'tensor')
Inputs may be any that keep to these rules, and one draw needn't show every extreme that they name: `live_ranks`: exactly one rank is dead. For every matrix the live ranks' segments [row_offsets, row_offsets + row_counts) are disjoint and cover all 576 rows, and one live rank holds exactly 288 rows. The dead rank's entries are stale and describe no rows. `row_offsets`: see row_counts.
All inputs are finite; a program needn't handle non-finite values.
Results may differ from a plain program's by a relative error of at most 0.0003.
Values sent between devices are 32-bit elements; how exact they have to be, the bound alone decides.
No kernel may reach another device: no remote copies, remote signals or barrier semaphores. Data moves between devices by JAX's collectives and lax.ppermute only.
A program may use at most 64 MiB of HBM per device.

v0:
```python
import math

import jax
import jax.numpy as jnp
from jax import lax
from jax.sharding import PartitionSpec as P

WIDTH = 7168
INNER = 576
ITERS = 2


MOMENTUM_RATE = 0.95
QUINTIC_FIRST = 3.4445
QUINTIC_SECOND = -4.775
QUINTIC_THIRD = 2.0315
EPSILON = 1e-07
HIGHEST = lax.Precision.HIGHEST


def matmul(left_side, right_side):
    return jnp.dot(left_side, right_side, precision=HIGHEST, preferred_element_type=jnp.float32)


def gram_matrix(iterate):
    shares = lax.psum_scatter(
        lax.dot_general(
            iterate,
            iterate,
            (((1,), (1,)), ((), ())),
            precision=HIGHEST,
            preferred_element_type=jnp.float32,
        ),
        "tensor",
        scatter_dimension=0,
        tiled=True,
    )
    return lax.all_gather(shares, "tensor", axis=0, tiled=True)


def on_device(momentum, gradient, live_ranks, owner_group, row_counts, row_offsets):
    rank_count = lax.axis_size("fsdp")
    my_rank = lax.axis_index("fsdp")
    slot_count = momentum.shape[1]
    columns = momentum.shape[2]
    matrices = owner_group.shape[0]
    rank_ids = jnp.arange(rank_count, dtype=jnp.int32)
    matrix_ids = jnp.arange(matrices, dtype=jnp.int32)
    owned_by = jnp.sum(
        matrix_ids[None, :] * (owner_group[None, :] == rank_ids[:, None]).astype(jnp.int32), axis=1
    )
    position = jnp.arange(slot_count, dtype=jnp.int32)
    owned_matrix = lax.dynamic_index_in_dim(owned_by, my_rank, 0, keepdims=False)
    source_counts = (
        lax.dynamic_index_in_dim(row_counts, owned_matrix, 0, keepdims=False) * live_ranks
    )
    source_offsets = lax.dynamic_index_in_dim(row_offsets, owned_matrix, 0, keepdims=False)
    keep_in = position[None, :] < source_counts[:, None]
    target = jnp.where(keep_in, source_offsets[:, None] + position[None, :], INNER).reshape(-1)
    own_alive = lax.dynamic_index_in_dim(live_ranks, my_rank, 0, keepdims=False)
    own_counts = lax.dynamic_index_in_dim(row_counts, my_rank, 1, keepdims=False) * own_alive
    keep_home = (position[None, :] < own_counts[:, None])[:, :, None]
    fresh_home = jnp.where(keep_home, MOMENTUM_RATE * momentum + gradient, 0.0)
    blended_home = gradient + MOMENTUM_RATE * fresh_home
    blended_in = lax.all_to_all(
        jnp.take(blended_home, owned_by, axis=0), "fsdp", split_axis=0, concat_axis=0, tiled=True
    )
    assembled = (
        jnp.zeros((INNER, columns), jnp.float32)
        .at[target]
        .add(blended_in.reshape(-1, columns), mode="drop")
    )
    square_total = lax.psum(jnp.sum(assembled * assembled), "tensor")
    iterate = assembled / (jnp.sqrt(square_total) + EPSILON)
    gram_now = gram_matrix(iterate)
    for repeat in range(ITERS):
        if repeat > 0:
            gram_now = gram_matrix(iterate)
        combined = QUINTIC_SECOND * gram_now + QUINTIC_THIRD * matmul(gram_now, gram_now)
        iterate = QUINTIC_FIRST * iterate + matmul(combined, iterate)
    result = iterate * (0.2 * math.sqrt(max(INNER, WIDTH)))
    picked = jnp.take(result, jnp.minimum(target, INNER - 1), axis=0).reshape(
        rank_count, slot_count, columns
    )
    sent_back = jnp.where(keep_in[:, :, None], picked, 0.0)
    update_home = lax.all_to_all(sent_back, "fsdp", split_axis=0, concat_axis=0, tiled=True)
    update_shards = jnp.take(update_home, owner_group, axis=0)
    return (fresh_home, update_shards, result[None])


def solution(mesh):
    placed = (P(None, "fsdp", "tensor"), P(None, "fsdp", "tensor"), P(), P(), P(), P())
    return jax.shard_map(
        on_device,
        mesh=mesh,
        in_specs=placed,
        out_specs=(P(None, "fsdp", "tensor"), P(None, "fsdp", "tensor"), P("fsdp", None, "tensor")),
        check_vma=False,
    )
```

profile of v0, /device:TPU:0, one launch (start us, length us, event | category | flops | bytes accessed | tf_op | source)
XLA Modules:
  0.0 444.6 jit_solution(5150633763657295221)
XLA Ops:
  9.2 1.5 multiply_reduce_fusion.1
  10.8 6.0 %multiply_add_fusion = (f32[4,288,896]{2,1,0:T(8,128)}, f32[4,288,896]{2,1,0:T(8,128)}) fusion(f32[4,288,896]{2,1,0:T(8,128)} %param.9, f32[4,288,896]{2,1,0:T(8,128)} %param.8, pred[4,288]{1,0:T(4,128)(4,1)S(1)} %iota_compare_fusion.1), kind=kLoop, calls=%fused_computation.5 | loop fusion | flops 5160960 | bytes 16516224 | tf_op jit(solution)/shard_map/add | solution.py:64
  16.8 4.9 %gather_fusion.1 = f32[4,288,896]{2,1,0:T(8,128)} fusion(f32[4,288,896]{2,1,0:T(8,128)} %get-tuple-element.6, s32[1024]{0:T(1024)S(1)} %pad_clamp_fusion.2), kind=kCustom, calls=%fused_computation.clone | custom fusion | bytes 8257552 | tf_op jit(solution)/shard_map/jit(_take)/gather | solution.py:66
  21.7 4.5 %broadcast_select_fusion.1 = f32[4,288,896]{2,1,0:T(8,128)} fusion(f32[4,288,896]{2,1,0:T(8,128)} %gather_fusion.1, pred[4]{0:T(512)(128)(4,1)S(1)} %compare_and_fusion.2), kind=kLoop, calls=%fused_computation.8 | loop fusion | flops 1032192 | bytes 8257540 | tf_op jit(solution)/shard_map/jit(_take)/select_n | solution.py:66
  26.2 6.4 %all-to-all-start = ((f32[4,288,896]{2,1,0:T(8,128)}), f32[4,288,896]{2,1,0:T(8,128)}, u32[]{:S(2)}, u32[]{:S(2)}) async-start(f32[4,288,896]{2,1,0:T(8,128)} %broadcast_select_fusion.1), calls=%async_computation | async-start | bytes 8257536 | tf_op jit(solution)/shard_map/all_to_all | solution.py:65
  36.1 88.6 %all-to-all-done = f32[4,288,896]{2,1,0:T(8,128)} async-done(((f32[4,288,896]{2,1,0:T(8,128)}), f32[4,288,896]{2,1,0:T(8,128)}, u32[]{:S(2)}, u32[]{:S(2)}) %all-to-all-start) | async-done | bytes 4128800 | tf_op jit(solution)/shard_map/all_to_all | solution.py:65
  124.7 15.1 %scatter_custom_fusion = f32[576,896]{1,0:T(8,128)S(1)} fusion(s32[1152]{0:T(1024)S(1)} %get-tuple-element.5, f32[1152,896]{1,0:T(8,128)} %bitcast.4, f32[]{:T(128)} %constant.39.clone.1), kind=kCustom, calls=%fused_computation.19 | custom fusion | flops 1032192 | bytes 2064896 | tf_op jit(solution)/shard_map/scatter-add | solution.py:71
  140.9 13.7 %psum.7 = f32[]{:T(128)} all-reduce(f32[]{:T(128)} %multiply_reduce_fusion), channel_id=1, replica_groups=mesh['fsdp'=4,'tensor'=8] {'tensor'}, use_global_device_ids=true, to_apply=%region_3.5 | all-reduce | flops 1 | bytes 8 | tf_op jit(solution)/shard_map/psum | solution.py:73
  155.3 6.7 %fusion.8 = f32[576,576]{1,0:T(8,128)} fusion(f32[576,896]{1,0:T(8,128)S(1)} %scatter_custom_fusion, f32[]{:T(128)S(6)} %add.111), kind=kOutput, calls=%fused_computation.21 | convolution fusion | flops 3567771648 | bytes 3391492 | tf_op jit(solution)/shard_map/dot_general | solution.py:27
  162.0 35.0 %reduce-scatter.7.cloned.1.call-done = f32[72,576]{1,0:T(8,128)} async-done(((f32[576,576]{1,0:T(8,128)}), f32[72,576]{1,0:T(8,128)}) %reduce-scatter.7.cloned.1.call-update) | async-done | bytes 165904
  197.4 27.1 %all-gather.3.cloned.1.call-done = f32[576,576]{1,0:T(8,128)} async-done(((f32[72,576]{1,0:T(8,128)}), f32[576,576]{1,0:T(8,128)}) %all-gather.3.cloned.1.call-update) | async-done | bytes 1327120 | tf_op jit(solution)/shard_map/all_gather | solution.py:38
  224.4 6.2 %fusion.22 = f32[576,576]{1,0:T(8,128)S(1)} fusion(f32[576,576]{1,0:T(8,128)} %all-gather.3.cloned.1.call-done), kind=kOutput, calls=%fused_computation.54 | convolution fusion | flops 2293235712 | bytes 2654208 | tf_op jit(solution)/shard_map/dot_general | solution.py:22
  230.7 5.9 %multiply_add_fusion.1 = f32[576,896]{1,0:T(8,128)S(1)} fusion(f32[576,576]{1,0:T(8,128)S(1)} %fusion.22, f32[576,576]{1,0:T(8,128)S(1)} %copy-done.5, f32[576,896]{1,0:T(8,128)S(1)} %scatter_custom_fusion, f32[]{:T(128)S(6)} %add.111), kind=kOutput, calls=%fused_computation.10 | convolution fusion | flops 3570315264 | bytes 6782980 | tf_op jit(solution)/shard_map/dot_general | solution.py:22
  237.9 7.0 %fusion.23 = f32[576,576]{1,0:T(8,128)} fusion(f32[576,896]{1,0:T(8,128)S(1)} %multiply_add_fusion.1), kind=kOutput, calls=%fused_computation.55 | convolution fusion | flops 3567255552 | bytes 3391488 | tf_op jit(solution)/shard_map/dot_general | solution.py:27
  244.9 37.9 %reduce-scatter.9.cloned.1.call-done = f32[72,576]{1,0:T(8,128)} async-done(((f32[576,576]{1,0:T(8,128)}), f32[72,576]{1,0:T(8,128)}) %reduce-scatter.9.cloned.1.call-update) | async-done | bytes 165904
  282.9 26.9 %all-gather.5.cloned.1.call-done = f32[576,576]{1,0:T(8,128)} async-done(((f32[72,576]{1,0:T(8,128)}), f32[576,576]{1,0:T(8,128)}) %all-gather.5.cloned.1.call-update) | async-done | bytes 1327120 | tf_op jit(solution)/shard_map/all_gather | solution.py:38
  309.8 6.2 %fusion.24 = f32[576,576]{1,0:T(8,128)S(1)} fusion(f32[576,576]{1,0:T(8,128)} %all-gather.5.cloned.1.call-done), kind=kOutput, calls=%fused_computation.56 | convolution fusion | flops 2293235712 | bytes 2654208 | tf_op jit(solution)/shard_map/dot_general | solution.py:22
  316.1 5.8 %add_multiply_fusion = f32[576,896]{1,0:T(8,128)S(1)} fusion(f32[576,896]{1,0:T(8,128)S(1)} %copy-done.3, f32[576,576]{1,0:T(8,128)S(1)} %fusion.24, f32[576,576]{1,0:T(8,128)S(1)} %copy-done.4), kind=kOutput, calls=%fused_computation.9 | convolution fusion | flops 3569799168 | bytes 6782976 | tf_op jit(solution)/shard_map/dot_general | solution.py:22
  321.9 4.9 %gather_fusion = f32[1152,896]{1,0:T(8,128)} fusion(f32[576,896]{1,0:T(8,128)S(1)} %add_multiply_fusion, s32[2048]{0:T(1024)S(1)} %pad_clamp_fusion), kind=kCustom, calls=%fused_computation.2 | custom fusion | bytes 8262144 | tf_op jit(solution)/shard_map/jit(_take)/gather | solution.py:82
  326.8 3.8 select_select_fusion
  330.7 5.0 %all-to-all-start.1 = ((f32[4,288,896]{2,1,0:T(8,128)}), f32[4,288,896]{2,1,0:T(8,128)}, u32[]{:S(2)}, u32[]{:S(2)}) async-start(f32[4,288,896]{2,1,0:T(8,128)} %select_select_fusion), calls=%async_computation.1 | async-start | bytes 8257536 | tf_op jit(solution)/shard_map/all_to_all | solution.py:86
  335.7 92.5 %all-to-all-done.1 = f32[4,288,896]{2,1,0:T(8,128)} async-done(((f32[4,288,896]{2,1,0:T(8,128)}), f32[4,288,896]{2,1,0:T(8,128)}, u32[]{:S(2)}, u32[]{:S(2)}) %all-to-all-start.1) | async-done | bytes 4128800 | tf_op jit(solution)/shard_map/all_to_all | solution.py:86
  428.2 5.0 %gather_fusion.2 = f32[4,288,896]{2,1,0:T(8,128)} fusion(f32[4,288,896]{2,1,0:T(8,128)} %all-to-all-done.1, s32[1024]{0:T(1024)S(1)} %pad_clamp_fusion.1), kind=kCustom, calls=%fused_computation.1.clone | custom fusion | bytes 8257552 | tf_op jit(solution)/shard_map/jit(_take)/gather | solution.py:87
  433.2 4.5 %broadcast_select_fusion = f32[4,288,896]{2,1,0:T(8,128)} fusion(f32[4,288,896]{2,1,0:T(8,128)} %gather_fusion.2, pred[4]{0:T(512)(128)(4,1)S(1)} %compare_and_fusion.1), kind=kLoop, calls=%fused_computation.7 | loop fusion | flops 1032192 | bytes 8257540 | tf_op jit(solution)/shard_map/jit(_take)/select_n | solution.py:87
  (42 shorter events, 6.6 us)
Async XLA Ops:
  7.2 28.0 %copy-start = (s32[4,4]{1,0:T(4,128)S(1)}, s32[4,4]{1,0:T(4,128)}, u32[]{:S(2)}) copy-start(s32[4,4]{1,0:T(4,128)} %param.13) | copy-start | bytes 196
  26.2 9.0 %copy-start.6 = (s32[4]{0:T(128)S(1)}, s32[4]{0:T(128)}, u32[]{:S(2)}) copy-start(s32[4]{0:T(128)} %param.10) | copy-start | bytes 52
  26.2 98.5 %all-to-all-start = ((f32[4,288,896]{2,1,0:T(8,128)}), f32[4,288,896]{2,1,0:T(8,128)}, u32[]{:S(2)}, u32[]{:S(2)}) async-start(f32[4,288,896]{2,1,0:T(8,128)} %broadcast_select_fusion.1), calls=%async_computation | async-start | bytes 8257536 | tf_op jit(solution)/shard_map/all_to_all | solution.py:65
  32.7 164.4 %reduce-scatter.7.cloned.1.call-start = ((), (), s32[]{:S(2)}) async-start(), calls=%async_computation.6 | async-start | bytes 1658880
  162.0 62.4 %all-gather.3.cloned.1.call-start = ((), (), s32[]{:S(2)}) async-start(), calls=%async_computation.4 | async-start | bytes 1658880 | tf_op jit(solution)/shard_map/all_gather | solution.py:38
  197.1 85.7 %reduce-scatter.9.cloned.1.call-start = ((), (), s32[]{:S(2)}) async-start(), calls=%async_computation.7 | async-start | bytes 1658880
  224.4 6.2 %copy-start.5 = (f32[576,576]{1,0:T(8,128)S(1)}, f32[576,576]{1,0:T(8,128)}, u32[]{:S(2)}) copy-start(f32[576,576]{1,0:T(8,128)} %all-gather.3.cloned.1.call-done) | copy-start | bytes 3981316
  236.6 1.3 copy-start.2
  244.8 65.0 %all-gather.5.cloned.1.call-start = ((), (), s32[]{:S(2)}) async-start(), calls=%async_computation.5 | async-start | bytes 1658880 | tf_op jit(solution)/shard_map/all_gather | solution.py:38
  309.8 6.2 %copy-start.3 = (f32[576,896]{1,0:T(8,128)S(1)}, f32[576,896]{1,0:T(8,128)}, u32[]{:S(2)}) copy-start(f32[576,896]{1,0:T(8,128)} %copy-done.2) | copy-start | bytes 6193156
  309.8 6.3 %copy-start.4 = (f32[576,576]{1,0:T(8,128)S(1)}, f32[576,576]{1,0:T(8,128)}, u32[]{:S(2)}) copy-start(f32[576,576]{1,0:T(8,128)} %all-gather.5.cloned.1.call-done) | copy-start | bytes 3981316
  321.9 4.9 %copy-start.1 = (f32[576,896]{1,0:T(8,128)}, f32[576,896]{1,0:T(8,128)S(1)}, u32[]{:S(2)}) copy-start(f32[576,896]{1,0:T(8,128)S(1)} %add_multiply_fusion) | copy-start | bytes 6193156
  330.7 5.0 %copy-start.7 = (s32[4]{0:T(128)S(1)}, s32[4]{0:T(128)}, u32[]{:S(2)}) copy-start(s32[4]{0:T(128)} %param.11) | copy-start | bytes 52
  330.7 97.5 %all-to-all-start.1 = ((f32[4,288,896]{2,1,0:T(8,128)}), f32[4,288,896]{2,1,0:T(8,128)}, u32[]{:S(2)}, u32[]{:S(2)}) async-start(f32[4,288,896]{2,1,0:T(8,128)} %select_select_fusion), calls=%async_computation.1 | async-start | bytes 8257536 | tf_op jit(solution)/shard_map/all_to_all | solution.py:86
Sparse Core Ops, SparseCore 0:
  162.1 34.9 reduce-scatter.6
  199.1 25.2 all-gather.2
  245.0 37.7 reduce-scatter.8
  284.5 25.2 all-gather.4
where the time goes:
time: 451 us; the launch traced here: 445 us
  waiting for transfers between devices  308 us (68%)
  other arithmetic  38.3 us (8%)
  matrix products  37.8 us (8%)
  local copies, waits for them, and re-layouts  18 us (4%)
  between operations  17 us (4%)
  blocking collectives  13.7 us (3%)
  starting transfers between devices  11.8 us (3%)
    all_to_all x1, waiting for transfers between devices, on_device(): lax.all_to_all(sent_back, 'fsdp', split_axis=0, concat_axis=0, tiled=True)  92.5 us
    all_to_all x1, waiting for transfers between devices, on_device(): lax.all_to_all(jnp.take(blended_home, owned_by, axis=0), 'fsdp', split_ax...  88.6 us
    unnamed x6, waiting for transfers between devices  73 us
    all_gather x2, waiting for transfers between devices, gram_matrix(): return lax.all_gather(shares, 'tensor', axis=0, tiled=True)  54 us
    dot_general x4, matrix products, matmul(): jnp.dot(left_side, right_side, precision=HIGHEST, preferred_element_type=...  24.2 us
    scatter-add x1, other arithmetic, on_device(): assembled = jnp.zeros((INNER, columns), jnp.float32).at[target].add(blend...  15.1 us
    psum x1, blocking collectives, on_device(): square_total = lax.psum(jnp.sum(assembled * assembled), 'tensor')  13.7 us
    dot_general x2, matrix products, gram_matrix(): lax.dot_general(iterate, iterate, (((1,), (1,)), ((), ())), precision=HIG...  13.6 us
  transfers between devices with their start and end apart: 6, of which 6 were waited for; matrix products, arithmetic and copies ran while one was open for 0% of the time, Pallas kernels for 0%

commit v1 on v0

v1 whole, which is shorter than its diff:
```python
import functools
import math

import jax
import jax.numpy as jnp
from jax import lax
from jax.experimental import pallas as pl
from jax.experimental.pallas import tpu as pltpu
from jax.sharding import PartitionSpec as P

WIDTH = 7168
INNER = 576
PANELS = 3
SUBLANES = 8
PANEL = INNER // PANELS

MOMENTUM_RATE = 0.95
QUINTIC_FIRST = 3.4445
QUINTIC_SECOND = -4.775
QUINTIC_THIRD = 2.0315
EPSILON = 1e-07
OUT_SCALE = 0.2 * math.sqrt(max(INNER, WIDTH))
VMEM_LIMIT = 48 * 1024 * 1024


def halves(value):
    high = value.astype(jnp.bfloat16)
    low = (value - high.astype(jnp.float32)).astype(jnp.bfloat16)
    return high, low


def dot(left, right, contract):
    return lax.dot_general(left, right, (contract, ((), ())), preferred_element_type=jnp.float32)


def dot_halves(left, right, contract=((1,), (0,))):
    (left_high, left_low), (right_high, right_low) = left, right
    return (
        dot(left_high, right_low, contract) + dot(left_low, right_high, contract)
    ) + dot(left_high, right_high, contract)


def aligned(start, slots):
    shift = start % SUBLANES
    return pl.ds(pl.multiple_of(start - shift, SUBLANES), slots + SUBLANES), shift


def gram_kernel(starts, *refs):
    *blocks, iterate, gram, padded = refs
    slots = blocks[0].shape[0]
    padded[...] = jnp.zeros_like(padded)
    tail = jnp.zeros((SUBLANES, blocks[0].shape[1]), jnp.float32)
    for place, block in enumerate(blocks):
        rows, shift = aligned(starts[place], slots)
        moved = pltpu.roll(jnp.concatenate([block[...], tail], axis=0), shift, 0)
        padded[rows, :] = padded[rows, :] + moved
    whole = padded[:INNER, :]
    iterate[...] = whole
    high, low = halves(whole)
    for panel in range(PANELS):
        here = slice(panel * PANEL, (panel + 1) * PANEL)
        after = (panel + 1) % PANELS
        there = slice(after * PANEL, (after + 1) * PANEL)
        gram[here, :PANEL] = dot_halves((high[here], low[here]), (high[here], low[here]), ((1,), (1,)))
        gram[here, PANEL:] = dot_halves((high[here], low[here]), (high[there], low[there]), ((1,), (1,)))


def update_kernel(starts, counts, packed, iterate, result, *refs):
    *blocks, gram, padded = refs
    slots, columns = blocks[0].shape
    for panel in range(PANELS):
        here = slice(panel * PANEL, (panel + 1) * PANEL)
        after = (panel + 1) % PANELS
        there = slice(after * PANEL, (after + 1) * PANEL)
        gram[here, here] = packed[here, :PANEL]
        side = packed[here, PANEL:]
        gram[here, there] = side
        gram[there, here] = side.T
    raw = gram[...]
    diagonal = lax.broadcasted_iota(jnp.int32, raw.shape, 0) == lax.broadcasted_iota(jnp.int32, raw.shape, 1)
    square_total = jnp.sum(jnp.where(diagonal, raw, 0.0))
    norm = jnp.sqrt(jnp.full((1, 1), square_total, jnp.float32)) + EPSILON
    inverse = 1.0 / norm
    first = (raw * inverse) * inverse
    first_halves = halves(first)
    second = dot_halves(first_halves, first_halves)
    inner = QUINTIC_SECOND * first + QUINTIC_THIRD * second + jnp.where(diagonal, QUINTIC_FIRST, 0.0)
    inner_halves = halves(inner)
    next_gram = dot_halves(inner_halves, halves(dot_halves(inner_halves, first_halves)))
    next_halves = halves(next_gram)
    outer = (
        QUINTIC_SECOND * next_gram
        + QUINTIC_THIRD * dot_halves(next_halves, next_halves)
        + jnp.where(diagonal, QUINTIC_FIRST, 0.0)
    )
    total = dot_halves(halves(outer), inner_halves) * (inverse * OUT_SCALE)
    update = dot_halves(halves(total), halves(iterate[...]))
    result[...] = update
    padded[:INNER, :] = update
    position = lax.broadcasted_iota(jnp.int32, (slots, columns), 0)
    for place, block in enumerate(blocks):
        rows, shift = aligned(starts[place], slots)
        back = jnp.where(shift == 0, 0, slots + SUBLANES - shift)
        moved = pltpu.roll(padded[rows, :], back, 0)[:slots]
        block[...] = jnp.where(position < counts[place], moved, 0.0)


def in_vmem(count):
    return [pl.BlockSpec(memory_space=pltpu.VMEM)] * count


def in_smem(count):
    return [pl.BlockSpec(memory_space=pltpu.SMEM)] * count


def assemble_and_gram(starts, blocks):
    slots, columns = blocks[0].shape
    flops = 2 * 3 * INNER * 2 * PANEL * columns
    return pl.pallas_call(
        gram_kernel,
        out_shape=[
            jax.ShapeDtypeStruct((INNER, columns), jnp.float32),
            jax.ShapeDtypeStruct((INNER, 2 * PANEL), jnp.float32),
        ],
        in_specs=in_smem(1) + in_vmem(len(blocks)),
        out_specs=in_vmem(2),
        scratch_shapes=[pltpu.VMEM((INNER + slots + SUBLANES, columns), jnp.float32)],
        compiler_params=pltpu.CompilerParams(vmem_limit_bytes=VMEM_LIMIT),
        cost_estimate=pl.CostEstimate(flops=flops, bytes_accessed=8 * INNER * columns, transcendentals=0),
        name="assemble_and_gram",
    )(starts, *blocks)


def apply_update(starts, counts, packed, iterate, slots):
    columns = iterate.shape[1]
    ranks = starts.shape[0]
    flops = 2 * 3 * INNER * INNER * (5 * INNER + columns)
    return pl.pallas_call(
        update_kernel,
        out_shape=[jax.ShapeDtypeStruct((INNER, columns), jnp.float32)]
        + [jax.ShapeDtypeStruct((slots, columns), jnp.float32)] * ranks,
        in_specs=in_smem(2) + in_vmem(2),
        out_specs=in_vmem(1 + ranks),
        scratch_shapes=[
            pltpu.VMEM((INNER, INNER), jnp.float32),
            pltpu.VMEM((INNER + slots + SUBLANES, columns), jnp.float32),
        ],
        compiler_params=pltpu.CompilerParams(vmem_limit_bytes=VMEM_LIMIT),
        cost_estimate=pl.CostEstimate(flops=flops, bytes_accessed=16 * INNER * columns, transcendentals=0),
        name="apply_update",
    )(starts, counts, packed, iterate)


def group_stages(size):
    stages, shift = [], 0
    while (1 << shift) < size:
        wide = 1 if shift == 0 or (2 << shift) >= size else 2
        stages.append((shift, 1 << wide))
        shift += wide
    return stages


def sum_over(block, axis):
    size = lax.axis_size(axis)
    if size & (size - 1) or block.shape[0] % size:
        return lax.psum(block, axis)
    index = lax.axis_index(axis)

    def exchange(piece, step):
        return lax.ppermute(piece, axis, [(i, i ^ step) for i in range(size)])

    stages = group_stages(size)
    for shift, group in stages:
        digit = (index >> shift) & (group - 1)
        part = block.shape[0] // group
        pieces = [
            lax.dynamic_slice_in_dim(block, (digit ^ step) * part, part, 0) for step in range(group)
        ]
        arrived = [exchange(pieces[step], step << shift) for step in range(1, group)]
        block = functools.reduce(jnp.add, arrived, pieces[0])
    for shift, group in reversed(stages):
        digit = (index >> shift) & (group - 1)
        part = block.shape[0]
        pieces = [block] + [exchange(block, step << shift) for step in range(1, group)]
        block = jnp.zeros((part * group, block.shape[1]), block.dtype)
        for step, piece in enumerate(pieces):
            block = lax.dynamic_update_slice_in_dim(block, piece, (digit ^ step) * part, 0)
    return block


def on_device(momentum, gradient, live_ranks, owner_group, row_counts, row_offsets):
    ranks = lax.axis_size("fsdp")
    my_rank = lax.axis_index("fsdp")
    matrices, slots, columns = momentum.shape
    matrix_ids = jnp.arange(matrices, dtype=jnp.int32)
    rank_ids = jnp.arange(ranks, dtype=jnp.int32)
    position = jnp.arange(slots, dtype=jnp.int32)
    owned_by = jnp.sum(
        matrix_ids[None, :] * (owner_group[None, :] == rank_ids[:, None]).astype(jnp.int32), axis=1
    )
    live_counts = row_counts * live_ranks[None, :]
    own_counts = lax.dynamic_index_in_dim(live_counts, my_rank, 1, keepdims=False)
    owned_matrix = owned_by[my_rank]

    def shifted(step):
        return lax.rem(my_rank + step + ranks, ranks)

    def passes(step):
        return [(i, (i + step) % ranks) for i in range(ranks)]

    def blended(matrix):
        old_state = lax.dynamic_index_in_dim(momentum, matrix, 0, keepdims=False)
        grad_now = lax.dynamic_index_in_dim(gradient, matrix, 0, keepdims=False)
        fresh = MOMENTUM_RATE * old_state + grad_now
        keep = (position < own_counts[matrix])[:, None]
        return jnp.where(keep, grad_now + MOMENTUM_RATE * fresh, 0.0)

    steps = sorted(range(1, ranks), key=lambda step: -min(step, ranks - step))
    blocks = {step: lax.ppermute(blended(owned_by[shifted(step)]), "fsdp", passes(step)) for step in steps}
    blocks[0] = blended(owned_matrix)
    keep_home = (position[None, :] < own_counts[:, None])[:, :, None]
    new_momentum = jnp.where(keep_home, MOMENTUM_RATE * momentum + gradient, 0.0)

    offsets_here = lax.dynamic_index_in_dim(row_offsets, owned_matrix, 0, keepdims=False)
    counts_here = lax.dynamic_index_in_dim(live_counts, owned_matrix, 0, keepdims=False)
    came_from = lax.rem(my_rank - rank_ids + ranks, ranks)
    goes_to = lax.rem(my_rank + rank_ids, ranks)
    iterate, gram_part = assemble_and_gram(offsets_here[came_from], [blocks[step] for step in range(ranks)])
    packed = sum_over(gram_part, "tensor")
    result, *home = apply_update(offsets_here[goes_to], counts_here[goes_to], packed, iterate, slots)

    update_shards = jnp.zeros_like(momentum)
    update_shards = lax.dynamic_update_index_in_dim(update_shards, home[0], owned_matrix, 0)
    returned = {step: lax.ppermute(home[step], "fsdp", passes(step)) for step in steps}
    for step in reversed(steps):
        update_shards = lax.dynamic_update_index_in_dim(
            update_shards, returned[step], owned_by[shifted(-step)], 0
        )
    return (new_momentum, update_shards, result[None])


def solution(mesh):
    placed = (P(None, "fsdp", "tensor"), P(None, "fsdp", "tensor"), P(), P(), P(), P())
    return jax.shard_map(
        on_device,
        mesh=mesh,
        in_specs=placed,
        out_specs=(P(None, "fsdp", "tensor"), P(None, "fsdp", "tensor"), P("fsdp", None, "tensor")),
        check_vma=False,
    )
```

time: 451 us -> 255 us (0.57); the launches traced: 445 us -> 255 us
  waiting for transfers between devices: 308 us -> 152 us
  matrix products: 37.8 us -> 0 us
  starting transfers between devices: 11.8 us -> 38.4 us
  blocking collectives: 13.7 us -> 0 us
  local copies, waits for them, and re-layouts: 18 us -> 9.1 us
  Pallas kernels: 0 us -> 6.61 us
    all_to_all x2 -> x0, waiting for transfers between devices: 181 us -> none  [the longest x1 92.5 us: on_device(): lax.all_to_all(sent_back, 'fsdp', split_axis=0, concat_axis=0, tiled=True)]
    ppermute x0 -> x14, waiting for transfers between devices: none -> 152 us  [the longest x3 75.1 us: on_device(): lax.ppermute(home[step], 'fsdp', passes(step))]
    unnamed x6 -> x0, waiting for transfers between devices: 73 us -> none
    all_gather x2 -> x0, waiting for transfers between devices: 54 us -> none  [gram_matrix(): return lax.all_gather(shares, 'tensor', axis=0, tiled=True)]
    ppermute x0 -> x14, starting transfers between devices: none -> 38.4 us  [the longest x3 24.2 us: on_device(): lax.ppermute(home[step], 'fsdp', passes(step))]
    dot_general x6 -> x0, matrix products: 37.8 us -> none  [the longest x4 24.2 us: matmul(): jnp.dot(left_side, right_side, precision=HIGHEST, preferred_element_type=...]
    pallas_call x0 -> x1, other arithmetic: none -> 18.8 us  [apply_update(): pl.pallas_call(update_kernel, out_shape=[jax.ShapeDtypeStruct((INNER, col...]
    scatter-add x1 -> x0, other arithmetic: 15.1 us -> none  [on_device(): assembled = jnp.zeros((INNER, columns), jnp.float32).at[target].add(blend...]
  transfers between devices with their start and end apart: 6 -> 14, of which waited for: 6 -> 13; matrix products, arithmetic and copies ran while one was open for 0% -> 4% of each run, Pallas kernels for 0% -> 0%
where the time goes in v1:
time: 255 us
  waiting for transfers between devices  152 us (60%)
  starting transfers between devices  38.4 us (15%)
  other arithmetic  34.8 us (14%)
  between operations  14.5 us (6%)
  local copies, waits for them, and re-layouts  9.1 us (4%)
  Pallas kernels  6.61 us (3%)
    ppermute x3, waiting for transfers between devices, on_device(): lax.ppermute(home[step], 'fsdp', passes(step))  75.1 us
    ppermute x3, waiting for transfers between devices, on_device(): lax.ppermute(blended(owned_by[shifted(step)]), 'fsdp', passes(step))  64.9 us
    ppermute x3, starting transfers between devices, on_device(): lax.ppermute(home[step], 'fsdp', passes(step))  24.2 us
    pallas_call x1, other arithmetic, apply_update(): pl.pallas_call(update_kernel, out_shape=[jax.ShapeDtypeStruct((INNER, col...  18.8 us
    ppermute x8, waiting for transfers between devices, exchange(): return lax.ppermute(piece, axis, [(i, i ^ step) for i in range(size)])  11.5 us
    ppermute x8, starting transfers between devices, exchange(): return lax.ppermute(piece, axis, [(i, i ^ step) for i in range(size)])  7.25 us
    ppermute x3, starting transfers between devices, on_device(): lax.ppermute(blended(owned_by[shifted(step)]), 'fsdp', passes(step))  6.96 us
    pallas_call x1, Pallas kernels, assemble_and_gram(): pl.pallas_call(gram_kernel, out_shape=[jax.ShapeDtypeStruct((INNER, colum...  6.61 us
  transfers between devices with their start and end apart: 14, of which 13 were waited for; matrix products, arithmetic and copies ran while one was open for 4% of the time, Pallas kernels for 0%

profile of v1, /device:TPU:0, one launch (start us, length us, event | category | flops | bytes accessed | tf_op | source)
XLA Modules:
  0.0 255.0 jit_solution(12408144158291253307)
XLA Ops:
  11.5 1.3 iota_compare_fusion.3
  12.8 1.3 iota_compare_fusion.1
  14.1 5.7 %fusion.2 = (f32[288,896]{1,0:T(8,128)}, f32[288,896]{1,0:T(8,128)}, f32[288,896]{1,0:T(8,128)S(1)}, f32[288,896]{1,0:T(8,128)}) fusion(f32[4,288,896]{2,1,0:T(8,128)} %param.6, s32[]{:T(128)S(6)} %select_n.147, f32[4,288,896]{2,1,0:T(8,128)} %param.7, pred[288]{0:T(512)(128)(4,1)S(1)} %get-tuple-element.49, s32[]{:T(128)S(6)} %select_n.139, ...), kind=kLoop, calls=%fused_computation.11 | loop fusion | flops 5160960 | bytes 12387472 | tf_op jit(solution)/shard_map/jit(_where)/select_n | solution.py:216
  19.8 3.0 %collective-permute-start = (f32[288,896]{1,0:T(8,128)}, f32[288,896]{1,0:T(8,128)S(1)}, u32[]{:S(2)}, u32[]{:S(2)}) collective-permute-start(f32[288,896]{1,0:T(8,128)} %get-tuple-element.30), channel_id=1, source_target_pairs={{0,8},{8,16},{16,24},{24,0},{1,9},{9,17},{17,25},{25,1},{2,10},{10... | collective-permute-start | bytes 3096584 | tf_op jit(solution)/shard_map/ppermute | solution.py:219
  22.8 2.6 %collective-permute-start.1 = (f32[288,896]{1,0:T(8,128)}, f32[288,896]{1,0:T(8,128)}, u32[]{:S(2)}, u32[]{:S(2)}) collective-permute-start(f32[288,896]{1,0:T(8,128)} %get-tuple-element.32), channel_id=1, source_target_pairs={{0,16},{8,24},{16,0},{24,8},{1,17},{9,25},{17,1},{25,9},{2,18},{10... | collective-permute-start | bytes 3096584 | tf_op jit(solution)/shard_map/ppermute | solution.py:219
  25.4 1.3 collective-permute-start.2
  27.4 21.4 %collective-permute-done.refs_1_ = f32[288,896]{1,0:T(8,128)S(1)} collective-permute-done((f32[288,896]{1,0:T(8,128)}, f32[288,896]{1,0:T(8,128)S(1)}, u32[]{:S(2)}, u32[]{:S(2)}) %collective-permute-start) | collective-permute-done | bytes 1032224 | tf_op jit(solution)/shard_map/ppermute | solution.py:219
  48.8 43.5 %collective-permute-done.1.refs_2_ = f32[288,896]{1,0:T(8,128)} collective-permute-done((f32[288,896]{1,0:T(8,128)}, f32[288,896]{1,0:T(8,128)}, u32[]{:S(2)}, u32[]{:S(2)}) %collective-permute-start.1) | collective-permute-done | bytes 1032224 | tf_op jit(solution)/shard_map/ppermute | solution.py:219
  92.3 6.6 %assemble_and_gram.1 = (f32[576,896]{1,0:T(8,128)}, f32[576,384]{1,0:T(8,128)S(1)}) custom-call(s32[4]{0:T(128)S(1)} %gather_fusion.2, f32[288,896]{1,0:T(8,128)S(1)} %get-tuple-element.31.refs_0_, f32[288,896]{1,0:T(8,128)S(1)} %collective-permute-done.refs_1_, f32[288,896]{1,0:T(8,128)} %collective-permute-done.1.refs_2_, ...), custom_call_target="tpu_custom_call" | custom-call | flops 1189085184 | bytes 4128768 | tf_op jit(solution)/shard_map/assemble_and_gram/pallas_call | solution.py:119
  99.1 1.8 collective-permute-done.3
  100.9 1.6 collective-permute-start.4
  102.5 1.5 collective-permute-start.5
  104.5 1.6 collective-permute-done.4
  106.1 2.6 %collective-permute-done.5 = f32[72,384]{1,0:T(8,128)S(1)} collective-permute-done((f32[72,384]{1,0:T(8,128)S(1)}, f32[72,384]{1,0:T(8,128)S(1)}, u32[]{:S(2)}, u32[]{:S(2)}) %collective-permute-start.5) | collective-permute-done | bytes 110624 | tf_op jit(solution)/shard_map/ppermute | solution.py:170
  109.8 1.3 collective-permute-start.7
  111.9 1.4 collective-permute-start.9
  113.3 2.0 collective-permute-done.7
  119.4 2.3 broadcast_in_dim.80
  121.7 18.8 %apply_update.1 = (f32[4,288,896]{2,1,0:T(8,128)}, f32[288,896]{1,0:T(8,128)}, f32[288,896]{1,0:T(8,128)S(1)}, f32[288,896]{1,0:T(8,128)S(1)}, f32[576,896]{1,0:T(8,128)}) fusion(f32[4,288,896]{2,1,0:T(8,128)} %broadcast_in_dim.80, s32[]{:T(128)S(6)} %select_n.132, s32[4]{0:T(128)S(1)} %gather_fusion, s32[4]{0:T(128)S(1)} %gather_fusion.1, ...), kind=kCustom, calls=%fused_computation.7 | custom fusion | flops 7516717056 | bytes 9142308 | tf_op jit(solution)/shard_map/apply_update/pallas_call | solution.py:138
  140.5 23.6 %collective-permute-start.11 = (f32[288,896]{1,0:T(8,128)}, f32[288,896]{1,0:T(8,128)S(1)}, u32[]{:S(2)}, u32[]{:S(2)}) collective-permute-start(f32[288,896]{1,0:T(8,128)} %get-tuple-element.20), channel_id=1, source_target_pairs={{0,24},{8,0},{16,8},{24,16},{1,25},{9,1},{17,9},{25,17},{2,26},{10... | collective-permute-start | bytes 3096584 | tf_op jit(solution)/shard_map/ppermute | solution.py:234
  170.8 6.0 %add_select_fusion = f32[4,288,896]{2,1,0:T(8,128)} fusion(f32[4,288,896]{2,1,0:T(8,128)} %param.7, f32[4,288,896]{2,1,0:T(8,128)} %param.6, pred[4,288]{1,0:T(4,128)(4,1)S(1)} %iota_compare_fusion), kind=kLoop, calls=%fused_computation.3 | loop fusion | flops 3096576 | bytes 12387456 | tf_op jit(solution)/shard_map/jit(_where)/select_n | solution.py:222
  176.8 10.9 %collective-permute-done.11 = f32[288,896]{1,0:T(8,128)S(1)} collective-permute-done((f32[288,896]{1,0:T(8,128)}, f32[288,896]{1,0:T(8,128)S(1)}, u32[]{:S(2)}, u32[]{:S(2)}) %collective-permute-start.11) | collective-permute-done | bytes 1032224 | tf_op jit(solution)/shard_map/ppermute | solution.py:234
  188.7 21.5 %collective-permute-done.12 = f32[288,896]{1,0:T(8,128)S(1)} collective-permute-done((f32[288,896]{1,0:T(8,128)S(1)}, f32[288,896]{1,0:T(8,128)S(1)}, u32[]{:S(2)}, u32[]{:S(2)}) %collective-permute-start.12) | collective-permute-done | bytes 1032224 | tf_op jit(solution)/shard_map/ppermute | solution.py:234
  211.2 42.8 %collective-permute-done.13 = f32[288,896]{1,0:T(8,128)S(1)} collective-permute-done((f32[288,896]{1,0:T(8,128)S(1)}, f32[288,896]{1,0:T(8,128)S(1)}, u32[]{:S(2)}, u32[]{:S(2)}) %collective-permute-start.13) | collective-permute-done | bytes 1032224 | tf_op jit(solution)/shard_map/ppermute | solution.py:234
  (41 shorter events, 14.0 us)
Async XLA Ops:
  0.6 26.1 %copy-start = (s32[4,4]{1,0:T(4,128)S(1)}, s32[4,4]{1,0:T(4,128)}, u32[]{:S(2)}) copy-start(s32[4,4]{1,0:T(4,128)} %param.11) | copy-start | bytes 196
  19.8 29.0 %collective-permute-start = (f32[288,896]{1,0:T(8,128)}, f32[288,896]{1,0:T(8,128)S(1)}, u32[]{:S(2)}, u32[]{:S(2)}) collective-permute-start(f32[288,896]{1,0:T(8,128)} %get-tuple-element.30), channel_id=1, source_target_pairs={{0,8},{8,16},{16,24},{24,0},{1,9},{9,17},{17,25},{25,1},{2,10},{10... | collective-permute-start | bytes 3096584 | tf_op jit(solution)/shard_map/ppermute | solution.py:219
  22.8 69.5 %collective-permute-start.1 = (f32[288,896]{1,0:T(8,128)}, f32[288,896]{1,0:T(8,128)}, u32[]{:S(2)}, u32[]{:S(2)}) collective-permute-start(f32[288,896]{1,0:T(8,128)} %get-tuple-element.32), channel_id=1, source_target_pairs={{0,16},{8,24},{16,0},{24,8},{1,17},{9,25},{17,1},{25,9},{2,18},{10... | collective-permute-start | bytes 3096584 | tf_op jit(solution)/shard_map/ppermute | solution.py:219
  25.4 66.9 %collective-permute-start.2 = (f32[288,896]{1,0:T(8,128)}, f32[288,896]{1,0:T(8,128)}, u32[]{:S(2)}, u32[]{:S(2)}) collective-permute-start(f32[288,896]{1,0:T(8,128)} %get-tuple-element.29), channel_id=1, source_target_pairs={{0,24},{8,0},{16,8},{24,16},{1,25},{9,1},{17,9},{25,17},{2,26},{10... | collective-permute-start | bytes 3096584 | tf_op jit(solution)/shard_map/ppermute | solution.py:219
  99.0 1.9 collective-permute-start.3
  100.9 5.2 %collective-permute-start.4 = (f32[72,384]{1,0:T(8,128)S(1)}, f32[72,384]{1,0:T(8,128)S(1)}, u32[]{:S(2)}, u32[]{:S(2)}) collective-permute-start(f32[72,384]{1,0:T(8,128)S(1)} %get-tuple-element.33), channel_id=1, source_target_pairs={{0,2},{1,3},{2,0},{3,1},{4,6},{5,7},{6,4},{7,5},{8,10},{9,11},{10,... | collective-permute-start | bytes 331784 | tf_op jit(solution)/shard_map/ppermute | solution.py:170
  102.5 6.2 %collective-permute-start.5 = (f32[72,384]{1,0:T(8,128)S(1)}, f32[72,384]{1,0:T(8,128)S(1)}, u32[]{:S(2)}, u32[]{:S(2)}) collective-permute-start(f32[72,384]{1,0:T(8,128)S(1)} %get-tuple-element.35), channel_id=1, source_target_pairs={{0,4},{1,5},{2,6},{3,7},{4,0},{5,1},{6,2},{7,3},{8,12},{9,13},{10,... | collective-permute-start | bytes 331784 | tf_op jit(solution)/shard_map/ppermute | solution.py:170
  104.0 5.7 %collective-permute-start.6 = (f32[72,384]{1,0:T(8,128)S(1)}, f32[72,384]{1,0:T(8,128)S(1)}, u32[]{:S(2)}, u32[]{:S(2)}) collective-permute-start(f32[72,384]{1,0:T(8,128)S(1)} %get-tuple-element.34), channel_id=1, source_target_pairs={{0,6},{1,7},{2,4},{3,5},{4,2},{5,3},{6,0},{7,1},{8,14},{9,15},{10,... | collective-permute-start | bytes 331784 | tf_op jit(solution)/shard_map/ppermute | solution.py:170
  109.8 5.6 %collective-permute-start.7 = (f32[72,384]{1,0:T(8,128)S(1)}, f32[72,384]{1,0:T(8,128)S(1)}, u32[]{:S(2)}, u32[]{:S(2)}) collective-permute-start(f32[72,384]{1,0:T(8,128)S(1)} %get-tuple-element.28), channel_id=1, source_target_pairs={{0,2},{1,3},{2,0},{3,1},{4,6},{5,7},{6,4},{7,5},{8,10},{9,11},{10,... | collective-permute-start | bytes 331784 | tf_op jit(solution)/shard_map/ppermute | solution.py:170
  111.1 5.3 %collective-permute-start.8 = (f32[72,384]{1,0:T(8,128)S(1)}, f32[72,384]{1,0:T(8,128)S(1)}, u32[]{:S(2)}, u32[]{:S(2)}) collective-permute-start(f32[72,384]{1,0:T(8,128)S(1)} %get-tuple-element.28), channel_id=1, source_target_pairs={{0,4},{1,5},{2,6},{3,7},{4,0},{5,1},{6,2},{7,3},{8,12},{9,13},{10,... | collective-permute-start | bytes 331784 | tf_op jit(solution)/shard_map/ppermute | solution.py:170
  111.9 5.6 %collective-permute-start.9 = (f32[72,384]{1,0:T(8,128)S(1)}, f32[72,384]{1,0:T(8,128)S(1)}, u32[]{:S(2)}, u32[]{:S(2)}) collective-permute-start(f32[72,384]{1,0:T(8,128)S(1)} %get-tuple-element.28), channel_id=1, source_target_pairs={{0,6},{1,7},{2,4},{3,5},{4,2},{5,3},{6,0},{7,1},{8,14},{9,15},{10,... | collective-permute-start | bytes 331784 | tf_op jit(solution)/shard_map/ppermute | solution.py:170
  117.6 1.9 collective-permute-start.10
  140.5 47.1 %collective-permute-start.11 = (f32[288,896]{1,0:T(8,128)}, f32[288,896]{1,0:T(8,128)S(1)}, u32[]{:S(2)}, u32[]{:S(2)}) collective-permute-start(f32[288,896]{1,0:T(8,128)} %get-tuple-element.20), channel_id=1, source_target_pairs={{0,24},{8,0},{16,8},{24,16},{1,25},{9,1},{17,9},{25,17},{2,26},{10... | collective-permute-start | bytes 3096584 | tf_op jit(solution)/shard_map/ppermute | solution.py:234
  170.1 40.1 %collective-permute-start.12 = (f32[288,896]{1,0:T(8,128)S(1)}, f32[288,896]{1,0:T(8,128)S(1)}, u32[]{:S(2)}, u32[]{:S(2)}) collective-permute-start(f32[288,896]{1,0:T(8,128)S(1)} %get-tuple-element.22), channel_id=1, source_target_pairs={{0,8},{8,16},{16,24},{24,0},{1,9},{9,17},{17,25},{25,1},{2,10},{10... | collective-permute-start | bytes 3096584 | tf_op jit(solution)/shard_map/ppermute | solution.py:234
  170.2 83.7 %collective-permute-start.13 = (f32[288,896]{1,0:T(8,128)S(1)}, f32[288,896]{1,0:T(8,128)S(1)}, u32[]{:S(2)}, u32[]{:S(2)}) collective-permute-start(f32[288,896]{1,0:T(8,128)S(1)} %get-tuple-element.24), channel_id=1, source_target_pairs={{0,16},{8,24},{16,0},{24,8},{1,17},{9,25},{17,1},{25,9},{2,18},{10... | collective-permute-start | bytes 3096584 | tf_op jit(solution)/shard_map/ppermute | solution.py:234

commit v2 on v1

v2 whole, which is shorter than its diff:
```python
import functools
import math

import jax
import jax.numpy as jnp
from jax import lax
from jax.experimental import pallas as pl
from jax.experimental.pallas import tpu as pltpu
from jax.sharding import PartitionSpec as P

WIDTH = 7168
INNER = 576
PANELS = 3
PANEL = INNER // PANELS
TILE = 256
SUBLANES = 8

MOMENTUM_RATE = 0.95
QUINTIC_FIRST = 3.4445
QUINTIC_SECOND = -4.775
QUINTIC_THIRD = 2.0315
EPSILON = 1e-07
OUT_SCALE = 0.2 * math.sqrt(max(INNER, WIDTH))
VMEM_LIMIT = 48 * 1024 * 1024


def halves(value):
    high = value.astype(jnp.bfloat16)
    low = (value - high.astype(jnp.float32)).astype(jnp.bfloat16)
    return high, low


def dot(left, right, contract):
    return lax.dot_general(left, right, (contract, ((), ())), preferred_element_type=jnp.float32)


def dot_halves(left, right, contract=((1,), (0,))):
    (left_high, left_low), (right_high, right_low) = left, right
    return (
        dot(left_high, right_low, contract) + dot(left_low, right_high, contract)
    ) + dot(left_high, right_high, contract)


def aligned(start, slots):
    shift = start % SUBLANES
    return pl.ds(pl.multiple_of(start - shift, SUBLANES), slots + SUBLANES), shift


def matrix_of(owner_group, rank):
    found = jnp.int32(0)
    for matrix in range(owner_group.shape[0]):
        found = jnp.where(owner_group[matrix] == rank, matrix, found)
    return found


def blend_kernel(step, chunks, owner_group, live_ranks, row_counts, momentum, gradient, out, olds, grads, mixed, arrive, leave):
    ranks = live_ranks.shape[0]
    rank = lax.axis_index("fsdp")
    matrix = matrix_of(owner_group, lax.rem(rank + step, ranks))
    count = row_counts[matrix, rank] * live_ranks[rank]
    slots, columns = mixed.shape
    size = slots // chunks

    def part(chunk):
        return pl.ds(chunk * size, size)

    incoming = [
        [
            pltpu.make_async_copy(source.at[matrix, part(chunk)], held.at[part(chunk)], arrive.at[chunk, side])
            for side, (source, held) in enumerate(((momentum, olds), (gradient, grads)))
        ]
        for chunk in range(chunks)
    ]
    outgoing = [
        pltpu.make_async_copy(mixed.at[part(chunk)], out.at[part(chunk)], leave.at[chunk]) for chunk in range(chunks)
    ]
    for pair in incoming:
        for copy in pair:
            copy.start()
    for chunk in range(chunks):
        for copy in incoming[chunk]:
            copy.wait()
        rows = slice(chunk * size, (chunk + 1) * size)
        grad_now = grads[rows, :]
        fresh = MOMENTUM_RATE * olds[rows, :] + grad_now
        position = lax.broadcasted_iota(jnp.int32, (size, columns), 0) + chunk * size
        mixed[rows, :] = jnp.where(position < count, grad_now + MOMENTUM_RATE * fresh, 0.0)
        outgoing[chunk].start()
    for copy in outgoing:
        copy.wait()


def gram_kernel(owner_group, row_offsets, *refs):
    *blocks, high_out, low_out, gram, padded = refs
    slots, columns = blocks[0].shape
    ranks = len(blocks)
    rank = lax.axis_index("fsdp")
    matrix = matrix_of(owner_group, rank)
    padded[...] = jnp.zeros_like(padded)
    tail = jnp.zeros((SUBLANES, columns), jnp.float32)
    for step, block in enumerate(blocks):
        source = lax.rem(rank + ranks - step, ranks)
        rows, shift = aligned(row_offsets[matrix, source], slots)
        moved = pltpu.roll(jnp.concatenate([block[...], tail], axis=0), shift, 0)
        padded[rows, :] = padded[rows, :] + moved
    high, low = halves(padded[:INNER, :])
    high_out[...] = high
    low_out[...] = low
    for panel in range(PANELS):
        here = slice(panel * PANEL, (panel + 1) * PANEL)
        after = (panel + 1) % PANELS
        there = slice(after * PANEL, (after + 1) * PANEL)
        gram[here, :PANEL] = dot_halves((high[here], low[here]), (high[here], low[here]), ((1,), (1,)))
        gram[here, PANEL:] = dot_halves((high[here], low[here]), (high[there], low[there]), ((1,), (1,)))


def symmetric_product(left, right, out):
    for begin in range(0, INNER, TILE):
        end = min(begin + TILE, INNER)
        part = dot_halves(
            tuple(half[begin:] for half in left), tuple(half[:, begin:end] for half in right)
        )
        out[begin:, begin:end] = part
        if end < INNER:
            out[begin:end, end:] = part[end - begin :].T
    return out[...]


def update_kernel(owner_group, live_ranks, row_counts, row_offsets, packed, high, low, result, shards, *refs):
    *sends, gram, padded, held, leave = refs
    ranks, slots, columns = held.shape
    rank = lax.axis_index("fsdp")
    matrix = matrix_of(owner_group, rank)
    for panel in range(PANELS):
        here = slice(panel * PANEL, (panel + 1) * PANEL)
        after = (panel + 1) % PANELS
        there = slice(after * PANEL, (after + 1) * PANEL)
        gram[here, here] = packed[here, :PANEL]
        side = packed[here, PANEL:]
        gram[here, there] = side
        gram[there, here] = side.T
    raw = gram[...]
    diagonal = lax.broadcasted_iota(jnp.int32, raw.shape, 0) == lax.broadcasted_iota(jnp.int32, raw.shape, 1)
    square_total = jnp.sum(jnp.where(diagonal, raw, 0.0))
    norm = jnp.sqrt(jnp.full((1, 1), square_total, jnp.float32)) + EPSILON
    inverse = 1.0 / norm
    first = (raw * inverse) * inverse
    first_halves = halves(first)
    second = symmetric_product(first_halves, first_halves, gram)
    inner = QUINTIC_SECOND * first + QUINTIC_THIRD * second + jnp.where(diagonal, QUINTIC_FIRST, 0.0)
    inner_halves = halves(inner)
    third_halves = halves(symmetric_product(inner_halves, first_halves, gram))
    next_gram = symmetric_product(inner_halves, third_halves, gram)
    next_halves = halves(next_gram)
    outer = (
        QUINTIC_SECOND * next_gram
        + QUINTIC_THIRD * symmetric_product(next_halves, next_halves, gram)
        + jnp.where(diagonal, QUINTIC_FIRST, 0.0)
    )
    total = symmetric_product(halves(outer), inner_halves, gram) * (inverse * OUT_SCALE)
    padded[:INNER, :] = dot_halves(halves(total), (high[...], low[...]))
    copies = [pltpu.make_async_copy(padded.at[pl.ds(0, INNER)], result, leave.at[ranks])]
    copies[0].start()
    position = lax.broadcasted_iota(jnp.int32, (slots, columns), 0)
    for step in [*range(1, ranks), 0]:
        target = lax.rem(rank + step, ranks)
        count = row_counts[matrix, target] * live_ranks[target]
        rows, shift = aligned(row_offsets[matrix, target], slots)
        back = jnp.where(shift == 0, 0, slots + SUBLANES - shift)
        moved = pltpu.roll(padded[rows, :], back, 0)[:slots]
        held[step] = jnp.where(position < count, moved, 0.0)
        place = sends[step - 1] if step else shards.at[matrix]
        copies.append(pltpu.make_async_copy(held.at[step], place, leave.at[step]))
        copies[-1].start()
    for copy in copies:
        copy.wait()


def in_vmem(count):
    return [pl.BlockSpec(memory_space=pltpu.VMEM)] * count


def in_smem(count):
    return [pl.BlockSpec(memory_space=pltpu.SMEM)] * count


def anywhere(count):
    return [pl.BlockSpec(memory_space=pl.ANY)] * count


PARAMS = pltpu.CompilerParams(vmem_limit_bytes=VMEM_LIMIT)


def blend(step, owner_group, live_ranks, row_counts, momentum, gradient):
    _, slots, columns = momentum.shape
    chunks = 4 if slots % (4 * SUBLANES) == 0 else 1
    block = (slots, columns)
    return pl.pallas_call(
        functools.partial(blend_kernel, step, chunks),
        out_shape=jax.ShapeDtypeStruct(block, jnp.float32),
        in_specs=in_smem(3) + anywhere(2),
        out_specs=pl.BlockSpec(memory_space=pl.ANY),
        scratch_shapes=[pltpu.VMEM(block, jnp.float32)] * 3
        + [pltpu.SemaphoreType.DMA((chunks, 2)), pltpu.SemaphoreType.DMA((chunks,))],
        compiler_params=PARAMS,
        cost_estimate=pl.CostEstimate(flops=4 * slots * columns, bytes_accessed=12 * slots * columns, transcendentals=0),
        name="blend",
    )(owner_group, live_ranks, row_counts, momentum, gradient)


def assemble_and_gram(owner_group, row_offsets, blocks):
    slots, columns = blocks[0].shape
    flops = 2 * 3 * INNER * 2 * PANEL * columns
    return pl.pallas_call(
        gram_kernel,
        out_shape=[jax.ShapeDtypeStruct((INNER, columns), jnp.bfloat16)] * 2
        + [jax.ShapeDtypeStruct((INNER, 2 * PANEL), jnp.float32)],
        in_specs=in_smem(2) + in_vmem(len(blocks)),
        out_specs=in_vmem(3),
        scratch_shapes=[pltpu.VMEM((INNER + slots + SUBLANES, columns), jnp.float32)],
        compiler_params=PARAMS,
        cost_estimate=pl.CostEstimate(flops=flops, bytes_accessed=16 * INNER * columns, transcendentals=0),
        name="assemble_and_gram",
    )(owner_group, row_offsets, *blocks)


def apply_update(owner_group, live_ranks, row_counts, row_offsets, packed, high, low, shape):
    ranks, (matrices, slots, columns) = live_ranks.shape[0], shape
    flops = 2 * 3 * INNER * INNER * (5 * INNER + columns)
    return pl.pallas_call(
        update_kernel,
        out_shape=[jax.ShapeDtypeStruct((INNER, columns), jnp.float32), jax.ShapeDtypeStruct(shape, jnp.float32)]
        + [jax.ShapeDtypeStruct((slots, columns), jnp.float32)] * (ranks - 1),
        in_specs=in_smem(4) + in_vmem(3),
        out_specs=anywhere(1 + ranks),
        scratch_shapes=[
            pltpu.VMEM((INNER, INNER), jnp.float32),
            pltpu.VMEM((INNER + slots + SUBLANES, columns), jnp.float32),
            pltpu.VMEM((ranks, slots, columns), jnp.float32),
            pltpu.SemaphoreType.DMA((ranks + 1,)),
        ],
        compiler_params=PARAMS,
        cost_estimate=pl.CostEstimate(flops=flops, bytes_accessed=16 * INNER * columns, transcendentals=0),
        name="apply_update",
    )(owner_group, live_ranks, row_counts, row_offsets, packed, high, low)


def group_stages(size):
    stages, shift = [], 0
    while (1 << shift) < size:
        wide = 1 if shift == 0 or (2 << shift) >= size else 2
        stages.append((shift, 1 << wide))
        shift += wide
    return stages


def sum_over(block, axis):
    size = lax.axis_size(axis)
    if size & (size - 1) or block.shape[0] % size:
        return lax.psum(block, axis)
    index = lax.axis_index(axis)

    def exchange(piece, step):
        return lax.ppermute(piece, axis, [(i, i ^ step) for i in range(size)])

    stages = group_stages(size)
    for shift, group in stages:
        digit = (index >> shift) & (group - 1)
        part = block.shape[0] // group
        pieces = [
            lax.dynamic_slice_in_dim(block, (digit ^ step) * part, part, 0) for step in range(group)
        ]
        arrived = [exchange(pieces[step], step << shift) for step in range(1, group)]
        block = functools.reduce(jnp.add, arrived, pieces[0])
    for shift, group in reversed(stages):
        digit = (index >> shift) & (group - 1)
        part = block.shape[0]
        pieces = [block] + [exchange(block, step << shift) for step in range(1, group)]
        block = jnp.zeros((part * group, block.shape[1]), block.dtype)
        for step, piece in enumerate(pieces):
            block = lax.dynamic_update_slice_in_dim(block, piece, (digit ^ step) * part, 0)
    return block


def on_device(momentum, gradient, live_ranks, owner_group, row_counts, row_offsets):
    ranks = lax.axis_size("fsdp")
    my_rank = lax.axis_index("fsdp")
    slots = momentum.shape[1]
    rank_ids = jnp.arange(ranks, dtype=jnp.int32)

    def passes(step):
        return [(i, (i + step) % ranks) for i in range(ranks)]

    steps = sorted(range(1, ranks), key=lambda step: -min(step, ranks - step))
    blocks = {}
    for step in [*steps, 0]:
        block = blend(step, owner_group, live_ranks, row_counts, momentum, gradient)
        blocks[step] = lax.ppermute(block, "fsdp", passes(step)) if step else block
    own = (rank_ids == my_rank).astype(jnp.int32)
    own_counts = jnp.sum(row_counts * (live_ranks * own)[None, :], axis=1)
    keep_home = (jnp.arange(slots, dtype=jnp.int32)[None, :] < own_counts[:, None])[:, :, None]
    new_momentum = jnp.where(keep_home, MOMENTUM_RATE * momentum + gradient, 0.0)

    high, low, gram_part = assemble_and_gram(owner_group, row_offsets, [blocks[step] for step in range(ranks)])
    packed = sum_over(gram_part, "tensor")
    result, update_shards, *home = apply_update(
        owner_group, live_ranks, row_counts, row_offsets, packed, high, low, momentum.shape
    )
    returned = {step: lax.ppermute(home[step - 1], "fsdp", passes(step)) for step in steps}
    for step in reversed(steps):
        source = lax.rem(my_rank + ranks - step, ranks)
        owned = jnp.sum(jnp.where(owner_group == source, jnp.arange(owner_group.shape[0], dtype=jnp.int32), 0))
        update_shards = lax.dynamic_update_index_in_dim(update_shards, returned[step], owned, 0)
    return (new_momentum, update_shards, result[None])


def solution(mesh):
    placed = (P(None, "fsdp", "tensor"), P(None, "fsdp", "tensor"), P(), P(), P(), P())
    return jax.shard_map(
        on_device,
        mesh=mesh,
        in_specs=placed,
        out_specs=(P(None, "fsdp", "tensor"), P(None, "fsdp", "tensor"), P("fsdp", None, "tensor")),
        check_vma=False,
    )
```

time: 255 us -> 246 us (0.965)
  other arithmetic: 34.8 us -> 4.54 us
  Pallas kernels: 6.61 us -> 36.6 us
  between operations: 14.5 us -> 6.71 us
    pallas_call x0 -> x5, Pallas kernels: none -> 29.7 us  [the longest x1 15.5 us: apply_update(): pl.pallas_call(update_kernel, out_shape=[jax.ShapeDtypeStruct((INNER, col...]
    pallas_call x1 -> x0, other arithmetic: 18.8 us -> none  [apply_update(): pl.pallas_call(update_kernel, out_shape=[jax.ShapeDtypeStruct((INNER, col...]
    unnamed x2 -> x26, local copies, waits for them, and re-layouts: 0.01 us -> 8.34 us
    select_n x2 -> x0, other arithmetic: 5.68 us -> none  [the longest x1 5.67 us: blended(): return jnp.where(keep, grad_now + MOMENTUM_RATE * fresh, 0.0)]
    select_n x1, other arithmetic: 6 us -> 2.57 us  [on_device(): jnp.where(keep_home, MOMENTUM_RATE * momentum + gradient, 0.0)]
    dynamic_update_slice x3, local copies, waits for them, and re-layouts: 3.08 us -> 0.21 us  [on_device(): lax.dynamic_update_index_in_dim(update_shards, returned[step], owned, 0)]
    lt x3 -> x1, other arithmetic: 2.71 us -> 0.07 us  [on_device(): jnp.arange(slots, dtype=jnp.int32)[None, :] < own_counts[:, None]]
  transfers between devices with their start and end apart: 14 -> 14, of which waited for: 13 -> 12; matrix products, arithmetic and copies ran while one was open for 4% -> 2% of each run, Pallas kernels for 0% -> 4%
where the time goes in v2:
time: 246 us; the launch traced here: 245 us
  waiting for transfers between devices  150 us (61%)
  starting transfers between devices  38.6 us (16%)
  Pallas kernels  36.6 us (15%)
  local copies, waits for them, and re-layouts  8.83 us (4%)
  between operations  6.71 us (3%)
  other arithmetic  4.54 us (2%)
    ppermute x3, waiting for transfers between devices, on_device(): lax.ppermute(home[step - 1], 'fsdp', passes(step))  86.4 us
    ppermute x3, waiting for transfers between devices, on_device(): blocks[step] = lax.ppermute(block, 'fsdp', passes(step)) if step else block  52.3 us
    ppermute x3, starting transfers between devices, on_device(): lax.ppermute(home[step - 1], 'fsdp', passes(step))  24.3 us
    pallas_call x1, Pallas kernels, apply_update(): pl.pallas_call(update_kernel, out_shape=[jax.ShapeDtypeStruct((INNER, col...  15.5 us
    pallas_call x4, Pallas kernels, blend(): pl.pallas_call(functools.partial(blend_kernel, step, chunks), out_shape=j...  14.3 us
    ppermute x8, waiting for transfers between devices, exchange(): return lax.ppermute(piece, axis, [(i, i ^ step) for i in range(size)])  11.3 us
    unnamed x26, local copies, waits for them, and re-layouts  8.34 us
    ppermute x8, starting transfers between devices, exchange(): return lax.ppermute(piece, axis, [(i, i ^ step) for i in range(size)])  7.25 us
  transfers between devices with their start and end apart: 14, of which 12 were waited for; matrix products, arithmetic and copies ran while one was open for 2% of the time, Pallas kernels for 4%

profile of v2, /device:TPU:0, one launch (start us, length us, event | category | flops | bytes accessed | tf_op | source)
XLA Modules:
  0.0 245.3 jit_solution(14093331261547666481)
XLA Ops:
  0.6 2.2 copy-done
  4.8 3.6 %blend.5 = f32[288,896]{1,0:T(8,128)S(1)} custom-call(s32[4]{0:T(128)S(1)} %copy-done.5, s32[4]{0:T(128)S(1)} %copy-done.7, s32[4,4]{1,0:T(4,128)S(1)} %copy-done.3, f32[4,288,896]{2,1,0:T(8,128)S(1)} %copy-done, f32[4,288,896]{2,1,0:T(8,128)} %gradient.7), custom_call_target="tpu_custom_call" | custom-call | flops 1032192 | bytes 3096576 | tf_op jit(solution)/shard_map/blend/pallas_call | solution.py:198
  8.4 3.1 %collective-permute-start = (f32[288,896]{1,0:T(8,128)S(1)}, f32[288,896]{1,0:T(8,128)}, u32[]{:S(2)}, u32[]{:S(2)}) collective-permute-start(f32[288,896]{1,0:T(8,128)S(1)} %blend.5), channel_id=1, source_target_pairs={{0,8},{8,16},{16,24},{24,0},{1,9},{9,17},{17,25},{25,1},{2,10},{10... | collective-permute-start | bytes 3096584 | tf_op jit(solution)/shard_map/ppermute | solution.py:298
  11.4 3.6 %blend.6 = f32[288,896]{1,0:T(8,128)S(1)} custom-call(s32[4]{0:T(128)S(1)} %copy-done.5, s32[4]{0:T(128)S(1)} %copy-done.7, s32[4,4]{1,0:T(4,128)S(1)} %copy-done.3, f32[4,288,896]{2,1,0:T(8,128)S(1)} %copy-done, f32[4,288,896]{2,1,0:T(8,128)} %gradient.7), custom_call_target="tpu_custom_call" | custom-call | flops 1032192 | bytes 3096576 | tf_op jit(solution)/shard_map/blend/pallas_call | solution.py:198
  15.1 2.7 %collective-permute-start.1 = (f32[288,896]{1,0:T(8,128)S(1)}, f32[288,896]{1,0:T(8,128)}, u32[]{:S(2)}, u32[]{:S(2)}) collective-permute-start(f32[288,896]{1,0:T(8,128)S(1)} %blend.6), channel_id=1, source_target_pairs={{0,16},{8,24},{16,0},{24,8},{1,17},{9,25},{17,1},{25,9},{2,18},{10... | collective-permute-start | bytes 3096584 | tf_op jit(solution)/shard_map/ppermute | solution.py:298
  17.7 3.6 %blend.7 = f32[288,896]{1,0:T(8,128)S(1)} custom-call(s32[4]{0:T(128)S(1)} %copy-done.5, s32[4]{0:T(128)S(1)} %copy-done.7, s32[4,4]{1,0:T(4,128)S(1)} %copy-done.3, f32[4,288,896]{2,1,0:T(8,128)S(1)} %copy-done, f32[4,288,896]{2,1,0:T(8,128)} %gradient.7), custom_call_target="tpu_custom_call" | custom-call | flops 1032192 | bytes 3096576 | tf_op jit(solution)/shard_map/blend/pallas_call | solution.py:198
  22.7 2.2 copy-done.1
  24.9 3.6 %blend.4.refs_0_ = f32[288,896]{1,0:T(8,128)S(1)} custom-call(s32[4]{0:T(128)S(1)} %copy-done.6, s32[4]{0:T(128)S(1)} %copy-done.8, s32[4,4]{1,0:T(4,128)S(1)} %copy-done.4, f32[4,288,896]{2,1,0:T(8,128)S(1)} %copy-done.1, f32[4,288,896]{2,1,0:T(8,128)} %gradient.7), custom_call_target="tpu_custom_call" | custom-call | flops 1032192 | bytes 3096576 | tf_op jit(solution)/shard_map/blend/pallas_call | solution.py:198
  28.4 8.9 %collective-permute-done.refs_1_ = f32[288,896]{1,0:T(8,128)} collective-permute-done((f32[288,896]{1,0:T(8,128)S(1)}, f32[288,896]{1,0:T(8,128)}, u32[]{:S(2)}, u32[]{:S(2)}) %collective-permute-start) | collective-permute-done | bytes 1032224 | tf_op jit(solution)/shard_map/ppermute | solution.py:298
  37.4 43.4 %collective-permute-done.1.refs_2_ = f32[288,896]{1,0:T(8,128)} collective-permute-done((f32[288,896]{1,0:T(8,128)S(1)}, f32[288,896]{1,0:T(8,128)}, u32[]{:S(2)}, u32[]{:S(2)}) %collective-permute-start.1) | collective-permute-done | bytes 1032224 | tf_op jit(solution)/shard_map/ppermute | solution.py:298
  80.8 6.9 %assemble_and_gram.1 = (bf16[576,896]{1,0:T(8,128)(2,1)S(1)}, bf16[576,896]{1,0:T(8,128)(2,1)S(1)}, f32[576,384]{1,0:T(8,128)S(1)}) custom-call(s32[4]{0:T(128)S(1)} %copy-done.6, s32[4,4]{1,0:T(4,128)S(1)} %copy-done.9, f32[288,896]{1,0:T(8,128)S(1)} %blend.4.refs_0_, f32[288,896]{1,0:T(8,128)} %collective-permute-done.refs_1_, ...), custom_call_target="tpu_custom_call" | custom-call | flops 1189085184 | bytes 8257536 | tf_op jit(solution)/shard_map/assemble_and_gram/pallas_call | solution.py:214
  87.8 1.9 collective-permute-done.3
  90.8 1.6 collective-permute-start.4
  92.3 1.5 collective-permute-start.5
  94.3 1.6 collective-permute-done.4
  95.9 2.6 %collective-permute-done.5 = f32[72,384]{1,0:T(8,128)S(1)} collective-permute-done((f32[72,384]{1,0:T(8,128)S(1)}, f32[72,384]{1,0:T(8,128)S(1)}, u32[]{:S(2)}, u32[]{:S(2)}) %collective-permute-start.5) | collective-permute-done | bytes 110624 | tf_op jit(solution)/shard_map/ppermute | solution.py:264
  103.2 2.0 collective-permute-done.7
  114.2 15.5 %apply_update.1 = (f32[576,896]{1,0:T(8,128)}, f32[4,288,896]{2,1,0:T(8,128)}, f32[288,896]{1,0:T(8,128)S(1)}, f32[288,896]{1,0:T(8,128)S(1)}, f32[288,896]{1,0:T(8,128)S(1)}) custom-call(s32[4]{0:T(128)S(1)} %copy-done.6, s32[4]{0:T(128)S(1)} %copy-done.8, s32[4,4]{1,0:T(4,128)S(1)} %copy-done.4, s32[4,4]{1,0:T(4,128)S(1)} %copy-done.9, ...), custom_call_target="tpu_custom_call" | custom-call | flops 7516717056 | bytes 8257536 | tf_op jit(solution)/shard_map/apply_update/pallas_call | solution.py:230
  129.6 23.6 %collective-permute-start.11 = (f32[288,896]{1,0:T(8,128)S(1)}, f32[288,896]{1,0:T(8,128)S(1)}, u32[]{:S(2)}, u32[]{:S(2)}) collective-permute-start(f32[288,896]{1,0:T(8,128)S(1)} %get-tuple-element.15), channel_id=1, source_target_pairs={{0,24},{8,0},{16,8},{24,16},{1,25},{9,1},{17,9},{25,17},{2,26},{10... | collective-permute-start | bytes 3096584 | tf_op jit(solution)/shard_map/ppermute | solution.py:309
  154.1 2.6 %add_select_fusion = f32[4,288,896]{2,1,0:T(8,128)} fusion(f32[4,288,896]{2,1,0:T(8,128)S(1)} %copy-done.10, f32[4,288,896]{2,1,0:T(8,128)S(1)} %copy-done.2, pred[4,288]{1,0:T(4,128)(4,1)S(1)} %iota_compare_fusion), kind=kLoop, calls=%fused_computation | loop fusion | flops 3096576 | bytes 12387456 | tf_op jit(solution)/shard_map/jit(_where)/select_n | solution.py:302
  156.7 19.8 %collective-permute-done.11 = f32[288,896]{1,0:T(8,128)S(1)} collective-permute-done((f32[288,896]{1,0:T(8,128)S(1)}, f32[288,896]{1,0:T(8,128)S(1)}, u32[]{:S(2)}, u32[]{:S(2)}) %collective-permute-start.11) | collective-permute-done | bytes 1032224 | tf_op jit(solution)/shard_map/ppermute | solution.py:309
  176.5 22.6 %collective-permute-done.12 = f32[288,896]{1,0:T(8,128)S(1)} collective-permute-done((f32[288,896]{1,0:T(8,128)S(1)}, f32[288,896]{1,0:T(8,128)S(1)}, u32[]{:S(2)}, u32[]{:S(2)}) %collective-permute-start.12) | collective-permute-done | bytes 1032224 | tf_op jit(solution)/shard_map/ppermute | solution.py:309
  199.2 44.0 %collective-permute-done.13 = f32[288,896]{1,0:T(8,128)S(1)} collective-permute-done((f32[288,896]{1,0:T(8,128)S(1)}, f32[288,896]{1,0:T(8,128)S(1)}, u32[]{:S(2)}, u32[]{:S(2)}) %collective-permute-start.13) | collective-permute-done | bytes 1032224 | tf_op jit(solution)/shard_map/ppermute | solution.py:309
  243.4 2.0 copy-done.12
  (55 shorter events, 13.8 us)
Async XLA Ops:
  0.6 2.2 copy-start
  8.4 29.0 %collective-permute-start = (f32[288,896]{1,0:T(8,128)S(1)}, f32[288,896]{1,0:T(8,128)}, u32[]{:S(2)}, u32[]{:S(2)}) collective-permute-start(f32[288,896]{1,0:T(8,128)S(1)} %blend.5), channel_id=1, source_target_pairs={{0,8},{8,16},{16,24},{24,0},{1,9},{9,17},{17,25},{25,1},{2,10},{10... | collective-permute-start | bytes 3096584 | tf_op jit(solution)/shard_map/ppermute | solution.py:298
  15.0 7.7 %copy-start.4 = (s32[4,4]{1,0:T(4,128)S(1)}, s32[4,4]{1,0:T(4,128)}, u32[]{:S(2)}) copy-start(s32[4,4]{1,0:T(4,128)} %row_counts.9) | copy-start | bytes 196
  15.0 7.7 %copy-start.6 = (s32[4]{0:T(128)S(1)}, s32[4]{0:T(128)}, u32[]{:S(2)}) copy-start(s32[4]{0:T(128)} %owner_group.11) | copy-start | bytes 52
  15.0 7.7 %copy-start.8 = (s32[4]{0:T(128)S(1)}, s32[4]{0:T(128)}, u32[]{:S(2)}) copy-start(s32[4]{0:T(128)} %live_ranks.9) | copy-start | bytes 52
  15.1 65.7 %collective-permute-start.1 = (f32[288,896]{1,0:T(8,128)S(1)}, f32[288,896]{1,0:T(8,128)}, u32[]{:S(2)}, u32[]{:S(2)}) collective-permute-start(f32[288,896]{1,0:T(8,128)S(1)} %blend.6), channel_id=1, source_target_pairs={{0,16},{8,24},{16,0},{24,8},{1,17},{9,25},{17,1},{25,9},{2,18},{10... | collective-permute-start | bytes 3096584 | tf_op jit(solution)/shard_map/ppermute | solution.py:298
  21.3 59.5 %collective-permute-start.2 = (f32[288,896]{1,0:T(8,128)S(1)}, f32[288,896]{1,0:T(8,128)}, u32[]{:S(2)}, u32[]{:S(2)}) collective-permute-start(f32[288,896]{1,0:T(8,128)S(1)} %blend.7), channel_id=1, source_target_pairs={{0,24},{8,0},{16,8},{24,16},{1,25},{9,1},{17,9},{25,17},{2,26},{10... | collective-permute-start | bytes 3096584 | tf_op jit(solution)/shard_map/ppermute | solution.py:298
  22.7 2.2 copy-start.1
  24.9 55.9 %copy-start.9 = (s32[4,4]{1,0:T(4,128)S(1)}, s32[4,4]{1,0:T(4,128)}, u32[]{:S(2)}) copy-start(s32[4,4]{1,0:T(4,128)} %row_offsets.3) | copy-start | bytes 196
  87.7 2.0 collective-permute-start.3
  90.8 5.2 %collective-permute-start.4 = (f32[72,384]{1,0:T(8,128)S(1)}, f32[72,384]{1,0:T(8,128)S(1)}, u32[]{:S(2)}, u32[]{:S(2)}) collective-permute-start(f32[72,384]{1,0:T(8,128)S(1)} %get-tuple-element.24), channel_id=1, source_target_pairs={{0,2},{1,3},{2,0},{3,1},{4,6},{5,7},{6,4},{7,5},{8,10},{9,11},{10,... | collective-permute-start | bytes 331784 | tf_op jit(solution)/shard_map/ppermute | solution.py:264
  92.3 6.2 %collective-permute-start.5 = (f32[72,384]{1,0:T(8,128)S(1)}, f32[72,384]{1,0:T(8,128)S(1)}, u32[]{:S(2)}, u32[]{:S(2)}) collective-permute-start(f32[72,384]{1,0:T(8,128)S(1)} %get-tuple-element.26), channel_id=1, source_target_pairs={{0,4},{1,5},{2,6},{3,7},{4,0},{5,1},{6,2},{7,3},{8,12},{9,13},{10,... | collective-permute-start | bytes 331784 | tf_op jit(solution)/shard_map/ppermute | solution.py:264
  93.9 5.7 %collective-permute-start.6 = (f32[72,384]{1,0:T(8,128)S(1)}, f32[72,384]{1,0:T(8,128)S(1)}, u32[]{:S(2)}, u32[]{:S(2)}) collective-permute-start(f32[72,384]{1,0:T(8,128)S(1)} %get-tuple-element.25), channel_id=1, source_target_pairs={{0,6},{1,7},{2,4},{3,5},{4,2},{5,3},{6,0},{7,1},{8,14},{9,15},{10,... | collective-permute-start | bytes 331784 | tf_op jit(solution)/shard_map/ppermute | solution.py:264
  99.6 5.6 %collective-permute-start.7 = (f32[72,384]{1,0:T(8,128)S(1)}, f32[72,384]{1,0:T(8,128)S(1)}, u32[]{:S(2)}, u32[]{:S(2)}) collective-permute-start(f32[72,384]{1,0:T(8,128)S(1)} %get-tuple-element.23), channel_id=1, source_target_pairs={{0,2},{1,3},{2,0},{3,1},{4,6},{5,7},{6,4},{7,5},{8,10},{9,11},{10,... | collective-permute-start | bytes 331784 | tf_op jit(solution)/shard_map/ppermute | solution.py:264
  100.9 5.3 %collective-permute-start.8 = (f32[72,384]{1,0:T(8,128)S(1)}, f32[72,384]{1,0:T(8,128)S(1)}, u32[]{:S(2)}, u32[]{:S(2)}) collective-permute-start(f32[72,384]{1,0:T(8,128)S(1)} %get-tuple-element.23), channel_id=1, source_target_pairs={{0,4},{1,5},{2,6},{3,7},{4,0},{5,1},{6,2},{7,3},{8,12},{9,13},{10,... | collective-permute-start | bytes 331784 | tf_op jit(solution)/shard_map/ppermute | solution.py:264
  101.7 5.6 %collective-permute-start.9 = (f32[72,384]{1,0:T(8,128)S(1)}, f32[72,384]{1,0:T(8,128)S(1)}, u32[]{:S(2)}, u32[]{:S(2)}) collective-permute-start(f32[72,384]{1,0:T(8,128)S(1)} %get-tuple-element.23), channel_id=1, source_target_pairs={{0,6},{1,7},{2,4},{3,5},{4,2},{5,3},{6,0},{7,1},{8,14},{9,15},{10,... | collective-permute-start | bytes 331784 | tf_op jit(solution)/shard_map/ppermute | solution.py:264
  107.4 6.7 %collective-permute-start.10 = (f32[288,384]{1,0:T(8,128)S(1)}, f32[288,384]{1,0:T(8,128)S(1)}, u32[]{:S(2)}, u32[]{:S(2)}) collective-permute-start(f32[288,384]{1,0:T(8,128)S(1)} %constant_dynamic-update-slice_fusion.2), channel_id=1, source_target_pairs={{0,1},{1,0},{2,3},{3,2},{4,5},{5,4},{6,7},{7,6},{8,9},{9,8},{10,11... | collective-permute-start | bytes 1327112 | tf_op jit(solution)/shard_map/ppermute | solution.py:264
  114.1 40.0 %copy-start.2 = (f32[4,288,896]{2,1,0:T(8,128)S(1)}, f32[4,288,896]{2,1,0:T(8,128)}, u32[]{:S(2)}) copy-start(f32[4,288,896]{2,1,0:T(8,128)} %momentum.7) | copy-start | bytes 12386308
  114.2 40.0 %copy-start.10 = (f32[4,288,896]{2,1,0:T(8,128)S(1)}, f32[4,288,896]{2,1,0:T(8,128)}, u32[]{:S(2)}) copy-start(f32[4,288,896]{2,1,0:T(8,128)} %gradient.7) | copy-start | bytes 12386308
  129.6 46.8 %collective-permute-start.11 = (f32[288,896]{1,0:T(8,128)S(1)}, f32[288,896]{1,0:T(8,128)S(1)}, u32[]{:S(2)}, u32[]{:S(2)}) collective-permute-start(f32[288,896]{1,0:T(8,128)S(1)} %get-tuple-element.15), channel_id=1, source_target_pairs={{0,24},{8,0},{16,8},{24,16},{1,25},{9,1},{17,9},{25,17},{2,26},{10... | collective-permute-start | bytes 3096584 | tf_op jit(solution)/shard_map/ppermute | solution.py:309
  153.4 45.8 %collective-permute-start.12 = (f32[288,896]{1,0:T(8,128)S(1)}, f32[288,896]{1,0:T(8,128)S(1)}, u32[]{:S(2)}, u32[]{:S(2)}) collective-permute-start(f32[288,896]{1,0:T(8,128)S(1)} %get-tuple-element.16), channel_id=1, source_target_pairs={{0,8},{8,16},{16,24},{24,0},{1,9},{9,17},{17,25},{25,1},{2,10},{10... | collective-permute-start | bytes 3096584 | tf_op jit(solution)/shard_map/ppermute | solution.py:309
  153.5 22.9 %copy-start.11 = (f32[4,288,896]{2,1,0:T(8,128)S(1)}, f32[4,288,896]{2,1,0:T(8,128)}, u32[]{:S(2)}) copy-start(f32[4,288,896]{2,1,0:T(8,128)} %get-tuple-element.14) | copy-start | bytes 12386308
  153.6 89.7 %collective-permute-start.13 = (f32[288,896]{1,0:T(8,128)S(1)}, f32[288,896]{1,0:T(8,128)S(1)}, u32[]{:S(2)}, u32[]{:S(2)}) collective-permute-start(f32[288,896]{1,0:T(8,128)S(1)} %get-tuple-element.17), channel_id=1, source_target_pairs={{0,16},{8,24},{16,0},{24,8},{1,17},{9,25},{17,1},{25,9},{2,18},{10... | collective-permute-start | bytes 3096584 | tf_op jit(solution)/shard_map/ppermute | solution.py:309
  243.3 2.0 copy-start.12
  (3 other events, 2.0 us)

commit v3 on v2

v3 whole, which is shorter than its diff:
```python
import functools
import math

import jax
import jax.numpy as jnp
from jax import lax
from jax.experimental import pallas as pl
from jax.experimental.pallas import tpu as pltpu
from jax.sharding import PartitionSpec as P

WIDTH = 7168
INNER = 576
PANEL = INNER // 3
TILE = 256
SUBLANES = 8

MOMENTUM_RATE = 0.95
QUINTIC_FIRST = 3.4445
QUINTIC_SECOND = -4.775
QUINTIC_THIRD = 2.0315
EPSILON = 1e-07
OUT_SCALE = 0.2 * math.sqrt(max(INNER, WIDTH))
FULL = pltpu.CompilerParams(vmem_limit_bytes=60 * 1024 * 1024)
PARAMS = pltpu.CompilerParams(vmem_limit_bytes=48 * 1024 * 1024)
HBM = pl.BlockSpec(memory_space=pltpu.HBM)
ANY = pl.BlockSpec(memory_space=pl.ANY)
VMEM = pl.BlockSpec(memory_space=pltpu.VMEM)


def halves(value):
    high = value.astype(jnp.bfloat16)
    low = (value - high.astype(jnp.float32)).astype(jnp.bfloat16)
    return high, low


def dot(left, right, contract):
    return lax.dot_general(left, right, (contract, ((), ())), preferred_element_type=jnp.float32)


def dot_halves(left, right, contract=((1,), (0,))):
    (left_high, left_low), (right_high, right_low) = left, right
    return (
        dot(left_high, right_low, contract) + dot(left_low, right_high, contract)
    ) + dot(left_high, right_high, contract)


def in_phase(rank, ranks, inner):
    low = ranks // 4
    return ((rank >= low) & (rank < ranks - low)) == inner


def table_scratch(matrices, ranks):
    return [
        pltpu.SMEM((matrices,), jnp.int32),
        pltpu.SMEM((ranks,), jnp.int32),
        pltpu.SMEM((matrices, ranks), jnp.int32),
        pltpu.SMEM((matrices, ranks), jnp.int32),
        pltpu.SemaphoreType.DMA((4,)),
    ]


def fetch_tables(tables, held):
    *places, arrive = held
    copies = [
        pltpu.make_async_copy(table, place, arrive.at[index])
        for index, (table, place) in enumerate(zip(tables, places))
    ]
    for copy in copies:
        copy.start()
    for copy in copies:
        copy.wait()
    return places


def matrix_of(owner_group, rank):
    found = jnp.int32(0)
    for matrix in range(owner_group.shape[0]):
        found = jnp.where(owner_group[matrix] == rank, matrix, found)
    return found


def send_step(place, ranks, inner):
    return (place + ranks - 3) % (ranks - 1) + 1 if inner else place


def blend_kernel(places, chunks, *refs):
    tables, (momentum, gradient) = refs[:4], refs[4:6]
    *outs, token, olds, grads, arrive = refs[-len(places) - 9 : -5]
    owner_group, live_ranks, row_counts, _ = fetch_tables(tables, refs[-5:])
    rank, ranks = lax.axis_index("fsdp"), live_ranks.shape[0]
    slots, columns = outs[0].shape
    size = slots // chunks
    incoming, counts = [], []
    for index, place in enumerate(places):
        early, late = (send_step(place, ranks, inner) for inner in (True, False))
        matrix = matrix_of(owner_group, rank ^ jnp.where(in_phase(rank, ranks, True), early, late))
        counts.append(row_counts[matrix, rank] * live_ranks[rank])
        for chunk in range(chunks):
            part = pl.ds(chunk * size, size)
            for side, (source, kept) in enumerate(((momentum, olds), (gradient, grads))):
                flag = arrive.at[index * chunks + chunk, side]
                incoming.append(pltpu.make_async_copy(source.at[matrix, part], kept.at[index, part], flag))
                incoming[-1].start()
    token[...] = jnp.zeros_like(token)
    for index, out in enumerate(outs):
        for chunk in range(chunks):
            first = 2 * (index * chunks + chunk)
            for copy in incoming[first : first + 2]:
                copy.wait()
            rows = slice(chunk * size, (chunk + 1) * size)
            grad_now = grads[index, rows, :]
            fresh = MOMENTUM_RATE * olds[index, rows, :] + grad_now
            position = lax.broadcasted_iota(jnp.int32, (size, columns), 0) + chunk * size
            out[rows, :] = jnp.where(position < counts[index], grad_now + MOMENTUM_RATE * fresh, 0.0)


def home_kernel(owner_group, live_ranks, row_counts, momentum, gradient, fresh_out, own):
    rank, matrix = lax.axis_index("fsdp"), pl.program_id(0)
    grad_now = gradient[...]
    position = lax.broadcasted_iota(jnp.int32, grad_now.shape, 0)
    keep = position < row_counts[matrix, rank] * live_ranks[rank]
    fresh = jnp.where(keep, MOMENTUM_RATE * momentum[...] + grad_now, 0.0)
    fresh_out[...] = fresh

    @pl.when(owner_group[matrix] == rank)
    def _():
        own[...] = jnp.where(keep, grad_now + MOMENTUM_RATE * fresh, 0.0)


def gram_kernel(ranks, *refs):
    tables, blocks, refs = refs[:4], refs[4 : 4 + ranks], refs[4 + ranks :]
    high_out, low_out, gram, landed, padded, arrive = refs[:6]
    held = refs[6:]
    rank = lax.axis_index("fsdp")
    slots, columns = blocks[0].shape
    copies = []
    for step in range(ranks):
        copies.append(pltpu.make_async_copy(blocks[step], landed.at[step], arrive.at[step]))
        copies[-1].start()
    owner_group, _, _, row_offsets = fetch_tables(tables, held)
    matrix = matrix_of(owner_group, rank)
    padded[...] = jnp.zeros_like(padded)
    sublane = lax.broadcasted_iota(jnp.int32, (SUBLANES, columns), 0)
    for step in range(ranks):
        start = row_offsets[matrix, rank ^ step]
        shift = start % SUBLANES
        base = start - shift
        copies[step].wait()

        def tile(index, before, base=base, shift=shift, step=step):
            moved = pltpu.roll(landed[step, pl.ds(pl.multiple_of(index * SUBLANES, SUBLANES), SUBLANES), :], shift, 0)
            rows = pl.ds(pl.multiple_of(base + index * SUBLANES, SUBLANES), SUBLANES)
            padded[rows, :] = padded[rows, :] + jnp.where(sublane < shift, before, moved)
            return moved

        after = lax.fori_loop(0, slots // SUBLANES, tile, jnp.zeros((SUBLANES, columns), jnp.float32))
        rows = pl.ds(pl.multiple_of(base + slots, SUBLANES), SUBLANES)
        padded[rows, :] = padded[rows, :] + jnp.where(sublane < shift, after, 0.0)
    high, low = halves(padded[:INNER, :])
    high_out[...] = high
    low_out[...] = low
    for panel in range(3):
        here = slice(panel * PANEL, (panel + 1) * PANEL)
        part = dot_halves((high[panel * PANEL :], low[panel * PANEL :]), (high[here], low[here]), ((1,), (1,)))
        if panel == 0:
            gram[:, :PANEL] = part
        elif panel == 1:
            gram[: 2 * PANEL, PANEL:] = part
        else:
            gram[2 * PANEL :, PANEL:] = part


def symmetric_product(left, right, out):
    for begin in range(0, INNER, TILE):
        end = min(begin + TILE, INNER)
        part = dot_halves(tuple(half[begin:] for half in left), tuple(half[:, begin:end] for half in right))
        out[begin:, begin:end] = part
        if end < INNER:
            out[begin:end, end:] = part[end - begin :].T
    return out[...]


def update_kernel(ranks, *refs):
    tables, (packed, high, low, result), refs = refs[:4], refs[4:8], refs[8:]
    homes, refs = refs[:ranks], refs[ranks:]
    gram, padded, staged, leave = refs[:4]
    held = refs[4:]
    _, slots, columns = staged.shape
    rank = lax.axis_index("fsdp")
    owner_group, live_ranks, row_counts, row_offsets = fetch_tables(tables, held)
    matrix = matrix_of(owner_group, rank)
    gram[:, :PANEL] = packed[:, :PANEL]
    gram[PANEL:, PANEL : 2 * PANEL] = packed[: 2 * PANEL, PANEL:]
    gram[2 * PANEL :, 2 * PANEL :] = packed[2 * PANEL :, PANEL:]
    gram[:PANEL, PANEL:] = packed[PANEL:, :PANEL].T
    gram[PANEL : 2 * PANEL, 2 * PANEL :] = packed[PANEL : 2 * PANEL, PANEL:].T
    raw = gram[...]
    diagonal = lax.broadcasted_iota(jnp.int32, raw.shape, 0) == lax.broadcasted_iota(jnp.int32, raw.shape, 1)
    square_total = jnp.sum(jnp.where(diagonal, raw, 0.0))
    norm = jnp.sqrt(jnp.full((1, 1), square_total, jnp.float32)) + EPSILON
    inverse = 1.0 / norm
    first = (raw * inverse) * inverse
    first_halves = halves(first)
    second = symmetric_product(first_halves, first_halves, gram)
    base = QUINTIC_SECOND * first + QUINTIC_THIRD * second + jnp.where(diagonal, QUINTIC_FIRST, 0.0)
    base_halves = halves(base)
    third_halves = halves(symmetric_product(base_halves, first_halves, gram))
    next_gram = symmetric_product(base_halves, third_halves, gram)
    next_halves = halves(next_gram)
    outer = (
        QUINTIC_SECOND * next_gram
        + QUINTIC_THIRD * symmetric_product(next_halves, next_halves, gram)
        + jnp.where(diagonal, QUINTIC_FIRST, 0.0)
    )
    total = symmetric_product(halves(outer), base_halves, gram) * (inverse * OUT_SCALE)
    padded[:INNER, :] = dot_halves(halves(total), (high[...], low[...]))
    copies = [pltpu.make_async_copy(padded.at[pl.ds(0, INNER)], result, leave.at[ranks])]
    copies[0].start()
    sublane = lax.broadcasted_iota(jnp.int32, (SUBLANES, columns), 0)
    for step in [*range(ranks - 1, 0, -1), 0]:
        target = rank ^ step
        count = row_counts[matrix, target] * live_ranks[target]
        start = row_offsets[matrix, target]
        shift = start % SUBLANES
        first_row = start - shift
        back = jnp.where(shift == 0, 0, SUBLANES - shift)

        def window(index, first_row=first_row, back=back):
            rows = pl.ds(pl.multiple_of(first_row + index * SUBLANES, SUBLANES), SUBLANES)
            return pltpu.roll(padded[rows, :], back, 0)

        def tile(index, here, step=step, count=count, shift=shift, window=window):
            after = window(index + 1)
            moved = jnp.where(sublane < SUBLANES - shift, here, after)
            rows = pl.ds(pl.multiple_of(index * SUBLANES, SUBLANES), SUBLANES)
            staged[step, rows, :] = jnp.where(sublane < count - index * SUBLANES, moved, 0.0)
            return after

        lax.fori_loop(0, slots // SUBLANES, tile, window(0))
        copies.append(pltpu.make_async_copy(staged.at[step], homes[step], leave.at[step]))
        copies[-1].start()
    for copy in copies:
        copy.wait()


def each_copy(copies, action):
    for condition, source, place, flag in copies:

        @pl.when(condition)
        def _(source=source, place=place, flag=flag):
            getattr(pltpu.make_async_copy(source, place, flag), action)()


def first_place_kernel(ranks, table, inner_result, outer_result, inner_own, outer_own, result, shards, *refs):
    owner_group, arrive, leave = refs
    rank = lax.axis_index("fsdp")
    fetch = pltpu.make_async_copy(table, owner_group, arrive)
    fetch.start()
    fetch.wait()
    matrix = matrix_of(owner_group, rank)
    copies = []
    for inner, update, own in ((True, inner_result, inner_own), (False, outer_result, outer_own)):
        mine = in_phase(rank, ranks, inner)
        copies += [(mine, update, result, leave.at[0]), (mine, own, shards.at[matrix], leave.at[1])]
    each_copy(copies, "start")
    each_copy(copies, "wait")


def place_kernel(inner, ranks, steps, *refs):
    table, blocks, shards = refs[0], refs[1 : 1 + len(steps)], refs[2 + len(steps)]
    owner_group, arrive, leave = refs[3 + len(steps) :]
    rank = lax.axis_index("fsdp")
    fetch = pltpu.make_async_copy(table, owner_group, arrive)
    fetch.start()
    fetch.wait()
    copies = [
        (
            in_phase(rank ^ step, ranks, inner),
            blocks[order],
            shards.at[matrix_of(owner_group, rank ^ step)],
            leave.at[order],
        )
        for order, step in enumerate(steps)
    ]
    each_copy(copies, "start")
    each_copy(copies, "wait")


def idle_kernel(*refs):
    pass


def blend(places, tables, momentum, gradient, before):
    _, slots, columns = momentum.shape
    chunks = 4 if slots % (4 * SUBLANES) == 0 else 1
    held = (len(places), slots, columns)
    return pl.pallas_call(
        functools.partial(blend_kernel, places, chunks),
        out_shape=[jax.ShapeDtypeStruct((slots, columns), jnp.float32)] * len(places)
        + [jax.ShapeDtypeStruct((SUBLANES, 128), jnp.float32)],
        in_specs=[HBM] * 6 + [ANY] * len(before),
        out_specs=[VMEM] * (len(places) + 1),
        scratch_shapes=[pltpu.VMEM(held, jnp.float32)] * 2
        + [pltpu.SemaphoreType.DMA((len(places) * chunks, 2))]
        + table_scratch(*tables[2].shape),
        compiler_params=FULL,
        cost_estimate=pl.CostEstimate(flops=0, bytes_accessed=0, transcendentals=0),
        name="blend",
    )(*tables, momentum, gradient, *before)


def home(tables, momentum, gradient, before):
    matrices, slots, columns = momentum.shape
    block = pl.BlockSpec((None, slots, columns), lambda matrix: (matrix, 0, 0))

    def body(*refs):
        home_kernel(*refs[:5], *refs[-2:])

    return pl.pallas_call(
        body,
        grid=(matrices,),
        out_shape=[
            jax.ShapeDtypeStruct(momentum.shape, jnp.float32),
            jax.ShapeDtypeStruct((slots, columns), jnp.float32),
        ],
        in_specs=[pl.BlockSpec(memory_space=pltpu.SMEM)] * 3 + [block] * 2 + [ANY],
        out_specs=[block, pl.BlockSpec((slots, columns), lambda matrix: (0, 0))],
        compiler_params=FULL,
        cost_estimate=pl.CostEstimate(flops=0, bytes_accessed=0, transcendentals=0),
        name="home",
    )(*tables[:3], momentum, gradient, before)


def assemble_and_gram(tables, blocks):
    slots, columns = blocks[0].shape
    ranks = len(blocks)
    flops = 2 * 3 * INNER * 2 * PANEL * columns
    return pl.pallas_call(
        functools.partial(gram_kernel, ranks),
        out_shape=[jax.ShapeDtypeStruct((INNER, columns), jnp.bfloat16)] * 2
        + [jax.ShapeDtypeStruct((INNER, 2 * PANEL), jnp.float32)],
        in_specs=[HBM] * 4 + [ANY] * ranks,
        out_specs=[VMEM] * 3,
        scratch_shapes=[
            pltpu.VMEM((ranks, slots, columns), jnp.float32),
            pltpu.VMEM((INNER + slots + SUBLANES, columns), jnp.float32),
            pltpu.SemaphoreType.DMA((ranks,)),
        ]
        + table_scratch(*tables[2].shape),
        compiler_params=PARAMS,
        cost_estimate=pl.CostEstimate(flops=flops, bytes_accessed=16 * INNER * columns, transcendentals=0),
        name="assemble_and_gram",
    )(*tables, *blocks)


def update_shapes(ranks, slots, columns):
    return [jax.ShapeDtypeStruct((INNER, columns), jnp.float32)] + [
        jax.ShapeDtypeStruct((slots, columns), jnp.float32)
    ] * ranks


def apply_update(tables, packed, high, low, slots):
    ranks, columns = tables[1].shape[0], high.shape[1]
    flops = 2 * 3 * INNER * INNER * (5 * INNER + columns)
    return pl.pallas_call(
        functools.partial(update_kernel, ranks),
        out_shape=update_shapes(ranks, slots, columns),
        in_specs=[HBM] * 4 + [VMEM] * 3,
        out_specs=[ANY] * (1 + ranks),
        scratch_shapes=[
            pltpu.VMEM((INNER, INNER), jnp.float32),
            pltpu.VMEM((INNER + slots + 2 * SUBLANES, columns), jnp.float32),
            pltpu.VMEM((ranks, slots, columns), jnp.float32),
            pltpu.SemaphoreType.DMA((ranks + 1,)),
        ]
        + table_scratch(*tables[2].shape),
        compiler_params=PARAMS,
        cost_estimate=pl.CostEstimate(flops=flops, bytes_accessed=16 * INNER * columns, transcendentals=0),
        name="apply_update",
    )(*tables, packed, high, low)


def nothing(ranks, slots, columns):
    return pl.pallas_call(
        idle_kernel,
        out_shape=update_shapes(ranks, slots, columns),
        out_specs=[ANY] * (1 + ranks),
        name="nothing",
    )()


def first_place(owner_group, results, owns, shape, ranks):
    return pl.pallas_call(
        functools.partial(first_place_kernel, ranks),
        out_shape=[
            jax.ShapeDtypeStruct(results[0].shape, jnp.float32),
            jax.ShapeDtypeStruct(shape, jnp.float32),
        ],
        in_specs=[HBM] + [ANY] * 4,
        out_specs=[HBM] * 2,
        scratch_shapes=[
            pltpu.SMEM(owner_group.shape, jnp.int32),
            pltpu.SemaphoreType.DMA(()),
            pltpu.SemaphoreType.DMA((2,)),
        ],
        compiler_params=PARAMS,
        cost_estimate=pl.CostEstimate(flops=0, bytes_accessed=8 * results[0].size, transcendentals=0),
        name="first_place",
    )(owner_group, *results, *owns)


def place_blocks(inner, owner_group, steps, blocks, shards, ranks):
    return pl.pallas_call(
        functools.partial(place_kernel, inner, ranks, steps),
        out_shape=jax.ShapeDtypeStruct(shards.shape, shards.dtype),
        in_specs=[HBM] + [ANY] * len(blocks) + [HBM],
        out_specs=HBM,
        scratch_shapes=[
            pltpu.SMEM(owner_group.shape, jnp.int32),
            pltpu.SemaphoreType.DMA(()),
            pltpu.SemaphoreType.DMA((len(steps),)),
        ],
        input_output_aliases={1 + len(blocks): 0},
        compiler_params=PARAMS,
        cost_estimate=pl.CostEstimate(flops=0, bytes_accessed=8 * blocks[0].size, transcendentals=0),
        name="place_blocks",
    )(owner_group, *blocks, shards)


def group_stages(size):
    stages, shift = [], 0
    while (1 << shift) < size:
        wide = 1 if shift == 0 or (2 << shift) >= size else 2
        stages.append((shift, 1 << wide))
        shift += wide
    return stages


def sum_over(block, axis):
    size = lax.axis_size(axis)
    if size & (size - 1) or block.shape[0] % size:
        return lax.psum(block, axis)
    index = lax.axis_index(axis)

    def exchange(piece, step):
        return lax.ppermute(piece, axis, [(i, i ^ step) for i in range(size)])

    stages = group_stages(size)
    for shift, group in stages:
        digit = (index >> shift) & (group - 1)
        part = block.shape[0] // group
        pieces = [lax.dynamic_slice_in_dim(block, (digit ^ step) * part, part, 0) for step in range(group)]
        arrived = [exchange(pieces[step], step << shift) for step in range(1, group)]
        block = functools.reduce(jnp.add, arrived, pieces[0])
    for shift, group in reversed(stages):
        digit = (index >> shift) & (group - 1)
        part = block.shape[0]
        pieces = [block] + [exchange(block, step << shift) for step in range(1, group)]
        block = jnp.zeros((part * group, block.shape[1]), block.dtype)
        for step, piece in enumerate(pieces):
            block = lax.dynamic_update_slice_in_dim(block, piece, (digit ^ step) * part, 0)
    return block


def on_device(momentum, gradient, live_ranks, owner_group, row_counts, row_offsets):
    ranks = lax.axis_size("fsdp")
    my_rank = lax.axis_index("fsdp")
    slots = momentum.shape[1]
    tables = (owner_group, live_ranks, row_counts, row_offsets)
    steps = list(range(1, ranks))

    def inside(rank, inner):
        return bool(in_phase(rank, ranks, inner))

    *blends, token = blend(steps[:-1], tables, momentum, gradient, [])
    last, token = blend(steps[-1:], tables, momentum, gradient, [token])
    blends.append(last)

    sent = {}
    for place in steps:
        for kind in (False, True, "cross"):
            pairs = []
            for i in range(ranks):
                target = i ^ send_step(place, ranks, inside(i, True))
                same = inside(i, True) == inside(target, True)
                if (kind == "cross" and not same) or (same and inside(i, True) == kind):
                    pairs.append((i, target))
            if pairs:
                sent[place, kind] = lax.ppermute(blends[place - 1], "fsdp", pairs)

    def received(step, inner):
        whole = None
        for source in (False, True):
            if any(inside(i, inner) and inside(i ^ step, source) for i in range(ranks)):
                place = next(place for place in steps if send_step(place, ranks, source) == step)
                part = sent[place, inner if source == inner else "cross"]
                pick = in_phase(my_rank ^ step, ranks, source)
                whole = part if whole is None else jnp.where(pick, part, whole)
        return whole

    def to_home(block, step, inner):
        return lax.ppermute(block, "fsdp", [(i, i ^ step) for i in range(ranks) if inside(i, inner)])

    new_momentum, own_block = home(tables, momentum, gradient, token)
    owner_blocks = {inner: [own_block] + [received(step, inner) for step in steps] for inner in (True, False)}

    def compute(blocks):
        high, low, gram_part = assemble_and_gram(tables, blocks)
        return apply_update(tables, sum_over(gram_part, "tensor"), high, low, slots)

    def skip(blocks):
        return nothing(ranks, *blocks[0].shape)

    results, owns, returned = [], [], {}
    for inner in (True, False):
        result, *homes = lax.cond(in_phase(my_rank, ranks, inner), compute, skip, owner_blocks[inner])
        results.append(result)
        owns.append(homes[0])
        returned[inner] = {step: to_home(homes[step], step, inner) for step in steps}
    result, shards = first_place(owner_group, results, owns, momentum.shape, ranks)
    shards = place_blocks(True, owner_group, steps, [returned[True][step] for step in steps], shards, ranks)
    for step in steps:
        shards = place_blocks(False, owner_group, [step], [returned[False][step]], shards, ranks)
    return (new_momentum, shards, result[None])


def solution(mesh):
    placed = (P(None, "fsdp", "tensor"), P(None, "fsdp", "tensor"), P(), P(), P(), P())
    return jax.shard_map(
        on_device,
        mesh=mesh,
        in_specs=placed,
        out_specs=(P(None, "fsdp", "tensor"), P(None, "fsdp", "tensor"), P("fsdp", None, "tensor")),
        check_vma=False,
    )
```

time: 246 us -> 254 us (1.033)
  Pallas kernels: 36.6 us -> 133 us
  waiting for transfers between devices: 150 us -> 82.8 us
  starting transfers between devices: 38.6 us -> 31.8 us
  local copies, waits for them, and re-layouts: 8.83 us -> 2.94 us
  between operations: 6.71 us -> 1.06 us
    pallas_call x6 -> x11, Pallas kernels: 36.6 us -> 133 us  [the longest x1 95.5 us: first_place(): pl.pallas_call(functools.partial(first_place_kernel, ranks), out_shape=[j...]
    ppermute x6 -> x11, waiting for transfers between devices: 139 us -> 67.8 us  [the longest x5 67.8 us: on_device(): sent[place, kind] = lax.ppermute(blends[place - 1], 'fsdp', pairs)]
    unnamed x26 -> x8, local copies, waits for them, and re-layouts: 8.34 us -> 0.02 us
    ppermute x6 -> x11, starting transfers between devices: 31.4 us -> 24.6 us  [the longest x5 14.2 us: on_device(): sent[place, kind] = lax.ppermute(blends[place - 1], 'fsdp', pairs)]
    ppermute x8, waiting for transfers between devices: 11.3 us -> 15 us  [exchange(): return lax.ppermute(piece, axis, [(i, i ^ step) for i in range(size)])]
    select_n x1 -> x0, other arithmetic: 2.57 us -> none  [on_device(): jnp.where(keep_home, MOMENTUM_RATE * momentum + gradient, 0.0)]
  transfers between devices with their start and end apart: 14 -> 19, of which waited for: 12 -> 11; matrix products, arithmetic and copies ran while one was open for 2% -> 1% of each run, Pallas kernels for 4% -> 50%
where the time goes in v3:
time: 254 us
  Pallas kernels  133 us (52%)
  waiting for transfers between devices  82.8 us (33%)
  starting transfers between devices  31.8 us (13%)
  local copies, waits for them, and re-layouts  2.94 us (1%)
    pallas_call x1, Pallas kernels, first_place(): pl.pallas_call(functools.partial(first_place_kernel, ranks), out_shape=[j...  95.5 us
    ppermute x5, waiting for transfers between devices, on_device(): sent[place, kind] = lax.ppermute(blends[place - 1], 'fsdp', pairs)  67.8 us
    ppermute x8, waiting for transfers between devices, exchange(): return lax.ppermute(piece, axis, [(i, i ^ step) for i in range(size)])  15 us
    ppermute x5, starting transfers between devices, on_device(): sent[place, kind] = lax.ppermute(blends[place - 1], 'fsdp', pairs)  14.2 us
    pallas_call x1, Pallas kernels, apply_update(): pl.pallas_call(functools.partial(update_kernel, ranks), out_shape=update_...  13.8 us
    ppermute x6, starting transfers between devices, to_home(): lax.ppermute(block, 'fsdp', [(i, i ^ step) for i in range(ranks) if insid...  10.4 us
    pallas_call x2, Pallas kernels, blend(): pl.pallas_call(functools.partial(blend_kernel, places, chunks), out_shape...  8.04 us
    ppermute x8, starting transfers between devices, exchange(): return lax.ppermute(piece, axis, [(i, i ^ step) for i in range(size)])  7.2 us
  transfers between devices with their start and end apart: 19, of which 11 were waited for; matrix products, arithmetic and copies ran while one was open for 1% of the time, Pallas kernels for 50%

profile of v3, /device:TPU:0, one launch (start us, length us, event | category | flops | bytes accessed | tf_op | source)
XLA Modules:
  0.0 253.9 jit_solution(12878173329324166299)
XLA Ops:
  0.7 4.6 %blend.2 = (f32[288,896]{1,0:T(8,128)}, f32[288,896]{1,0:T(8,128)}, f32[8,128]{1,0:T(8,128)}) custom-call(s32[4]{0:T(128)} %refs_0_.13, s32[4]{0:T(128)} %refs_1_.5, s32[4,4]{1,0:T(4,128)} %refs_2_.5, s32[4,4]{1,0:T(4,128)} %refs_3_.4, f32[4,288,896]{2,1,0:T(8,128)} %refs_3_.5, f32[4,288,896]{2,1,0:T(8,128)} %refs_4_.5), custom_call_target="tpu_custom_call" | custom-call | tf_op jit(solution)/shard_map/blend/pallas_call | solution.py:297
  5.3 4.1 %collective-permute-start.16 = (f32[288,896]{1,0:T(8,128)}, f32[288,896]{1,0:T(8,128)}, u32[]{:S(2)}, u32[]{:S(2)}) collective-permute-start(f32[288,896]{1,0:T(8,128)} %get-tuple-element.80), channel_id=1, source_target_pairs={{0,16},{8,0},{16,24},{24,8},{1,17},{9,1},{17,25},{25,9},{2,18},{10... | collective-permute-start | bytes 3096584 | tf_op jit(solution)/shard_map/ppermute | solution.py:489
  10.1 5.3 %collective-permute-start.22 = (f32[288,896]{1,0:T(8,128)}, f32[288,896]{1,0:T(8,128)S(1)}, u32[]{:S(2)}, u32[]{:S(2)}) collective-permute-start(f32[288,896]{1,0:T(8,128)} %get-tuple-element.85), channel_id=1, source_target_pairs={{0,8},{24,16},{1,9},{25,17},{2,10},{26,18},{3,11},{27,19},{4,12},{... | collective-permute-start | bytes 3096584 | tf_op jit(solution)/shard_map/ppermute | solution.py:489
  15.5 3.4 %blend.3 = (f32[288,896]{1,0:T(8,128)}, f32[8,128]{1,0:T(8,128)}) custom-call(s32[4]{0:T(128)S(1)} %copy-done.4, s32[4]{0:T(128)S(1)} %copy-done.7, s32[4,4]{1,0:T(4,128)S(1)} %copy-done.5, s32[4,4]{1,0:T(4,128)S(1)} %copy-done.6, f32[4,288,896]{2,1,0:T(8,128)} %refs_3_.5, f32[4,288,896]{2,1,0:T(8,128)} %refs_4_.5, f32[8,128]{1,0:T(8,128)} %get-tuple-element.76.refs_6_), custom_call_target="tpu_custom_call" | custom-call | tf_op jit(solution)/shard_map/blend/pallas_call | solution.py:297
  18.9 2.8 %collective-permute-start.18 = (f32[288,896]{1,0:T(8,128)}, f32[288,896]{1,0:T(8,128)}, u32[]{:S(2)}, u32[]{:S(2)}) collective-permute-start(f32[288,896]{1,0:T(8,128)} %get-tuple-element.81), channel_id=1, source_target_pairs={{0,24},{24,0},{1,25},{25,1},{2,26},{26,2},{3,27},{27,3},{4,28},{28... | collective-permute-start | bytes 3096584 | tf_op jit(solution)/shard_map/ppermute | solution.py:489
  23.0 6.5 %home.1 = (f32[4,288,896]{2,1,0:T(8,128)}, f32[288,896]{1,0:T(8,128)}) custom-call(s32[4]{0:T(128)S(1)} %copy-done.4, s32[4]{0:T(128)S(1)} %copy-done.7, s32[4,4]{1,0:T(4,128)S(1)} %copy-done.5, f32[4,288,896]{2,1,0:T(8,128)} %refs_3_.5, f32[4,288,896]{2,1,0:T(8,128)} %refs_4_.5, f32[8,128]{1,0:T(8,128)} %get-tuple-element.77.refs_5_), custom_call_target="tpu_custom_call" | custom-call | tf_op jit(solution)/shard_map/home/pallas_call | solution.py:319
  29.5 3.5 %collective-permute-done.16 = f32[288,896]{1,0:T(8,128)} collective-permute-done((f32[288,896]{1,0:T(8,128)}, f32[288,896]{1,0:T(8,128)}, u32[]{:S(2)}, u32[]{:S(2)}) %collective-permute-start.16) | collective-permute-done | bytes 1032224 | tf_op jit(solution)/shard_map/ppermute | solution.py:489
  33.0 22.1 %collective-permute-done.22 = f32[288,896]{1,0:T(8,128)S(1)} collective-permute-done((f32[288,896]{1,0:T(8,128)}, f32[288,896]{1,0:T(8,128)S(1)}, u32[]{:S(2)}, u32[]{:S(2)}) %collective-permute-start.22) | collective-permute-done | bytes 1032224 | tf_op jit(solution)/shard_map/ppermute | solution.py:489
  57.7 20.3 %collective-permute-done.18 = f32[288,896]{1,0:T(8,128)} collective-permute-done((f32[288,896]{1,0:T(8,128)}, f32[288,896]{1,0:T(8,128)}, u32[]{:S(2)}, u32[]{:S(2)}) %collective-permute-start.18) | collective-permute-done | bytes 1032224 | tf_op jit(solution)/shard_map/ppermute | solution.py:489
  78.0 22.0 %collective-permute-done.17 = f32[288,896]{1,0:T(8,128)} collective-permute-done((f32[288,896]{1,0:T(8,128)}, f32[288,896]{1,0:T(8,128)}, u32[]{:S(2)}, u32[]{:S(2)}) %collective-permute-start.17) | collective-permute-done | bytes 1032224 | tf_op jit(solution)/shard_map/ppermute | solution.py:489
  99.9 45.8 %conditional.2 = ((f32[576,896]{1,0:T(8,128)}, f32[288,896]{1,0:T(8,128)}, f32[288,896]{1,0:T(8,128)}, f32[288,896]{1,0:T(8,128)}, f32[288,896]{1,0:T(8,128)})) conditional(s32[]{:T(128)} %convert_element_type.6, () %tuple.20, (s32[4]{0:T(128)S(1)}, s32[4]{0:T(128)S(1)}, s32[4,4]{1,0:T(4,128)S(1)}, s32[4,4]{1,0:T(4,128)S(1)}, f32[288,896]{1,0:T(8,128)}, ...), branch_computations={%region_0.0_spmd, %region_1.0_spmd} | conditional | flops 8705995776 | bytes 46523252 | solution.py:516
  99.9 4.7 %assemble_and_gram.2 = (bf16[576,896]{1,0:T(8,128)(2,1)S(1)}, bf16[576,896]{1,0:T(8,128)(2,1)S(1)}, f32[576,384]{1,0:T(8,128)S(1)}) custom-call(s32[4]{0:T(128)S(1)} %get-tuple-element.32.refs_0_, s32[4]{0:T(128)S(1)} %get-tuple-element.33.refs_1_, s32[4,4]{1,0:T(4,128)S(1)} %get-tuple-element.34.refs_2_, s32[4,4]{1,0:T(4,128)S(1)} %get-tuple-element.35.refs_3_, ...), custom_call_target="tpu_custom_call" | custom-call | flops 1189085184 | bytes 8257536 | tf_op jit(solution)/shard_map/cond/branch_1_fun/assemble_and_gram/pallas_call | solution.py:338
  106.8 1.9 collective-permute-done
  114.0 2.1 collective-permute-done.1
  116.0 3.3 %collective-permute-done.3 = f32[72,384]{1,0:T(8,128)} collective-permute-done((f32[72,384]{1,0:T(8,128)}, f32[72,384]{1,0:T(8,128)}, u32[]{:S(2)}, u32[]{:S(2)}) %collective-permute-start.3) | collective-permute-done | bytes 110624 | tf_op jit(solution)/shard_map/cond/branch_1_fun/ppermute | solution.py:446
  121.8 1.6 collective-permute-start.4
  125.3 1.7 collective-permute-done.4
  127.1 2.9 %collective-permute-done.5 = f32[72,384]{1,0:T(8,128)S(1)} collective-permute-done((f32[72,384]{1,0:T(8,128)S(1)}, f32[72,384]{1,0:T(8,128)S(1)}, u32[]{:S(2)}, u32[]{:S(2)}) %collective-permute-start.5) | collective-permute-done | bytes 110624 | tf_op jit(solution)/shard_map/cond/branch_1_fun/ppermute | solution.py:446
  130.3 1.7 collective-permute-done.7
  132.0 13.8 %apply_update.2 = (f32[576,896]{1,0:T(8,128)}, f32[288,896]{1,0:T(8,128)}, f32[288,896]{1,0:T(8,128)}, f32[288,896]{1,0:T(8,128)}, f32[288,896]{1,0:T(8,128)}) custom-call(s32[4]{0:T(128)S(1)} %get-tuple-element.32.refs_0_, s32[4]{0:T(128)S(1)} %get-tuple-element.33.refs_1_, s32[4,4]{1,0:T(4,128)S(1)} %get-tuple-element.34.refs_2_, ...), custom_call_target="tpu_custom_call" | custom-call | flops 7516717056 | bytes 8257536 | tf_op jit(solution)/shard_map/cond/branch_1_fun/apply_update/pallas_call | solution.py:365
  149.3 4.4 %collective-permute-start.19 = (f32[288,896]{1,0:T(8,128)}, f32[288,896]{1,0:T(8,128)S(1)}, u32[]{:S(2)}, u32[]{:S(2)}) collective-permute-start(f32[288,896]{1,0:T(8,128)} %get-tuple-element.82), channel_id=1, source_target_pairs={{0,24},{24,0},{1,25},{25,1},{2,26},{26,2},{3,27},{27,3},{4,28},{28... | collective-permute-start | bytes 3096584 | tf_op jit(solution)/shard_map/ppermute | solution.py:502
  153.6 95.5 %first_place.1 = (f32[576,896]{1,0:T(8,128)}, f32[4,288,896]{2,1,0:T(8,128)}) custom-call(s32[4]{0:T(128)S(1)} %copy-done.4, f32[576,896]{1,0:T(8,128)} %get-tuple-element.89.inner_result, f32[576,896]{1,0:T(8,128)} %get-tuple-element.90.outer_result, f32[288,896]{1,0:T(8,128)} %get-tuple-element.91.inner_own, f32[288,896]{1,0:T(8,128)} %get-tuple-element.92.outer_own), custom_call_target="tpu_custom_call" | custom-call | bytes 4128768 | tf_op jit(solution)/shard_map/first_place/pallas_call | solution.py:393
  249.2 1.9 place_blocks.4.refs_2_
  252.2 1.5 place_blocks.7
  (54 shorter events, 21.2 us)
Async XLA Ops:
  0.6 14.8 %copy-start.4 = (s32[4]{0:T(128)S(1)}, s32[4]{0:T(128)}, u32[]{:S(2)}) copy-start(s32[4]{0:T(128)} %refs_0_.13) | copy-start | bytes 52
  0.6 14.8 %copy-start.5 = (s32[4,4]{1,0:T(4,128)S(1)}, s32[4,4]{1,0:T(4,128)}, u32[]{:S(2)}) copy-start(s32[4,4]{1,0:T(4,128)} %refs_2_.5) | copy-start | bytes 196
  0.7 14.8 %copy-start.7 = (s32[4]{0:T(128)S(1)}, s32[4]{0:T(128)}, u32[]{:S(2)}) copy-start(s32[4]{0:T(128)} %refs_1_.5) | copy-start | bytes 52
  5.3 27.7 %collective-permute-start.16 = (f32[288,896]{1,0:T(8,128)}, f32[288,896]{1,0:T(8,128)}, u32[]{:S(2)}, u32[]{:S(2)}) collective-permute-start(f32[288,896]{1,0:T(8,128)} %get-tuple-element.80), channel_id=1, source_target_pairs={{0,16},{8,0},{16,24},{24,8},{1,17},{9,1},{17,25},{25,9},{2,18},{10... | collective-permute-start | bytes 3096584 | tf_op jit(solution)/shard_map/ppermute | solution.py:489
  9.4 23.6 %collective-permute-start.23 = (f32[288,896]{1,0:T(8,128)}, f32[288,896]{1,0:T(8,128)S(1)}, u32[]{:S(2)}, u32[]{:S(2)}) collective-permute-start(f32[288,896]{1,0:T(8,128)} %get-tuple-element.85), channel_id=1, source_target_pairs={{8,16},{16,8},{9,17},{17,9},{10,18},{18,10},{11,19},{19,11},{12,20... | collective-permute-start | bytes 3096584 | tf_op jit(solution)/shard_map/ppermute | solution.py:489
  10.1 45.0 %collective-permute-start.22 = (f32[288,896]{1,0:T(8,128)}, f32[288,896]{1,0:T(8,128)S(1)}, u32[]{:S(2)}, u32[]{:S(2)}) collective-permute-start(f32[288,896]{1,0:T(8,128)} %get-tuple-element.85), channel_id=1, source_target_pairs={{0,8},{24,16},{1,9},{25,17},{2,10},{26,18},{3,11},{27,19},{4,12},{... | collective-permute-start | bytes 3096584 | tf_op jit(solution)/shard_map/ppermute | solution.py:489
  18.9 59.1 %collective-permute-start.18 = (f32[288,896]{1,0:T(8,128)}, f32[288,896]{1,0:T(8,128)}, u32[]{:S(2)}, u32[]{:S(2)}) collective-permute-start(f32[288,896]{1,0:T(8,128)} %get-tuple-element.81), channel_id=1, source_target_pairs={{0,24},{24,0},{1,25},{25,1},{2,26},{26,2},{3,27},{27,3},{4,28},{28... | collective-permute-start | bytes 3096584 | tf_op jit(solution)/shard_map/ppermute | solution.py:489
  21.7 78.2 %collective-permute-start.17 = (f32[288,896]{1,0:T(8,128)}, f32[288,896]{1,0:T(8,128)}, u32[]{:S(2)}, u32[]{:S(2)}) collective-permute-start(f32[288,896]{1,0:T(8,128)} %get-tuple-element.81), channel_id=1, source_target_pairs={{8,24},{16,0},{9,25},{17,1},{10,26},{18,2},{11,27},{19,3},{12,28},... | collective-permute-start | bytes 3096584 | tf_op jit(solution)/shard_map/ppermute | solution.py:489
  55.1 94.2 %collective-permute-start.24 = (f32[288,896]{1,0:T(8,128)}, f32[288,896]{1,0:T(8,128)S(1)}, u32[]{:S(2)}, u32[]{:S(2)}) collective-permute-start(f32[288,896]{1,0:T(8,128)} %get-tuple-element.86), channel_id=1, source_target_pairs={{8,0},{16,24},{9,1},{17,25},{10,2},{18,26},{11,3},{19,27},{12,4},{... | collective-permute-start | bytes 3096584 | tf_op jit(solution)/shard_map/ppermute | solution.py:502
  56.4 192.8 %collective-permute-start.25 = (f32[288,896]{1,0:T(8,128)}, f32[288,896]{1,0:T(8,128)S(1)}, u32[]{:S(2)}, u32[]{:S(2)}) collective-permute-start(f32[288,896]{1,0:T(8,128)} %get-tuple-element.87), channel_id=1, source_target_pairs={{8,24},{16,0},{9,25},{17,1},{10,26},{18,2},{11,27},{19,3},{12,28},... | collective-permute-start | bytes 3096584 | tf_op jit(solution)/shard_map/ppermute | solution.py:502
  106.7 2.0 collective-permute-start
  109.7 22.3 %copy-start.1 = (bf16[576,896]{1,0:T(8,128)(2,1)S(1)}, bf16[576,896]{1,0:T(8,128)(2,1)}, u32[]{:S(2)}) copy-start(bf16[576,896]{1,0:T(8,128)(2,1)} %copy-done) | copy-start | bytes 3096580 | tf_op jit(solution)/shard_map/cond
  110.5 5.6 %collective-permute-start.1 = (f32[72,384]{1,0:T(8,128)}, f32[72,384]{1,0:T(8,128)}, u32[]{:S(2)}, u32[]{:S(2)}) collective-permute-start(f32[72,384]{1,0:T(8,128)} %get-tuple-element.99), channel_id=1, source_target_pairs={{0,2},{1,3},{2,0},{3,1},{4,6},{5,7},{6,4},{7,5},{8,10},{9,11},{10,... | collective-permute-start | bytes 331784 | tf_op jit(solution)/shard_map/cond/branch_1_fun/ppermute | solution.py:446
  112.0 7.4 %collective-permute-start.3 = (f32[72,384]{1,0:T(8,128)}, f32[72,384]{1,0:T(8,128)}, u32[]{:S(2)}, u32[]{:S(2)}) collective-permute-start(f32[72,384]{1,0:T(8,128)} %get-tuple-element.100), channel_id=1, source_target_pairs={{0,6},{1,7},{2,4},{3,5},{4,2},{5,3},{6,0},{7,1},{8,14},{9,15},{10,... | collective-permute-start | bytes 331784 | tf_op jit(solution)/shard_map/cond/branch_1_fun/ppermute | solution.py:446
  113.5 7.2 %collective-permute-start.2 = (f32[72,384]{1,0:T(8,128)}, f32[72,384]{1,0:T(8,128)}, u32[]{:S(2)}, u32[]{:S(2)}) collective-permute-start(f32[72,384]{1,0:T(8,128)} %get-tuple-element.101), channel_id=1, source_target_pairs={{0,4},{1,5},{2,6},{3,7},{4,0},{5,1},{6,2},{7,3},{8,12},{9,13},{10,... | collective-permute-start | bytes 331784 | tf_op jit(solution)/shard_map/cond/branch_1_fun/ppermute | solution.py:446
  114.0 18.0 %copy-start.3 = (bf16[576,896]{1,0:T(8,128)(2,1)S(1)}, bf16[576,896]{1,0:T(8,128)(2,1)}, u32[]{:S(2)}) copy-start(bf16[576,896]{1,0:T(8,128)(2,1)} %copy-done.2) | copy-start | bytes 3096580 | tf_op jit(solution)/shard_map/cond
  121.8 5.3 %collective-permute-start.4 = (f32[72,384]{1,0:T(8,128)S(1)}, f32[72,384]{1,0:T(8,128)S(1)}, u32[]{:S(2)}, u32[]{:S(2)}) collective-permute-start(f32[72,384]{1,0:T(8,128)S(1)} %get-tuple-element.96), channel_id=1, source_target_pairs={{0,2},{1,3},{2,0},{3,1},{4,6},{5,7},{6,4},{7,5},{8,10},{9,11},{10,... | collective-permute-start | bytes 331784 | tf_op jit(solution)/shard_map/cond/branch_1_fun/ppermute | solution.py:446
  123.3 6.7 %collective-permute-start.5 = (f32[72,384]{1,0:T(8,128)S(1)}, f32[72,384]{1,0:T(8,128)S(1)}, u32[]{:S(2)}, u32[]{:S(2)}) collective-permute-start(f32[72,384]{1,0:T(8,128)S(1)} %get-tuple-element.96), channel_id=1, source_target_pairs={{0,4},{1,5},{2,6},{3,7},{4,0},{5,1},{6,2},{7,3},{8,12},{9,13},{10,... | collective-permute-start | bytes 331784 | tf_op jit(solution)/shard_map/cond/branch_1_fun/ppermute | solution.py:446
  123.8 6.2 %collective-permute-start.6 = (f32[72,384]{1,0:T(8,128)S(1)}, f32[72,384]{1,0:T(8,128)S(1)}, u32[]{:S(2)}, u32[]{:S(2)}) collective-permute-start(f32[72,384]{1,0:T(8,128)S(1)} %get-tuple-element.96), channel_id=1, source_target_pairs={{0,6},{1,7},{2,4},{3,5},{4,2},{5,3},{6,0},{7,1},{8,14},{9,15},{10,... | collective-permute-start | bytes 331784 | tf_op jit(solution)/shard_map/cond/branch_1_fun/ppermute | solution.py:446
  130.1 1.9 collective-permute-start.7
  145.8 103.4 %collective-permute-start.26 = (f32[288,896]{1,0:T(8,128)}, f32[288,896]{1,0:T(8,128)S(1)}, u32[]{:S(2)}, u32[]{:S(2)}) collective-permute-start(f32[288,896]{1,0:T(8,128)} %get-tuple-element.88), channel_id=1, source_target_pairs={{8,16},{16,8},{9,17},{17,9},{10,18},{18,10},{11,19},{19,11},{12,20... | collective-permute-start | bytes 3096584 | tf_op jit(solution)/shard_map/ppermute | solution.py:502
  146.5 104.5 %collective-permute-start.21 = (f32[288,896]{1,0:T(8,128)}, f32[288,896]{1,0:T(8,128)S(1)}, u32[]{:S(2)}, u32[]{:S(2)}) collective-permute-start(f32[288,896]{1,0:T(8,128)} %get-tuple-element.84), channel_id=1, source_target_pairs={{0,8},{24,16},{1,9},{25,17},{2,10},{26,18},{3,11},{27,19},{4,12},{... | collective-permute-start | bytes 3096584 | tf_op jit(solution)/shard_map/ppermute | solution.py:502
  147.9 103.8 %collective-permute-start.20 = (f32[288,896]{1,0:T(8,128)}, f32[288,896]{1,0:T(8,128)S(1)}, u32[]{:S(2)}, u32[]{:S(2)}) collective-permute-start(f32[288,896]{1,0:T(8,128)} %get-tuple-element.83), channel_id=1, source_target_pairs={{0,16},{24,8},{1,17},{25,9},{2,18},{26,10},{3,19},{27,11},{4,20},{... | collective-permute-start | bytes 3096584 | tf_op jit(solution)/shard_map/ppermute | solution.py:502
  149.3 103.0 %collective-permute-start.19 = (f32[288,896]{1,0:T(8,128)}, f32[288,896]{1,0:T(8,128)S(1)}, u32[]{:S(2)}, u32[]{:S(2)}) collective-permute-start(f32[288,896]{1,0:T(8,128)} %get-tuple-element.82), channel_id=1, source_target_pairs={{0,24},{24,0},{1,25},{25,1},{2,26},{26,2},{3,27},{27,3},{4,28},{28... | collective-permute-start | bytes 3096584 | tf_op jit(solution)/shard_map/ppermute | solution.py:502
  (3 other events, 16.7 us)

commit v4 on v3

--- a/solution.py
+++ b/solution.py
@@ -396,7 +396,7 @@
             jax.ShapeDtypeStruct(results[0].shape, jnp.float32),
             jax.ShapeDtypeStruct(shape, jnp.float32),
         ],
-        in_specs=[HBM] + [ANY] * 4,
+        in_specs=[HBM] + [VMEM] * 4,
         out_specs=[HBM] * 2,
         scratch_shapes=[
             pltpu.SMEM(owner_group.shape, jnp.int32),
@@ -413,7 +413,7 @@
     return pl.pallas_call(
         functools.partial(place_kernel, inner, ranks, steps),
         out_shape=jax.ShapeDtypeStruct(shards.shape, shards.dtype),
-        in_specs=[HBM] + [ANY] * len(blocks) + [HBM],
+        in_specs=[HBM] + [VMEM] * len(blocks) + [HBM],
         out_specs=HBM,
         scratch_shapes=[
             pltpu.SMEM(owner_group.shape, jnp.int32),

time: 254 us -> 220 us (0.87)
  Pallas kernels: 133 us -> 42.5 us
  waiting for transfers between devices: 82.8 us -> 139 us
    pallas_call x1, Pallas kernels: 95.5 us -> 4.98 us  [first_place(): pl.pallas_call(functools.partial(first_place_kernel, ranks), out_shape=[j...]
    ppermute x6, waiting for transfers between devices: 0.02 us -> 56.1 us  [to_home(): lax.ppermute(block, 'fsdp', [(i, i ^ step) for i in range(ranks) if insid...]
  transfers between devices with their start and end apart: 19 -> 19, of which waited for: 11 -> 14; matrix products, arithmetic and copies ran while one was open for 1% -> 1% of each run, Pallas kernels for 50% -> 17%
where the time goes in v4:
time: 220 us
  waiting for transfers between devices  139 us (63%)
  Pallas kernels  42.5 us (19%)
  starting transfers between devices  31.8 us (14%)
  local copies, waits for them, and re-layouts  2.94 us (1%)
    ppermute x5, waiting for transfers between devices, on_device(): sent[place, kind] = lax.ppermute(blends[place - 1], 'fsdp', pairs)  68 us
    ppermute x6, waiting for transfers between devices, to_home(): lax.ppermute(block, 'fsdp', [(i, i ^ step) for i in range(ranks) if insid...  56.1 us
    ppermute x8, waiting for transfers between devices, exchange(): return lax.ppermute(piece, axis, [(i, i ^ step) for i in range(size)])  15 us
    ppermute x5, starting transfers between devices, on_device(): sent[place, kind] = lax.ppermute(blends[place - 1], 'fsdp', pairs)  14.2 us
    pallas_call x1, Pallas kernels, apply_update(): pl.pallas_call(functools.partial(update_kernel, ranks), out_shape=update_...  13.8 us
    ppermute x6, starting transfers between devices, to_home(): lax.ppermute(block, 'fsdp', [(i, i ^ step) for i in range(ranks) if insid...  10.4 us
    pallas_call x2, Pallas kernels, blend(): pl.pallas_call(functools.partial(blend_kernel, places, chunks), out_shape...  8.04 us
    ppermute x8, starting transfers between devices, exchange(): return lax.ppermute(piece, axis, [(i, i ^ step) for i in range(size)])  7.2 us
  transfers between devices with their start and end apart: 19, of which 14 were waited for; matrix products, arithmetic and copies ran while one was open for 1% of the time, Pallas kernels for 17%

profile of v4, /device:TPU:0, one launch (start us, length us, event | category | flops | bytes accessed | tf_op | source)
XLA Modules:
  0.0 219.5 jit_solution(12040226287179516240)
XLA Ops:
  0.7 4.6 %blend.2 = (f32[288,896]{1,0:T(8,128)}, f32[288,896]{1,0:T(8,128)}, f32[8,128]{1,0:T(8,128)}) custom-call(s32[4]{0:T(128)} %refs_0_.13, s32[4]{0:T(128)} %refs_1_.5, s32[4,4]{1,0:T(4,128)} %refs_2_.5, s32[4,4]{1,0:T(4,128)} %refs_3_.4, f32[4,288,896]{2,1,0:T(8,128)} %refs_3_.5, f32[4,288,896]{2,1,0:T(8,128)} %refs_4_.5), custom_call_target="tpu_custom_call" | custom-call | tf_op jit(solution)/shard_map/blend/pallas_call | solution.py:297
  5.3 4.1 %collective-permute-start.16 = (f32[288,896]{1,0:T(8,128)}, f32[288,896]{1,0:T(8,128)}, u32[]{:S(2)}, u32[]{:S(2)}) collective-permute-start(f32[288,896]{1,0:T(8,128)} %get-tuple-element.80), channel_id=1, source_target_pairs={{0,16},{8,0},{16,24},{24,8},{1,17},{9,1},{17,25},{25,9},{2,18},{10... | collective-permute-start | bytes 3096584 | tf_op jit(solution)/shard_map/ppermute | solution.py:489
  10.1 5.3 %collective-permute-start.22 = (f32[288,896]{1,0:T(8,128)}, f32[288,896]{1,0:T(8,128)S(1)}, u32[]{:S(2)}, u32[]{:S(2)}) collective-permute-start(f32[288,896]{1,0:T(8,128)} %get-tuple-element.85), channel_id=1, source_target_pairs={{0,8},{24,16},{1,9},{25,17},{2,10},{26,18},{3,11},{27,19},{4,12},{... | collective-permute-start | bytes 3096584 | tf_op jit(solution)/shard_map/ppermute | solution.py:489
  15.5 3.4 %blend.3 = (f32[288,896]{1,0:T(8,128)}, f32[8,128]{1,0:T(8,128)}) custom-call(s32[4]{0:T(128)S(1)} %copy-done.4, s32[4]{0:T(128)S(1)} %copy-done.7, s32[4,4]{1,0:T(4,128)S(1)} %copy-done.5, s32[4,4]{1,0:T(4,128)S(1)} %copy-done.6, f32[4,288,896]{2,1,0:T(8,128)} %refs_3_.5, f32[4,288,896]{2,1,0:T(8,128)} %refs_4_.5, f32[8,128]{1,0:T(8,128)} %get-tuple-element.76.refs_6_), custom_call_target="tpu_custom_call" | custom-call | tf_op jit(solution)/shard_map/blend/pallas_call | solution.py:297
  18.9 2.8 %collective-permute-start.18 = (f32[288,896]{1,0:T(8,128)}, f32[288,896]{1,0:T(8,128)}, u32[]{:S(2)}, u32[]{:S(2)}) collective-permute-start(f32[288,896]{1,0:T(8,128)} %get-tuple-element.81), channel_id=1, source_target_pairs={{0,24},{24,0},{1,25},{25,1},{2,26},{26,2},{3,27},{27,3},{4,28},{28... | collective-permute-start | bytes 3096584 | tf_op jit(solution)/shard_map/ppermute | solution.py:489
  23.0 6.4 %home.1 = (f32[4,288,896]{2,1,0:T(8,128)}, f32[288,896]{1,0:T(8,128)}) custom-call(s32[4]{0:T(128)S(1)} %copy-done.4, s32[4]{0:T(128)S(1)} %copy-done.7, s32[4,4]{1,0:T(4,128)S(1)} %copy-done.5, f32[4,288,896]{2,1,0:T(8,128)} %refs_3_.5, f32[4,288,896]{2,1,0:T(8,128)} %refs_4_.5, f32[8,128]{1,0:T(8,128)} %get-tuple-element.77.refs_5_), custom_call_target="tpu_custom_call" | custom-call | tf_op jit(solution)/shard_map/home/pallas_call | solution.py:319
  29.4 3.6 %collective-permute-done.16 = f32[288,896]{1,0:T(8,128)} collective-permute-done((f32[288,896]{1,0:T(8,128)}, f32[288,896]{1,0:T(8,128)}, u32[]{:S(2)}, u32[]{:S(2)}) %collective-permute-start.16) | collective-permute-done | bytes 1032224 | tf_op jit(solution)/shard_map/ppermute | solution.py:489
  33.0 22.1 %collective-permute-done.22 = f32[288,896]{1,0:T(8,128)S(1)} collective-permute-done((f32[288,896]{1,0:T(8,128)}, f32[288,896]{1,0:T(8,128)S(1)}, u32[]{:S(2)}, u32[]{:S(2)}) %collective-permute-start.22) | collective-permute-done | bytes 1032224 | tf_op jit(solution)/shard_map/ppermute | solution.py:489
  57.7 20.3 %collective-permute-done.18 = f32[288,896]{1,0:T(8,128)} collective-permute-done((f32[288,896]{1,0:T(8,128)}, f32[288,896]{1,0:T(8,128)}, u32[]{:S(2)}, u32[]{:S(2)}) %collective-permute-start.18) | collective-permute-done | bytes 1032224 | tf_op jit(solution)/shard_map/ppermute | solution.py:489
  78.0 22.0 %collective-permute-done.17 = f32[288,896]{1,0:T(8,128)} collective-permute-done((f32[288,896]{1,0:T(8,128)}, f32[288,896]{1,0:T(8,128)}, u32[]{:S(2)}, u32[]{:S(2)}) %collective-permute-start.17) | collective-permute-done | bytes 1032224 | tf_op jit(solution)/shard_map/ppermute | solution.py:489
  99.9 45.8 %conditional.2 = ((f32[576,896]{1,0:T(8,128)}, f32[288,896]{1,0:T(8,128)}, f32[288,896]{1,0:T(8,128)}, f32[288,896]{1,0:T(8,128)}, f32[288,896]{1,0:T(8,128)})) conditional(s32[]{:T(128)} %convert_element_type.6, () %tuple.20, (s32[4]{0:T(128)S(1)}, s32[4]{0:T(128)S(1)}, s32[4,4]{1,0:T(4,128)S(1)}, s32[4,4]{1,0:T(4,128)S(1)}, f32[288,896]{1,0:T(8,128)}, ...), branch_computations={%region_0.0_spmd, %region_1.0_spmd} | conditional | flops 8705995776 | bytes 46523252 | solution.py:516
  99.9 4.7 %assemble_and_gram.2 = (bf16[576,896]{1,0:T(8,128)(2,1)S(1)}, bf16[576,896]{1,0:T(8,128)(2,1)S(1)}, f32[576,384]{1,0:T(8,128)S(1)}) custom-call(s32[4]{0:T(128)S(1)} %get-tuple-element.32.refs_0_, s32[4]{0:T(128)S(1)} %get-tuple-element.33.refs_1_, s32[4,4]{1,0:T(4,128)S(1)} %get-tuple-element.34.refs_2_, s32[4,4]{1,0:T(4,128)S(1)} %get-tuple-element.35.refs_3_, ...), custom_call_target="tpu_custom_call" | custom-call | flops 1189085184 | bytes 8257536 | tf_op jit(solution)/shard_map/cond/branch_1_fun/assemble_and_gram/pallas_call | solution.py:338
  106.8 1.9 collective-permute-done
  114.0 2.1 collective-permute-done.1
  116.0 3.3 %collective-permute-done.3 = f32[72,384]{1,0:T(8,128)} collective-permute-done((f32[72,384]{1,0:T(8,128)}, f32[72,384]{1,0:T(8,128)}, u32[]{:S(2)}, u32[]{:S(2)}) %collective-permute-start.3) | collective-permute-done | bytes 110624 | tf_op jit(solution)/shard_map/cond/branch_1_fun/ppermute | solution.py:446
  125.3 1.7 collective-permute-done.4
  127.1 2.9 %collective-permute-done.5 = f32[72,384]{1,0:T(8,128)S(1)} collective-permute-done((f32[72,384]{1,0:T(8,128)S(1)}, f32[72,384]{1,0:T(8,128)S(1)}, u32[]{:S(2)}, u32[]{:S(2)}) %collective-permute-start.5) | collective-permute-done | bytes 110624 | tf_op jit(solution)/shard_map/cond/branch_1_fun/ppermute | solution.py:446
  132.0 13.8 %apply_update.2 = (f32[576,896]{1,0:T(8,128)}, f32[288,896]{1,0:T(8,128)}, f32[288,896]{1,0:T(8,128)}, f32[288,896]{1,0:T(8,128)}, f32[288,896]{1,0:T(8,128)}) custom-call(s32[4]{0:T(128)S(1)} %get-tuple-element.32.refs_0_, s32[4]{0:T(128)S(1)} %get-tuple-element.33.refs_1_, s32[4,4]{1,0:T(4,128)S(1)} %get-tuple-element.34.refs_2_, ...), custom_call_target="tpu_custom_call" | custom-call | flops 7516717056 | bytes 8257536 | tf_op jit(solution)/shard_map/cond/branch_1_fun/apply_update/pallas_call | solution.py:365
  149.3 4.4 %collective-permute-start.19 = (f32[288,896]{1,0:T(8,128)}, f32[288,896]{1,0:T(8,128)S(1)}, u32[]{:S(2)}, u32[]{:S(2)}) collective-permute-start(f32[288,896]{1,0:T(8,128)} %get-tuple-element.82), channel_id=1, source_target_pairs={{0,24},{24,0},{1,25},{25,1},{2,26},{26,2},{3,27},{27,3},{4,28},{28... | collective-permute-start | bytes 3096584 | tf_op jit(solution)/shard_map/ppermute | solution.py:502
  153.6 5.0 %first_place.1 = (f32[576,896]{1,0:T(8,128)}, f32[4,288,896]{2,1,0:T(8,128)}) custom-call(s32[4]{0:T(128)S(1)} %copy-done.4, f32[576,896]{1,0:T(8,128)} %get-tuple-element.89.inner_result, f32[576,896]{1,0:T(8,128)} %get-tuple-element.90.outer_result, f32[288,896]{1,0:T(8,128)} %get-tuple-element.91.inner_own, f32[288,896]{1,0:T(8,128)} %get-tuple-element.92.outer_own), custom_call_target="tpu_custom_call" | custom-call | bytes 4128768 | tf_op jit(solution)/shard_map/first_place/pallas_call | solution.py:393
  158.7 1.9 place_blocks.4.refs_2_
  160.6 10.7 %collective-permute-done.21.refs_1_ = f32[288,896]{1,0:T(8,128)S(1)} collective-permute-done((f32[288,896]{1,0:T(8,128)}, f32[288,896]{1,0:T(8,128)S(1)}, u32[]{:S(2)}, u32[]{:S(2)}) %collective-permute-start.21) | collective-permute-done | bytes 1032224 | tf_op jit(solution)/shard_map/ppermute | solution.py:502
  171.8 21.5 %collective-permute-done.20.refs_1_ = f32[288,896]{1,0:T(8,128)S(1)} collective-permute-done((f32[288,896]{1,0:T(8,128)}, f32[288,896]{1,0:T(8,128)S(1)}, u32[]{:S(2)}, u32[]{:S(2)}) %collective-permute-start.20) | collective-permute-done | bytes 1032224 | tf_op jit(solution)/shard_map/ppermute | solution.py:502
  193.9 23.9 %collective-permute-done.19.refs_1_ = f32[288,896]{1,0:T(8,128)S(1)} collective-permute-done((f32[288,896]{1,0:T(8,128)}, f32[288,896]{1,0:T(8,128)S(1)}, u32[]{:S(2)}, u32[]{:S(2)}) %collective-permute-start.19) | collective-permute-done | bytes 1032224 | tf_op jit(solution)/shard_map/ppermute | solution.py:502
  (54 shorter events, 26.0 us)
Async XLA Ops:
  0.6 14.8 %copy-start.4 = (s32[4]{0:T(128)S(1)}, s32[4]{0:T(128)}, u32[]{:S(2)}) copy-start(s32[4]{0:T(128)} %refs_0_.13) | copy-start | bytes 52
  0.6 14.8 %copy-start.5 = (s32[4,4]{1,0:T(4,128)S(1)}, s32[4,4]{1,0:T(4,128)}, u32[]{:S(2)}) copy-start(s32[4,4]{1,0:T(4,128)} %refs_2_.5) | copy-start | bytes 196
  0.7 14.8 %copy-start.7 = (s32[4]{0:T(128)S(1)}, s32[4]{0:T(128)}, u32[]{:S(2)}) copy-start(s32[4]{0:T(128)} %refs_1_.5) | copy-start | bytes 52
  5.3 27.7 %collective-permute-start.16 = (f32[288,896]{1,0:T(8,128)}, f32[288,896]{1,0:T(8,128)}, u32[]{:S(2)}, u32[]{:S(2)}) collective-permute-start(f32[288,896]{1,0:T(8,128)} %get-tuple-element.80), channel_id=1, source_target_pairs={{0,16},{8,0},{16,24},{24,8},{1,17},{9,1},{17,25},{25,9},{2,18},{10... | collective-permute-start | bytes 3096584 | tf_op jit(solution)/shard_map/ppermute | solution.py:489
  9.4 23.6 %collective-permute-start.23 = (f32[288,896]{1,0:T(8,128)}, f32[288,896]{1,0:T(8,128)S(1)}, u32[]{:S(2)}, u32[]{:S(2)}) collective-permute-start(f32[288,896]{1,0:T(8,128)} %get-tuple-element.85), channel_id=1, source_target_pairs={{8,16},{16,8},{9,17},{17,9},{10,18},{18,10},{11,19},{19,11},{12,20... | collective-permute-start | bytes 3096584 | tf_op jit(solution)/shard_map/ppermute | solution.py:489
  10.1 45.0 %collective-permute-start.22 = (f32[288,896]{1,0:T(8,128)}, f32[288,896]{1,0:T(8,128)S(1)}, u32[]{:S(2)}, u32[]{:S(2)}) collective-permute-start(f32[288,896]{1,0:T(8,128)} %get-tuple-element.85), channel_id=1, source_target_pairs={{0,8},{24,16},{1,9},{25,17},{2,10},{26,18},{3,11},{27,19},{4,12},{... | collective-permute-start | bytes 3096584 | tf_op jit(solution)/shard_map/ppermute | solution.py:489
  18.9 59.1 %collective-permute-start.18 = (f32[288,896]{1,0:T(8,128)}, f32[288,896]{1,0:T(8,128)}, u32[]{:S(2)}, u32[]{:S(2)}) collective-permute-start(f32[288,896]{1,0:T(8,128)} %get-tuple-element.81), channel_id=1, source_target_pairs={{0,24},{24,0},{1,25},{25,1},{2,26},{26,2},{3,27},{27,3},{4,28},{28... | collective-permute-start | bytes 3096584 | tf_op jit(solution)/shard_map/ppermute | solution.py:489
  21.7 78.2 %collective-permute-start.17 = (f32[288,896]{1,0:T(8,128)}, f32[288,896]{1,0:T(8,128)}, u32[]{:S(2)}, u32[]{:S(2)}) collective-permute-start(f32[288,896]{1,0:T(8,128)} %get-tuple-element.81), channel_id=1, source_target_pairs={{8,24},{16,0},{9,25},{17,1},{10,26},{18,2},{11,27},{19,3},{12,28},... | collective-permute-start | bytes 3096584 | tf_op jit(solution)/shard_map/ppermute | solution.py:489
  55.1 94.2 %collective-permute-start.24 = (f32[288,896]{1,0:T(8,128)}, f32[288,896]{1,0:T(8,128)S(1)}, u32[]{:S(2)}, u32[]{:S(2)}) collective-permute-start(f32[288,896]{1,0:T(8,128)} %get-tuple-element.86), channel_id=1, source_target_pairs={{8,0},{16,24},{9,1},{17,25},{10,2},{18,26},{11,3},{19,27},{12,4},{... | collective-permute-start | bytes 3096584 | tf_op jit(solution)/shard_map/ppermute | solution.py:502
  56.4 102.3 %collective-permute-start.25 = (f32[288,896]{1,0:T(8,128)}, f32[288,896]{1,0:T(8,128)S(1)}, u32[]{:S(2)}, u32[]{:S(2)}) collective-permute-start(f32[288,896]{1,0:T(8,128)} %get-tuple-element.87), channel_id=1, source_target_pairs={{8,24},{16,0},{9,25},{17,1},{10,26},{18,2},{11,27},{19,3},{12,28},... | collective-permute-start | bytes 3096584 | tf_op jit(solution)/shard_map/ppermute | solution.py:502
  106.7 2.0 collective-permute-start
  109.7 22.3 %copy-start.1 = (bf16[576,896]{1,0:T(8,128)(2,1)S(1)}, bf16[576,896]{1,0:T(8,128)(2,1)}, u32[]{:S(2)}) copy-start(bf16[576,896]{1,0:T(8,128)(2,1)} %copy-done) | copy-start | bytes 3096580 | tf_op jit(solution)/shard_map/cond
  110.5 5.6 %collective-permute-start.1 = (f32[72,384]{1,0:T(8,128)}, f32[72,384]{1,0:T(8,128)}, u32[]{:S(2)}, u32[]{:S(2)}) collective-permute-start(f32[72,384]{1,0:T(8,128)} %get-tuple-element.99), channel_id=1, source_target_pairs={{0,2},{1,3},{2,0},{3,1},{4,6},{5,7},{6,4},{7,5},{8,10},{9,11},{10,... | collective-permute-start | bytes 331784 | tf_op jit(solution)/shard_map/cond/branch_1_fun/ppermute | solution.py:446
  112.0 7.4 %collective-permute-start.3 = (f32[72,384]{1,0:T(8,128)}, f32[72,384]{1,0:T(8,128)}, u32[]{:S(2)}, u32[]{:S(2)}) collective-permute-start(f32[72,384]{1,0:T(8,128)} %get-tuple-element.100), channel_id=1, source_target_pairs={{0,6},{1,7},{2,4},{3,5},{4,2},{5,3},{6,0},{7,1},{8,14},{9,15},{10,... | collective-permute-start | bytes 331784 | tf_op jit(solution)/shard_map/cond/branch_1_fun/ppermute | solution.py:446
  113.5 7.2 %collective-permute-start.2 = (f32[72,384]{1,0:T(8,128)}, f32[72,384]{1,0:T(8,128)}, u32[]{:S(2)}, u32[]{:S(2)}) collective-permute-start(f32[72,384]{1,0:T(8,128)} %get-tuple-element.101), channel_id=1, source_target_pairs={{0,4},{1,5},{2,6},{3,7},{4,0},{5,1},{6,2},{7,3},{8,12},{9,13},{10,... | collective-permute-start | bytes 331784 | tf_op jit(solution)/shard_map/cond/branch_1_fun/ppermute | solution.py:446
  114.0 18.0 %copy-start.3 = (bf16[576,896]{1,0:T(8,128)(2,1)S(1)}, bf16[576,896]{1,0:T(8,128)(2,1)}, u32[]{:S(2)}) copy-start(bf16[576,896]{1,0:T(8,128)(2,1)} %copy-done.2) | copy-start | bytes 3096580 | tf_op jit(solution)/shard_map/cond
  121.8 5.3 %collective-permute-start.4 = (f32[72,384]{1,0:T(8,128)S(1)}, f32[72,384]{1,0:T(8,128)S(1)}, u32[]{:S(2)}, u32[]{:S(2)}) collective-permute-start(f32[72,384]{1,0:T(8,128)S(1)} %get-tuple-element.96), channel_id=1, source_target_pairs={{0,2},{1,3},{2,0},{3,1},{4,6},{5,7},{6,4},{7,5},{8,10},{9,11},{10,... | collective-permute-start | bytes 331784 | tf_op jit(solution)/shard_map/cond/branch_1_fun/ppermute | solution.py:446
  123.3 6.7 %collective-permute-start.5 = (f32[72,384]{1,0:T(8,128)S(1)}, f32[72,384]{1,0:T(8,128)S(1)}, u32[]{:S(2)}, u32[]{:S(2)}) collective-permute-start(f32[72,384]{1,0:T(8,128)S(1)} %get-tuple-element.96), channel_id=1, source_target_pairs={{0,4},{1,5},{2,6},{3,7},{4,0},{5,1},{6,2},{7,3},{8,12},{9,13},{10,... | collective-permute-start | bytes 331784 | tf_op jit(solution)/shard_map/cond/branch_1_fun/ppermute | solution.py:446
  123.8 6.2 %collective-permute-start.6 = (f32[72,384]{1,0:T(8,128)S(1)}, f32[72,384]{1,0:T(8,128)S(1)}, u32[]{:S(2)}, u32[]{:S(2)}) collective-permute-start(f32[72,384]{1,0:T(8,128)S(1)} %get-tuple-element.96), channel_id=1, source_target_pairs={{0,6},{1,7},{2,4},{3,5},{4,2},{5,3},{6,0},{7,1},{8,14},{9,15},{10,... | collective-permute-start | bytes 331784 | tf_op jit(solution)/shard_map/cond/branch_1_fun/ppermute | solution.py:446
  130.1 1.9 collective-permute-start.7
  145.8 12.9 %collective-permute-start.26 = (f32[288,896]{1,0:T(8,128)}, f32[288,896]{1,0:T(8,128)S(1)}, u32[]{:S(2)}, u32[]{:S(2)}) collective-permute-start(f32[288,896]{1,0:T(8,128)} %get-tuple-element.88), channel_id=1, source_target_pairs={{8,16},{16,8},{9,17},{17,9},{10,18},{18,10},{11,19},{19,11},{12,20... | collective-permute-start | bytes 3096584 | tf_op jit(solution)/shard_map/ppermute | solution.py:502
  146.5 24.7 %collective-permute-start.21 = (f32[288,896]{1,0:T(8,128)}, f32[288,896]{1,0:T(8,128)S(1)}, u32[]{:S(2)}, u32[]{:S(2)}) collective-permute-start(f32[288,896]{1,0:T(8,128)} %get-tuple-element.84), channel_id=1, source_target_pairs={{0,8},{24,16},{1,9},{25,17},{2,10},{26,18},{3,11},{27,19},{4,12},{... | collective-permute-start | bytes 3096584 | tf_op jit(solution)/shard_map/ppermute | solution.py:502
  147.9 45.5 %collective-permute-start.20 = (f32[288,896]{1,0:T(8,128)}, f32[288,896]{1,0:T(8,128)S(1)}, u32[]{:S(2)}, u32[]{:S(2)}) collective-permute-start(f32[288,896]{1,0:T(8,128)} %get-tuple-element.83), channel_id=1, source_target_pairs={{0,16},{24,8},{1,17},{25,9},{2,18},{26,10},{3,19},{27,11},{4,20},{... | collective-permute-start | bytes 3096584 | tf_op jit(solution)/shard_map/ppermute | solution.py:502
  149.3 68.6 %collective-permute-start.19 = (f32[288,896]{1,0:T(8,128)}, f32[288,896]{1,0:T(8,128)S(1)}, u32[]{:S(2)}, u32[]{:S(2)}) collective-permute-start(f32[288,896]{1,0:T(8,128)} %get-tuple-element.82), channel_id=1, source_target_pairs={{0,24},{24,0},{1,25},{25,1},{2,26},{26,2},{3,27},{27,3},{4,28},{28... | collective-permute-start | bytes 3096584 | tf_op jit(solution)/shard_map/ppermute | solution.py:502
  (3 other events, 16.7 us)

commit v5 on v0

v5 whole, which is shorter than its diff:
```python
import functools
import math

import jax
import jax.numpy as jnp
from jax import lax
from jax.experimental import pallas as pl
from jax.experimental.pallas import tpu as pltpu
from jax.sharding import PartitionSpec as P

WIDTH = 7168
INNER = 576
PANEL = INNER // 3
TILE = 256
SUBLANES = 8

MOMENTUM_RATE = 0.95
QUINTIC_FIRST = 3.4445
QUINTIC_SECOND = -4.775
QUINTIC_THIRD = 2.0315
EPSILON = 1e-07
OUT_SCALE = 0.2 * math.sqrt(max(INNER, WIDTH))
FULL = pltpu.CompilerParams(vmem_limit_bytes=60 * 1024 * 1024)
PARAMS = pltpu.CompilerParams(vmem_limit_bytes=48 * 1024 * 1024)
HBM = pl.BlockSpec(memory_space=pltpu.HBM)
ANY = pl.BlockSpec(memory_space=pl.ANY)
VMEM = pl.BlockSpec(memory_space=pltpu.VMEM)


def halves(value):
    high = value.astype(jnp.bfloat16)
    low = (value - high.astype(jnp.float32)).astype(jnp.bfloat16)
    return high, low


def dot(left, right, contract):
    return lax.dot_general(left, right, (contract, ((), ())), preferred_element_type=jnp.float32)


def dot_halves(left, right, contract=((1,), (0,))):
    (left_high, left_low), (right_high, right_low) = left, right
    return (
        dot(left_high, right_low, contract) + dot(left_low, right_high, contract)
    ) + dot(left_high, right_high, contract)


def is_inner(rank, ranks):
    low = ranks // 4
    return (rank >= low) & (rank < ranks - low)


def mate(ranks):
    return ranks // 4


def table_scratch(matrices, ranks):
    return [
        pltpu.SMEM((matrices,), jnp.int32),
        pltpu.SMEM((ranks,), jnp.int32),
        pltpu.SMEM((matrices, ranks), jnp.int32),
        pltpu.SMEM((matrices, ranks), jnp.int32),
        pltpu.SemaphoreType.DMA((4,)),
    ]


def fetch_tables(tables, held):
    *places, arrive = held
    copies = [
        pltpu.make_async_copy(table, place, arrive.at[index])
        for index, (table, place) in enumerate(zip(tables, places))
    ]
    for copy in copies:
        copy.start()
    for copy in copies:
        copy.wait()
    return places


def matrix_of(owner_group, rank):
    found = jnp.int32(0)
    for matrix in range(owner_group.shape[0]):
        found = jnp.where(owner_group[matrix] == rank, matrix, found)
    return found


def each_copy(copies, action):
    for condition, source, place, flag in copies:

        @pl.when(condition)
        def _(source=source, place=place, flag=flag):
            getattr(pltpu.make_async_copy(source, place, flag), action)()


def blend_kernel(first, chunks, *refs):
    tables, (momentum, gradient) = refs[:4], refs[4:6]
    ranks = tables[1].shape[0]
    *outs, token, olds, grads, arrive, leave = refs[-ranks - 10 : -5]
    owner_group, live_ranks, row_counts, _ = fetch_tables(tables, refs[-5:])
    rank = lax.axis_index("fsdp")
    slots, columns = outs[0].shape
    size = slots // chunks
    jobs = []
    for step in [*range(1, ranks), 0]:
        target = rank ^ step
        matrix = matrix_of(owner_group, target ^ mate(ranks) if first else target)
        count = row_counts[matrix, rank] * live_ranks[rank]
        for chunk in range(chunks):
            part = pl.ds(chunk * size, size)
            flags = arrive.at[step, chunk, 0], arrive.at[step, chunk, 1]
            incoming = (
                (is_inner(target, ranks), momentum.at[matrix, part], olds.at[step, part], flags[0]),
                (is_inner(target, ranks), gradient.at[matrix, part], grads.at[step, part], flags[1]),
            )
            outgoing = (is_inner(target, ranks), olds.at[step, part], outs[step].at[part], leave.at[step, chunk])
            jobs.append((step, chunk, count, incoming, outgoing))
            each_copy(incoming, "start")
    token[...] = jnp.zeros_like(token)
    for step, chunk, count, incoming, outgoing in jobs:

        @pl.when(incoming[0][0])
        def _(step=step, chunk=chunk, count=count, incoming=incoming, outgoing=outgoing):
            for _, source, place, flag in incoming:
                pltpu.make_async_copy(source, place, flag).wait()
            rows = slice(chunk * size, (chunk + 1) * size)
            grad_now = grads[step, rows, :]
            fresh = MOMENTUM_RATE * olds[step, rows, :] + grad_now
            position = lax.broadcasted_iota(jnp.int32, (size, columns), 0) + chunk * size
            olds[step, rows, :] = jnp.where(position < count, grad_now + MOMENTUM_RATE * fresh, 0.0)
            pltpu.make_async_copy(*outgoing[1:]).start()

    each_copy([job[-1] for job in jobs], "wait")


def fresh_kernel(live_ranks, row_counts, momentum, gradient, _, out):
    rank, matrix = lax.axis_index("fsdp"), pl.program_id(0)
    position = lax.broadcasted_iota(jnp.int32, out.shape, 0)
    keep = position < row_counts[matrix, rank] * live_ranks[rank]
    out[...] = jnp.where(keep, MOMENTUM_RATE * momentum[...] + gradient[...], 0.0)


def gram_kernel(first, ranks, *refs):
    tables, blocks, refs = refs[:4], refs[4 : 4 + ranks], refs[5 + ranks :]
    high_out, low_out, gram = refs[:3]
    landed, padded, high_held, low_held, arrive, leave = refs[-11:-5]
    slots, columns = blocks[0].shape
    rank = lax.axis_index("fsdp")

    @pl.when(is_inner(rank, ranks))
    def _():
        copies = []
        for step in range(ranks):
            copies.append(pltpu.make_async_copy(blocks[step], landed.at[step], arrive.at[step]))
            copies[-1].start()
        owner_group, _, _, row_offsets = fetch_tables(tables, refs[-5:])
        matrix = matrix_of(owner_group, rank ^ mate(ranks) if first else rank)
        padded[...] = jnp.zeros_like(padded)
        sublane = lax.broadcasted_iota(jnp.int32, (SUBLANES, columns), 0)
        for step in range(ranks):
            start = row_offsets[matrix, rank ^ step]
            shift = start % SUBLANES
            base = start - shift
            copies[step].wait()

            def tile(index, before, base=base, shift=shift, step=step):
                moved = pltpu.roll(landed[step, pl.ds(pl.multiple_of(index * SUBLANES, SUBLANES), SUBLANES), :], shift, 0)
                rows = pl.ds(pl.multiple_of(base + index * SUBLANES, SUBLANES), SUBLANES)
                padded[rows, :] = padded[rows, :] + jnp.where(sublane < shift, before, moved)
                return moved

            after = lax.fori_loop(0, slots // SUBLANES, tile, jnp.zeros((SUBLANES, columns), jnp.float32))
            rows = pl.ds(pl.multiple_of(base + slots, SUBLANES), SUBLANES)
            padded[rows, :] = padded[rows, :] + jnp.where(sublane < shift, after, 0.0)
        high, low = halves(padded[:INNER, :])
        high_held[...] = high
        low_held[...] = low
        outgoing = [
            pltpu.make_async_copy(high_held, high_out, leave.at[0]),
            pltpu.make_async_copy(low_held, low_out, leave.at[1]),
        ]
        if first:
            outgoing.append(pltpu.make_async_copy(padded.at[pl.ds(0, INNER)], refs[3], leave.at[2]))
        for copy in outgoing:
            copy.start()
        for panel in range(3):
            here = slice(panel * PANEL, (panel + 1) * PANEL)
            part = dot_halves((high[panel * PANEL :], low[panel * PANEL :]), (high[here], low[here]), ((1,), (1,)))
            store_panel(gram, panel, part)
        for copy in outgoing:
            copy.wait()


def store_panel(packed, panel, part):
    if panel == 0:
        packed[:, :PANEL] = part
    elif panel == 1:
        packed[: 2 * PANEL, PANEL:] = part
    else:
        packed[2 * PANEL :, PANEL:] = part


def unpack(packed, gram):
    gram[:, :PANEL] = packed[:, :PANEL]
    gram[PANEL:, PANEL : 2 * PANEL] = packed[: 2 * PANEL, PANEL:]
    gram[2 * PANEL :, 2 * PANEL :] = packed[2 * PANEL :, PANEL:]
    gram[:PANEL, PANEL:] = packed[PANEL:, :PANEL].T
    gram[PANEL : 2 * PANEL, 2 * PANEL :] = packed[PANEL : 2 * PANEL, PANEL:].T
    return gram[...]


def symmetric_product(left, right, out):
    for begin in range(0, INNER, TILE):
        end = min(begin + TILE, INNER)
        part = dot_halves(tuple(half[begin:] for half in left), tuple(half[:, begin:end] for half in right))
        out[begin:, begin:end] = part
        if end < INNER:
            out[begin:end, end:] = part[end - begin :].T
    return out[...]


def polynomial(raw, gram):
    diagonal = lax.broadcasted_iota(jnp.int32, raw.shape, 0) == lax.broadcasted_iota(jnp.int32, raw.shape, 1)
    square_total = jnp.sum(jnp.where(diagonal, raw, 0.0))
    norm = jnp.sqrt(jnp.full((1, 1), square_total, jnp.float32)) + EPSILON
    inverse = 1.0 / norm
    first = (raw * inverse) * inverse
    first_halves = halves(first)
    second = symmetric_product(first_halves, first_halves, gram)
    base = QUINTIC_SECOND * first + QUINTIC_THIRD * second + jnp.where(diagonal, QUINTIC_FIRST, 0.0)
    base_halves = halves(base)
    third_halves = halves(symmetric_product(base_halves, first_halves, gram))
    next_gram = symmetric_product(base_halves, third_halves, gram)
    next_halves = halves(next_gram)
    outer = (
        QUINTIC_SECOND * next_gram
        + QUINTIC_THIRD * symmetric_product(next_halves, next_halves, gram)
        + jnp.where(diagonal, QUINTIC_FIRST, 0.0)
    )
    return symmetric_product(halves(outer), base_halves, gram) * (inverse * OUT_SCALE)


def extract(padded, start, count, staged, step):
    _, slots, columns = staged.shape
    sublane = lax.broadcasted_iota(jnp.int32, (SUBLANES, columns), 0)
    shift = start % SUBLANES
    base = start - shift
    back = jnp.where(shift == 0, 0, SUBLANES - shift)

    def window(index):
        rows = pl.ds(pl.multiple_of(base + index * SUBLANES, SUBLANES), SUBLANES)
        return pltpu.roll(padded[rows, :], back, 0)

    def tile(index, here):
        after = window(index + 1)
        moved = jnp.where(sublane < SUBLANES - shift, here, after)
        rows = pl.ds(pl.multiple_of(index * SUBLANES, SUBLANES), SUBLANES)
        staged[step, rows, :] = jnp.where(sublane < count - index * SUBLANES, moved, 0.0)
        return after

    lax.fori_loop(0, slots // SUBLANES, tile, window(0))


def update_kernel(first, steps, *refs):
    tables, (packed, high, low, whole), refs = refs[:4], refs[4:8], refs[8:]
    homes, refs = refs[: len(steps)], refs[len(steps) :]
    gram, padded, staged, high_held, low_held, held, arrive, leave = refs[:8]
    ranks = tables[1].shape[0]
    rank = lax.axis_index("fsdp")
    incoming = [
        pltpu.make_async_copy(high, high_held, arrive.at[0]),
        pltpu.make_async_copy(low, low_held, arrive.at[1]),
    ]
    for copy in incoming:
        copy.start()
    owner_group, live_ranks, row_counts, row_offsets = fetch_tables(tables, refs[8:])
    matrix = matrix_of(owner_group, rank ^ mate(ranks) if first else rank)
    total = polynomial(unpack(packed, gram), gram)
    if first:
        for panel in range(3):
            store_panel(held, panel, total[panel * PANEL :, panel * PANEL : (panel + 1) * PANEL])
        copies = [pltpu.make_async_copy(held, whole, leave.at[len(steps)])]
        copies[0].start()
    for copy in incoming:
        copy.wait()
    padded[:INNER, :] = dot_halves(halves(total), (high_held[...], low_held[...]))
    if not first:
        copies = [pltpu.make_async_copy(padded.at[pl.ds(0, INNER)], whole, leave.at[len(steps)])]
        copies[0].start()
    for index, step in enumerate(steps):
        target = rank ^ step
        extract(padded, row_offsets[matrix, target], row_counts[matrix, target] * live_ranks[target], staged, index)
        copies.append(pltpu.make_async_copy(staged.at[index], homes[index], leave.at[index]))
        copies[-1].start()
    for copy in copies:
        copy.wait()


def finish_kernel(ranks, *refs):
    tables, (packed, iterate, inner_result, own_first, own_last, result, shards), refs = refs[:4], refs[4:11], refs[11:]
    gram, padded, staged, whole, held, arrive, leave = refs[:7]
    rank = lax.axis_index("fsdp")
    owner_group, live_ranks, row_counts, row_offsets = fetch_tables(tables, refs[7:])
    matrix = matrix_of(owner_group, rank)

    def run(jobs):
        copies = [pltpu.make_async_copy(*job) for job in jobs]
        for copy in copies:
            copy.start()
        for copy in copies:
            copy.wait()

    @pl.when(is_inner(rank, ranks))
    def _():
        run(
            [
                (inner_result, whole, arrive.at[0]),
                (own_first, staged.at[0], arrive.at[1]),
                (own_last, staged.at[1], arrive.at[2]),
            ]
        )
        other = matrix_of(owner_group, rank ^ mate(ranks))
        run(
            [
                (whole, result, leave.at[0]),
                (staged.at[0], shards.at[other], leave.at[1]),
                (staged.at[1], shards.at[matrix], leave.at[2]),
            ]
        )

    @pl.when(jnp.logical_not(is_inner(rank, ranks)))
    def _():
        run([(iterate, whole, arrive.at[0]), (packed, held, arrive.at[1])])
        padded[:INNER, :] = dot_halves(halves(unpack(held, gram)), halves(whole[...]))
        extract(padded, row_offsets[matrix, rank], row_counts[matrix, rank] * live_ranks[rank], staged, 0)
        run(
            [
                (padded.at[pl.ds(0, INNER)], result, leave.at[0]),
                (staged.at[0], shards.at[matrix], leave.at[1]),
            ]
        )


def place_kernel(first, ranks, steps, *refs):
    table, blocks, shards = refs[0], refs[1 : 1 + len(steps)], refs[2 + len(steps)]
    owner_group, arrive, leave = refs[3 + len(steps) :]
    rank = lax.axis_index("fsdp")
    fetch = pltpu.make_async_copy(table, owner_group, arrive)
    fetch.start()
    fetch.wait()
    copies = []
    for index, step in enumerate(steps):
        source = rank ^ step
        matrix = matrix_of(owner_group, source ^ mate(ranks) if first else source)
        copies.append((is_inner(source, ranks), blocks[index], shards.at[matrix], leave.at[index]))
    each_copy(copies, "start")
    each_copy(copies, "wait")


def idle_kernel(*refs):
    pass


def floats(*shape):
    return jax.ShapeDtypeStruct(shape, jnp.float32)


def vmem(*shape, dtype=jnp.float32):
    return pltpu.VMEM(shape, dtype)


def flags(*shape):
    return pltpu.SemaphoreType.DMA(shape)


FREE = pl.CostEstimate(flops=0, bytes_accessed=0, transcendentals=0)


def blend(first, tables, momentum, gradient, before):
    _, slots, columns = momentum.shape
    ranks = tables[1].shape[0]
    chunks = 4 if slots % (4 * SUBLANES) == 0 else 1
    return pl.pallas_call(
        functools.partial(blend_kernel, first, chunks),
        out_shape=[floats(slots, columns)] * ranks + [floats(SUBLANES, 128)],
        in_specs=[HBM] * 6 + [ANY] * len(before),
        out_specs=[ANY] * ranks + [VMEM],
        scratch_shapes=[vmem(ranks, slots, columns)] * 2
        + [flags(ranks, chunks, 2), flags(ranks, chunks)]
        + table_scratch(*tables[2].shape),
        compiler_params=FULL,
        cost_estimate=FREE,
        name="blend",
    )(*tables, momentum, gradient, *before)


def fresh_momentum(tables, momentum, gradient, before):
    matrices, slots, columns = momentum.shape
    block = pl.BlockSpec((None, slots, columns), lambda matrix: (matrix, 0, 0))
    return pl.pallas_call(
        fresh_kernel,
        grid=(matrices,),
        out_shape=floats(*momentum.shape),
        in_specs=[pl.BlockSpec(memory_space=pltpu.SMEM)] * 2 + [block] * 2 + [ANY],
        out_specs=block,
        compiler_params=FULL,
        cost_estimate=FREE,
        name="fresh_momentum",
    )(*tables[1:3], momentum, gradient, before)


def assemble_and_gram(first, tables, blocks, after):
    slots, columns = blocks[0].shape
    ranks = len(blocks)
    half = jax.ShapeDtypeStruct((INNER, columns), jnp.bfloat16)
    return pl.pallas_call(
        functools.partial(gram_kernel, first, ranks),
        out_shape=[half, half, floats(INNER, 2 * PANEL)] + [floats(INNER, columns)] * first,
        in_specs=[HBM] * 4 + [ANY] * (ranks + 1),
        out_specs=[ANY, ANY, VMEM] + [ANY] * first,
        scratch_shapes=[
            vmem(ranks, slots, columns),
            vmem(INNER + slots + SUBLANES, columns),
            vmem(INNER, columns, dtype=jnp.bfloat16),
            vmem(INNER, columns, dtype=jnp.bfloat16),
            flags(ranks),
            flags(3),
        ]
        + table_scratch(*tables[2].shape),
        compiler_params=PARAMS,
        cost_estimate=FREE,
        name="assemble_and_gram",
    )(*tables, *blocks, after)


def update_shapes(first, steps, slots, columns):
    whole = floats(INNER, 2 * PANEL if first else columns)
    return [whole] + [floats(slots, columns)] * len(steps)


def apply_update(first, steps, tables, packed, high, low, slots):
    columns = high.shape[1]
    return pl.pallas_call(
        functools.partial(update_kernel, first, steps),
        out_shape=update_shapes(first, steps, slots, columns),
        in_specs=[HBM] * 4 + [VMEM] + [ANY] * 2,
        out_specs=[ANY] * (1 + len(steps)),
        scratch_shapes=[
            vmem(INNER, INNER),
            vmem(INNER + slots + 2 * SUBLANES, columns),
            vmem(len(steps), slots, columns),
            vmem(INNER, columns, dtype=jnp.bfloat16),
            vmem(INNER, columns, dtype=jnp.bfloat16),
            vmem(INNER, 2 * PANEL),
            flags(2),
            flags(len(steps) + 1),
        ]
        + table_scratch(*tables[2].shape),
        compiler_params=PARAMS,
        cost_estimate=FREE,
        name="apply_update",
    )(*tables, packed, high, low)


def nothing(shapes):
    return pl.pallas_call(idle_kernel, out_shape=shapes, out_specs=[ANY] * len(shapes), name="nothing")()


def finish(tables, packed, iterate, inner_result, own_first, own_last, shape):
    slots, columns = own_first.shape
    return pl.pallas_call(
        functools.partial(finish_kernel, tables[1].shape[0]),
        out_shape=[floats(INNER, columns), floats(*shape)],
        in_specs=[HBM] * 4 + [ANY] * 5,
        out_specs=[HBM] * 2,
        scratch_shapes=[
            vmem(INNER, INNER),
            vmem(INNER + slots + 2 * SUBLANES, columns),
            vmem(2, slots, columns),
            vmem(INNER, columns),
            vmem(INNER, 2 * PANEL),
            flags(3),
            flags(3),
        ]
        + table_scratch(*tables[2].shape),
        compiler_params=PARAMS,
        cost_estimate=FREE,
        name="finish",
    )(*tables, packed, iterate, inner_result, own_first, own_last)


def place_blocks(first, owner_group, steps, blocks, shards, ranks):
    return pl.pallas_call(
        functools.partial(place_kernel, first, ranks, steps),
        out_shape=floats(*shards.shape),
        in_specs=[HBM] + [VMEM] * len(blocks) + [HBM],
        out_specs=HBM,
        scratch_shapes=[pltpu.SMEM(owner_group.shape, jnp.int32), flags(), flags(len(steps))],
        input_output_aliases={1 + len(blocks): 0},
        compiler_params=PARAMS,
        cost_estimate=FREE,
        name="place_blocks",
    )(owner_group, *blocks, shards)


def group_stages(size):
    stages, shift = [], 0
    while (1 << shift) < size:
        wide = 1 if shift == 0 or (2 << shift) >= size else 2
        stages.append((shift, 1 << wide))
        shift += wide
    return stages


def sum_over(block, axis):
    size = lax.axis_size(axis)
    if size & (size - 1) or block.shape[0] % size:
        return lax.psum(block, axis)
    index = lax.axis_index(axis)

    def exchange(piece, step):
        return lax.ppermute(piece, axis, [(i, i ^ step) for i in range(size)])

    stages = group_stages(size)
    for shift, group in stages:
        digit = (index >> shift) & (group - 1)
        part = block.shape[0] // group
        pieces = [lax.dynamic_slice_in_dim(block, (digit ^ step) * part, part, 0) for step in range(group)]
        arrived = [exchange(pieces[step], step << shift) for step in range(1, group)]
        block = functools.reduce(jnp.add, arrived, pieces[0])
    for shift, group in reversed(stages):
        digit = (index >> shift) & (group - 1)
        part = block.shape[0]
        pieces = [block] + [exchange(block, step << shift) for step in range(1, group)]
        block = jnp.zeros((part * group, block.shape[1]), block.dtype)
        for step, piece in enumerate(pieces):
            block = lax.dynamic_update_slice_in_dim(block, piece, (digit ^ step) * part, 0)
    return block


def on_device(momentum, gradient, live_ranks, owner_group, row_counts, row_offsets):
    ranks = lax.axis_size("fsdp")
    my_rank = lax.axis_index("fsdp")
    _, slots, columns = momentum.shape
    tables = (owner_group, live_ranks, row_counts, row_offsets)
    inner = is_inner(my_rank, ranks)
    last = [2, 1, *range(3, ranks)]
    early = [step for step in last if step != mate(ranks)]

    def pairs(step, inward):
        return [(i, i ^ step) for i in range(ranks) if is_inner(i ^ step if inward else i, ranks)]

    def to_inner(block, step):
        return lax.ppermute(block, "fsdp", pairs(step, True))

    def from_inner(block, step):
        return lax.ppermute(block, "fsdp", pairs(step, False))

    *blends, token = blend(True, tables, momentum, gradient, [])
    first_blocks = [blends[0]] + [to_inner(blends[step], step) for step in range(1, ranks)]
    *blends, token = blend(False, tables, momentum, gradient, [token])
    last_blocks = [blends[0]] + [to_inner(blends[step], step) for step in range(1, ranks)]
    new_momentum = fresh_momentum(tables, momentum, gradient, token)

    high, low, gram_part, iterate = assemble_and_gram(True, tables, first_blocks, new_momentum)
    iterate = from_inner(iterate, mate(ranks))

    def first_update(high, low, gram_part):
        return apply_update(True, [0, *early], tables, sum_over(gram_part, "tensor"), high, low, slots)

    def first_skip(high, low, gram_part):
        return nothing(update_shapes(True, [0, *early], slots, columns))

    packed, own_first, *homes = lax.cond(inner, first_update, first_skip, high, low, gram_part)
    packed_there = from_inner(packed, mate(ranks))
    first_home = [from_inner(block, step) for step, block in zip(early, homes)]

    def last_update(after, *blocks):
        high, low, gram_part = assemble_and_gram(False, tables, blocks, after)
        return apply_update(False, [0, *last], tables, sum_over(gram_part, "tensor"), high, low, slots)

    def last_skip(after, *blocks):
        return nothing(update_shapes(False, [0, *last], slots, columns))

    result, own_last, *homes = lax.cond(inner, last_update, last_skip, packed, *last_blocks)
    last_home = [from_inner(block, step) for step, block in zip(last, homes)]

    result, shards = finish(tables, packed_there, iterate, result, own_first, own_last, momentum.shape)
    shards = place_blocks(True, owner_group, early, first_home, shards, ranks)
    for step, block in zip(last, last_home):
        shards = place_blocks(False, owner_group, [step], [block], shards, ranks)
    return (new_momentum, shards, result[None])


def solution(mesh):
    placed = (P(None, "fsdp", "tensor"), P(None, "fsdp", "tensor"), P(), P(), P(), P())
    return jax.shard_map(
        on_device,
        mesh=mesh,
        in_specs=placed,
        out_specs=(P(None, "fsdp", "tensor"), P(None, "fsdp", "tensor"), P("fsdp", None, "tensor")),
        check_vma=False,
    )
```

time: 451 us -> 300 us (0.67)
  the two profiles are of different devices: /device:TPU:0 before, /device:TPU:8 now
where the time goes in v5:
time: 300 us; the launch traced here: 299 us
  waiting for transfers between devices  176 us (59%)
  Pallas kernels  67.7 us (23%)
  starting transfers between devices  43.5 us (14%)
  local copies, waits for them, and re-layouts  5.88 us (2%)
  other arithmetic  4.46 us (1%)
    ppermute x7, waiting for transfers between devices, from_inner(): return lax.ppermute(block, 'fsdp', pairs(step, False))  74.9 us
    ppermute x6, waiting for transfers between devices, to_inner(): return lax.ppermute(block, 'fsdp', pairs(step, True))  74.1 us
    pallas_call x2, Pallas kernels, apply_update(): pl.pallas_call(functools.partial(update_kernel, first, steps), out_shape=...  29.3 us
    ppermute x16, waiting for transfers between devices, exchange(): return lax.ppermute(piece, axis, [(i, i ^ step) for i in range(size)])  26.9 us
    ppermute x7, starting transfers between devices, from_inner(): return lax.ppermute(block, 'fsdp', pairs(step, False))  16.9 us
    ppermute x16, starting transfers between devices, exchange(): return lax.ppermute(piece, axis, [(i, i ^ step) for i in range(size)])  14.4 us
    pallas_call x2, Pallas kernels, assemble_and_gram(): pl.pallas_call(functools.partial(gram_kernel, first, ranks), out_shape=[h...  13.2 us
    ppermute x6, starting transfers between devices, to_inner(): return lax.ppermute(block, 'fsdp', pairs(step, True))  12.1 us
  transfers between devices with their start and end apart: 29, of which 24 were waited for; matrix products, arithmetic and copies ran while one was open for 2% of the time, Pallas kernels for 18%

profile of v5, /device:TPU:8, one launch (start us, length us, event | category | flops | bytes accessed | tf_op | source)
XLA Modules:
  0.0 299.3 jit_solution(2435271065828203885)
XLA Ops:
  0.7 5.2 %blend.2 = (f32[288,896]{1,0:T(8,128)}, f32[288,896]{1,0:T(8,128)}, f32[288,896]{1,0:T(8,128)}, f32[288,896]{1,0:T(8,128)}, f32[8,128]{1,0:T(8,128)}) custom-call(s32[4]{0:T(128)} %refs_0_.15, s32[4]{0:T(128)} %refs_1_.7, s32[4,4]{1,0:T(4,128)} %refs_2_.7, s32[4,4]{1,0:T(4,128)} %refs_3_.7, f32[4,288,896]{2,1,0:T(8,128)} %momentum.1, f32[4,288,896]{2,1,0:T(8,128)} %gradient.1), custom_call_target="tpu_custom_call" | custom-call | tf_op jit(solution)/shard_map/blend/pallas_call | solution.py:381
  8.5 3.5 %collective-permute-start.21 = (f32[288,896]{1,0:T(8,128)}, f32[288,896]{1,0:T(8,128)S(1)}, u32[]{:S(2)}, u32[]{:S(2)}) collective-permute-start(f32[288,896]{1,0:T(8,128)} %get-tuple-element.88), channel_id=1, source_target_pairs={{8,16},{16,8},{9,17},{17,9},{10,18},{18,10},{11,19},{19,11},{12,20... | collective-permute-start | bytes 3096584 | tf_op jit(solution)/shard_map/ppermute | solution.py:552
  12.0 4.9 %blend.3 = (f32[288,896]{1,0:T(8,128)}, f32[288,896]{1,0:T(8,128)}, f32[288,896]{1,0:T(8,128)}, f32[288,896]{1,0:T(8,128)}, f32[8,128]{1,0:T(8,128)}) custom-call(s32[4]{0:T(128)S(1)} %copy-done.13, s32[4]{0:T(128)S(1)} %copy-done.17, s32[4,4]{1,0:T(4,128)S(1)} %copy-done.7, s32[4,4]{1,0:T(4,128)S(1)} %copy-done.10, f32[4,288,896]{2,1,0:T(8,128)} %momentum.1, ...), custom_call_target="tpu_custom_call" | custom-call | tf_op jit(solution)/shard_map/blend/pallas_call | solution.py:381
  17.0 5.9 %fresh_momentum.1.refs_8_ = f32[4,288,896]{2,1,0:T(8,128)} custom-call(s32[4]{0:T(128)} %refs_1_.7, s32[4,4]{1,0:T(4,128)} %refs_2_.7, f32[4,288,896]{2,1,0:T(8,128)} %momentum.1, f32[4,288,896]{2,1,0:T(8,128)} %gradient.1, f32[8,128]{1,0:T(8,128)} %get-tuple-element.80._), custom_call_target="tpu_custom_call" | custom-call | tf_op jit(solution)/shard_map/fresh_momentum/pallas_call | solution.py:398
  22.9 10.8 %collective-permute-done.19.refs_5_ = f32[288,896]{1,0:T(8,128)S(1)} collective-permute-done((f32[288,896]{1,0:T(8,128)}, f32[288,896]{1,0:T(8,128)S(1)}, u32[]{:S(2)}, u32[]{:S(2)}) %collective-permute-start.19) | collective-permute-done | bytes 1032224 | tf_op jit(solution)/shard_map/ppermute | solution.py:552
  33.7 22.1 %collective-permute-done.20.refs_6_ = f32[288,896]{1,0:T(8,128)S(1)} collective-permute-done((f32[288,896]{1,0:T(8,128)}, f32[288,896]{1,0:T(8,128)S(1)}, u32[]{:S(2)}, u32[]{:S(2)}) %collective-permute-start.20) | collective-permute-done | bytes 1032224 | tf_op jit(solution)/shard_map/ppermute | solution.py:552
  57.3 7.2 %assemble_and_gram.3 = (bf16[576,896]{1,0:T(8,128)(2,1)}, bf16[576,896]{1,0:T(8,128)(2,1)}, f32[576,384]{1,0:T(8,128)}, f32[576,896]{1,0:T(8,128)}) custom-call(s32[4]{0:T(128)} %refs_0_.15, s32[4]{0:T(128)} %refs_1_.7, s32[4,4]{1,0:T(4,128)} %refs_2_.7, s32[4,4]{1,0:T(4,128)} %refs_3_.7, f32[288,896]{1,0:T(8,128)S(1)} %copy-done.2, ...), custom_call_target="tpu_custom_call" | custom-call | tf_op jit(solution)/shard_map/assemble_and_gram/pallas_call | solution.py:414
  67.2 39.5 %conditional.2 = ((f32[576,384]{1,0:T(8,128)}, f32[288,896]{1,0:T(8,128)}, f32[288,896]{1,0:T(8,128)}, f32[288,896]{1,0:T(8,128)})) conditional(s32[]{:T(128)} %convert_element_type.4, () %tuple.21, (f32[576,384]{1,0:T(8,128)}, s32[4]{0:T(128)}, s32[4]{0:T(128)}, s32[4,4]{1,0:T(4,128)}, s32[4,4]{1,0:T(4,128)}, /*index=5*/bf16[576,896]{1,0:T(8,128)(2,1)}, ...), branch_computations={%region_0.0_spmd, %region_1.0_spmd} | conditional | flops 193570 | bytes 21751340 | solution.py:572
  77.9 2.6 collective-permute-done.2
  92.3 14.4 %apply_update.2 = (f32[576,384]{1,0:T(8,128)}, f32[288,896]{1,0:T(8,128)}, f32[288,896]{1,0:T(8,128)}, f32[288,896]{1,0:T(8,128)}) custom-call(s32[4]{0:T(128)S(1)} %copy-done.15, s32[4]{0:T(128)S(1)} %copy-done.18, s32[4,4]{1,0:T(4,128)S(1)} %copy-done.8, s32[4,4]{1,0:T(4,128)S(1)} %copy-done.11, f32[576,384]{1,0:T(8,128)S(1)} %constant_dynamic-update-slice_fusion.refs_4_, ...), custom_call_target="tpu_custom_call" | custom-call | tf_op jit(solution)/shard_map/cond/branch_1_fun/apply_update/pallas_call | solution.py:441
  107.9 3.5 %collective-permute-start.18 = (f32[288,896]{1,0:T(8,128)}, f32[288,896]{1,0:T(8,128)}, u32[]{:S(2)}, u32[]{:S(2)}) collective-permute-start(f32[288,896]{1,0:T(8,128)} %get-tuple-element.84), channel_id=1, source_target_pairs={{8,16},{16,8},{9,17},{17,9},{10,18},{18,10},{11,19},{19,11},{12,20... | collective-permute-start | bytes 3096584 | tf_op jit(solution)/shard_map/ppermute | solution.py:552
  111.4 5.6 %collective-permute-start.27 = (f32[576,384]{1,0:T(8,128)}, f32[576,384]{1,0:T(8,128)}, u32[]{:S(2)}, u32[]{:S(2)}) collective-permute-start(f32[576,384]{1,0:T(8,128)} %get-tuple-element.92), channel_id=1, source_target_pairs={{8,0},{16,24},{9,1},{17,25},{10,2},{18,26},{11,3},{19,27},{12,4},{... | collective-permute-start | bytes 2654216 | tf_op jit(solution)/shard_map/ppermute | solution.py:555
  117.0 17.7 %collective-permute-done.17 = f32[288,896]{1,0:T(8,128)} collective-permute-done((f32[288,896]{1,0:T(8,128)}, f32[288,896]{1,0:T(8,128)}, u32[]{:S(2)}, u32[]{:S(2)}) %collective-permute-start.17) | collective-permute-done | bytes 1032224 | tf_op jit(solution)/shard_map/ppermute | solution.py:552
  134.7 22.0 %collective-permute-done.18 = f32[288,896]{1,0:T(8,128)} collective-permute-done((f32[288,896]{1,0:T(8,128)}, f32[288,896]{1,0:T(8,128)}, u32[]{:S(2)}, u32[]{:S(2)}) %collective-permute-start.18) | collective-permute-done | bytes 1032224 | tf_op jit(solution)/shard_map/ppermute | solution.py:552
  156.7 48.3 %conditional.3 = ((f32[576,896]{1,0:T(8,128)}, f32[288,896]{1,0:T(8,128)}, f32[288,896]{1,0:T(8,128)}, f32[288,896]{1,0:T(8,128)}, f32[288,896]{1,0:T(8,128)})) conditional(s32[]{:T(128)} %convert_element_type.4, () %tuple.20, (s32[4]{0:T(128)}, s32[4]{0:T(128)}, s32[4,4]{1,0:T(4,128)}, s32[4,4]{1,0:T(4,128)}, f32[288,896]{1,0:T(8,128)}, ...), branch_computations={%region_2.0_spmd, %region_3.0_spmd} | conditional | flops 193570 | bytes 29419108 | solution.py:583
  157.7 6.1 %assemble_and_gram.2 = (bf16[576,896]{1,0:T(8,128)(2,1)S(1)}, bf16[576,896]{1,0:T(8,128)(2,1)S(1)}, f32[576,384]{1,0:T(8,128)S(1)}) custom-call(s32[4]{0:T(128)} %get-tuple-element.39.refs_0_, s32[4]{0:T(128)} %get-tuple-element.40.refs_1_, s32[4,4]{1,0:T(4,128)} %get-tuple-element.41.refs_2_, s32[4,4]{1,0:T(4,128)} %get-tuple-element.42.refs_3_, ...), custom_call_target="tpu_custom_call" | custom-call | tf_op jit(solution)/shard_map/cond/branch_1_fun/assemble_and_gram/pallas_call | solution.py:414
  173.1 3.5 %collective-permute-done.10 = f32[72,384]{1,0:T(8,128)} collective-permute-done((f32[72,384]{1,0:T(8,128)}, f32[72,384]{1,0:T(8,128)}, u32[]{:S(2)}, u32[]{:S(2)}) %collective-permute-start.10) | collective-permute-done | bytes 110624 | tf_op jit(solution)/shard_map/cond/branch_1_fun/ppermute | solution.py:520
  189.8 15.0 %apply_update.3 = (f32[576,896]{1,0:T(8,128)}, f32[288,896]{1,0:T(8,128)}, f32[288,896]{1,0:T(8,128)}, f32[288,896]{1,0:T(8,128)}, f32[288,896]{1,0:T(8,128)}) custom-call(s32[4]{0:T(128)S(1)} %copy-done.16, s32[4]{0:T(128)S(1)} %copy-done.19, s32[4,4]{1,0:T(4,128)S(1)} %copy-done.9, s32[4,4]{1,0:T(4,128)S(1)} %copy-done.12, ...), custom_call_target="tpu_custom_call" | custom-call | tf_op jit(solution)/shard_map/cond/branch_1_fun/apply_update/pallas_call | solution.py:441
  206.4 3.5 %collective-permute-start.26 = (f32[288,896]{1,0:T(8,128)}, f32[288,896]{1,0:T(8,128)S(1)}, u32[]{:S(2)}, u32[]{:S(2)}) collective-permute-start(f32[288,896]{1,0:T(8,128)} %get-tuple-element.97), channel_id=1, source_target_pairs={{8,16},{16,8},{9,17},{17,9},{10,18},{18,10},{11,19},{19,11},{12,20... | collective-permute-start | bytes 3096584 | tf_op jit(solution)/shard_map/ppermute | solution.py:555
  215.0 5.0 %finish.1 = (f32[576,896]{1,0:T(8,128)}, f32[4,288,896]{2,1,0:T(8,128)}) custom-call(s32[4]{0:T(128)} %refs_0_.15, s32[4]{0:T(128)} %refs_1_.7, s32[4,4]{1,0:T(4,128)} %refs_2_.7, s32[4,4]{1,0:T(4,128)} %refs_3_.7, f32[576,384]{1,0:T(8,128)} %collective-permute-done.27.refs_4_, f32[576,896]{1,0:T(8,128)S(1)} %collective-permute-done.28.refs_5_, ...), custom_call_target="tpu_custom_call" | custom-call | tf_op jit(solution)/shard_map/finish/pallas_call | solution.py:469
  220.0 9.8 %collective-permute-done.25.refs_1_ = f32[288,896]{1,0:T(8,128)S(1)} collective-permute-done((f32[288,896]{1,0:T(8,128)}, f32[288,896]{1,0:T(8,128)S(1)}, u32[]{:S(2)}, u32[]{:S(2)}) %collective-permute-start.25) | collective-permute-done | bytes 1032224 | tf_op jit(solution)/shard_map/ppermute | solution.py:555
  229.8 24.0 %collective-permute-done.26.refs_2_ = f32[288,896]{1,0:T(8,128)S(1)} collective-permute-done((f32[288,896]{1,0:T(8,128)}, f32[288,896]{1,0:T(8,128)S(1)}, u32[]{:S(2)}, u32[]{:S(2)}) %collective-permute-start.26) | collective-permute-done | bytes 1032224 | tf_op jit(solution)/shard_map/ppermute | solution.py:555
  255.4 18.7 %collective-permute-done.24.refs_1_ = f32[288,896]{1,0:T(8,128)S(1)} collective-permute-done((f32[288,896]{1,0:T(8,128)}, f32[288,896]{1,0:T(8,128)S(1)}, u32[]{:S(2)}, u32[]{:S(2)}) %collective-permute-start.24) | collective-permute-done | bytes 1032224 | tf_op jit(solution)/shard_map/ppermute | solution.py:555
  275.2 22.4 %collective-permute-done.22.refs_1_ = f32[288,896]{1,0:T(8,128)S(1)} collective-permute-done((f32[288,896]{1,0:T(8,128)}, f32[288,896]{1,0:T(8,128)S(1)}, u32[]{:S(2)}, u32[]{:S(2)}) %collective-permute-start.22) | collective-permute-done | bytes 1032224 | tf_op jit(solution)/shard_map/ppermute | solution.py:555
  (110 shorter events, 64.2 us)
Async XLA Ops:
  5.9 27.8 %collective-permute-start.19 = (f32[288,896]{1,0:T(8,128)}, f32[288,896]{1,0:T(8,128)S(1)}, u32[]{:S(2)}, u32[]{:S(2)}) collective-permute-start(f32[288,896]{1,0:T(8,128)} %get-tuple-element.86), channel_id=1, source_target_pairs={{0,8},{24,16},{1,9},{25,17},{2,10},{26,18},{3,11},{27,19},{4,12},{... | collective-permute-start | bytes 3096584 | tf_op jit(solution)/shard_map/ppermute | solution.py:552
  7.2 48.6 %collective-permute-start.20 = (f32[288,896]{1,0:T(8,128)}, f32[288,896]{1,0:T(8,128)S(1)}, u32[]{:S(2)}, u32[]{:S(2)}) collective-permute-start(f32[288,896]{1,0:T(8,128)} %get-tuple-element.87), channel_id=1, source_target_pairs={{0,16},{24,8},{1,17},{25,9},{2,18},{26,10},{3,19},{27,11},{4,20},{... | collective-permute-start | bytes 3096584 | tf_op jit(solution)/shard_map/ppermute | solution.py:552
  8.5 48.8 %collective-permute-start.21 = (f32[288,896]{1,0:T(8,128)}, f32[288,896]{1,0:T(8,128)S(1)}, u32[]{:S(2)}, u32[]{:S(2)}) collective-permute-start(f32[288,896]{1,0:T(8,128)} %get-tuple-element.88), channel_id=1, source_target_pairs={{8,16},{16,8},{9,17},{17,9},{10,18},{18,10},{11,19},{19,11},{12,20... | collective-permute-start | bytes 3096584 | tf_op jit(solution)/shard_map/ppermute | solution.py:552
  64.4 148.2 %collective-permute-start.28 = (f32[576,896]{1,0:T(8,128)}, f32[576,896]{1,0:T(8,128)S(1)}, u32[]{:S(2)}, u32[]{:S(2)}) collective-permute-start(f32[576,896]{1,0:T(8,128)} %get-tuple-element.98), channel_id=1, source_target_pairs={{8,0},{16,24},{9,1},{17,25},{10,2},{18,26},{11,3},{19,27},{12,4},{... | collective-permute-start | bytes 6193160 | tf_op jit(solution)/shard_map/ppermute | solution.py:555
  65.9 51.2 %collective-permute-start.16 = (f32[288,896]{1,0:T(8,128)}, f32[288,896]{1,0:T(8,128)S(1)}, u32[]{:S(2)}, u32[]{:S(2)}) collective-permute-start(f32[288,896]{1,0:T(8,128)} %get-tuple-element.82), channel_id=1, source_target_pairs={{0,8},{24,16},{1,9},{25,17},{2,10},{26,18},{3,11},{27,19},{4,12},{... | collective-permute-start | bytes 3096584 | tf_op jit(solution)/shard_map/ppermute | solution.py:552
  72.4 5.4 %collective-permute-start.1 = (f32[72,384]{1,0:T(8,128)}, f32[72,384]{1,0:T(8,128)}, u32[]{:S(2)}, u32[]{:S(2)}) collective-permute-start(f32[72,384]{1,0:T(8,128)} %get-tuple-element.108), channel_id=1, source_target_pairs={{0,2},{1,3},{2,0},{3,1},{4,6},{5,7},{6,4},{7,5},{8,10},{9,11},{10,... | collective-permute-start | bytes 331784 | tf_op jit(solution)/shard_map/cond/branch_1_fun/ppermute | solution.py:520
  73.9 6.5 %collective-permute-start.2 = (f32[72,384]{1,0:T(8,128)}, f32[72,384]{1,0:T(8,128)}, u32[]{:S(2)}, u32[]{:S(2)}) collective-permute-start(f32[72,384]{1,0:T(8,128)} %get-tuple-element.110), channel_id=1, source_target_pairs={{0,4},{1,5},{2,6},{3,7},{4,0},{5,1},{6,2},{7,3},{8,12},{9,13},{10,... | collective-permute-start | bytes 331784 | tf_op jit(solution)/shard_map/cond/branch_1_fun/ppermute | solution.py:520
  75.5 6.0 %collective-permute-start.3 = (f32[72,384]{1,0:T(8,128)}, f32[72,384]{1,0:T(8,128)}, u32[]{:S(2)}, u32[]{:S(2)}) collective-permute-start(f32[72,384]{1,0:T(8,128)} %get-tuple-element.109), channel_id=1, source_target_pairs={{0,6},{1,7},{2,4},{3,5},{4,2},{5,3},{6,0},{7,1},{8,14},{9,15},{10,... | collective-permute-start | bytes 331784 | tf_op jit(solution)/shard_map/cond/branch_1_fun/ppermute | solution.py:520
  82.5 5.6 %collective-permute-start.4 = (f32[72,384]{1,0:T(8,128)S(1)}, f32[72,384]{1,0:T(8,128)S(1)}, u32[]{:S(2)}, u32[]{:S(2)}) collective-permute-start(f32[72,384]{1,0:T(8,128)S(1)} %get-tuple-element.105), channel_id=1, source_target_pairs={{0,2},{1,3},{2,0},{3,1},{4,6},{5,7},{6,4},{7,5},{8,10},{9,11},{10,... | collective-permute-start | bytes 331784 | tf_op jit(solution)/shard_map/cond/branch_1_fun/ppermute | solution.py:520
  84.6 5.6 %collective-permute-start.6 = (f32[72,384]{1,0:T(8,128)S(1)}, f32[72,384]{1,0:T(8,128)S(1)}, u32[]{:S(2)}, u32[]{:S(2)}) collective-permute-start(f32[72,384]{1,0:T(8,128)S(1)} %get-tuple-element.105), channel_id=1, source_target_pairs={{0,6},{1,7},{2,4},{3,5},{4,2},{5,3},{6,0},{7,1},{8,14},{9,15},{10,... | collective-permute-start | bytes 331784 | tf_op jit(solution)/shard_map/cond/branch_1_fun/ppermute | solution.py:520
  106.6 28.1 %collective-permute-start.17 = (f32[288,896]{1,0:T(8,128)}, f32[288,896]{1,0:T(8,128)}, u32[]{:S(2)}, u32[]{:S(2)}) collective-permute-start(f32[288,896]{1,0:T(8,128)} %get-tuple-element.83), channel_id=1, source_target_pairs={{0,16},{24,8},{1,17},{25,9},{2,18},{26,10},{3,19},{27,11},{4,20},{... | collective-permute-start | bytes 3096584 | tf_op jit(solution)/shard_map/ppermute | solution.py:552
  107.9 48.8 %collective-permute-start.18 = (f32[288,896]{1,0:T(8,128)}, f32[288,896]{1,0:T(8,128)}, u32[]{:S(2)}, u32[]{:S(2)}) collective-permute-start(f32[288,896]{1,0:T(8,128)} %get-tuple-element.84), channel_id=1, source_target_pairs={{8,16},{16,8},{9,17},{17,9},{10,18},{18,10},{11,19},{19,11},{12,20... | collective-permute-start | bytes 3096584 | tf_op jit(solution)/shard_map/ppermute | solution.py:552
  111.4 99.8 %collective-permute-start.27 = (f32[576,384]{1,0:T(8,128)}, f32[576,384]{1,0:T(8,128)}, u32[]{:S(2)}, u32[]{:S(2)}) collective-permute-start(f32[576,384]{1,0:T(8,128)} %get-tuple-element.92), channel_id=1, source_target_pairs={{8,0},{16,24},{9,1},{17,25},{10,2},{18,26},{11,3},{19,27},{12,4},{... | collective-permute-start | bytes 2654216 | tf_op jit(solution)/shard_map/ppermute | solution.py:555
  169.6 7.0 %collective-permute-start.10 = (f32[72,384]{1,0:T(8,128)}, f32[72,384]{1,0:T(8,128)}, u32[]{:S(2)}, u32[]{:S(2)}) collective-permute-start(f32[72,384]{1,0:T(8,128)} %get-tuple-element.113), channel_id=1, source_target_pairs={{0,4},{1,5},{2,6},{3,7},{4,0},{5,1},{6,2},{7,3},{8,12},{9,13},{10,... | collective-permute-start | bytes 331784 | tf_op jit(solution)/shard_map/cond/branch_1_fun/ppermute | solution.py:520
  171.0 7.2 %collective-permute-start.11 = (f32[72,384]{1,0:T(8,128)}, f32[72,384]{1,0:T(8,128)}, u32[]{:S(2)}, u32[]{:S(2)}) collective-permute-start(f32[72,384]{1,0:T(8,128)} %get-tuple-element.112), channel_id=1, source_target_pairs={{0,6},{1,7},{2,4},{3,5},{4,2},{5,3},{6,0},{7,1},{8,14},{9,15},{10,... | collective-permute-start | bytes 331784 | tf_op jit(solution)/shard_map/cond/branch_1_fun/ppermute | solution.py:520
  172.6 6.1 %collective-permute-start.9 = (f32[72,384]{1,0:T(8,128)}, f32[72,384]{1,0:T(8,128)}, u32[]{:S(2)}, u32[]{:S(2)}) collective-permute-start(f32[72,384]{1,0:T(8,128)} %get-tuple-element.111), channel_id=1, source_target_pairs={{0,2},{1,3},{2,0},{3,1},{4,6},{5,7},{6,4},{7,5},{8,10},{9,11},{10,... | collective-permute-start | bytes 331784 | tf_op jit(solution)/shard_map/cond/branch_1_fun/ppermute | solution.py:520
  179.7 5.6 %collective-permute-start.12 = (f32[72,384]{1,0:T(8,128)S(1)}, f32[72,384]{1,0:T(8,128)S(1)}, u32[]{:S(2)}, u32[]{:S(2)}) collective-permute-start(f32[72,384]{1,0:T(8,128)S(1)} %get-tuple-element.107), channel_id=1, source_target_pairs={{0,2},{1,3},{2,0},{3,1},{4,6},{5,7},{6,4},{7,5},{8,10},{9,11},{10,... | collective-permute-start | bytes 331784 | tf_op jit(solution)/shard_map/cond/branch_1_fun/ppermute | solution.py:520
  181.2 6.6 %collective-permute-start.13 = (f32[72,384]{1,0:T(8,128)S(1)}, f32[72,384]{1,0:T(8,128)S(1)}, u32[]{:S(2)}, u32[]{:S(2)}) collective-permute-start(f32[72,384]{1,0:T(8,128)S(1)} %get-tuple-element.107), channel_id=1, source_target_pairs={{0,4},{1,5},{2,6},{3,7},{4,0},{5,1},{6,2},{7,3},{8,12},{9,13},{10,... | collective-permute-start | bytes 331784 | tf_op jit(solution)/shard_map/cond/branch_1_fun/ppermute | solution.py:520
  182.0 5.9 %collective-permute-start.14 = (f32[72,384]{1,0:T(8,128)S(1)}, f32[72,384]{1,0:T(8,128)S(1)}, u32[]{:S(2)}, u32[]{:S(2)}) collective-permute-start(f32[72,384]{1,0:T(8,128)S(1)} %get-tuple-element.107), channel_id=1, source_target_pairs={{0,6},{1,7},{2,4},{3,5},{4,2},{5,3},{6,0},{7,1},{8,14},{9,15},{10,... | collective-permute-start | bytes 331784 | tf_op jit(solution)/shard_map/cond/branch_1_fun/ppermute | solution.py:520
  205.0 24.8 %collective-permute-start.25 = (f32[288,896]{1,0:T(8,128)}, f32[288,896]{1,0:T(8,128)S(1)}, u32[]{:S(2)}, u32[]{:S(2)}) collective-permute-start(f32[288,896]{1,0:T(8,128)} %get-tuple-element.96), channel_id=1, source_target_pairs={{8,24},{16,0},{9,25},{17,1},{10,26},{18,2},{11,27},{19,3},{12,28},... | collective-permute-start | bytes 3096584 | tf_op jit(solution)/shard_map/ppermute | solution.py:555
  206.4 47.4 %collective-permute-start.26 = (f32[288,896]{1,0:T(8,128)}, f32[288,896]{1,0:T(8,128)S(1)}, u32[]{:S(2)}, u32[]{:S(2)}) collective-permute-start(f32[288,896]{1,0:T(8,128)} %get-tuple-element.97), channel_id=1, source_target_pairs={{8,16},{16,8},{9,17},{17,9},{10,18},{18,10},{11,19},{19,11},{12,20... | collective-permute-start | bytes 3096584 | tf_op jit(solution)/shard_map/ppermute | solution.py:555
  209.9 64.2 %collective-permute-start.24 = (f32[288,896]{1,0:T(8,128)}, f32[288,896]{1,0:T(8,128)S(1)}, u32[]{:S(2)}, u32[]{:S(2)}) collective-permute-start(f32[288,896]{1,0:T(8,128)} %get-tuple-element.95), channel_id=1, source_target_pairs={{8,24},{16,0},{9,25},{17,1},{10,26},{18,2},{11,27},{19,3},{12,28},... | collective-permute-start | bytes 3096584 | tf_op jit(solution)/shard_map/ppermute | solution.py:555
  211.2 63.4 %collective-permute-start.23 = (f32[288,896]{1,0:T(8,128)}, f32[288,896]{1,0:T(8,128)S(1)}, u32[]{:S(2)}, u32[]{:S(2)}) collective-permute-start(f32[288,896]{1,0:T(8,128)} %get-tuple-element.94), channel_id=1, source_target_pairs={{8,0},{16,24},{9,1},{17,25},{10,2},{18,26},{11,3},{19,27},{12,4},{... | collective-permute-start | bytes 3096584 | tf_op jit(solution)/shard_map/ppermute | solution.py:555
  212.6 85.0 %collective-permute-start.22 = (f32[288,896]{1,0:T(8,128)}, f32[288,896]{1,0:T(8,128)S(1)}, u32[]{:S(2)}, u32[]{:S(2)}) collective-permute-start(f32[288,896]{1,0:T(8,128)} %get-tuple-element.93), channel_id=1, source_target_pairs={{8,16},{16,8},{9,17},{17,9},{10,18},{18,10},{11,19},{19,11},{12,20... | collective-permute-start | bytes 3096584 | tf_op jit(solution)/shard_map/ppermute | solution.py:555
  (25 other events, 399.3 us)

commit v6 on v5

--- a/solution.py
+++ b/solution.py
@@ -260,7 +260,8 @@
 
 
 def update_kernel(first, steps, *refs):
-    tables, (packed, high, low, whole), refs = refs[:4], refs[4:8], refs[8:]
+    tables, (packed, high, low), refs = refs[:4], refs[4:7], refs[8 if first else 7 :]
+    whole, refs = refs[0], refs[1:]
     homes, refs = refs[: len(steps)], refs[len(steps) :]
     gram, padded, staged, high_held, low_held, held, arrive, leave = refs[:8]
     ranks = tables[1].shape[0]
@@ -382,7 +383,7 @@
         functools.partial(blend_kernel, first, chunks),
         out_shape=[floats(slots, columns)] * ranks + [floats(SUBLANES, 128)],
         in_specs=[HBM] * 6 + [ANY] * len(before),
-        out_specs=[ANY] * ranks + [VMEM],
+        out_specs=[HBM] * ranks + [VMEM],
         scratch_shapes=[vmem(ranks, slots, columns)] * 2
         + [flags(ranks, chunks, 2), flags(ranks, chunks)]
         + table_scratch(*tables[2].shape),
@@ -436,12 +437,12 @@
     return [whole] + [floats(slots, columns)] * len(steps)
 
 
-def apply_update(first, steps, tables, packed, high, low, slots):
+def apply_update(first, steps, tables, packed, high, low, slots, *after):
     columns = high.shape[1]
     return pl.pallas_call(
         functools.partial(update_kernel, first, steps),
         out_shape=update_shapes(first, steps, slots, columns),
-        in_specs=[HBM] * 4 + [VMEM] + [ANY] * 2,
+        in_specs=[HBM] * 4 + [VMEM] + [ANY] * (2 + len(after)),
         out_specs=[ANY] * (1 + len(steps)),
         scratch_shapes=[
             vmem(INNER, INNER),
@@ -457,11 +458,22 @@
         compiler_params=PARAMS,
         cost_estimate=FREE,
         name="apply_update",
-    )(*tables, packed, high, low)
+    )(*tables, packed, high, low, *after)
 
 
 def nothing(shapes):
     return pl.pallas_call(idle_kernel, out_shape=shapes, out_specs=[ANY] * len(shapes), name="nothing")()
+
+
+def settle(value):
+    return pl.pallas_call(
+        idle_kernel,
+        out_shape=floats(SUBLANES, 128),
+        in_specs=[ANY],
+        out_specs=ANY,
+        cost_estimate=pl.CostEstimate(flops=10**11, bytes_accessed=0, transcendentals=0),
+        name="settle",
+    )(value)
 
 
 def finish(tables, packed, iterate, inner_result, own_first, own_last, shape):
@@ -501,38 +513,28 @@
     )(owner_group, *blocks, shards)
 
 
-def group_stages(size):
-    stages, shift = [], 0
-    while (1 << shift) < size:
-        wide = 1 if shift == 0 or (2 << shift) >= size else 2
-        stages.append((shift, 1 << wide))
-        shift += wide
-    return stages
-
-
 def sum_over(block, axis):
     size = lax.axis_size(axis)
     if size & (size - 1) or block.shape[0] % size:
         return lax.psum(block, axis)
     index = lax.axis_index(axis)
 
-    def exchange(piece, step):
-        return lax.ppermute(piece, axis, [(i, i ^ step) for i in range(size)])
-
-    stages = group_stages(size)
-    for shift, group in stages:
-        digit = (index >> shift) & (group - 1)
-        part = block.shape[0] // group
-        pieces = [lax.dynamic_slice_in_dim(block, (digit ^ step) * part, part, 0) for step in range(group)]
-        arrived = [exchange(pieces[step], step << shift) for step in range(1, group)]
-        block = functools.reduce(jnp.add, arrived, pieces[0])
-    for shift, group in reversed(stages):
-        digit = (index >> shift) & (group - 1)
+    def exchange(piece, bit):
+        return lax.ppermute(piece, axis, [(i, i ^ bit) for i in range(size)])
+
+    bits = [1 << shift for shift in range(size.bit_length() - 1)]
+    for bit in bits:
+        part = block.shape[0] // 2
+        mine = jnp.where(index & bit, part, 0)
+        away = exchange(lax.dynamic_slice_in_dim(block, part - mine, part, 0), bit)
+        block = lax.dynamic_slice_in_dim(block, mine, part, 0) + away
+    for bit in reversed(bits):
         part = block.shape[0]
-        pieces = [block] + [exchange(block, step << shift) for step in range(1, group)]
-        block = jnp.zeros((part * group, block.shape[1]), block.dtype)
-        for step, piece in enumerate(pieces):
-            block = lax.dynamic_update_slice_in_dim(block, piece, (digit ^ step) * part, 0)
+        mine = jnp.where(index & bit, part, 0)
+        away = exchange(block, bit)
+        whole = jnp.zeros((2 * part, block.shape[1]), block.dtype)
+        whole = lax.dynamic_update_slice_in_dim(whole, block, mine, 0)
+        block = lax.dynamic_update_slice_in_dim(whole, away, part - mine, 0)
     return block
 
 
@@ -563,13 +565,13 @@
     high, low, gram_part, iterate = assemble_and_gram(True, tables, first_blocks, new_momentum)
     iterate = from_inner(iterate, mate(ranks))
 
-    def first_update(high, low, gram_part):
-        return apply_update(True, [0, *early], tables, sum_over(gram_part, "tensor"), high, low, slots)
-
-    def first_skip(high, low, gram_part):
+    def first_update(high, low, gram_part, after):
+        return apply_update(True, [0, *early], tables, sum_over(gram_part, "tensor"), high, low, slots, after)
+
+    def first_skip(high, low, gram_part, after):
         return nothing(update_shapes(True, [0, *early], slots, columns))
 
-    packed, own_first, *homes = lax.cond(inner, first_update, first_skip, high, low, gram_part)
+    packed, own_first, *homes = lax.cond(inner, first_update, first_skip, high, low, gram_part, settle(gram_part))
     packed_there = from_inner(packed, mate(ranks))
     first_home = [from_inner(block, step) for step, block in zip(early, homes)]
 

time: 300 us -> 228 us (0.76)
  the two profiles are of different devices: /device:TPU:8 before, /device:TPU:0 now
where the time goes in v6:
time: 228 us; the launch traced here: 227 us
  waiting for transfers between devices  169 us (74%)
  Pallas kernels  31 us (14%)
  starting transfers between devices  24.9 us (11%)
    ppermute x7, waiting for transfers between devices, from_inner(): return lax.ppermute(block, 'fsdp', pairs(step, False))  108 us
    ppermute x6, waiting for transfers between devices, to_inner(): return lax.ppermute(block, 'fsdp', pairs(step, True))  60.8 us
    ppermute x6, starting transfers between devices, to_inner(): return lax.ppermute(block, 'fsdp', pairs(step, True))  16 us
    pallas_call x2, Pallas kernels, blend(): pl.pallas_call(functools.partial(blend_kernel, first, chunks), out_shape=...  10.1 us
    ppermute x7, starting transfers between devices, from_inner(): return lax.ppermute(block, 'fsdp', pairs(step, False))  8.88 us
    pallas_call x1, Pallas kernels, finish(): pl.pallas_call(functools.partial(finish_kernel, tables[1].shape[0]), out_...  7.35 us
    pallas_call x4, Pallas kernels, place_blocks(): pl.pallas_call(functools.partial(place_kernel, first, ranks, steps), out_...  6.68 us
    pallas_call x1, Pallas kernels, fresh_momentum(): pl.pallas_call(fresh_kernel, grid=(matrices,), out_shape=floats(*momentum...  5.86 us
  transfers between devices with their start and end apart: 13, of which 7 were waited for; matrix products, arithmetic and copies ran while one was open for 0% of the time, Pallas kernels for 11%

profile of v6, /device:TPU:0, one launch (start us, length us, event | category | flops | bytes accessed | tf_op | source)
XLA Modules:
  0.0 226.9 jit_solution(16042430272182473335)
XLA Ops:
  0.7 5.2 %blend.2 = (f32[288,896]{1,0:T(8,128)}, f32[288,896]{1,0:T(8,128)}, f32[288,896]{1,0:T(8,128)}, f32[288,896]{1,0:T(8,128)}, f32[8,128]{1,0:T(8,128)}) custom-call(s32[4]{0:T(128)} %refs_0_.15, s32[4]{0:T(128)} %refs_1_.7, s32[4,4]{1,0:T(4,128)} %refs_2_.7, s32[4,4]{1,0:T(4,128)} %refs_3_.7, f32[4,288,896]{2,1,0:T(8,128)} %momentum.1, f32[4,288,896]{2,1,0:T(8,128)} %gradient.1), custom_call_target="tpu_custom_call" | custom-call | tf_op jit(solution)/shard_map/blend/pallas_call | solution.py:382
  5.9 5.0 %collective-permute-start.15 = (f32[288,896]{1,0:T(8,128)}, f32[288,896]{1,0:T(8,128)S(1)}, u32[]{:S(2)}, u32[]{:S(2)}) collective-permute-start(f32[288,896]{1,0:T(8,128)} %get-tuple-element.89), channel_id=1, source_target_pairs={{0,8},{24,16},{1,9},{25,17},{2,10},{26,18},{3,11},{27,19},{4,12},{... | collective-permute-start | bytes 3096584 | tf_op jit(solution)/shard_map/ppermute | solution.py:554
  10.9 2.3 %collective-permute-start.16 = (f32[288,896]{1,0:T(8,128)}, f32[288,896]{1,0:T(8,128)S(1)}, u32[]{:S(2)}, u32[]{:S(2)}) collective-permute-start(f32[288,896]{1,0:T(8,128)} %get-tuple-element.90), channel_id=1, source_target_pairs={{0,16},{24,8},{1,17},{25,9},{2,18},{26,10},{3,19},{27,11},{4,20},{... | collective-permute-start | bytes 3096584 | tf_op jit(solution)/shard_map/ppermute | solution.py:554
  13.2 1.7 collective-permute-start.17
  14.9 4.9 %blend.3 = (f32[288,896]{1,0:T(8,128)}, f32[288,896]{1,0:T(8,128)}, f32[288,896]{1,0:T(8,128)}, f32[288,896]{1,0:T(8,128)}, f32[8,128]{1,0:T(8,128)}) custom-call(s32[4]{0:T(128)S(1)} %copy-done.8, s32[4]{0:T(128)S(1)} %copy-done.9, s32[4,4]{1,0:T(4,128)S(1)} %copy-done.6, s32[4,4]{1,0:T(4,128)S(1)} %copy-done.7, f32[4,288,896]{2,1,0:T(8,128)} %momentum.1, ...), custom_call_target="tpu_custom_call" | custom-call | tf_op jit(solution)/shard_map/blend/pallas_call | solution.py:382
  19.8 3.1 %collective-permute-start.12 = (f32[288,896]{1,0:T(8,128)}, f32[288,896]{1,0:T(8,128)}, u32[]{:S(2)}, u32[]{:S(2)}) collective-permute-start(f32[288,896]{1,0:T(8,128)} %get-tuple-element.85), channel_id=1, source_target_pairs={{0,8},{24,16},{1,9},{25,17},{2,10},{26,18},{3,11},{27,19},{4,12},{... | collective-permute-start | bytes 3096584 | tf_op jit(solution)/shard_map/ppermute | solution.py:554
  22.9 2.3 %collective-permute-start.13 = (f32[288,896]{1,0:T(8,128)}, f32[288,896]{1,0:T(8,128)}, u32[]{:S(2)}, u32[]{:S(2)}) collective-permute-start(f32[288,896]{1,0:T(8,128)} %get-tuple-element.86), channel_id=1, source_target_pairs={{0,16},{24,8},{1,17},{25,9},{2,18},{26,10},{3,19},{27,11},{4,20},{... | collective-permute-start | bytes 3096584 | tf_op jit(solution)/shard_map/ppermute | solution.py:554
  25.1 5.9 %fresh_momentum.1.refs_8_ = f32[4,288,896]{2,1,0:T(8,128)} custom-call(s32[4]{0:T(128)S(1)} %copy-done.9, s32[4,4]{1,0:T(4,128)S(1)} %copy-done.6, f32[4,288,896]{2,1,0:T(8,128)} %momentum.1, f32[4,288,896]{2,1,0:T(8,128)} %gradient.1, f32[8,128]{1,0:T(8,128)} %get-tuple-element.83._), custom_call_target="tpu_custom_call" | custom-call | tf_op jit(solution)/shard_map/fresh_momentum/pallas_call | solution.py:399
  31.0 3.3 %collective-permute-done.15.refs_5_ = f32[288,896]{1,0:T(8,128)S(1)} collective-permute-done((f32[288,896]{1,0:T(8,128)}, f32[288,896]{1,0:T(8,128)S(1)}, u32[]{:S(2)}, u32[]{:S(2)}) %collective-permute-start.15) | collective-permute-done | bytes 1032224 | tf_op jit(solution)/shard_map/ppermute | solution.py:554
  34.3 1.7 collective-permute-start.14
  36.0 20.5 %collective-permute-done.16.refs_6_ = f32[288,896]{1,0:T(8,128)S(1)} collective-permute-done((f32[288,896]{1,0:T(8,128)}, f32[288,896]{1,0:T(8,128)S(1)}, u32[]{:S(2)}, u32[]{:S(2)}) %collective-permute-start.16) | collective-permute-done | bytes 1032224 | tf_op jit(solution)/shard_map/ppermute | solution.py:554
  57.5 1.3 collective-permute-start.24
  61.3 17.3 %collective-permute-done.12 = f32[288,896]{1,0:T(8,128)} collective-permute-done((f32[288,896]{1,0:T(8,128)}, f32[288,896]{1,0:T(8,128)}, u32[]{:S(2)}, u32[]{:S(2)}) %collective-permute-start.12) | collective-permute-done | bytes 1032224 | tf_op jit(solution)/shard_map/ppermute | solution.py:554
  79.9 19.7 %collective-permute-done.13 = f32[288,896]{1,0:T(8,128)} collective-permute-done((f32[288,896]{1,0:T(8,128)}, f32[288,896]{1,0:T(8,128)}, u32[]{:S(2)}, u32[]{:S(2)}) %collective-permute-start.13) | collective-permute-done | bytes 1032224 | tf_op jit(solution)/shard_map/ppermute | solution.py:554
  99.6 1.7 collective-permute-start.22
  101.4 1.3 collective-permute-start.20
  102.7 57.6 %collective-permute-done.23.refs_4_ = f32[576,384]{1,0:T(8,128)} collective-permute-done((f32[576,384]{1,0:T(8,128)}, f32[576,384]{1,0:T(8,128)}, u32[]{:S(2)}, u32[]{:S(2)}) %collective-permute-start.23) | collective-permute-done | bytes 884768 | tf_op jit(solution)/shard_map/ppermute | solution.py:557
  160.2 1.3 collective-permute-start.19
  162.3 7.3 %finish.1 = (f32[576,896]{1,0:T(8,128)}, f32[4,288,896]{2,1,0:T(8,128)}) custom-call(s32[4]{0:T(128)S(1)} %copy-done.8, s32[4]{0:T(128)S(1)} %copy-done.9, s32[4,4]{1,0:T(4,128)S(1)} %copy-done.6, s32[4,4]{1,0:T(4,128)S(1)} %copy-done.7, f32[576,384]{1,0:T(8,128)} %collective-permute-done.23.refs_4_, f32[576,896]{1,0:T(8,128)S(1)} %collective-permute-done.24.refs_5_, ...), custom_call_target="tpu_custom_call" | custom-call | tf_op jit(solution)/shard_map/finish/pallas_call | solution.py:481
  169.6 3.1 %place_blocks.4.refs_2_ = f32[4,288,896]{2,1,0:T(8,128)} custom-call(s32[4]{0:T(128)S(1)} %copy-done.8, f32[288,896]{1,0:T(8,128)} %collective-permute-done.21.refs_1_, f32[288,896]{1,0:T(8,128)} %collective-permute-done.22.refs_2_, f32[4,288,896]{2,1,0:T(8,128)} %get-tuple-element.105.refs_3_), custom_call_target="tpu_custom_call", output_to_operand_aliasing={{}: (3, {})} | custom-call | tf_op jit(solution)/shard_map/place_blocks/pallas_call | solution.py:503
  172.7 30.3 %collective-permute-done.20.refs_1_ = f32[288,896]{1,0:T(8,128)S(1)} collective-permute-done((f32[288,896]{1,0:T(8,128)}, f32[288,896]{1,0:T(8,128)S(1)}, u32[]{:S(2)}, u32[]{:S(2)}) %collective-permute-start.20) | collective-permute-done | bytes 1032224 | tf_op jit(solution)/shard_map/ppermute | solution.py:557
  203.0 1.5 place_blocks.5.refs_2_
  204.5 20.1 %collective-permute-done.19.refs_1_ = f32[288,896]{1,0:T(8,128)S(1)} collective-permute-done((f32[288,896]{1,0:T(8,128)}, f32[288,896]{1,0:T(8,128)S(1)}, u32[]{:S(2)}, u32[]{:S(2)}) %collective-permute-start.19) | collective-permute-done | bytes 1032224 | tf_op jit(solution)/shard_map/ppermute | solution.py:557
  224.6 1.5 place_blocks.6.refs_2_
  (28 shorter events, 6.1 us)
Async XLA Ops:
  0.6 14.2 %copy-start.9 = (s32[4]{0:T(128)S(1)}, s32[4]{0:T(128)}, u32[]{:S(2)}) copy-start(s32[4]{0:T(128)} %refs_1_.7) | copy-start | bytes 52
  0.6 14.2 %copy-start.8 = (s32[4]{0:T(128)S(1)}, s32[4]{0:T(128)}, u32[]{:S(2)}) copy-start(s32[4]{0:T(128)} %refs_0_.15) | copy-start | bytes 52
  0.7 14.2 %copy-start.6 = (s32[4,4]{1,0:T(4,128)S(1)}, s32[4,4]{1,0:T(4,128)}, u32[]{:S(2)}) copy-start(s32[4,4]{1,0:T(4,128)} %refs_2_.7) | copy-start | bytes 196
  0.7 14.2 %copy-start.7 = (s32[4,4]{1,0:T(4,128)S(1)}, s32[4,4]{1,0:T(4,128)}, u32[]{:S(2)}) copy-start(s32[4,4]{1,0:T(4,128)} %refs_3_.7) | copy-start | bytes 196
  5.9 28.5 %collective-permute-start.15 = (f32[288,896]{1,0:T(8,128)}, f32[288,896]{1,0:T(8,128)S(1)}, u32[]{:S(2)}, u32[]{:S(2)}) collective-permute-start(f32[288,896]{1,0:T(8,128)} %get-tuple-element.89), channel_id=1, source_target_pairs={{0,8},{24,16},{1,9},{25,17},{2,10},{26,18},{3,11},{27,19},{4,12},{... | collective-permute-start | bytes 3096584 | tf_op jit(solution)/shard_map/ppermute | solution.py:554
  10.9 45.6 %collective-permute-start.16 = (f32[288,896]{1,0:T(8,128)}, f32[288,896]{1,0:T(8,128)S(1)}, u32[]{:S(2)}, u32[]{:S(2)}) collective-permute-start(f32[288,896]{1,0:T(8,128)} %get-tuple-element.90), channel_id=1, source_target_pairs={{0,16},{24,8},{1,17},{25,9},{2,18},{26,10},{3,19},{27,11},{4,20},{... | collective-permute-start | bytes 3096584 | tf_op jit(solution)/shard_map/ppermute | solution.py:554
  13.2 43.3 %collective-permute-start.17 = (f32[288,896]{1,0:T(8,128)}, f32[288,896]{1,0:T(8,128)}, u32[]{:S(2)}, u32[]{:S(2)}) collective-permute-start(f32[288,896]{1,0:T(8,128)} %get-tuple-element.91), channel_id=1, source_target_pairs={{8,16},{16,8},{9,17},{17,9},{10,18},{18,10},{11,19},{19,11},{12,20... | collective-permute-start | bytes 3096584 | tf_op jit(solution)/shard_map/ppermute | solution.py:554
  19.8 58.8 %collective-permute-start.12 = (f32[288,896]{1,0:T(8,128)}, f32[288,896]{1,0:T(8,128)}, u32[]{:S(2)}, u32[]{:S(2)}) collective-permute-start(f32[288,896]{1,0:T(8,128)} %get-tuple-element.85), channel_id=1, source_target_pairs={{0,8},{24,16},{1,9},{25,17},{2,10},{26,18},{3,11},{27,19},{4,12},{... | collective-permute-start | bytes 3096584 | tf_op jit(solution)/shard_map/ppermute | solution.py:554
  22.9 76.8 %collective-permute-start.13 = (f32[288,896]{1,0:T(8,128)}, f32[288,896]{1,0:T(8,128)}, u32[]{:S(2)}, u32[]{:S(2)}) collective-permute-start(f32[288,896]{1,0:T(8,128)} %get-tuple-element.86), channel_id=1, source_target_pairs={{0,16},{24,8},{1,17},{25,9},{2,18},{26,10},{3,19},{27,11},{4,20},{... | collective-permute-start | bytes 3096584 | tf_op jit(solution)/shard_map/ppermute | solution.py:554
  25.1 31.3 %copy-start.2 = (f32[288,896]{1,0:T(8,128)S(1)}, f32[288,896]{1,0:T(8,128)}, u32[]{:S(2)}) copy-start(f32[288,896]{1,0:T(8,128)} %get-tuple-element.88.refs_4_) | copy-start | bytes 3096580
  34.3 67.0 %collective-permute-start.14 = (f32[288,896]{1,0:T(8,128)}, f32[288,896]{1,0:T(8,128)}, u32[]{:S(2)}, u32[]{:S(2)}) collective-permute-start(f32[288,896]{1,0:T(8,128)} %get-tuple-element.87), channel_id=1, source_target_pairs={{8,16},{16,8},{9,17},{17,9},{10,18},{18,10},{11,19},{19,11},{12,20... | collective-permute-start | bytes 3096584 | tf_op jit(solution)/shard_map/ppermute | solution.py:554
  57.5 104.0 %collective-permute-start.24 = (f32[576,896]{1,0:T(8,128)}, f32[576,896]{1,0:T(8,128)S(1)}, u32[]{:S(2)}, u32[]{:S(2)}) collective-permute-start(f32[576,896]{1,0:T(8,128)} %get-tuple-element.101), channel_id=1, source_target_pairs={{8,0},{16,24},{9,1},{17,25},{10,2},{18,26},{11,3},{19,27},{12,4},{... | collective-permute-start | bytes 6193160 | tf_op jit(solution)/shard_map/ppermute | solution.py:557
  58.8 1.2 copy-start.4
  60.1 100.2 %collective-permute-start.23 = (f32[576,384]{1,0:T(8,128)}, f32[576,384]{1,0:T(8,128)}, u32[]{:S(2)}, u32[]{:S(2)}) collective-permute-start(f32[576,384]{1,0:T(8,128)} %get-tuple-element.95), channel_id=1, source_target_pairs={{8,0},{16,24},{9,1},{17,25},{10,2},{18,26},{11,3},{19,27},{12,4},{... | collective-permute-start | bytes 2654216 | tf_op jit(solution)/shard_map/ppermute | solution.py:557
  78.6 91.0 %collective-permute-start.21 = (f32[288,896]{1,0:T(8,128)}, f32[288,896]{1,0:T(8,128)}, u32[]{:S(2)}, u32[]{:S(2)}) collective-permute-start(f32[288,896]{1,0:T(8,128)} %get-tuple-element.99), channel_id=1, source_target_pairs={{8,24},{16,0},{9,25},{17,1},{10,26},{18,2},{11,27},{19,3},{12,28},... | collective-permute-start | bytes 3096584 | tf_op jit(solution)/shard_map/ppermute | solution.py:557
  99.6 70.0 %collective-permute-start.22 = (f32[288,896]{1,0:T(8,128)}, f32[288,896]{1,0:T(8,128)}, u32[]{:S(2)}, u32[]{:S(2)}) collective-permute-start(f32[288,896]{1,0:T(8,128)} %get-tuple-element.100), channel_id=1, source_target_pairs={{8,16},{16,8},{9,17},{17,9},{10,18},{18,10},{11,19},{19,11},{12,20... | collective-permute-start | bytes 3096584 | tf_op jit(solution)/shard_map/ppermute | solution.py:557
  101.4 101.6 %collective-permute-start.20 = (f32[288,896]{1,0:T(8,128)}, f32[288,896]{1,0:T(8,128)S(1)}, u32[]{:S(2)}, u32[]{:S(2)}) collective-permute-start(f32[288,896]{1,0:T(8,128)} %get-tuple-element.98), channel_id=1, source_target_pairs={{8,24},{16,0},{9,25},{17,1},{10,26},{18,2},{11,27},{19,3},{12,28},... | collective-permute-start | bytes 3096584 | tf_op jit(solution)/shard_map/ppermute | solution.py:557
  160.2 64.4 %collective-permute-start.19 = (f32[288,896]{1,0:T(8,128)}, f32[288,896]{1,0:T(8,128)S(1)}, u32[]{:S(2)}, u32[]{:S(2)}) collective-permute-start(f32[288,896]{1,0:T(8,128)} %get-tuple-element.97), channel_id=1, source_target_pairs={{8,0},{16,24},{9,1},{17,25},{10,2},{18,26},{11,3},{19,27},{12,4},{... | collective-permute-start | bytes 3096584 | tf_op jit(solution)/shard_map/ppermute | solution.py:557
  161.5 64.6 %collective-permute-start.18 = (f32[288,896]{1,0:T(8,128)}, f32[288,896]{1,0:T(8,128)S(1)}, u32[]{:S(2)}, u32[]{:S(2)}) collective-permute-start(f32[288,896]{1,0:T(8,128)} %get-tuple-element.96), channel_id=1, source_target_pairs={{8,16},{16,8},{9,17},{17,9},{10,18},{18,10},{11,19},{19,11},{12,20... | collective-permute-start | bytes 3096584 | tf_op jit(solution)/shard_map/ppermute | solution.py:557

commit v7 on v6

--- a/solution.py
+++ b/solution.py
@@ -21,7 +21,7 @@
 EPSILON = 1e-07
 OUT_SCALE = 0.2 * math.sqrt(max(INNER, WIDTH))
 FULL = pltpu.CompilerParams(vmem_limit_bytes=60 * 1024 * 1024)
-PARAMS = pltpu.CompilerParams(vmem_limit_bytes=48 * 1024 * 1024)
+PARAMS = pltpu.CompilerParams(vmem_limit_bytes=24 * 1024 * 1024)
 HBM = pl.BlockSpec(memory_space=pltpu.HBM)
 ANY = pl.BlockSpec(memory_space=pl.ANY)
 VMEM = pl.BlockSpec(memory_space=pltpu.VMEM)
@@ -39,6 +39,14 @@
 
 def dot_halves(left, right, contract=((1,), (0,))):
     (left_high, left_low), (right_high, right_low) = left, right
+    depth = left_high.shape[1]
+    body = depth // TILE * TILE
+    if contract == ((1,), (0,)) and 0 < 3 * (depth - body) <= TILE:
+        rest_left = jnp.concatenate([left_high[:, body:], left_low[:, body:], left_high[:, body:]], axis=1)
+        rest_right = jnp.concatenate([right_low[body:], right_high[body:], right_high[body:]], axis=0)
+        left = left_high[:, :body], left_low[:, :body]
+        right = right_high[:body], right_low[:body]
+        return dot(rest_left, rest_right, contract) + dot_halves(left, right)
     return (
         dot(left_high, right_low, contract) + dot(left_low, right_high, contract)
     ) + dot(left_high, right_high, contract)
@@ -81,6 +89,17 @@
     for matrix in range(owner_group.shape[0]):
         found = jnp.where(owner_group[matrix] == rank, matrix, found)
     return found
+
+
+def over_tiles(tiles, body, carry):
+    group = next(group for group in (6, 3, 2, 1) if tiles % group == 0)
+
+    def step(index, carry):
+        for member in range(group):
+            carry = body(index * group + member, carry)
+        return carry
+
+    return lax.fori_loop(0, tiles // group, step, carry)
 
 
 def each_copy(copies, action):
@@ -131,7 +150,8 @@
     each_copy([job[-1] for job in jobs], "wait")
 
 
-def fresh_kernel(live_ranks, row_counts, momentum, gradient, _, out):
+def fresh_kernel(live_ranks, row_counts, momentum, gradient, _, out, token):
+    token[...] = jnp.zeros_like(token)
     rank, matrix = lax.axis_index("fsdp"), pl.program_id(0)
     position = lax.broadcasted_iota(jnp.int32, out.shape, 0)
     keep = position < row_counts[matrix, rank] * live_ranks[rank]
@@ -167,7 +187,7 @@
                 padded[rows, :] = padded[rows, :] + jnp.where(sublane < shift, before, moved)
                 return moved
 
-            after = lax.fori_loop(0, slots // SUBLANES, tile, jnp.zeros((SUBLANES, columns), jnp.float32))
+            after = over_tiles(slots // SUBLANES, tile, jnp.zeros((SUBLANES, columns), jnp.float32))
             rows = pl.ds(pl.multiple_of(base + slots, SUBLANES), SUBLANES)
             padded[rows, :] = padded[rows, :] + jnp.where(sublane < shift, after, 0.0)
         high, low = halves(padded[:INNER, :])
@@ -256,7 +276,7 @@
         staged[step, rows, :] = jnp.where(sublane < count - index * SUBLANES, moved, 0.0)
         return after
 
-    lax.fori_loop(0, slots // SUBLANES, tile, window(0))
+    over_tiles(slots // SUBLANES, tile, window(0))
 
 
 def update_kernel(first, steps, *refs):
@@ -399,9 +419,9 @@
     return pl.pallas_call(
         fresh_kernel,
         grid=(matrices,),
-        out_shape=floats(*momentum.shape),
+        out_shape=[floats(*momentum.shape), floats(SUBLANES, 128)],
         in_specs=[pl.BlockSpec(memory_space=pltpu.SMEM)] * 2 + [block] * 2 + [ANY],
-        out_specs=block,
+        out_specs=[block, pl.BlockSpec((SUBLANES, 128), lambda matrix: (0, 0))],
         compiler_params=FULL,
         cost_estimate=FREE,
         name="fresh_momentum",
@@ -519,22 +539,27 @@
         return lax.psum(block, axis)
     index = lax.axis_index(axis)
 
-    def exchange(piece, bit):
-        return lax.ppermute(piece, axis, [(i, i ^ bit) for i in range(size)])
-
-    bits = [1 << shift for shift in range(size.bit_length() - 1)]
-    for bit in bits:
+    def exchange(piece, bits):
+        return lax.ppermute(piece, axis, [(i, i ^ bits[i & 1]) for i in range(size)])
+
+    def mine(bits, part):
+        bit = jnp.where(index & 1, bits[1], bits[0])
+        return jnp.where(index & bit, part, 0)
+
+    chips = [1 << shift for shift in range(1, size.bit_length() - 1)]
+    stages = [(1, 1), *zip(chips, reversed(chips))]
+    for bits in stages:
         part = block.shape[0] // 2
-        mine = jnp.where(index & bit, part, 0)
-        away = exchange(lax.dynamic_slice_in_dim(block, part - mine, part, 0), bit)
-        block = lax.dynamic_slice_in_dim(block, mine, part, 0) + away
-    for bit in reversed(bits):
+        keep = mine(bits, part)
+        away = exchange(lax.dynamic_slice_in_dim(block, part - keep, part, 0), bits)
+        block = lax.dynamic_slice_in_dim(block, keep, part, 0) + away
+    for bits in reversed(stages):
         part = block.shape[0]
-        mine = jnp.where(index & bit, part, 0)
-        away = exchange(block, bit)
+        keep = mine(bits, part)
+        away = exchange(block, bits)
         whole = jnp.zeros((2 * part, block.shape[1]), block.dtype)
-        whole = lax.dynamic_update_slice_in_dim(whole, block, mine, 0)
-        block = lax.dynamic_update_slice_in_dim(whole, away, part - mine, 0)
+        whole = lax.dynamic_update_slice_in_dim(whole, block, keep, 0)
+        block = lax.dynamic_update_slice_in_dim(whole, away, part - keep, 0)
     return block
 
 
@@ -560,9 +585,9 @@
     first_blocks = [blends[0]] + [to_inner(blends[step], step) for step in range(1, ranks)]
     *blends, token = blend(False, tables, momentum, gradient, [token])
     last_blocks = [blends[0]] + [to_inner(blends[step], step) for step in range(1, ranks)]
-    new_momentum = fresh_momentum(tables, momentum, gradient, token)
-
-    high, low, gram_part, iterate = assemble_and_gram(True, tables, first_blocks, new_momentum)
+    new_momentum, token = fresh_momentum(tables, momentum, gradient, token)
+
+    high, low, gram_part, iterate = assemble_and_gram(True, tables, first_blocks, token)
     iterate = from_inner(iterate, mate(ranks))
 
     def first_update(high, low, gram_part, after):

time: 228 us -> 223 us (0.978)
  waiting for transfers between devices: 169 us -> 164 us
    ppermute x7, waiting for transfers between devices: 108 us -> 104 us  [from_inner(): return lax.ppermute(block, 'fsdp', pairs(step, False))]
where the time goes in v7:
time: 223 us; the launch traced here: 222 us
  waiting for transfers between devices  164 us (74%)
  Pallas kernels  30.3 us (14%)
  starting transfers between devices  24.9 us (11%)
    ppermute x7, waiting for transfers between devices, from_inner(): return lax.ppermute(block, 'fsdp', pairs(step, False))  104 us
    ppermute x6, waiting for transfers between devices, to_inner(): return lax.ppermute(block, 'fsdp', pairs(step, True))  60.2 us
    ppermute x6, starting transfers between devices, to_inner(): return lax.ppermute(block, 'fsdp', pairs(step, True))  16 us
    pallas_call x2, Pallas kernels, blend(): pl.pallas_call(functools.partial(blend_kernel, first, chunks), out_shape=...  10.1 us
    ppermute x7, starting transfers between devices, from_inner(): return lax.ppermute(block, 'fsdp', pairs(step, False))  8.88 us
    pallas_call x4, Pallas kernels, place_blocks(): pl.pallas_call(functools.partial(place_kernel, first, ranks, steps), out_...  6.68 us
    pallas_call x1, Pallas kernels, finish(): pl.pallas_call(functools.partial(finish_kernel, tables[1].shape[0]), out_...  6.61 us
    pallas_call x1, Pallas kernels, fresh_momentum(): pl.pallas_call(fresh_kernel, grid=(matrices,), out_shape=[floats(*momentu...  5.86 us
  transfers between devices with their start and end apart: 13, of which 7 were waited for; matrix products, arithmetic and copies ran while one was open for 0% of the time, Pallas kernels for 11%

profile of v7, /device:TPU:0, one launch (start us, length us, event | category | flops | bytes accessed | tf_op | source)
XLA Modules:
  0.0 221.9 jit_solution(17326096167679511382)
XLA Ops:
  0.7 5.2 %blend.2 = (f32[288,896]{1,0:T(8,128)}, f32[288,896]{1,0:T(8,128)}, f32[288,896]{1,0:T(8,128)}, f32[288,896]{1,0:T(8,128)}, f32[8,128]{1,0:T(8,128)}) custom-call(s32[4]{0:T(128)} %refs_0_.15, s32[4]{0:T(128)} %refs_1_.7, s32[4,4]{1,0:T(4,128)} %refs_2_.7, s32[4,4]{1,0:T(4,128)} %refs_3_.7, f32[4,288,896]{2,1,0:T(8,128)} %momentum.1, f32[4,288,896]{2,1,0:T(8,128)} %gradient.1), custom_call_target="tpu_custom_call" | custom-call | tf_op jit(solution)/shard_map/blend/pallas_call | solution.py:402
  5.9 5.0 %collective-permute-start.15 = (f32[288,896]{1,0:T(8,128)}, f32[288,896]{1,0:T(8,128)S(1)}, u32[]{:S(2)}, u32[]{:S(2)}) collective-permute-start(f32[288,896]{1,0:T(8,128)} %get-tuple-element.92), channel_id=1, source_target_pairs={{0,8},{24,16},{1,9},{25,17},{2,10},{26,18},{3,11},{27,19},{4,12},{... | collective-permute-start | bytes 3096584 | tf_op jit(solution)/shard_map/ppermute | solution.py:579
  10.9 2.3 %collective-permute-start.16 = (f32[288,896]{1,0:T(8,128)}, f32[288,896]{1,0:T(8,128)S(1)}, u32[]{:S(2)}, u32[]{:S(2)}) collective-permute-start(f32[288,896]{1,0:T(8,128)} %get-tuple-element.93), channel_id=1, source_target_pairs={{0,16},{24,8},{1,17},{25,9},{2,18},{26,10},{3,19},{27,11},{4,20},{... | collective-permute-start | bytes 3096584 | tf_op jit(solution)/shard_map/ppermute | solution.py:579
  13.2 1.6 collective-permute-start.17
  14.8 4.9 %blend.3 = (f32[288,896]{1,0:T(8,128)}, f32[288,896]{1,0:T(8,128)}, f32[288,896]{1,0:T(8,128)}, f32[288,896]{1,0:T(8,128)}, f32[8,128]{1,0:T(8,128)}) custom-call(s32[4]{0:T(128)S(1)} %copy-done.9, s32[4]{0:T(128)S(1)} %copy-done.10, s32[4,4]{1,0:T(4,128)S(1)} %copy-done.7, s32[4,4]{1,0:T(4,128)S(1)} %copy-done.8, f32[4,288,896]{2,1,0:T(8,128)} %momentum.1, ...), custom_call_target="tpu_custom_call" | custom-call | tf_op jit(solution)/shard_map/blend/pallas_call | solution.py:402
  19.7 3.1 %collective-permute-start.12 = (f32[288,896]{1,0:T(8,128)}, f32[288,896]{1,0:T(8,128)}, u32[]{:S(2)}, u32[]{:S(2)}) collective-permute-start(f32[288,896]{1,0:T(8,128)} %get-tuple-element.88), channel_id=1, source_target_pairs={{0,8},{24,16},{1,9},{25,17},{2,10},{26,18},{3,11},{27,19},{4,12},{... | collective-permute-start | bytes 3096584 | tf_op jit(solution)/shard_map/ppermute | solution.py:579
  22.8 2.3 %collective-permute-start.13 = (f32[288,896]{1,0:T(8,128)}, f32[288,896]{1,0:T(8,128)}, u32[]{:S(2)}, u32[]{:S(2)}) collective-permute-start(f32[288,896]{1,0:T(8,128)} %get-tuple-element.89), channel_id=1, source_target_pairs={{0,16},{24,8},{1,17},{25,9},{2,18},{26,10},{3,19},{27,11},{4,20},{... | collective-permute-start | bytes 3096584 | tf_op jit(solution)/shard_map/ppermute | solution.py:579
  25.1 5.9 %fresh_momentum.1 = (f32[4,288,896]{2,1,0:T(8,128)}, f32[8,128]{1,0:T(8,128)}) custom-call(s32[4]{0:T(128)S(1)} %copy-done.10, s32[4,4]{1,0:T(4,128)S(1)} %copy-done.7, f32[4,288,896]{2,1,0:T(8,128)} %momentum.1, f32[4,288,896]{2,1,0:T(8,128)} %gradient.1, f32[8,128]{1,0:T(8,128)} %get-tuple-element.85._), custom_call_target="tpu_custom_call" | custom-call | tf_op jit(solution)/shard_map/fresh_momentum/pallas_call | solution.py:419
  31.0 3.3 %collective-permute-done.15.refs_5_ = f32[288,896]{1,0:T(8,128)S(1)} collective-permute-done((f32[288,896]{1,0:T(8,128)}, f32[288,896]{1,0:T(8,128)S(1)}, u32[]{:S(2)}, u32[]{:S(2)}) %collective-permute-start.15) | collective-permute-done | bytes 1032224 | tf_op jit(solution)/shard_map/ppermute | solution.py:579
  34.3 1.7 collective-permute-start.14
  36.0 20.5 %collective-permute-done.16.refs_6_ = f32[288,896]{1,0:T(8,128)S(1)} collective-permute-done((f32[288,896]{1,0:T(8,128)}, f32[288,896]{1,0:T(8,128)S(1)}, u32[]{:S(2)}, u32[]{:S(2)}) %collective-permute-start.16) | collective-permute-done | bytes 1032224 | tf_op jit(solution)/shard_map/ppermute | solution.py:579
  58.2 1.3 collective-permute-start.24
  62.0 16.6 %collective-permute-done.12 = f32[288,896]{1,0:T(8,128)} collective-permute-done((f32[288,896]{1,0:T(8,128)}, f32[288,896]{1,0:T(8,128)}, u32[]{:S(2)}, u32[]{:S(2)}) %collective-permute-start.12) | collective-permute-done | bytes 1032224 | tf_op jit(solution)/shard_map/ppermute | solution.py:579
  79.9 19.7 %collective-permute-done.13 = f32[288,896]{1,0:T(8,128)} collective-permute-done((f32[288,896]{1,0:T(8,128)}, f32[288,896]{1,0:T(8,128)}, u32[]{:S(2)}, u32[]{:S(2)}) %collective-permute-start.13) | collective-permute-done | bytes 1032224 | tf_op jit(solution)/shard_map/ppermute | solution.py:579
  99.6 1.7 collective-permute-start.22
  101.4 1.3 collective-permute-start.20
  102.7 55.1 %collective-permute-done.23.refs_4_ = f32[576,384]{1,0:T(8,128)} collective-permute-done((f32[576,384]{1,0:T(8,128)}, f32[576,384]{1,0:T(8,128)}, u32[]{:S(2)}, u32[]{:S(2)}) %collective-permute-start.23) | collective-permute-done | bytes 884768 | tf_op jit(solution)/shard_map/ppermute | solution.py:582
  157.8 1.3 collective-permute-start.19
  159.8 6.6 %finish.1 = (f32[576,896]{1,0:T(8,128)}, f32[4,288,896]{2,1,0:T(8,128)}) custom-call(s32[4]{0:T(128)S(1)} %copy-done.9, s32[4]{0:T(128)S(1)} %copy-done.10, s32[4,4]{1,0:T(4,128)S(1)} %copy-done.7, s32[4,4]{1,0:T(4,128)S(1)} %copy-done.8, f32[576,384]{1,0:T(8,128)} %collective-permute-done.23.refs_4_, f32[576,896]{1,0:T(8,128)S(1)} %collective-permute-done.24.refs_5_, ...), custom_call_target="tpu_custom_call" | custom-call | tf_op jit(solution)/shard_map/finish/pallas_call | solution.py:501
  166.5 3.1 %place_blocks.4.refs_2_ = f32[4,288,896]{2,1,0:T(8,128)} custom-call(s32[4]{0:T(128)S(1)} %copy-done.9, f32[288,896]{1,0:T(8,128)} %collective-permute-done.21.refs_1_, f32[288,896]{1,0:T(8,128)} %collective-permute-done.22.refs_2_, f32[4,288,896]{2,1,0:T(8,128)} %get-tuple-element.109.refs_3_), custom_call_target="tpu_custom_call", output_to_operand_aliasing={{}: (3, {})} | custom-call | tf_op jit(solution)/shard_map/place_blocks/pallas_call | solution.py:523
  169.6 28.4 %collective-permute-done.20.refs_1_ = f32[288,896]{1,0:T(8,128)S(1)} collective-permute-done((f32[288,896]{1,0:T(8,128)}, f32[288,896]{1,0:T(8,128)S(1)}, u32[]{:S(2)}, u32[]{:S(2)}) %collective-permute-start.20) | collective-permute-done | bytes 1032224 | tf_op jit(solution)/shard_map/ppermute | solution.py:582
  198.0 1.5 place_blocks.5.refs_2_
  199.5 20.1 %collective-permute-done.19.refs_1_ = f32[288,896]{1,0:T(8,128)S(1)} collective-permute-done((f32[288,896]{1,0:T(8,128)}, f32[288,896]{1,0:T(8,128)S(1)}, u32[]{:S(2)}, u32[]{:S(2)}) %collective-permute-start.19) | collective-permute-done | bytes 1032224 | tf_op jit(solution)/shard_map/ppermute | solution.py:582
  219.6 1.5 place_blocks.6.refs_2_
  (30 shorter events, 6.8 us)
Async XLA Ops:
  0.6 14.2 %copy-start.10 = (s32[4]{0:T(128)S(1)}, s32[4]{0:T(128)}, u32[]{:S(2)}) copy-start(s32[4]{0:T(128)} %refs_1_.7) | copy-start | bytes 52
  0.6 14.2 %copy-start.7 = (s32[4,4]{1,0:T(4,128)S(1)}, s32[4,4]{1,0:T(4,128)}, u32[]{:S(2)}) copy-start(s32[4,4]{1,0:T(4,128)} %refs_2_.7) | copy-start | bytes 196
  0.7 14.2 %copy-start.9 = (s32[4]{0:T(128)S(1)}, s32[4]{0:T(128)}, u32[]{:S(2)}) copy-start(s32[4]{0:T(128)} %refs_0_.15) | copy-start | bytes 52
  0.7 14.2 %copy-start.8 = (s32[4,4]{1,0:T(4,128)S(1)}, s32[4,4]{1,0:T(4,128)}, u32[]{:S(2)}) copy-start(s32[4,4]{1,0:T(4,128)} %refs_3_.7) | copy-start | bytes 196
  5.9 28.5 %collective-permute-start.15 = (f32[288,896]{1,0:T(8,128)}, f32[288,896]{1,0:T(8,128)S(1)}, u32[]{:S(2)}, u32[]{:S(2)}) collective-permute-start(f32[288,896]{1,0:T(8,128)} %get-tuple-element.92), channel_id=1, source_target_pairs={{0,8},{24,16},{1,9},{25,17},{2,10},{26,18},{3,11},{27,19},{4,12},{... | collective-permute-start | bytes 3096584 | tf_op jit(solution)/shard_map/ppermute | solution.py:579
  10.9 45.6 %collective-permute-start.16 = (f32[288,896]{1,0:T(8,128)}, f32[288,896]{1,0:T(8,128)S(1)}, u32[]{:S(2)}, u32[]{:S(2)}) collective-permute-start(f32[288,896]{1,0:T(8,128)} %get-tuple-element.93), channel_id=1, source_target_pairs={{0,16},{24,8},{1,17},{25,9},{2,18},{26,10},{3,19},{27,11},{4,20},{... | collective-permute-start | bytes 3096584 | tf_op jit(solution)/shard_map/ppermute | solution.py:579
  13.2 43.3 %collective-permute-start.17 = (f32[288,896]{1,0:T(8,128)}, f32[288,896]{1,0:T(8,128)}, u32[]{:S(2)}, u32[]{:S(2)}) collective-permute-start(f32[288,896]{1,0:T(8,128)} %get-tuple-element.94), channel_id=1, source_target_pairs={{8,16},{16,8},{9,17},{17,9},{10,18},{18,10},{11,19},{19,11},{12,20... | collective-permute-start | bytes 3096584 | tf_op jit(solution)/shard_map/ppermute | solution.py:579
  19.7 58.9 %collective-permute-start.12 = (f32[288,896]{1,0:T(8,128)}, f32[288,896]{1,0:T(8,128)}, u32[]{:S(2)}, u32[]{:S(2)}) collective-permute-start(f32[288,896]{1,0:T(8,128)} %get-tuple-element.88), channel_id=1, source_target_pairs={{0,8},{24,16},{1,9},{25,17},{2,10},{26,18},{3,11},{27,19},{4,12},{... | collective-permute-start | bytes 3096584 | tf_op jit(solution)/shard_map/ppermute | solution.py:579
  22.8 76.8 %collective-permute-start.13 = (f32[288,896]{1,0:T(8,128)}, f32[288,896]{1,0:T(8,128)}, u32[]{:S(2)}, u32[]{:S(2)}) collective-permute-start(f32[288,896]{1,0:T(8,128)} %get-tuple-element.89), channel_id=1, source_target_pairs={{0,16},{24,8},{1,17},{25,9},{2,18},{26,10},{3,19},{27,11},{4,20},{... | collective-permute-start | bytes 3096584 | tf_op jit(solution)/shard_map/ppermute | solution.py:579
  25.1 31.4 %copy-start = (f32[288,896]{1,0:T(8,128)S(1)}, f32[288,896]{1,0:T(8,128)}, u32[]{:S(2)}) copy-start(f32[288,896]{1,0:T(8,128)} %get-tuple-element.91.refs_4_) | copy-start | bytes 3096580
  34.3 67.0 %collective-permute-start.14 = (f32[288,896]{1,0:T(8,128)}, f32[288,896]{1,0:T(8,128)}, u32[]{:S(2)}, u32[]{:S(2)}) collective-permute-start(f32[288,896]{1,0:T(8,128)} %get-tuple-element.90), channel_id=1, source_target_pairs={{8,16},{16,8},{9,17},{17,9},{10,18},{18,10},{11,19},{19,11},{12,20... | collective-permute-start | bytes 3096584 | tf_op jit(solution)/shard_map/ppermute | solution.py:579
  56.5 0.7 copy-start.4
  58.2 100.9 %collective-permute-start.24 = (f32[576,896]{1,0:T(8,128)}, f32[576,896]{1,0:T(8,128)S(1)}, u32[]{:S(2)}, u32[]{:S(2)}) collective-permute-start(f32[576,896]{1,0:T(8,128)} %get-tuple-element.105), channel_id=1, source_target_pairs={{8,0},{16,24},{9,1},{17,25},{10,2},{18,26},{11,3},{19,27},{12,4},{... | collective-permute-start | bytes 6193160 | tf_op jit(solution)/shard_map/ppermute | solution.py:582
  59.5 1.2 copy-start.5
  60.7 97.1 %collective-permute-start.23 = (f32[576,384]{1,0:T(8,128)}, f32[576,384]{1,0:T(8,128)}, u32[]{:S(2)}, u32[]{:S(2)}) collective-permute-start(f32[576,384]{1,0:T(8,128)} %get-tuple-element.99), channel_id=1, source_target_pairs={{8,0},{16,24},{9,1},{17,25},{10,2},{18,26},{11,3},{19,27},{12,4},{... | collective-permute-start | bytes 2654216 | tf_op jit(solution)/shard_map/ppermute | solution.py:582
  78.6 87.9 %collective-permute-start.21 = (f32[288,896]{1,0:T(8,128)}, f32[288,896]{1,0:T(8,128)}, u32[]{:S(2)}, u32[]{:S(2)}) collective-permute-start(f32[288,896]{1,0:T(8,128)} %get-tuple-element.103), channel_id=1, source_target_pairs={{8,24},{16,0},{9,25},{17,1},{10,26},{18,2},{11,27},{19,3},{12,28},... | collective-permute-start | bytes 3096584 | tf_op jit(solution)/shard_map/ppermute | solution.py:582
  99.6 66.8 %collective-permute-start.22 = (f32[288,896]{1,0:T(8,128)}, f32[288,896]{1,0:T(8,128)}, u32[]{:S(2)}, u32[]{:S(2)}) collective-permute-start(f32[288,896]{1,0:T(8,128)} %get-tuple-element.104), channel_id=1, source_target_pairs={{8,16},{16,8},{9,17},{17,9},{10,18},{18,10},{11,19},{19,11},{12,20... | collective-permute-start | bytes 3096584 | tf_op jit(solution)/shard_map/ppermute | solution.py:582
  101.4 96.6 %collective-permute-start.20 = (f32[288,896]{1,0:T(8,128)}, f32[288,896]{1,0:T(8,128)S(1)}, u32[]{:S(2)}, u32[]{:S(2)}) collective-permute-start(f32[288,896]{1,0:T(8,128)} %get-tuple-element.102), channel_id=1, source_target_pairs={{8,24},{16,0},{9,25},{17,1},{10,26},{18,2},{11,27},{19,3},{12,28},... | collective-permute-start | bytes 3096584 | tf_op jit(solution)/shard_map/ppermute | solution.py:582
  157.8 61.8 %collective-permute-start.19 = (f32[288,896]{1,0:T(8,128)}, f32[288,896]{1,0:T(8,128)S(1)}, u32[]{:S(2)}, u32[]{:S(2)}) collective-permute-start(f32[288,896]{1,0:T(8,128)} %get-tuple-element.101), channel_id=1, source_target_pairs={{8,0},{16,24},{9,1},{17,25},{10,2},{18,26},{11,3},{19,27},{12,4},{... | collective-permute-start | bytes 3096584 | tf_op jit(solution)/shard_map/ppermute | solution.py:582
  159.1 62.0 %collective-permute-start.18 = (f32[288,896]{1,0:T(8,128)}, f32[288,896]{1,0:T(8,128)S(1)}, u32[]{:S(2)}, u32[]{:S(2)}) collective-permute-start(f32[288,896]{1,0:T(8,128)} %get-tuple-element.100), channel_id=1, source_target_pairs={{8,16},{16,8},{9,17},{17,9},{10,18},{18,10},{11,19},{19,11},{12,20... | collective-permute-start | bytes 3096584 | tf_op jit(solution)/shard_map/ppermute | solution.py:582

commit v8 on v7

--- a/solution.py
+++ b/solution.py
@@ -20,6 +20,7 @@
 QUINTIC_THIRD = 2.0315
 EPSILON = 1e-07
 OUT_SCALE = 0.2 * math.sqrt(max(INNER, WIDTH))
+SMALL = pltpu.CompilerParams(vmem_limit_bytes=1024 * 1024)
 FULL = pltpu.CompilerParams(vmem_limit_bytes=60 * 1024 * 1024)
 PARAMS = pltpu.CompilerParams(vmem_limit_bytes=24 * 1024 * 1024)
 HBM = pl.BlockSpec(memory_space=pltpu.HBM)
@@ -160,8 +161,8 @@
 
 def gram_kernel(first, ranks, *refs):
     tables, blocks, refs = refs[:4], refs[4 : 4 + ranks], refs[5 + ranks :]
-    high_out, low_out, gram = refs[:3]
-    landed, padded, high_held, low_held, arrive, leave = refs[-11:-5]
+    high_out, low_out, keep, send = refs[:4]
+    landed, padded, high_held, low_held, gram, arrive, leave = refs[-12:-5]
     slots, columns = blocks[0].shape
     rank = lax.axis_index("fsdp")
 
@@ -198,15 +199,24 @@
             pltpu.make_async_copy(low_held, low_out, leave.at[1]),
         ]
         if first:
-            outgoing.append(pltpu.make_async_copy(padded.at[pl.ds(0, INNER)], refs[3], leave.at[2]))
+            outgoing.append(pltpu.make_async_copy(padded.at[pl.ds(0, INNER)], refs[4], leave.at[2]))
         for copy in outgoing:
             copy.start()
         for panel in range(3):
             here = slice(panel * PANEL, (panel + 1) * PANEL)
             part = dot_halves((high[panel * PANEL :], low[panel * PANEL :]), (high[here], low[here]), ((1,), (1,)))
             store_panel(gram, panel, part)
+        mine, other = core_rows()
+        keep[...] = gram[mine, :]
+        send[...] = gram[other, :]
         for copy in outgoing:
             copy.wait()
+
+
+def core_rows():
+    half = INNER // 2
+    first = (lax.axis_index("tensor") & 1) * half
+    return tuple(pl.ds(pl.multiple_of(start, SUBLANES), half) for start in (first, half - first))
 
 
 def store_panel(packed, panel, part):
@@ -280,39 +290,47 @@
 
 
 def update_kernel(first, steps, *refs):
-    tables, (packed, high, low), refs = refs[:4], refs[4:7], refs[8 if first else 7 :]
+    tables, (keep, away, high, low), refs = refs[:4], refs[4:8], refs[9 if first else 8 :]
     whole, refs = refs[0], refs[1:]
     homes, refs = refs[: len(steps)], refs[len(steps) :]
     gram, padded, staged, high_held, low_held, held, arrive, leave = refs[:8]
     ranks = tables[1].shape[0]
     rank = lax.axis_index("fsdp")
-    incoming = [
-        pltpu.make_async_copy(high, high_held, arrive.at[0]),
-        pltpu.make_async_copy(low, low_held, arrive.at[1]),
-    ]
-    for copy in incoming:
-        copy.start()
-    owner_group, live_ranks, row_counts, row_offsets = fetch_tables(tables, refs[8:])
-    matrix = matrix_of(owner_group, rank ^ mate(ranks) if first else rank)
-    total = polynomial(unpack(packed, gram), gram)
-    if first:
-        for panel in range(3):
-            store_panel(held, panel, total[panel * PANEL :, panel * PANEL : (panel + 1) * PANEL])
-        copies = [pltpu.make_async_copy(held, whole, leave.at[len(steps)])]
-        copies[0].start()
-    for copy in incoming:
-        copy.wait()
-    padded[:INNER, :] = dot_halves(halves(total), (high_held[...], low_held[...]))
-    if not first:
-        copies = [pltpu.make_async_copy(padded.at[pl.ds(0, INNER)], whole, leave.at[len(steps)])]
-        copies[0].start()
-    for index, step in enumerate(steps):
-        target = rank ^ step
-        extract(padded, row_offsets[matrix, target], row_counts[matrix, target] * live_ranks[target], staged, index)
-        copies.append(pltpu.make_async_copy(staged.at[index], homes[index], leave.at[index]))
-        copies[-1].start()
-    for copy in copies:
-        copy.wait()
+
+    @pl.when(is_inner(rank, ranks))
+    def _():
+        incoming = [
+            pltpu.make_async_copy(high, high_held, arrive.at[0]),
+            pltpu.make_async_copy(low, low_held, arrive.at[1]),
+        ]
+        for copy in incoming:
+            copy.start()
+        owner_group, live_ranks, row_counts, row_offsets = fetch_tables(tables, refs[8:])
+        matrix = matrix_of(owner_group, rank ^ mate(ranks) if first else rank)
+        mine, other = core_rows()
+        held[mine, :] = keep[...]
+        held[other, :] = away[...]
+        total = polynomial(unpack(held, gram), gram)
+        copies = []
+        if first:
+            for panel in range(3):
+                store_panel(held, panel, total[panel * PANEL :, panel * PANEL : (panel + 1) * PANEL])
+            copies = [pltpu.make_async_copy(held, whole, leave.at[len(steps)])]
+            copies[0].start()
+        for copy in incoming:
+            copy.wait()
+        padded[:INNER, :] = dot_halves(halves(total), (high_held[...], low_held[...]))
+        if not first:
+            copies = [pltpu.make_async_copy(padded.at[pl.ds(0, INNER)], whole, leave.at[len(steps)])]
+            copies[0].start()
+        for index, step in enumerate(steps):
+            target = rank ^ step
+            count = row_counts[matrix, target] * live_ranks[target]
+            extract(padded, row_offsets[matrix, target], count, staged, index)
+            copies.append(pltpu.make_async_copy(staged.at[index], homes[index], leave.at[index]))
+            copies[-1].start()
+        for copy in copies:
+            copy.wait()
 
 
 def finish_kernel(ranks, *refs):
@@ -434,14 +452,15 @@
     half = jax.ShapeDtypeStruct((INNER, columns), jnp.bfloat16)
     return pl.pallas_call(
         functools.partial(gram_kernel, first, ranks),
-        out_shape=[half, half, floats(INNER, 2 * PANEL)] + [floats(INNER, columns)] * first,
-        in_specs=[HBM] * 4 + [ANY] * (ranks + 1),
-        out_specs=[ANY, ANY, VMEM] + [ANY] * first,
+        out_shape=[half, half] + [floats(INNER // 2, 2 * PANEL)] * 2 + [floats(INNER, columns)] * first,
+        in_specs=[HBM] * 4 + [ANY] * ranks + [HBM],
+        out_specs=[HBM, HBM, VMEM, VMEM] + [ANY] * first,
         scratch_shapes=[
             vmem(ranks, slots, columns),
             vmem(INNER + slots + SUBLANES, columns),
             vmem(INNER, columns, dtype=jnp.bfloat16),
             vmem(INNER, columns, dtype=jnp.bfloat16),
+            vmem(INNER, 2 * PANEL),
             flags(ranks),
             flags(3),
         ]
@@ -457,12 +476,18 @@
     return [whole] + [floats(slots, columns)] * len(steps)
 
 
-def apply_update(first, steps, tables, packed, high, low, slots, *after):
+def nothing(shapes):
+    return pl.pallas_call(
+        idle_kernel, out_shape=shapes, out_specs=[ANY] * len(shapes), compiler_params=SMALL, name="nothing"
+    )()
+
+
+def apply_update(first, steps, tables, keep, away, high, low, slots, *after):
     columns = high.shape[1]
     return pl.pallas_call(
         functools.partial(update_kernel, first, steps),
         out_shape=update_shapes(first, steps, slots, columns),
-        in_specs=[HBM] * 4 + [VMEM] + [ANY] * (2 + len(after)),
+        in_specs=[HBM] * 4 + [VMEM] * 2 + [HBM] * 2 + [ANY] * len(after),
         out_specs=[ANY] * (1 + len(steps)),
         scratch_shapes=[
             vmem(INNER, INNER),
@@ -478,11 +503,7 @@
         compiler_params=PARAMS,
         cost_estimate=FREE,
         name="apply_update",
-    )(*tables, packed, high, low, *after)
-
-
-def nothing(shapes):
-    return pl.pallas_call(idle_kernel, out_shape=shapes, out_specs=[ANY] * len(shapes), name="nothing")()
+    )(*tables, keep, away, high, low, *after)
 
 
 def settle(value):
@@ -491,6 +512,7 @@
         out_shape=floats(SUBLANES, 128),
         in_specs=[ANY],
         out_specs=ANY,
+        compiler_params=SMALL,
         cost_estimate=pl.CostEstimate(flops=10**11, bytes_accessed=0, transcendentals=0),
         name="settle",
     )(value)
@@ -533,42 +555,24 @@
     )(owner_group, *blocks, shards)
 
 
-def sum_over(block, axis):
+def sum_halves(keep, send, axis):
     size = lax.axis_size(axis)
-    if size & (size - 1) or block.shape[0] % size:
-        return lax.psum(block, axis)
-    index = lax.axis_index(axis)
 
     def exchange(piece, bits):
         return lax.ppermute(piece, axis, [(i, i ^ bits[i & 1]) for i in range(size)])
 
-    def mine(bits, part):
-        bit = jnp.where(index & 1, bits[1], bits[0])
-        return jnp.where(index & bit, part, 0)
-
     chips = [1 << shift for shift in range(1, size.bit_length() - 1)]
-    stages = [(1, 1), *zip(chips, reversed(chips))]
-    for bits in stages:
-        part = block.shape[0] // 2
-        keep = mine(bits, part)
-        away = exchange(lax.dynamic_slice_in_dim(block, part - keep, part, 0), bits)
-        block = lax.dynamic_slice_in_dim(block, keep, part, 0) + away
-    for bits in reversed(stages):
-        part = block.shape[0]
-        keep = mine(bits, part)
-        away = exchange(block, bits)
-        whole = jnp.zeros((2 * part, block.shape[1]), block.dtype)
-        whole = lax.dynamic_update_slice_in_dim(whole, block, keep, 0)
-        block = lax.dynamic_update_slice_in_dim(whole, away, part - keep, 0)
-    return block
+    keep = keep + exchange(send, (1, 1))
+    for bits in zip(chips, reversed(chips)):
+        keep = keep + exchange(keep, bits)
+    return keep, exchange(keep, (1, 1))
 
 
 def on_device(momentum, gradient, live_ranks, owner_group, row_counts, row_offsets):
     ranks = lax.axis_size("fsdp")
-    my_rank = lax.axis_index("fsdp")
     _, slots, columns = momentum.shape
+    inner = is_inner(lax.axis_index("fsdp"), ranks)
     tables = (owner_group, live_ranks, row_counts, row_offsets)
-    inner = is_inner(my_rank, ranks)
     last = [2, 1, *range(3, ranks)]
     early = [step for step in last if step != mate(ranks)]
 
@@ -587,24 +591,26 @@
     last_blocks = [blends[0]] + [to_inner(blends[step], step) for step in range(1, ranks)]
     new_momentum, token = fresh_momentum(tables, momentum, gradient, token)
 
-    high, low, gram_part, iterate = assemble_and_gram(True, tables, first_blocks, token)
+    high, low, keep, send, iterate = assemble_and_gram(True, tables, first_blocks, token)
     iterate = from_inner(iterate, mate(ranks))
 
-    def first_update(high, low, gram_part, after):
-        return apply_update(True, [0, *early], tables, sum_over(gram_part, "tensor"), high, low, slots, after)
-
-    def first_skip(high, low, gram_part, after):
+    def first_update(high, low, keep, send, after):
+        return apply_update(
+            True, [0, *early], tables, *sum_halves(keep, send, "tensor"), high, low, slots, after
+        )
+
+    def first_skip(*_):
         return nothing(update_shapes(True, [0, *early], slots, columns))
 
-    packed, own_first, *homes = lax.cond(inner, first_update, first_skip, high, low, gram_part, settle(gram_part))
+    packed, own_first, *homes = lax.cond(inner, first_update, first_skip, high, low, keep, send, settle(keep))
     packed_there = from_inner(packed, mate(ranks))
     first_home = [from_inner(block, step) for step, block in zip(early, homes)]
 
     def last_update(after, *blocks):
-        high, low, gram_part = assemble_and_gram(False, tables, blocks, after)
-        return apply_update(False, [0, *last], tables, sum_over(gram_part, "tensor"), high, low, slots)
-
-    def last_skip(after, *blocks):
+        high, low, keep, send = assemble_and_gram(False, tables, blocks, after)
+        return apply_update(False, [0, *last], tables, *sum_halves(keep, send, "tensor"), high, low, slots)
+
+    def last_skip(*_):
         return nothing(update_shapes(False, [0, *last], slots, columns))
 
     result, own_last, *homes = lax.cond(inner, last_update, last_skip, packed, *last_blocks)

time: 223 us -> 203 us (0.910)
  waiting for transfers between devices: 164 us -> 145 us
    ppermute x7, waiting for transfers between devices: 104 us -> 84.3 us  [from_inner(): return lax.ppermute(block, 'fsdp', pairs(step, False))]
  transfers between devices with their start and end apart: 13 -> 13, of which waited for: 7 -> 7; matrix products, arithmetic and copies ran while one was open for 0% -> 0% of each run, Pallas kernels for 11% -> 12%
where the time goes in v8:
time: 203 us; the launch traced here: 202 us
  waiting for transfers between devices  145 us (71%)
  Pallas kernels  29.8 us (15%)
  starting transfers between devices  24.8 us (12%)
    ppermute x7, waiting for transfers between devices, from_inner(): return lax.ppermute(block, 'fsdp', pairs(step, False))  84.3 us
    ppermute x6, waiting for transfers between devices, to_inner(): return lax.ppermute(block, 'fsdp', pairs(step, True))  60.3 us
    ppermute x6, starting transfers between devices, to_inner(): return lax.ppermute(block, 'fsdp', pairs(step, True))  16 us
    pallas_call x2, Pallas kernels, blend(): pl.pallas_call(functools.partial(blend_kernel, first, chunks), out_shape=...  10.1 us
    ppermute x7, starting transfers between devices, from_inner(): return lax.ppermute(block, 'fsdp', pairs(step, False))  8.75 us
    pallas_call x1, Pallas kernels, finish(): pl.pallas_call(functools.partial(finish_kernel, tables[1].shape[0]), out_...  6.61 us
    pallas_call x4, Pallas kernels, place_blocks(): pl.pallas_call(functools.partial(place_kernel, first, ranks, steps), out_...  6.37 us
    pallas_call x1, Pallas kernels, fresh_momentum(): pl.pallas_call(fresh_kernel, grid=(matrices,), out_shape=[floats(*momentu...  5.86 us
  transfers between devices with their start and end apart: 13, of which 7 were waited for; matrix products, arithmetic and copies ran while one was open for 0% of the time, Pallas kernels for 12%

profile of v8, /device:TPU:0, one launch (start us, length us, event | category | flops | bytes accessed | tf_op | source)
XLA Modules:
  0.0 202.1 jit_solution(6250396354973079733)
XLA Ops:
  0.7 5.2 %blend.2 = (f32[288,896]{1,0:T(8,128)}, f32[288,896]{1,0:T(8,128)}, f32[288,896]{1,0:T(8,128)}, f32[288,896]{1,0:T(8,128)}, f32[8,128]{1,0:T(8,128)}) custom-call(s32[4]{0:T(128)} %refs_0_.15, s32[4]{0:T(128)} %refs_1_.7, s32[4,4]{1,0:T(4,128)} %refs_2_.7, s32[4,4]{1,0:T(4,128)} %refs_3_.7, f32[4,288,896]{2,1,0:T(8,128)} %momentum.1, f32[4,288,896]{2,1,0:T(8,128)} %gradient.1), custom_call_target="tpu_custom_call" | custom-call | tf_op jit(solution)/shard_map/blend/pallas_call | solution.py:420
  5.9 5.0 %collective-permute-start.11 = (f32[288,896]{1,0:T(8,128)}, f32[288,896]{1,0:T(8,128)S(1)}, u32[]{:S(2)}, u32[]{:S(2)}) collective-permute-start(f32[288,896]{1,0:T(8,128)} %get-tuple-element.97), channel_id=1, source_target_pairs={{0,8},{24,16},{1,9},{25,17},{2,10},{26,18},{3,11},{27,19},{4,12},{... | collective-permute-start | bytes 3096584 | tf_op jit(solution)/shard_map/ppermute | solution.py:583
  10.9 2.3 %collective-permute-start.12 = (f32[288,896]{1,0:T(8,128)}, f32[288,896]{1,0:T(8,128)S(1)}, u32[]{:S(2)}, u32[]{:S(2)}) collective-permute-start(f32[288,896]{1,0:T(8,128)} %get-tuple-element.98), channel_id=1, source_target_pairs={{0,16},{24,8},{1,17},{25,9},{2,18},{26,10},{3,19},{27,11},{4,20},{... | collective-permute-start | bytes 3096584 | tf_op jit(solution)/shard_map/ppermute | solution.py:583
  13.2 1.7 collective-permute-start.13
  14.9 4.9 %blend.3 = (f32[288,896]{1,0:T(8,128)}, f32[288,896]{1,0:T(8,128)}, f32[288,896]{1,0:T(8,128)}, f32[288,896]{1,0:T(8,128)}, f32[8,128]{1,0:T(8,128)}) custom-call(s32[4]{0:T(128)S(1)} %copy-done.6, s32[4]{0:T(128)S(1)} %copy-done.7, s32[4,4]{1,0:T(4,128)S(1)} %copy-done.4, s32[4,4]{1,0:T(4,128)S(1)} %copy-done.5, f32[4,288,896]{2,1,0:T(8,128)} %momentum.1, ...), custom_call_target="tpu_custom_call" | custom-call | tf_op jit(solution)/shard_map/blend/pallas_call | solution.py:420
  19.8 3.0 %collective-permute-start.8 = (f32[288,896]{1,0:T(8,128)}, f32[288,896]{1,0:T(8,128)}, u32[]{:S(2)}, u32[]{:S(2)}) collective-permute-start(f32[288,896]{1,0:T(8,128)} %get-tuple-element.93), channel_id=1, source_target_pairs={{0,8},{24,16},{1,9},{25,17},{2,10},{26,18},{3,11},{27,19},{4,12},{... | collective-permute-start | bytes 3096584 | tf_op jit(solution)/shard_map/ppermute | solution.py:583
  22.8 2.3 %collective-permute-start.9 = (f32[288,896]{1,0:T(8,128)}, f32[288,896]{1,0:T(8,128)}, u32[]{:S(2)}, u32[]{:S(2)}) collective-permute-start(f32[288,896]{1,0:T(8,128)} %get-tuple-element.94), channel_id=1, source_target_pairs={{0,16},{24,8},{1,17},{25,9},{2,18},{26,10},{3,19},{27,11},{4,20},{... | collective-permute-start | bytes 3096584 | tf_op jit(solution)/shard_map/ppermute | solution.py:583
  25.2 5.9 %fresh_momentum.1 = (f32[4,288,896]{2,1,0:T(8,128)}, f32[8,128]{1,0:T(8,128)}) custom-call(s32[4]{0:T(128)S(1)} %copy-done.7, s32[4,4]{1,0:T(4,128)S(1)} %copy-done.4, f32[4,288,896]{2,1,0:T(8,128)} %momentum.1, f32[4,288,896]{2,1,0:T(8,128)} %gradient.1, f32[8,128]{1,0:T(8,128)} %get-tuple-element.90._), custom_call_target="tpu_custom_call" | custom-call | tf_op jit(solution)/shard_map/fresh_momentum/pallas_call | solution.py:437
  31.0 3.3 %collective-permute-done.11.refs_5_ = f32[288,896]{1,0:T(8,128)S(1)} collective-permute-done((f32[288,896]{1,0:T(8,128)}, f32[288,896]{1,0:T(8,128)S(1)}, u32[]{:S(2)}, u32[]{:S(2)}) %collective-permute-start.11) | collective-permute-done | bytes 1032224 | tf_op jit(solution)/shard_map/ppermute | solution.py:583
  34.3 1.6 collective-permute-start.10
  36.0 20.5 %collective-permute-done.12.refs_6_ = f32[288,896]{1,0:T(8,128)S(1)} collective-permute-done((f32[288,896]{1,0:T(8,128)}, f32[288,896]{1,0:T(8,128)S(1)}, u32[]{:S(2)}, u32[]{:S(2)}) %collective-permute-start.12) | collective-permute-done | bytes 1032224 | tf_op jit(solution)/shard_map/ppermute | solution.py:583
  58.0 1.3 collective-permute-start.20
  61.9 16.7 %collective-permute-done.8 = f32[288,896]{1,0:T(8,128)} collective-permute-done((f32[288,896]{1,0:T(8,128)}, f32[288,896]{1,0:T(8,128)}, u32[]{:S(2)}, u32[]{:S(2)}) %collective-permute-start.8) | collective-permute-done | bytes 1032224 | tf_op jit(solution)/shard_map/ppermute | solution.py:583
  79.9 19.7 %collective-permute-done.9 = f32[288,896]{1,0:T(8,128)} collective-permute-done((f32[288,896]{1,0:T(8,128)}, f32[288,896]{1,0:T(8,128)}, u32[]{:S(2)}, u32[]{:S(2)}) %collective-permute-start.9) | collective-permute-done | bytes 1032224 | tf_op jit(solution)/shard_map/ppermute | solution.py:583
  99.6 1.6 collective-permute-start.18
  101.2 1.3 collective-permute-start.16
  102.5 50.6 %collective-permute-done.19.refs_4_ = f32[576,384]{1,0:T(8,128)} collective-permute-done((f32[576,384]{1,0:T(8,128)}, f32[576,384]{1,0:T(8,128)}, u32[]{:S(2)}, u32[]{:S(2)}) %collective-permute-start.19) | collective-permute-done | bytes 884768 | tf_op jit(solution)/shard_map/ppermute | solution.py:586
  153.2 1.3 collective-permute-start.15
  155.2 6.6 %finish.1 = (f32[576,896]{1,0:T(8,128)}, f32[4,288,896]{2,1,0:T(8,128)}) custom-call(s32[4]{0:T(128)S(1)} %copy-done.6, s32[4]{0:T(128)S(1)} %copy-done.7, s32[4,4]{1,0:T(4,128)S(1)} %copy-done.4, s32[4,4]{1,0:T(4,128)S(1)} %copy-done.5, f32[576,384]{1,0:T(8,128)} %collective-permute-done.19.refs_4_, f32[576,896]{1,0:T(8,128)S(1)} %collective-permute-done.20.refs_5_, ...), custom_call_target="tpu_custom_call" | custom-call | tf_op jit(solution)/shard_map/finish/pallas_call | solution.py:523
  161.8 2.8 %place_blocks.4.refs_2_ = f32[4,288,896]{2,1,0:T(8,128)} custom-call(s32[4]{0:T(128)S(1)} %copy-done.6, f32[288,896]{1,0:T(8,128)S(1)} %collective-permute-done.17.refs_1_, f32[288,896]{1,0:T(8,128)} %collective-permute-done.18.refs_2_, f32[4,288,896]{2,1,0:T(8,128)} %get-tuple-element.115.refs_3_), custom_call_target="tpu_custom_call", output_to_operand_aliasing={{}: (3, {})} | custom-call | tf_op jit(solution)/shard_map/place_blocks/pallas_call | solution.py:545
  164.6 13.6 %collective-permute-done.16.refs_1_ = f32[288,896]{1,0:T(8,128)S(1)} collective-permute-done((f32[288,896]{1,0:T(8,128)}, f32[288,896]{1,0:T(8,128)S(1)}, u32[]{:S(2)}, u32[]{:S(2)}) %collective-permute-start.16) | collective-permute-done | bytes 1032224 | tf_op jit(solution)/shard_map/ppermute | solution.py:586
  178.2 1.5 place_blocks.5.refs_2_
  179.7 20.1 %collective-permute-done.15.refs_1_ = f32[288,896]{1,0:T(8,128)S(1)} collective-permute-done((f32[288,896]{1,0:T(8,128)}, f32[288,896]{1,0:T(8,128)S(1)}, u32[]{:S(2)}, u32[]{:S(2)}) %collective-permute-start.15) | collective-permute-done | bytes 1032224 | tf_op jit(solution)/shard_map/ppermute | solution.py:586
  199.8 1.5 place_blocks.6.refs_2_
  (30 shorter events, 6.7 us)
Async XLA Ops:
  0.6 14.3 %copy-start.7 = (s32[4]{0:T(128)S(1)}, s32[4]{0:T(128)}, u32[]{:S(2)}) copy-start(s32[4]{0:T(128)} %refs_1_.7) | copy-start | bytes 52
  0.6 14.3 %copy-start.4 = (s32[4,4]{1,0:T(4,128)S(1)}, s32[4,4]{1,0:T(4,128)}, u32[]{:S(2)}) copy-start(s32[4,4]{1,0:T(4,128)} %refs_2_.7) | copy-start | bytes 196
  0.7 14.3 %copy-start.6 = (s32[4]{0:T(128)S(1)}, s32[4]{0:T(128)}, u32[]{:S(2)}) copy-start(s32[4]{0:T(128)} %refs_0_.15) | copy-start | bytes 52
  0.7 14.3 %copy-start.5 = (s32[4,4]{1,0:T(4,128)S(1)}, s32[4,4]{1,0:T(4,128)}, u32[]{:S(2)}) copy-start(s32[4,4]{1,0:T(4,128)} %refs_3_.7) | copy-start | bytes 196
  5.9 28.5 %collective-permute-start.11 = (f32[288,896]{1,0:T(8,128)}, f32[288,896]{1,0:T(8,128)S(1)}, u32[]{:S(2)}, u32[]{:S(2)}) collective-permute-start(f32[288,896]{1,0:T(8,128)} %get-tuple-element.97), channel_id=1, source_target_pairs={{0,8},{24,16},{1,9},{25,17},{2,10},{26,18},{3,11},{27,19},{4,12},{... | collective-permute-start | bytes 3096584 | tf_op jit(solution)/shard_map/ppermute | solution.py:583
  10.9 45.6 %collective-permute-start.12 = (f32[288,896]{1,0:T(8,128)}, f32[288,896]{1,0:T(8,128)S(1)}, u32[]{:S(2)}, u32[]{:S(2)}) collective-permute-start(f32[288,896]{1,0:T(8,128)} %get-tuple-element.98), channel_id=1, source_target_pairs={{0,16},{24,8},{1,17},{25,9},{2,18},{26,10},{3,19},{27,11},{4,20},{... | collective-permute-start | bytes 3096584 | tf_op jit(solution)/shard_map/ppermute | solution.py:583
  13.2 43.3 %collective-permute-start.13 = (f32[288,896]{1,0:T(8,128)}, f32[288,896]{1,0:T(8,128)}, u32[]{:S(2)}, u32[]{:S(2)}) collective-permute-start(f32[288,896]{1,0:T(8,128)} %get-tuple-element.99), channel_id=1, source_target_pairs={{8,16},{16,8},{9,17},{17,9},{10,18},{18,10},{11,19},{19,11},{12,20... | collective-permute-start | bytes 3096584 | tf_op jit(solution)/shard_map/ppermute | solution.py:583
  19.8 58.8 %collective-permute-start.8 = (f32[288,896]{1,0:T(8,128)}, f32[288,896]{1,0:T(8,128)}, u32[]{:S(2)}, u32[]{:S(2)}) collective-permute-start(f32[288,896]{1,0:T(8,128)} %get-tuple-element.93), channel_id=1, source_target_pairs={{0,8},{24,16},{1,9},{25,17},{2,10},{26,18},{3,11},{27,19},{4,12},{... | collective-permute-start | bytes 3096584 | tf_op jit(solution)/shard_map/ppermute | solution.py:583
  22.8 76.8 %collective-permute-start.9 = (f32[288,896]{1,0:T(8,128)}, f32[288,896]{1,0:T(8,128)}, u32[]{:S(2)}, u32[]{:S(2)}) collective-permute-start(f32[288,896]{1,0:T(8,128)} %get-tuple-element.94), channel_id=1, source_target_pairs={{0,16},{24,8},{1,17},{25,9},{2,18},{26,10},{3,19},{27,11},{4,20},{... | collective-permute-start | bytes 3096584 | tf_op jit(solution)/shard_map/ppermute | solution.py:583
  25.2 31.3 %copy-start = (f32[288,896]{1,0:T(8,128)S(1)}, f32[288,896]{1,0:T(8,128)}, u32[]{:S(2)}) copy-start(f32[288,896]{1,0:T(8,128)} %get-tuple-element.96.refs_4_) | copy-start | bytes 3096580
  34.3 66.9 %collective-permute-start.10 = (f32[288,896]{1,0:T(8,128)}, f32[288,896]{1,0:T(8,128)}, u32[]{:S(2)}, u32[]{:S(2)}) collective-permute-start(f32[288,896]{1,0:T(8,128)} %get-tuple-element.95), channel_id=1, source_target_pairs={{8,16},{16,8},{9,17},{17,9},{10,18},{18,10},{11,19},{19,11},{12,20... | collective-permute-start | bytes 3096584 | tf_op jit(solution)/shard_map/ppermute | solution.py:583
  56.5 0.7 copy-start.1
  58.0 96.4 %collective-permute-start.20 = (f32[576,896]{1,0:T(8,128)}, f32[576,896]{1,0:T(8,128)S(1)}, u32[]{:S(2)}, u32[]{:S(2)}) collective-permute-start(f32[576,896]{1,0:T(8,128)} %get-tuple-element.111), channel_id=1, source_target_pairs={{8,0},{16,24},{9,1},{17,25},{10,2},{18,26},{11,3},{19,27},{12,4},{... | collective-permute-start | bytes 6193160 | tf_op jit(solution)/shard_map/ppermute | solution.py:586
  59.3 1.2 copy-start.2
  60.6 92.6 %collective-permute-start.19 = (f32[576,384]{1,0:T(8,128)}, f32[576,384]{1,0:T(8,128)}, u32[]{:S(2)}, u32[]{:S(2)}) collective-permute-start(f32[576,384]{1,0:T(8,128)} %get-tuple-element.105), channel_id=1, source_target_pairs={{8,0},{16,24},{9,1},{17,25},{10,2},{18,26},{11,3},{19,27},{12,4},{... | collective-permute-start | bytes 2654216 | tf_op jit(solution)/shard_map/ppermute | solution.py:586
  78.6 83.2 %collective-permute-start.17 = (f32[288,896]{1,0:T(8,128)}, f32[288,896]{1,0:T(8,128)S(1)}, u32[]{:S(2)}, u32[]{:S(2)}) collective-permute-start(f32[288,896]{1,0:T(8,128)} %get-tuple-element.109), channel_id=1, source_target_pairs={{8,24},{16,0},{9,25},{17,1},{10,26},{18,2},{11,27},{19,3},{12,28},... | collective-permute-start | bytes 3096584 | tf_op jit(solution)/shard_map/ppermute | solution.py:586
  99.6 62.2 %collective-permute-start.18 = (f32[288,896]{1,0:T(8,128)}, f32[288,896]{1,0:T(8,128)}, u32[]{:S(2)}, u32[]{:S(2)}) collective-permute-start(f32[288,896]{1,0:T(8,128)} %get-tuple-element.110), channel_id=1, source_target_pairs={{8,16},{16,8},{9,17},{17,9},{10,18},{18,10},{11,19},{19,11},{12,20... | collective-permute-start | bytes 3096584 | tf_op jit(solution)/shard_map/ppermute | solution.py:586
  101.2 77.0 %collective-permute-start.16 = (f32[288,896]{1,0:T(8,128)}, f32[288,896]{1,0:T(8,128)S(1)}, u32[]{:S(2)}, u32[]{:S(2)}) collective-permute-start(f32[288,896]{1,0:T(8,128)} %get-tuple-element.108), channel_id=1, source_target_pairs={{8,24},{16,0},{9,25},{17,1},{10,26},{18,2},{11,27},{19,3},{12,28},... | collective-permute-start | bytes 3096584 | tf_op jit(solution)/shard_map/ppermute | solution.py:586
  153.2 46.6 %collective-permute-start.15 = (f32[288,896]{1,0:T(8,128)}, f32[288,896]{1,0:T(8,128)S(1)}, u32[]{:S(2)}, u32[]{:S(2)}) collective-permute-start(f32[288,896]{1,0:T(8,128)} %get-tuple-element.107), channel_id=1, source_target_pairs={{8,0},{16,24},{9,1},{17,25},{10,2},{18,26},{11,3},{19,27},{12,4},{... | collective-permute-start | bytes 3096584 | tf_op jit(solution)/shard_map/ppermute | solution.py:586
  154.5 46.9 %collective-permute-start.14 = (f32[288,896]{1,0:T(8,128)}, f32[288,896]{1,0:T(8,128)S(1)}, u32[]{:S(2)}, u32[]{:S(2)}) collective-permute-start(f32[288,896]{1,0:T(8,128)} %get-tuple-element.106), channel_id=1, source_target_pairs={{8,16},{16,8},{9,17},{17,9},{10,18},{18,10},{11,19},{19,11},{12,20... | collective-permute-start | bytes 3096584 | tf_op jit(solution)/shard_map/ppermute | solution.py:586

commit v9 on v8

--- a/solution.py
+++ b/solution.py
@@ -34,23 +34,24 @@
     return high, low
 
 
-def dot(left, right, contract):
+def dot(left, right, contract=((1,), (0,))):
     return lax.dot_general(left, right, (contract, ((), ())), preferred_element_type=jnp.float32)
 
 
-def dot_halves(left, right, contract=((1,), (0,))):
-    (left_high, left_low), (right_high, right_low) = left, right
-    depth = left_high.shape[1]
-    body = depth // TILE * TILE
-    if contract == ((1,), (0,)) and 0 < 3 * (depth - body) <= TILE:
-        rest_left = jnp.concatenate([left_high[:, body:], left_low[:, body:], left_high[:, body:]], axis=1)
-        rest_right = jnp.concatenate([right_low[body:], right_high[body:], right_high[body:]], axis=0)
-        left = left_high[:, :body], left_low[:, :body]
-        right = right_high[:body], right_low[:body]
-        return dot(rest_left, rest_right, contract) + dot_halves(left, right)
-    return (
-        dot(left_high, right_low, contract) + dot(left_low, right_high, contract)
-    ) + dot(left_high, right_high, contract)
+DEPTH = INNER // TILE * TILE
+PARTS = [(side, rows) for rows in ((0, DEPTH), (DEPTH, INNER)) if rows[0] < rows[1] for side in (1, 0, 0)]
+
+
+def passes_left(value):
+    high, low = halves(value)
+    return jnp.concatenate(
+        [part[:, first:last] for first, last in ((0, DEPTH), (DEPTH, INNER)) for part in (high, low, high)], axis=1
+    )
+
+
+def passes_right(value):
+    sides = halves(value)
+    return jnp.concatenate([sides[side][first:last] for side, (first, last) in PARTS], axis=0)
 
 
 def is_inner(rank, ranks):
@@ -160,8 +161,8 @@
 
 
 def gram_kernel(first, ranks, *refs):
-    tables, blocks, refs = refs[:4], refs[4 : 4 + ranks], refs[5 + ranks :]
-    high_out, low_out, keep, send = refs[:4]
+    tables, blocks, refs = refs[:4], refs[4 : 4 + ranks], refs[(4 if first else 5) + ranks :]
+    pair, keep, send = refs[:3]
     landed, padded, high_held, low_held, gram, arrive, leave = refs[-12:-5]
     slots, columns = blocks[0].shape
     rank = lax.axis_index("fsdp")
@@ -195,17 +196,18 @@
         high_held[...] = high
         low_held[...] = low
         outgoing = [
-            pltpu.make_async_copy(high_held, high_out, leave.at[0]),
-            pltpu.make_async_copy(low_held, low_out, leave.at[1]),
+            pltpu.make_async_copy(high_held, pair.at[0], leave.at[0]),
+            pltpu.make_async_copy(low_held, pair.at[1], leave.at[1]),
         ]
         if first:
-            outgoing.append(pltpu.make_async_copy(padded.at[pl.ds(0, INNER)], refs[4], leave.at[2]))
+            outgoing.append(pltpu.make_async_copy(padded.at[pl.ds(0, INNER)], refs[3], leave.at[2]))
         for copy in outgoing:
             copy.start()
+        left = jnp.concatenate([high, low, high], axis=1)
+        right = jnp.concatenate([low, high, high], axis=1)
         for panel in range(3):
             here = slice(panel * PANEL, (panel + 1) * PANEL)
-            part = dot_halves((high[panel * PANEL :], low[panel * PANEL :]), (high[here], low[here]), ((1,), (1,)))
-            store_panel(gram, panel, part)
+            store_panel(gram, panel, dot(left[panel * PANEL :], right[here], ((1,), (1,))))
         mine, other = core_rows()
         keep[...] = gram[mine, :]
         send[...] = gram[other, :]
@@ -240,7 +242,7 @@
 def symmetric_product(left, right, out):
     for begin in range(0, INNER, TILE):
         end = min(begin + TILE, INNER)
-        part = dot_halves(tuple(half[begin:] for half in left), tuple(half[:, begin:end] for half in right))
+        part = dot(left[begin:], right[:, begin:end])
         out[begin:, begin:end] = part
         if end < INNER:
             out[begin:end, end:] = part[end - begin :].T
@@ -253,19 +255,15 @@
     norm = jnp.sqrt(jnp.full((1, 1), square_total, jnp.float32)) + EPSILON
     inverse = 1.0 / norm
     first = (raw * inverse) * inverse
-    first_halves = halves(first)
-    second = symmetric_product(first_halves, first_halves, gram)
+    first_right = passes_right(first)
+    second = symmetric_product(passes_left(first), first_right, gram)
     base = QUINTIC_SECOND * first + QUINTIC_THIRD * second + jnp.where(diagonal, QUINTIC_FIRST, 0.0)
-    base_halves = halves(base)
-    third_halves = halves(symmetric_product(base_halves, first_halves, gram))
-    next_gram = symmetric_product(base_halves, third_halves, gram)
-    next_halves = halves(next_gram)
-    outer = (
-        QUINTIC_SECOND * next_gram
-        + QUINTIC_THIRD * symmetric_product(next_halves, next_halves, gram)
-        + jnp.where(diagonal, QUINTIC_FIRST, 0.0)
-    )
-    return symmetric_product(halves(outer), base_halves, gram) * (inverse * OUT_SCALE)
+    base_left = passes_left(base)
+    third = symmetric_product(base_left, first_right, gram)
+    next_gram = symmetric_product(base_left, passes_right(third), gram)
+    square = symmetric_product(passes_left(next_gram), passes_right(next_gram), gram)
+    outer = QUINTIC_SECOND * next_gram + QUINTIC_THIRD * square + jnp.where(diagonal, QUINTIC_FIRST, 0.0)
+    return symmetric_product(passes_left(outer), passes_right(base), gram) * (inverse * OUT_SCALE)
 
 
 def extract(padded, start, count, staged, step):
@@ -290,22 +288,23 @@
 
 
 def update_kernel(first, steps, *refs):
-    tables, (keep, away, high, low), refs = refs[:4], refs[4:8], refs[9 if first else 8 :]
+    tables, (keep, away, pair), refs = refs[:4], refs[4:7], refs[8 if first else 7 :]
     whole, refs = refs[0], refs[1:]
     homes, refs = refs[: len(steps)], refs[len(steps) :]
-    gram, padded, staged, high_held, low_held, held, arrive, leave = refs[:8]
+    gram, padded, staged, stacked, held, arrive, leave = refs[:7]
     ranks = tables[1].shape[0]
     rank = lax.axis_index("fsdp")
 
     @pl.when(is_inner(rank, ranks))
     def _():
-        incoming = [
-            pltpu.make_async_copy(high, high_held, arrive.at[0]),
-            pltpu.make_async_copy(low, low_held, arrive.at[1]),
-        ]
-        for copy in incoming:
-            copy.start()
-        owner_group, live_ranks, row_counts, row_offsets = fetch_tables(tables, refs[8:])
+        incoming, begin = [], 0
+        for index, (side, (first_row, last_row)) in enumerate(PARTS):
+            size = last_row - first_row
+            source = pair.at[side, pl.ds(first_row, size)]
+            incoming.append(pltpu.make_async_copy(source, stacked.at[pl.ds(begin, size)], arrive.at[index]))
+            incoming[-1].start()
+            begin += size
+        owner_group, live_ranks, row_counts, row_offsets = fetch_tables(tables, refs[7:])
         matrix = matrix_of(owner_group, rank ^ mate(ranks) if first else rank)
         mine, other = core_rows()
         held[mine, :] = keep[...]
@@ -319,7 +318,7 @@
             copies[0].start()
         for copy in incoming:
             copy.wait()
-        padded[:INNER, :] = dot_halves(halves(total), (high_held[...], low_held[...]))
+        padded[:INNER, :] = dot(passes_left(total), stacked[...])
         if not first:
             copies = [pltpu.make_async_copy(padded.at[pl.ds(0, INNER)], whole, leave.at[len(steps)])]
             copies[0].start()
@@ -334,7 +333,8 @@
 
 
 def finish_kernel(ranks, *refs):
-    tables, (packed, iterate, inner_result, own_first, own_last, result, shards), refs = refs[:4], refs[4:11], refs[11:]
+    tables, (packed, iterate, inner_result, own_first, own_last), refs = refs[:4], refs[4:9], refs[10:]
+    (result, shards), refs = refs[:2], refs[2:]
     gram, padded, staged, whole, held, arrive, leave = refs[:7]
     rank = lax.axis_index("fsdp")
     owner_group, live_ranks, row_counts, row_offsets = fetch_tables(tables, refs[7:])
@@ -368,7 +368,7 @@
     @pl.when(jnp.logical_not(is_inner(rank, ranks)))
     def _():
         run([(iterate, whole, arrive.at[0]), (packed, held, arrive.at[1])])
-        padded[:INNER, :] = dot_halves(halves(unpack(held, gram)), halves(whole[...]))
+        padded[:INNER, :] = dot(passes_left(unpack(held, gram)), passes_right(whole[...]))
         extract(padded, row_offsets[matrix, rank], row_counts[matrix, rank] * live_ranks[rank], staged, 0)
         run(
             [
@@ -446,15 +446,15 @@
     )(*tables[1:3], momentum, gradient, before)
 
 
-def assemble_and_gram(first, tables, blocks, after):
+def assemble_and_gram(first, tables, blocks, *after):
     slots, columns = blocks[0].shape
     ranks = len(blocks)
-    half = jax.ShapeDtypeStruct((INNER, columns), jnp.bfloat16)
+    pair = jax.ShapeDtypeStruct((4, INNER, columns), jnp.bfloat16)
     return pl.pallas_call(
         functools.partial(gram_kernel, first, ranks),
-        out_shape=[half, half] + [floats(INNER // 2, 2 * PANEL)] * 2 + [floats(INNER, columns)] * first,
-        in_specs=[HBM] * 4 + [ANY] * ranks + [HBM],
-        out_specs=[HBM, HBM, VMEM, VMEM] + [ANY] * first,
+        out_shape=[pair] + [floats(INNER // 2, 2 * PANEL)] * 2 + [floats(INNER, columns)] * first,
+        in_specs=[HBM] * 4 + [ANY] * (ranks + len(after)),
+        out_specs=[ANY, VMEM, VMEM] + [ANY] * first,
         scratch_shapes=[
             vmem(ranks, slots, columns),
             vmem(INNER + slots + SUBLANES, columns),
@@ -468,7 +468,7 @@
         compiler_params=PARAMS,
         cost_estimate=FREE,
         name="assemble_and_gram",
-    )(*tables, *blocks, after)
+    )(*tables, *blocks, *after)
 
 
 def update_shapes(first, steps, slots, columns):
@@ -482,28 +482,27 @@
     )()
 
 
-def apply_update(first, steps, tables, keep, away, high, low, slots, *after):
-    columns = high.shape[1]
+def apply_update(first, steps, tables, keep, away, pair, slots, *after):
+    columns = pair.shape[2]
     return pl.pallas_call(
         functools.partial(update_kernel, first, steps),
         out_shape=update_shapes(first, steps, slots, columns),
-        in_specs=[HBM] * 4 + [VMEM] * 2 + [HBM] * 2 + [ANY] * len(after),
+        in_specs=[HBM] * 4 + [VMEM] * 2 + [ANY] * (1 + len(after)),
         out_specs=[ANY] * (1 + len(steps)),
         scratch_shapes=[
             vmem(INNER, INNER),
             vmem(INNER + slots + 2 * SUBLANES, columns),
             vmem(len(steps), slots, columns),
-            vmem(INNER, columns, dtype=jnp.bfloat16),
-            vmem(INNER, columns, dtype=jnp.bfloat16),
+            vmem(3 * INNER, columns, dtype=jnp.bfloat16),
             vmem(INNER, 2 * PANEL),
-            flags(2),
+            flags(len(PARTS)),
             flags(len(steps) + 1),
         ]
         + table_scratch(*tables[2].shape),
         compiler_params=PARAMS,
         cost_estimate=FREE,
         name="apply_update",
-    )(*tables, keep, away, high, low, *after)
+    )(*tables, keep, away, pair, *after)
 
 
 def settle(value):
@@ -518,12 +517,12 @@
     )(value)
 
 
-def finish(tables, packed, iterate, inner_result, own_first, own_last, shape):
+def finish(tables, packed, iterate, inner_result, own_first, own_last, shape, after):
     slots, columns = own_first.shape
     return pl.pallas_call(
         functools.partial(finish_kernel, tables[1].shape[0]),
         out_shape=[floats(INNER, columns), floats(*shape)],
-        in_specs=[HBM] * 4 + [ANY] * 5,
+        in_specs=[HBM] * 4 + [ANY] * 6,
         out_specs=[HBM] * 2,
         scratch_shapes=[
             vmem(INNER, INNER),
@@ -538,7 +537,7 @@
         compiler_params=PARAMS,
         cost_estimate=FREE,
         name="finish",
-    )(*tables, packed, iterate, inner_result, own_first, own_last)
+    )(*tables, packed, iterate, inner_result, own_first, own_last, after)
 
 
 def place_blocks(first, owner_group, steps, blocks, shards, ranks):
@@ -591,24 +590,22 @@
     last_blocks = [blends[0]] + [to_inner(blends[step], step) for step in range(1, ranks)]
     new_momentum, token = fresh_momentum(tables, momentum, gradient, token)
 
-    high, low, keep, send, iterate = assemble_and_gram(True, tables, first_blocks, token)
+    pair, keep, send, iterate = assemble_and_gram(True, tables, first_blocks)
     iterate = from_inner(iterate, mate(ranks))
 
-    def first_update(high, low, keep, send, after):
-        return apply_update(
-            True, [0, *early], tables, *sum_halves(keep, send, "tensor"), high, low, slots, after
-        )
+    def first_update(pair, keep, send, after):
+        return apply_update(True, [0, *early], tables, *sum_halves(keep, send, "tensor"), pair, slots, after)
 
     def first_skip(*_):
         return nothing(update_shapes(True, [0, *early], slots, columns))
 
-    packed, own_first, *homes = lax.cond(inner, first_update, first_skip, high, low, keep, send, settle(keep))
+    packed, own_first, *homes = lax.cond(inner, first_update, first_skip, pair, keep, send, settle(keep))
     packed_there = from_inner(packed, mate(ranks))
     first_home = [from_inner(block, step) for step, block in zip(early, homes)]
 
     def last_update(after, *blocks):
-        high, low, keep, send = assemble_and_gram(False, tables, blocks, after)
-        return apply_update(False, [0, *last], tables, *sum_halves(keep, send, "tensor"), high, low, slots)
+        pair, keep, send = assemble_and_gram(False, tables, blocks, after)
+        return apply_update(False, [0, *last], tables, *sum_halves(keep, send, "tensor"), pair, slots)
 
     def last_skip(*_):
         return nothing(update_shapes(False, [0, *last], slots, columns))
@@ -616,7 +613,7 @@
     result, own_last, *homes = lax.cond(inner, last_update, last_skip, packed, *last_blocks)
     last_home = [from_inner(block, step) for step, block in zip(last, homes)]
 
-    result, shards = finish(tables, packed_there, iterate, result, own_first, own_last, momentum.shape)
+    result, shards = finish(tables, packed_there, iterate, result, own_first, own_last, momentum.shape, token)
     shards = place_blocks(True, owner_group, early, first_home, shards, ranks)
     for step, block in zip(last, last_home):
         shards = place_blocks(False, owner_group, [step], [block], shards, ranks)

time: 203 us -> 204 us (level)
  waiting for transfers between devices: 145 us -> 137 us
  starting transfers between devices: 24.8 us -> 30.5 us
  Pallas kernels: 29.8 us -> 32.7 us
    ppermute x7, waiting for transfers between devices: 84.3 us -> 76.1 us  [from_inner(): return lax.ppermute(block, 'fsdp', pairs(step, False))]
    ppermute x6, starting transfers between devices: 16 us -> 20.7 us  [to_inner(): return lax.ppermute(block, 'fsdp', pairs(step, True))]
    pallas_call x4, Pallas kernels: 6.37 us -> 9.12 us  [place_blocks(): pl.pallas_call(functools.partial(place_kernel, first, ranks, steps), out_...]
  transfers between devices with their start and end apart: 13 -> 13, of which waited for: 7 -> 6; matrix products, arithmetic and copies ran while one was open for 0% -> 0% of each run, Pallas kernels for 12% -> 13%
where the time goes in v9:
time: 204 us; the launch traced here: 203 us
  waiting for transfers between devices  137 us (67%)
  Pallas kernels  32.7 us (16%)
  starting transfers between devices  30.5 us (15%)
    ppermute x7, waiting for transfers between devices, from_inner(): return lax.ppermute(block, 'fsdp', pairs(step, False))  76.1 us
    ppermute x6, waiting for transfers between devices, to_inner(): return lax.ppermute(block, 'fsdp', pairs(step, True))  61.3 us
    ppermute x6, starting transfers between devices, to_inner(): return lax.ppermute(block, 'fsdp', pairs(step, True))  20.7 us
    pallas_call x2, Pallas kernels, blend(): pl.pallas_call(functools.partial(blend_kernel, first, chunks), out_shape=...  10.1 us
    ppermute x7, starting transfers between devices, from_inner(): return lax.ppermute(block, 'fsdp', pairs(step, False))  9.82 us
    pallas_call x4, Pallas kernels, place_blocks(): pl.pallas_call(functools.partial(place_kernel, first, ranks, steps), out_...  9.12 us
    pallas_call x1, Pallas kernels, finish(): pl.pallas_call(functools.partial(finish_kernel, tables[1].shape[0]), out_...  6.73 us
    pallas_call x1, Pallas kernels, fresh_momentum(): pl.pallas_call(fresh_kernel, grid=(matrices,), out_shape=[floats(*momentu...  5.86 us
  transfers between devices with their start and end apart: 13, of which 6 were waited for; matrix products, arithmetic and copies ran while one was open for 0% of the time, Pallas kernels for 13%

profile of v9, /device:TPU:0, one launch (start us, length us, event | category | flops | bytes accessed | tf_op | source)
XLA Modules:
  0.0 202.6 jit_solution(5700938336292789043)
XLA Ops:
  0.7 5.2 %blend.2 = (f32[288,896]{1,0:T(8,128)}, f32[288,896]{1,0:T(8,128)}, f32[288,896]{1,0:T(8,128)}, f32[288,896]{1,0:T(8,128)}, f32[8,128]{1,0:T(8,128)}) custom-call(s32[4]{0:T(128)} %refs_0_.15, s32[4]{0:T(128)} %refs_1_.7, s32[4,4]{1,0:T(4,128)} %refs_2_.7, s32[4,4]{1,0:T(4,128)} %refs_3_.7, f32[4,288,896]{2,1,0:T(8,128)} %momentum.1, f32[4,288,896]{2,1,0:T(8,128)} %gradient.1), custom_call_target="tpu_custom_call" | custom-call | tf_op jit(solution)/shard_map/blend/pallas_call | solution.py:420
  5.8 5.0 %collective-permute-start.11 = (f32[288,896]{1,0:T(8,128)}, f32[288,896]{1,0:T(8,128)S(1)}, u32[]{:S(2)}, u32[]{:S(2)}) collective-permute-start(f32[288,896]{1,0:T(8,128)} %get-tuple-element.92), channel_id=1, source_target_pairs={{0,8},{24,16},{1,9},{25,17},{2,10},{26,18},{3,11},{27,19},{4,12},{... | collective-permute-start | bytes 3096584 | tf_op jit(solution)/shard_map/ppermute | solution.py:582
  10.9 2.3 %collective-permute-start.12 = (f32[288,896]{1,0:T(8,128)}, f32[288,896]{1,0:T(8,128)S(1)}, u32[]{:S(2)}, u32[]{:S(2)}) collective-permute-start(f32[288,896]{1,0:T(8,128)} %get-tuple-element.93), channel_id=1, source_target_pairs={{0,16},{24,8},{1,17},{25,9},{2,18},{26,10},{3,19},{27,11},{4,20},{... | collective-permute-start | bytes 3096584 | tf_op jit(solution)/shard_map/ppermute | solution.py:582
  13.2 1.7 collective-permute-start.13
  15.0 4.9 %blend.3 = (f32[288,896]{1,0:T(8,128)}, f32[288,896]{1,0:T(8,128)}, f32[288,896]{1,0:T(8,128)}, f32[288,896]{1,0:T(8,128)}, f32[8,128]{1,0:T(8,128)}) custom-call(s32[4]{0:T(128)S(1)} %copy-done.6, s32[4]{0:T(128)S(1)} %copy-done.8, s32[4,4]{1,0:T(4,128)S(1)} %copy-done.4, s32[4,4]{1,0:T(4,128)S(1)} %copy-done.5, f32[4,288,896]{2,1,0:T(8,128)} %momentum.1, ...), custom_call_target="tpu_custom_call" | custom-call | tf_op jit(solution)/shard_map/blend/pallas_call | solution.py:420
  19.9 1.7 collective-permute-start.10
  21.6 3.7 %collective-permute-start.8 = (f32[288,896]{1,0:T(8,128)}, f32[288,896]{1,0:T(8,128)}, u32[]{:S(2)}, u32[]{:S(2)}) collective-permute-start(f32[288,896]{1,0:T(8,128)} %get-tuple-element.88), channel_id=1, source_target_pairs={{0,8},{24,16},{1,9},{25,17},{2,10},{26,18},{3,11},{27,19},{4,12},{... | collective-permute-start | bytes 3096584 | tf_op jit(solution)/shard_map/ppermute | solution.py:582
  25.2 9.1 %collective-permute-done.11.refs_5_ = f32[288,896]{1,0:T(8,128)S(1)} collective-permute-done((f32[288,896]{1,0:T(8,128)}, f32[288,896]{1,0:T(8,128)S(1)}, u32[]{:S(2)}, u32[]{:S(2)}) %collective-permute-start.11) | collective-permute-done | bytes 1032224 | tf_op jit(solution)/shard_map/ppermute | solution.py:582
  34.3 6.3 %collective-permute-start.9 = (f32[288,896]{1,0:T(8,128)}, f32[288,896]{1,0:T(8,128)}, u32[]{:S(2)}, u32[]{:S(2)}) collective-permute-start(f32[288,896]{1,0:T(8,128)} %get-tuple-element.89), channel_id=1, source_target_pairs={{0,16},{24,8},{1,17},{25,9},{2,18},{26,10},{3,19},{27,11},{4,20},{... | collective-permute-start | bytes 3096584 | tf_op jit(solution)/shard_map/ppermute | solution.py:582
  40.6 15.9 %collective-permute-done.12.refs_6_ = f32[288,896]{1,0:T(8,128)S(1)} collective-permute-done((f32[288,896]{1,0:T(8,128)}, f32[288,896]{1,0:T(8,128)S(1)}, u32[]{:S(2)}, u32[]{:S(2)}) %collective-permute-start.12) | collective-permute-done | bytes 1032224 | tf_op jit(solution)/shard_map/ppermute | solution.py:582
  57.4 1.3 collective-permute-start.20
  59.0 1.4 collective-permute-start.19
  60.4 1.3 collective-permute-start.17
  61.7 16.9 %collective-permute-done.8 = f32[288,896]{1,0:T(8,128)} collective-permute-done((f32[288,896]{1,0:T(8,128)}, f32[288,896]{1,0:T(8,128)}, u32[]{:S(2)}, u32[]{:S(2)}) %collective-permute-start.8) | collective-permute-done | bytes 1032224 | tf_op jit(solution)/shard_map/ppermute | solution.py:582
  78.6 1.6 collective-permute-start.18
  80.2 19.4 %collective-permute-done.9 = f32[288,896]{1,0:T(8,128)} collective-permute-done((f32[288,896]{1,0:T(8,128)}, f32[288,896]{1,0:T(8,128)}, u32[]{:S(2)}, u32[]{:S(2)}) %collective-permute-start.9) | collective-permute-done | bytes 1032224 | tf_op jit(solution)/shard_map/ppermute | solution.py:582
  100.9 75.5 %collective-permute-done.19.refs_4_ = f32[576,384]{1,0:T(8,128)} collective-permute-done((f32[576,384]{1,0:T(8,128)}, f32[576,384]{1,0:T(8,128)}, u32[]{:S(2)}, u32[]{:S(2)}) %collective-permute-start.19) | collective-permute-done | bytes 884768 | tf_op jit(solution)/shard_map/ppermute | solution.py:585
  177.7 1.7 collective-permute-start.14
  179.4 5.9 %fresh_momentum.1 = (f32[4,288,896]{2,1,0:T(8,128)}, f32[8,128]{1,0:T(8,128)}) custom-call(s32[4]{0:T(128)} %refs_1_.7, s32[4,4]{1,0:T(4,128)} %refs_2_.7, f32[4,288,896]{2,1,0:T(8,128)} %momentum.1, f32[4,288,896]{2,1,0:T(8,128)} %gradient.1, f32[8,128]{1,0:T(8,128)} %get-tuple-element.85._), custom_call_target="tpu_custom_call" | custom-call | tf_op jit(solution)/shard_map/fresh_momentum/pallas_call | solution.py:437
  186.0 6.7 %finish.1 = (f32[576,896]{1,0:T(8,128)}, f32[4,288,896]{2,1,0:T(8,128)}) custom-call(s32[4]{0:T(128)} %refs_0_.15, s32[4]{0:T(128)} %refs_1_.7, s32[4,4]{1,0:T(4,128)} %refs_2_.7, s32[4,4]{1,0:T(4,128)} %refs_3_.7, f32[576,384]{1,0:T(8,128)} %collective-permute-done.19.refs_4_, f32[576,896]{1,0:T(8,128)S(1)} %collective-permute-done.20.refs_5_, ...), custom_call_target="tpu_custom_call" | custom-call | tf_op jit(solution)/shard_map/finish/pallas_call | solution.py:522
  192.7 3.1 %place_blocks.4.refs_2_ = f32[4,288,896]{2,1,0:T(8,128)} custom-call(s32[4]{0:T(128)S(1)} %copy-done.7, f32[288,896]{1,0:T(8,128)} %collective-permute-done.17.refs_1_, f32[288,896]{1,0:T(8,128)} %collective-permute-done.18.refs_2_, f32[4,288,896]{2,1,0:T(8,128)} %get-tuple-element.109.refs_3_), custom_call_target="tpu_custom_call", output_to_operand_aliasing={{}: (3, {})} | custom-call | tf_op jit(solution)/shard_map/place_blocks/pallas_call | solution.py:544
  195.8 1.5 place_blocks.5.refs_2_
  197.9 2.7 %place_blocks.6.refs_2_ = f32[4,288,896]{2,1,0:T(8,128)} custom-call(s32[4]{0:T(128)S(1)} %copy-done.7, f32[288,896]{1,0:T(8,128)} %collective-permute-done.15.refs_1_, f32[4,288,896]{2,1,0:T(8,128)} %place_blocks.5.refs_2_), custom_call_target="tpu_custom_call", output_to_operand_aliasing={{}: (2, {})} | custom-call | tf_op jit(solution)/shard_map/place_blocks/pallas_call | solution.py:544
  200.6 1.8 place_blocks.7
  (34 shorter events, 5.0 us)
Async XLA Ops:
  0.6 14.3 %copy-start.8 = (s32[4]{0:T(128)S(1)}, s32[4]{0:T(128)}, u32[]{:S(2)}) copy-start(s32[4]{0:T(128)} %refs_1_.7) | copy-start | bytes 52
  0.6 14.3 %copy-start.6 = (s32[4]{0:T(128)S(1)}, s32[4]{0:T(128)}, u32[]{:S(2)}) copy-start(s32[4]{0:T(128)} %refs_0_.15) | copy-start | bytes 52
  0.7 14.3 %copy-start.4 = (s32[4,4]{1,0:T(4,128)S(1)}, s32[4,4]{1,0:T(4,128)}, u32[]{:S(2)}) copy-start(s32[4,4]{1,0:T(4,128)} %refs_2_.7) | copy-start | bytes 196
  0.7 14.3 %copy-start.5 = (s32[4,4]{1,0:T(4,128)S(1)}, s32[4,4]{1,0:T(4,128)}, u32[]{:S(2)}) copy-start(s32[4,4]{1,0:T(4,128)} %refs_3_.7) | copy-start | bytes 196
  5.8 28.5 %collective-permute-start.11 = (f32[288,896]{1,0:T(8,128)}, f32[288,896]{1,0:T(8,128)S(1)}, u32[]{:S(2)}, u32[]{:S(2)}) collective-permute-start(f32[288,896]{1,0:T(8,128)} %get-tuple-element.92), channel_id=1, source_target_pairs={{0,8},{24,16},{1,9},{25,17},{2,10},{26,18},{3,11},{27,19},{4,12},{... | collective-permute-start | bytes 3096584 | tf_op jit(solution)/shard_map/ppermute | solution.py:582
  10.9 45.6 %collective-permute-start.12 = (f32[288,896]{1,0:T(8,128)}, f32[288,896]{1,0:T(8,128)S(1)}, u32[]{:S(2)}, u32[]{:S(2)}) collective-permute-start(f32[288,896]{1,0:T(8,128)} %get-tuple-element.93), channel_id=1, source_target_pairs={{0,16},{24,8},{1,17},{25,9},{2,18},{26,10},{3,19},{27,11},{4,20},{... | collective-permute-start | bytes 3096584 | tf_op jit(solution)/shard_map/ppermute | solution.py:582
  13.2 43.3 %collective-permute-start.13 = (f32[288,896]{1,0:T(8,128)}, f32[288,896]{1,0:T(8,128)}, u32[]{:S(2)}, u32[]{:S(2)}) collective-permute-start(f32[288,896]{1,0:T(8,128)} %get-tuple-element.94), channel_id=1, source_target_pairs={{8,16},{16,8},{9,17},{17,9},{10,18},{18,10},{11,19},{19,11},{12,20... | collective-permute-start | bytes 3096584 | tf_op jit(solution)/shard_map/ppermute | solution.py:582
  14.9 41.5 %copy-start = (f32[288,896]{1,0:T(8,128)S(1)}, f32[288,896]{1,0:T(8,128)}, u32[]{:S(2)}) copy-start(f32[288,896]{1,0:T(8,128)} %get-tuple-element.91.refs_4_) | copy-start | bytes 3096580
  19.9 40.5 %collective-permute-start.10 = (f32[288,896]{1,0:T(8,128)}, f32[288,896]{1,0:T(8,128)}, u32[]{:S(2)}, u32[]{:S(2)}) collective-permute-start(f32[288,896]{1,0:T(8,128)} %get-tuple-element.90), channel_id=1, source_target_pairs={{8,16},{16,8},{9,17},{17,9},{10,18},{18,10},{11,19},{19,11},{12,20... | collective-permute-start | bytes 3096584 | tf_op jit(solution)/shard_map/ppermute | solution.py:582
  21.6 57.0 %collective-permute-start.8 = (f32[288,896]{1,0:T(8,128)}, f32[288,896]{1,0:T(8,128)}, u32[]{:S(2)}, u32[]{:S(2)}) collective-permute-start(f32[288,896]{1,0:T(8,128)} %get-tuple-element.88), channel_id=1, source_target_pairs={{0,8},{24,16},{1,9},{25,17},{2,10},{26,18},{3,11},{27,19},{4,12},{... | collective-permute-start | bytes 3096584 | tf_op jit(solution)/shard_map/ppermute | solution.py:582
  34.3 65.3 %collective-permute-start.9 = (f32[288,896]{1,0:T(8,128)}, f32[288,896]{1,0:T(8,128)}, u32[]{:S(2)}, u32[]{:S(2)}) collective-permute-start(f32[288,896]{1,0:T(8,128)} %get-tuple-element.89), channel_id=1, source_target_pairs={{0,16},{24,8},{1,17},{25,9},{2,18},{26,10},{3,19},{27,11},{4,20},{... | collective-permute-start | bytes 3096584 | tf_op jit(solution)/shard_map/ppermute | solution.py:582
  57.4 120.3 %collective-permute-start.20 = (f32[576,896]{1,0:T(8,128)}, f32[576,896]{1,0:T(8,128)S(1)}, u32[]{:S(2)}, u32[]{:S(2)}) collective-permute-start(f32[576,896]{1,0:T(8,128)} %get-tuple-element.104), channel_id=1, source_target_pairs={{8,0},{16,24},{9,1},{17,25},{10,2},{18,26},{11,3},{19,27},{12,4},{... | collective-permute-start | bytes 6193160 | tf_op jit(solution)/shard_map/ppermute | solution.py:585
  58.7 40.9 %copy-start.2 = (f32[288,896]{1,0:T(8,128)S(1)}, f32[288,896]{1,0:T(8,128)}, u32[]{:S(2)}) copy-start(f32[288,896]{1,0:T(8,128)} %get-tuple-element.87) | copy-start | bytes 3096580
  59.0 117.5 %collective-permute-start.19 = (f32[576,384]{1,0:T(8,128)}, f32[576,384]{1,0:T(8,128)}, u32[]{:S(2)}, u32[]{:S(2)}) collective-permute-start(f32[576,384]{1,0:T(8,128)} %get-tuple-element.98), channel_id=1, source_target_pairs={{8,0},{16,24},{9,1},{17,25},{10,2},{18,26},{11,3},{19,27},{12,4},{... | collective-permute-start | bytes 2654216 | tf_op jit(solution)/shard_map/ppermute | solution.py:585
  60.4 132.3 %collective-permute-start.17 = (f32[288,896]{1,0:T(8,128)}, f32[288,896]{1,0:T(8,128)}, u32[]{:S(2)}, u32[]{:S(2)}) collective-permute-start(f32[288,896]{1,0:T(8,128)} %get-tuple-element.102), channel_id=1, source_target_pairs={{8,24},{16,0},{9,25},{17,1},{10,26},{18,2},{11,27},{19,3},{12,28},... | collective-permute-start | bytes 3096584 | tf_op jit(solution)/shard_map/ppermute | solution.py:585
  78.6 114.1 %collective-permute-start.18 = (f32[288,896]{1,0:T(8,128)}, f32[288,896]{1,0:T(8,128)}, u32[]{:S(2)}, u32[]{:S(2)}) collective-permute-start(f32[288,896]{1,0:T(8,128)} %get-tuple-element.103), channel_id=1, source_target_pairs={{8,16},{16,8},{9,17},{17,9},{10,18},{18,10},{11,19},{19,11},{12,20... | collective-permute-start | bytes 3096584 | tf_op jit(solution)/shard_map/ppermute | solution.py:585
  99.6 96.2 %collective-permute-start.16 = (f32[288,896]{1,0:T(8,128)}, f32[288,896]{1,0:T(8,128)S(1)}, u32[]{:S(2)}, u32[]{:S(2)}) collective-permute-start(f32[288,896]{1,0:T(8,128)} %get-tuple-element.101), channel_id=1, source_target_pairs={{8,24},{16,0},{9,25},{17,1},{10,26},{18,2},{11,27},{19,3},{12,28},... | collective-permute-start | bytes 3096584 | tf_op jit(solution)/shard_map/ppermute | solution.py:585
  176.4 21.4 %collective-permute-start.15 = (f32[288,896]{1,0:T(8,128)}, f32[288,896]{1,0:T(8,128)}, u32[]{:S(2)}, u32[]{:S(2)}) collective-permute-start(f32[288,896]{1,0:T(8,128)} %get-tuple-element.100), channel_id=1, source_target_pairs={{8,0},{16,24},{9,1},{17,25},{10,2},{18,26},{11,3},{19,27},{12,4},{... | collective-permute-start | bytes 3096584 | tf_op jit(solution)/shard_map/ppermute | solution.py:585
  177.7 22.9 %collective-permute-start.14 = (f32[288,896]{1,0:T(8,128)}, f32[288,896]{1,0:T(8,128)}, u32[]{:S(2)}, u32[]{:S(2)}) collective-permute-start(f32[288,896]{1,0:T(8,128)} %get-tuple-element.99), channel_id=1, source_target_pairs={{8,16},{16,8},{9,17},{17,9},{10,18},{18,10},{11,19},{19,11},{12,20... | collective-permute-start | bytes 3096584 | tf_op jit(solution)/shard_map/ppermute | solution.py:585
  179.4 5.9 %copy-start.3 = (f32[288,896]{1,0:T(8,128)S(1)}, f32[288,896]{1,0:T(8,128)}, u32[]{:S(2)}) copy-start(f32[288,896]{1,0:T(8,128)} %get-tuple-element.107.refs_8_) | copy-start | bytes 3096580
  185.3 7.5 %copy-start.7 = (s32[4]{0:T(128)S(1)}, s32[4]{0:T(128)}, u32[]{:S(2)}) copy-start(s32[4]{0:T(128)} %refs_0_.15) | copy-start | bytes 52
  185.3 0.7 copy-start.1

commit v10 on v9

--- a/solution.py
+++ b/solution.py
@@ -121,18 +121,25 @@
     slots, columns = outs[0].shape
     size = slots // chunks
     jobs = []
-    for step in [*range(1, ranks), 0]:
+    for step in range(1, ranks + 1):
+        step = step % ranks
+        if first and step == 0:
+            continue
         target = rank ^ step
+        wanted = is_inner(target, ranks)
         matrix = matrix_of(owner_group, target ^ mate(ranks) if first else target)
+        if first and step == mate(ranks):
+            matrix = matrix_of(owner_group, jnp.where(wanted, rank, target))
+            wanted = rank >= 0
         count = row_counts[matrix, rank] * live_ranks[rank]
         for chunk in range(chunks):
             part = pl.ds(chunk * size, size)
             flags = arrive.at[step, chunk, 0], arrive.at[step, chunk, 1]
             incoming = (
-                (is_inner(target, ranks), momentum.at[matrix, part], olds.at[step, part], flags[0]),
-                (is_inner(target, ranks), gradient.at[matrix, part], grads.at[step, part], flags[1]),
+                (wanted, momentum.at[matrix, part], olds.at[step, part], flags[0]),
+                (wanted, gradient.at[matrix, part], grads.at[step, part], flags[1]),
             )
-            outgoing = (is_inner(target, ranks), olds.at[step, part], outs[step].at[part], leave.at[step, chunk])
+            outgoing = (wanted, olds.at[step, part], outs[step].at[part], leave.at[step, chunk])
             jobs.append((step, chunk, count, incoming, outgoing))
             each_copy(incoming, "start")
     token[...] = jnp.zeros_like(token)
@@ -160,38 +167,53 @@
     out[...] = jnp.where(keep, MOMENTUM_RATE * momentum[...] + gradient[...], 0.0)
 
 
+def assemble(blocks, landed, padded, arrive, tables, held, first):
+    ranks, slots, columns = landed.shape
+    copies = []
+    for step in range(ranks):
+        copies.append(pltpu.make_async_copy(blocks[step], landed.at[step], arrive.at[step]))
+        copies[-1].start()
+    owner_group, _, _, row_offsets = fetch_tables(tables, held)
+    rank = lax.axis_index("fsdp")
+    base = jnp.where(is_inner(rank, ranks), rank, rank ^ mate(ranks))
+    matrix = matrix_of(owner_group, base ^ mate(ranks) if first else base)
+    padded[...] = jnp.zeros_like(padded)
+    sublane = lax.broadcasted_iota(jnp.int32, (SUBLANES, columns), 0)
+    for step in range(ranks):
+        start = row_offsets[matrix, base ^ step]
+        shift = start % SUBLANES
+        origin = start - shift
+        copies[step].wait()
+
+        def tile(index, before, origin=origin, shift=shift, step=step):
+            moved = pltpu.roll(landed[step, pl.ds(pl.multiple_of(index * SUBLANES, SUBLANES), SUBLANES), :], shift, 0)
+            rows = pl.ds(pl.multiple_of(origin + index * SUBLANES, SUBLANES), SUBLANES)
+            padded[rows, :] = padded[rows, :] + jnp.where(sublane < shift, before, moved)
+            return moved
+
+        after = over_tiles(slots // SUBLANES, tile, jnp.zeros((SUBLANES, columns), jnp.float32))
+        rows = pl.ds(pl.multiple_of(origin + slots, SUBLANES), SUBLANES)
+        padded[rows, :] = padded[rows, :] + jnp.where(sublane < shift, after, 0.0)
+
+
+def outer_kernel(ranks, *refs):
+    landed, padded, arrive, leave = refs[-9:-5]
+
+    @pl.when(jnp.logical_not(is_inner(lax.axis_index("fsdp"), ranks)))
+    def _():
+        assemble(refs[4 : 4 + ranks], landed, padded, arrive, refs[:4], refs[-5:], True)
+        copy = pltpu.make_async_copy(padded.at[pl.ds(0, INNER)], refs[4 + ranks], leave.at[0])
+        copy.start()
+        copy.wait()
+
+
 def gram_kernel(first, ranks, *refs):
-    tables, blocks, refs = refs[:4], refs[4 : 4 + ranks], refs[(4 if first else 5) + ranks :]
-    pair, keep, send = refs[:3]
+    pair, keep, send = refs[-15:-12]
     landed, padded, high_held, low_held, gram, arrive, leave = refs[-12:-5]
-    slots, columns = blocks[0].shape
-    rank = lax.axis_index("fsdp")
-
-    @pl.when(is_inner(rank, ranks))
+
+    @pl.when(is_inner(lax.axis_index("fsdp"), ranks))
     def _():
-        copies = []
-        for step in range(ranks):
-            copies.append(pltpu.make_async_copy(blocks[step], landed.at[step], arrive.at[step]))
-            copies[-1].start()
-        owner_group, _, _, row_offsets = fetch_tables(tables, refs[-5:])
-        matrix = matrix_of(owner_group, rank ^ mate(ranks) if first else rank)
-        padded[...] = jnp.zeros_like(padded)
-        sublane = lax.broadcasted_iota(jnp.int32, (SUBLANES, columns), 0)
-        for step in range(ranks):
-            start = row_offsets[matrix, rank ^ step]
-            shift = start % SUBLANES
-            base = start - shift
-            copies[step].wait()
-
-            def tile(index, before, base=base, shift=shift, step=step):
-                moved = pltpu.roll(landed[step, pl.ds(pl.multiple_of(index * SUBLANES, SUBLANES), SUBLANES), :], shift, 0)
-                rows = pl.ds(pl.multiple_of(base + index * SUBLANES, SUBLANES), SUBLANES)
-                padded[rows, :] = padded[rows, :] + jnp.where(sublane < shift, before, moved)
-                return moved
-
-            after = over_tiles(slots // SUBLANES, tile, jnp.zeros((SUBLANES, columns), jnp.float32))
-            rows = pl.ds(pl.multiple_of(base + slots, SUBLANES), SUBLANES)
-            padded[rows, :] = padded[rows, :] + jnp.where(sublane < shift, after, 0.0)
+        assemble(refs[4 : 4 + ranks], landed, padded, arrive, refs[:4], refs[-5:], first)
         high, low = halves(padded[:INNER, :])
         high_held[...] = high
         low_held[...] = low
@@ -199,8 +221,6 @@
             pltpu.make_async_copy(high_held, pair.at[0], leave.at[0]),
             pltpu.make_async_copy(low_held, pair.at[1], leave.at[1]),
         ]
-        if first:
-            outgoing.append(pltpu.make_async_copy(padded.at[pl.ds(0, INNER)], refs[3], leave.at[2]))
         for copy in outgoing:
             copy.start()
         left = jnp.concatenate([high, low, high], axis=1)
@@ -452,9 +472,9 @@
     pair = jax.ShapeDtypeStruct((4, INNER, columns), jnp.bfloat16)
     return pl.pallas_call(
         functools.partial(gram_kernel, first, ranks),
-        out_shape=[pair] + [floats(INNER // 2, 2 * PANEL)] * 2 + [floats(INNER, columns)] * first,
+        out_shape=[pair] + [floats(INNER // 2, 2 * PANEL)] * 2,
         in_specs=[HBM] * 4 + [ANY] * (ranks + len(after)),
-        out_specs=[ANY, VMEM, VMEM] + [ANY] * first,
+        out_specs=[ANY, VMEM, VMEM],
         scratch_shapes=[
             vmem(ranks, slots, columns),
             vmem(INNER + slots + SUBLANES, columns),
@@ -462,13 +482,34 @@
             vmem(INNER, columns, dtype=jnp.bfloat16),
             vmem(INNER, 2 * PANEL),
             flags(ranks),
-            flags(3),
+            flags(2),
         ]
         + table_scratch(*tables[2].shape),
         compiler_params=PARAMS,
         cost_estimate=FREE,
         name="assemble_and_gram",
     )(*tables, *blocks, *after)
+
+
+def assemble_outer(tables, blocks):
+    slots, columns = blocks[0].shape
+    ranks = len(blocks)
+    return pl.pallas_call(
+        functools.partial(outer_kernel, ranks),
+        out_shape=floats(INNER, columns),
+        in_specs=[HBM] * 4 + [ANY] * ranks,
+        out_specs=ANY,
+        scratch_shapes=[
+            vmem(ranks, slots, columns),
+            vmem(INNER + slots + SUBLANES, columns),
+            flags(ranks),
+            flags(1),
+        ]
+        + table_scratch(*tables[2].shape),
+        compiler_params=PARAMS,
+        cost_estimate=FREE,
+        name="assemble_outer",
+    )(*tables, *blocks)
 
 
 def update_shapes(first, steps, slots, columns):
@@ -505,15 +546,15 @@
     )(*tables, keep, away, pair, *after)
 
 
-def settle(value):
+def touch(value, flops=0):
     return pl.pallas_call(
         idle_kernel,
         out_shape=floats(SUBLANES, 128),
         in_specs=[ANY],
         out_specs=ANY,
         compiler_params=SMALL,
-        cost_estimate=pl.CostEstimate(flops=10**11, bytes_accessed=0, transcendentals=0),
-        name="settle",
+        cost_estimate=pl.CostEstimate(flops=flops, bytes_accessed=0, transcendentals=0),
+        name="touch",
     )(value)
 
 
@@ -584,14 +625,22 @@
     def from_inner(block, step):
         return lax.ppermute(block, "fsdp", pairs(step, False))
 
+    near = mate(ranks)
+    far = [step for step in last if step != near]
     *blends, token = blend(True, tables, momentum, gradient, [])
-    first_blocks = [blends[0]] + [to_inner(blends[step], step) for step in range(1, ranks)]
-    *blends, token = blend(False, tables, momentum, gradient, [token])
+    own = blends[near]
+    swapped = lax.ppermute(own, "fsdp", [(i, i ^ near) for i in range(ranks)])
+    arrived = {step: to_inner(blends[step], step) for step in far}
+    *blends, token = blend(False, tables, momentum, gradient, [token, touch(swapped)])
     last_blocks = [blends[0]] + [to_inner(blends[step], step) for step in range(1, ranks)]
     new_momentum, token = fresh_momentum(tables, momentum, gradient, token)
-
-    pair, keep, send, iterate = assemble_and_gram(True, tables, first_blocks)
-    iterate = from_inner(iterate, mate(ranks))
+    handed = {step: from_inner(arrived[step], near) for step in far}
+
+    def ordered(base, opposite, others):
+        return [{0: base, near: opposite, **others}[step] for step in range(ranks)]
+
+    first_blocks = ordered(own, swapped, arrived)
+    pair, keep, send = assemble_and_gram(True, tables, first_blocks, *[handed[step] for step in far[1:]])
 
     def first_update(pair, keep, send, after):
         return apply_update(True, [0, *early], tables, *sum_halves(keep, send, "tensor"), pair, slots, after)
@@ -599,8 +648,9 @@
     def first_skip(*_):
         return nothing(update_shapes(True, [0, *early], slots, columns))
 
-    packed, own_first, *homes = lax.cond(inner, first_update, first_skip, pair, keep, send, settle(keep))
-    packed_there = from_inner(packed, mate(ranks))
+    packed, own_first, *homes = lax.cond(inner, first_update, first_skip, pair, keep, send, touch(keep, 10**11))
+    packed_there = from_inner(packed, near)
+    iterate = assemble_outer(tables, ordered(swapped, own, handed))
     first_home = [from_inner(block, step) for step, block in zip(early, homes)]
 
     def last_update(after, *blocks):
@@ -610,7 +660,7 @@
     def last_skip(*_):
         return nothing(update_shapes(False, [0, *last], slots, columns))
 
-    result, own_last, *homes = lax.cond(inner, last_update, last_skip, packed, *last_blocks)
+    result, own_last, *homes = lax.cond(inner, last_update, last_skip, iterate, *last_blocks)
     last_home = [from_inner(block, step) for step, block in zip(last, homes)]
 
     result, shards = finish(tables, packed_there, iterate, result, own_first, own_last, momentum.shape, token)

time: 204 us -> 198 us (0.971)
  waiting for transfers between devices: 137 us -> 132 us
    ppermute x6 -> x5, waiting for transfers between devices: 61.3 us -> 19.8 us  [to_inner(): return lax.ppermute(block, 'fsdp', pairs(step, True))]
    ppermute x0 -> x1, waiting for transfers between devices: none -> 18.6 us  [on_device(): swapped = lax.ppermute(own, 'fsdp', [(i, i ^ near) for i in range(ranks)])]
    ppermute x7 -> x8, waiting for transfers between devices: 76.1 us -> 93.5 us  [from_inner(): return lax.ppermute(block, 'fsdp', pairs(step, False))]
    ppermute x6 -> x5, starting transfers between devices: 20.7 us -> 14.5 us  [to_inner(): return lax.ppermute(block, 'fsdp', pairs(step, True))]
    ppermute x0 -> x1, starting transfers between devices: none -> 4.93 us  [on_device(): swapped = lax.ppermute(own, 'fsdp', [(i, i ^ near) for i in range(ranks)])]
    pallas_call x1 -> x3, Pallas kernels: 0.01 us -> 4.24 us  [the longest x1 4.24 us: assemble_outer(): pl.pallas_call(functools.partial(outer_kernel, ranks), out_shape=floats(I...]
    pallas_call x4, Pallas kernels: 9.12 us -> 6.37 us  [place_blocks(): pl.pallas_call(functools.partial(place_kernel, first, ranks, steps), out_...]
    ppermute x7 -> x8, starting transfers between devices: 9.82 us -> 9.15 us  [from_inner(): return lax.ppermute(block, 'fsdp', pairs(step, False))]
  transfers between devices with their start and end apart: 13 -> 14, of which waited for: 6 -> 7; matrix products, arithmetic and copies ran while one was open for 0% -> 0% of each run, Pallas kernels for 13% -> 14%
where the time goes in v10:
time: 198 us; the launch traced here: 197 us
  waiting for transfers between devices  132 us (67%)
  Pallas kernels  34.3 us (17%)
  starting transfers between devices  28.6 us (14%)
    ppermute x8, waiting for transfers between devices, from_inner(): return lax.ppermute(block, 'fsdp', pairs(step, False))  93.5 us
    ppermute x5, waiting for transfers between devices, to_inner(): return lax.ppermute(block, 'fsdp', pairs(step, True))  19.8 us
    ppermute x1, waiting for transfers between devices, on_device(): swapped = lax.ppermute(own, 'fsdp', [(i, i ^ near) for i in range(ranks)])  18.6 us
    ppermute x5, starting transfers between devices, to_inner(): return lax.ppermute(block, 'fsdp', pairs(step, True))  14.5 us
    pallas_call x2, Pallas kernels, blend(): pl.pallas_call(functools.partial(blend_kernel, first, chunks), out_shape=...  10.1 us
    ppermute x8, starting transfers between devices, from_inner(): return lax.ppermute(block, 'fsdp', pairs(step, False))  9.15 us
    pallas_call x1, Pallas kernels, finish(): pl.pallas_call(functools.partial(finish_kernel, tables[1].shape[0]), out_...  6.92 us
    pallas_call x4, Pallas kernels, place_blocks(): pl.pallas_call(functools.partial(place_kernel, first, ranks, steps), out_...  6.37 us
  transfers between devices with their start and end apart: 14, of which 7 were waited for; matrix products, arithmetic and copies ran while one was open for 0% of the time, Pallas kernels for 14%

profile of v10, /device:TPU:0, one launch (start us, length us, event | category | flops | bytes accessed | tf_op | source)
XLA Modules:
  0.0 197.4 jit_solution(14733995521367637652)
XLA Ops:
  0.7 5.2 %blend.2 = (f32[288,896]{1,0:T(8,128)}, f32[288,896]{1,0:T(8,128)}, f32[288,896]{1,0:T(8,128)}, f32[288,896]{1,0:T(8,128)}, f32[8,128]{1,0:T(8,128)}) custom-call(s32[4]{0:T(128)} %refs_0_.17, s32[4]{0:T(128)} %refs_1_.9, s32[4,4]{1,0:T(4,128)} %refs_2_.9, s32[4,4]{1,0:T(4,128)} %refs_3_.9, f32[4,288,896]{2,1,0:T(8,128)} %momentum.1, f32[4,288,896]{2,1,0:T(8,128)} %gradient.1), custom_call_target="tpu_custom_call" | custom-call | tf_op jit(solution)/shard_map/blend/pallas_call | solution.py:440
  5.8 1.7 collective-permute-start.14
  7.5 4.9 %collective-permute-start.8 = (f32[288,896]{1,0:T(8,128)}, f32[288,896]{1,0:T(8,128)S(1)}, u32[]{:S(2)}, u32[]{:S(2)}) collective-permute-start(f32[288,896]{1,0:T(8,128)} %get-tuple-element.83.refs_5_.refs_4_), channel_id=1, source_target_pairs={{0,8},{8,0},{16,24},{24,16},{1,9},{9,1},{17,25},{25,17},{2,10},{10... | collective-permute-start | bytes 3096584 | tf_op jit(solution)/shard_map/ppermute | solution.py:632
  12.4 3.7 %collective-permute-start.12 = (f32[288,896]{1,0:T(8,128)}, f32[288,896]{1,0:T(8,128)}, u32[]{:S(2)}, u32[]{:S(2)}) collective-permute-start(f32[288,896]{1,0:T(8,128)} %get-tuple-element.90), channel_id=1, source_target_pairs={{0,16},{24,8},{1,17},{25,9},{2,18},{26,10},{3,19},{27,11},{4,20},{... | collective-permute-start | bytes 3096584 | tf_op jit(solution)/shard_map/ppermute | solution.py:623
  16.1 1.3 collective-permute-start.15
  17.4 18.6 %collective-permute-done.8.refs_0_.refs_4_.refs_5_ = f32[288,896]{1,0:T(8,128)S(1)} collective-permute-done((f32[288,896]{1,0:T(8,128)}, f32[288,896]{1,0:T(8,128)S(1)}, u32[]{:S(2)}, u32[]{:S(2)}) %collective-permute-start.8) | collective-permute-done | bytes 1032224 | tf_op jit(solution)/shard_map/ppermute | solution.py:632
  36.6 4.9 %blend.3 = (f32[288,896]{1,0:T(8,128)}, f32[288,896]{1,0:T(8,128)}, f32[288,896]{1,0:T(8,128)}, f32[288,896]{1,0:T(8,128)}, f32[8,128]{1,0:T(8,128)}) custom-call(s32[4]{0:T(128)S(1)} %copy-done.7, s32[4]{0:T(128)S(1)} %copy-done.10, s32[4,4]{1,0:T(4,128)S(1)} %copy-done.3, s32[4,4]{1,0:T(4,128)S(1)} %copy-done.5, f32[4,288,896]{2,1,0:T(8,128)} %momentum.1, ...), custom_call_target="tpu_custom_call" | custom-call | tf_op jit(solution)/shard_map/blend/pallas_call | solution.py:440
  41.5 5.3 %collective-permute-start.9 = (f32[288,896]{1,0:T(8,128)}, f32[288,896]{1,0:T(8,128)}, u32[]{:S(2)}, u32[]{:S(2)}) collective-permute-start(f32[288,896]{1,0:T(8,128)} %get-tuple-element.87), channel_id=1, source_target_pairs={{0,8},{24,16},{1,9},{25,17},{2,10},{26,18},{3,11},{27,19},{4,12},{... | collective-permute-start | bytes 3096584 | tf_op jit(solution)/shard_map/ppermute | solution.py:623
  46.8 2.3 %collective-permute-start.10 = (f32[288,896]{1,0:T(8,128)}, f32[288,896]{1,0:T(8,128)}, u32[]{:S(2)}, u32[]{:S(2)}) collective-permute-start(f32[288,896]{1,0:T(8,128)} %get-tuple-element.88), channel_id=1, source_target_pairs={{0,16},{24,8},{1,17},{25,9},{2,18},{26,10},{3,19},{27,11},{4,20},{... | collective-permute-start | bytes 3096584 | tf_op jit(solution)/shard_map/ppermute | solution.py:623
  49.1 1.6 collective-permute-start.11
  50.7 7.4 %collective-permute-done.12.refs_6_ = f32[288,896]{1,0:T(8,128)} collective-permute-done((f32[288,896]{1,0:T(8,128)}, f32[288,896]{1,0:T(8,128)}, u32[]{:S(2)}, u32[]{:S(2)}) %collective-permute-start.12) | collective-permute-done | bytes 1032224 | tf_op jit(solution)/shard_map/ppermute | solution.py:623
  60.6 1.3 collective-permute-start.21
  61.9 20.3 %collective-permute-done.13.refs_6_ = f32[288,896]{1,0:T(8,128)} collective-permute-done((f32[288,896]{1,0:T(8,128)}, f32[288,896]{1,0:T(8,128)}, u32[]{:S(2)}, u32[]{:S(2)}) %collective-permute-start.13) | collective-permute-done | bytes 1032224 | tf_op jit(solution)/shard_map/ppermute | solution.py:626
  83.5 4.2 %assemble_outer.1.refs_5_ = f32[576,896]{1,0:T(8,128)} custom-call(s32[4]{0:T(128)S(1)} %copy-done.7, s32[4]{0:T(128)S(1)} %copy-done.10, s32[4,4]{1,0:T(4,128)S(1)} %copy-done.3, s32[4,4]{1,0:T(4,128)S(1)} %copy-done.5, f32[288,896]{1,0:T(8,128)S(1)} %collective-permute-done.8.refs_0_.refs_4_.refs_5_, f32[288,896]{1,0:T(8,128)S(1)} %copy-done, ...), custom_call_target="tpu_custom_call" | custom-call | tf_op jit(solution)/shard_map/assemble_outer/pallas_call | solution.py:497
  88.5 12.4 %collective-permute-done.10 = f32[288,896]{1,0:T(8,128)} collective-permute-done((f32[288,896]{1,0:T(8,128)}, f32[288,896]{1,0:T(8,128)}, u32[]{:S(2)}, u32[]{:S(2)}) %collective-permute-start.10) | collective-permute-done | bytes 1032224 | tf_op jit(solution)/shard_map/ppermute | solution.py:623
  102.2 1.3 collective-permute-start.17
  103.5 40.9 %collective-permute-done.21.refs_4_ = f32[576,384]{1,0:T(8,128)} collective-permute-done((f32[576,384]{1,0:T(8,128)}, f32[576,384]{1,0:T(8,128)}, u32[]{:S(2)}, u32[]{:S(2)}) %collective-permute-start.21) | collective-permute-done | bytes 884768 | tf_op jit(solution)/shard_map/ppermute | solution.py:626
  145.1 5.8 %fresh_momentum.1 = (f32[4,288,896]{2,1,0:T(8,128)}, f32[8,128]{1,0:T(8,128)}) custom-call(s32[4]{0:T(128)} %refs_1_.9, s32[4,4]{1,0:T(4,128)} %refs_2_.9, f32[4,288,896]{2,1,0:T(8,128)} %momentum.1, f32[4,288,896]{2,1,0:T(8,128)} %gradient.1, f32[8,128]{1,0:T(8,128)} %get-tuple-element.84._), custom_call_target="tpu_custom_call" | custom-call | tf_op jit(solution)/shard_map/fresh_momentum/pallas_call | solution.py:457
  151.6 6.9 %finish.1 = (f32[576,896]{1,0:T(8,128)}, f32[4,288,896]{2,1,0:T(8,128)}) custom-call(s32[4]{0:T(128)} %refs_0_.17, s32[4]{0:T(128)} %refs_1_.9, s32[4,4]{1,0:T(4,128)} %refs_2_.9, s32[4,4]{1,0:T(4,128)} %refs_3_.9, f32[576,384]{1,0:T(8,128)} %collective-permute-done.21.refs_4_, f32[576,896]{1,0:T(8,128)} %assemble_outer.1.refs_5_, ...), custom_call_target="tpu_custom_call" | custom-call | tf_op jit(solution)/shard_map/finish/pallas_call | solution.py:563
  158.6 2.8 %place_blocks.4.refs_2_ = f32[4,288,896]{2,1,0:T(8,128)} custom-call(s32[4]{0:T(128)S(1)} %copy-done.8, f32[288,896]{1,0:T(8,128)} %collective-permute-done.19.refs_1_, f32[288,896]{1,0:T(8,128)S(1)} %collective-permute-done.20.refs_2_, f32[4,288,896]{2,1,0:T(8,128)} %get-tuple-element.105.refs_3_), custom_call_target="tpu_custom_call", output_to_operand_aliasing={{}: (3, {})} | custom-call | tf_op jit(solution)/shard_map/place_blocks/pallas_call | solution.py:585
  161.3 12.2 %collective-permute-done.18.refs_1_ = f32[288,896]{1,0:T(8,128)S(1)} collective-permute-done((f32[288,896]{1,0:T(8,128)}, f32[288,896]{1,0:T(8,128)S(1)}, u32[]{:S(2)}, u32[]{:S(2)}) %collective-permute-start.18) | collective-permute-done | bytes 1032224 | tf_op jit(solution)/shard_map/ppermute | solution.py:626
  173.5 1.5 place_blocks.5.refs_2_
  175.1 20.1 %collective-permute-done.17.refs_1_ = f32[288,896]{1,0:T(8,128)S(1)} collective-permute-done((f32[288,896]{1,0:T(8,128)}, f32[288,896]{1,0:T(8,128)S(1)}, u32[]{:S(2)}, u32[]{:S(2)}) %collective-permute-start.17) | collective-permute-done | bytes 1032224 | tf_op jit(solution)/shard_map/ppermute | solution.py:626
  195.1 1.5 place_blocks.6.refs_2_
  (36 shorter events, 8.3 us)
Async XLA Ops:
  0.6 35.9 %copy-start.7 = (s32[4]{0:T(128)S(1)}, s32[4]{0:T(128)}, u32[]{:S(2)}) copy-start(s32[4]{0:T(128)} %refs_0_.17) | copy-start | bytes 52
  0.6 35.9 %copy-start.3 = (s32[4,4]{1,0:T(4,128)S(1)}, s32[4,4]{1,0:T(4,128)}, u32[]{:S(2)}) copy-start(s32[4,4]{1,0:T(4,128)} %refs_2_.9) | copy-start | bytes 196
  0.7 35.9 %copy-start.10 = (s32[4]{0:T(128)S(1)}, s32[4]{0:T(128)}, u32[]{:S(2)}) copy-start(s32[4]{0:T(128)} %refs_1_.9) | copy-start | bytes 52
  0.7 35.9 %copy-start.5 = (s32[4,4]{1,0:T(4,128)S(1)}, s32[4,4]{1,0:T(4,128)}, u32[]{:S(2)}) copy-start(s32[4,4]{1,0:T(4,128)} %refs_3_.9) | copy-start | bytes 196
  5.8 10.2 %collective-permute-start.14 = (f32[288,896]{1,0:T(8,128)}, f32[288,896]{1,0:T(8,128)}, u32[]{:S(2)}, u32[]{:S(2)}) collective-permute-start(f32[288,896]{1,0:T(8,128)} %get-tuple-element.91), channel_id=1, source_target_pairs={{8,16},{16,8},{9,17},{17,9},{10,18},{18,10},{11,19},{19,11},{12,20... | collective-permute-start | bytes 3096584 | tf_op jit(solution)/shard_map/ppermute | solution.py:623
  7.5 28.5 %collective-permute-start.8 = (f32[288,896]{1,0:T(8,128)}, f32[288,896]{1,0:T(8,128)S(1)}, u32[]{:S(2)}, u32[]{:S(2)}) collective-permute-start(f32[288,896]{1,0:T(8,128)} %get-tuple-element.83.refs_5_.refs_4_), channel_id=1, source_target_pairs={{0,8},{8,0},{16,24},{24,16},{1,9},{9,1},{17,25},{25,17},{2,10},{10... | collective-permute-start | bytes 3096584 | tf_op jit(solution)/shard_map/ppermute | solution.py:632
  12.4 45.7 %collective-permute-start.12 = (f32[288,896]{1,0:T(8,128)}, f32[288,896]{1,0:T(8,128)}, u32[]{:S(2)}, u32[]{:S(2)}) collective-permute-start(f32[288,896]{1,0:T(8,128)} %get-tuple-element.90), channel_id=1, source_target_pairs={{0,16},{24,8},{1,17},{25,9},{2,18},{26,10},{3,19},{27,11},{4,20},{... | collective-permute-start | bytes 3096584 | tf_op jit(solution)/shard_map/ppermute | solution.py:623
  16.1 43.4 %collective-permute-start.15 = (f32[288,896]{1,0:T(8,128)}, f32[288,896]{1,0:T(8,128)S(1)}, u32[]{:S(2)}, u32[]{:S(2)}) collective-permute-start(f32[288,896]{1,0:T(8,128)} %collective-permute-done.14.refs_7_), channel_id=1, source_target_pairs={{8,0},{16,24},{9,1},{17,25},{10,2},{18,26},{11,3},{19,27},{12,4},{... | collective-permute-start | bytes 3096584 | tf_op jit(solution)/shard_map/ppermute | solution.py:626
  36.0 0.6 copy-start.1
  36.6 22.9 %copy-start = (f32[288,896]{1,0:T(8,128)S(1)}, f32[288,896]{1,0:T(8,128)}, u32[]{:S(2)}) copy-start(f32[288,896]{1,0:T(8,128)} %get-tuple-element.83.refs_5_.refs_4_) | copy-start | bytes 3096580
  41.5 46.3 %collective-permute-start.9 = (f32[288,896]{1,0:T(8,128)}, f32[288,896]{1,0:T(8,128)}, u32[]{:S(2)}, u32[]{:S(2)}) collective-permute-start(f32[288,896]{1,0:T(8,128)} %get-tuple-element.87), channel_id=1, source_target_pairs={{0,8},{24,16},{1,9},{25,17},{2,10},{26,18},{3,11},{27,19},{4,12},{... | collective-permute-start | bytes 3096584 | tf_op jit(solution)/shard_map/ppermute | solution.py:623
  46.8 54.1 %collective-permute-start.10 = (f32[288,896]{1,0:T(8,128)}, f32[288,896]{1,0:T(8,128)}, u32[]{:S(2)}, u32[]{:S(2)}) collective-permute-start(f32[288,896]{1,0:T(8,128)} %get-tuple-element.88), channel_id=1, source_target_pairs={{0,16},{24,8},{1,17},{25,9},{2,18},{26,10},{3,19},{27,11},{4,20},{... | collective-permute-start | bytes 3096584 | tf_op jit(solution)/shard_map/ppermute | solution.py:623
  49.1 51.8 %collective-permute-start.11 = (f32[288,896]{1,0:T(8,128)}, f32[288,896]{1,0:T(8,128)}, u32[]{:S(2)}, u32[]{:S(2)}) collective-permute-start(f32[288,896]{1,0:T(8,128)} %get-tuple-element.89), channel_id=1, source_target_pairs={{8,16},{16,8},{9,17},{17,9},{10,18},{18,10},{11,19},{19,11},{12,20... | collective-permute-start | bytes 3096584 | tf_op jit(solution)/shard_map/ppermute | solution.py:623
  58.2 24.1 %collective-permute-start.13 = (f32[288,896]{1,0:T(8,128)}, f32[288,896]{1,0:T(8,128)}, u32[]{:S(2)}, u32[]{:S(2)}) collective-permute-start(f32[288,896]{1,0:T(8,128)} %collective-permute-done.12.refs_6_), channel_id=1, source_target_pairs={{8,0},{16,24},{9,1},{17,25},{10,2},{18,26},{11,3},{19,27},{12,4},{... | collective-permute-start | bytes 3096584 | tf_op jit(solution)/shard_map/ppermute | solution.py:626
  60.6 83.8 %collective-permute-start.21 = (f32[576,384]{1,0:T(8,128)}, f32[576,384]{1,0:T(8,128)}, u32[]{:S(2)}, u32[]{:S(2)}) collective-permute-start(f32[576,384]{1,0:T(8,128)} %get-tuple-element.100), channel_id=1, source_target_pairs={{8,0},{16,24},{9,1},{17,25},{10,2},{18,26},{11,3},{19,27},{12,4},{... | collective-permute-start | bytes 2654216 | tf_op jit(solution)/shard_map/ppermute | solution.py:626
  82.3 76.3 %collective-permute-start.19 = (f32[288,896]{1,0:T(8,128)}, f32[288,896]{1,0:T(8,128)}, u32[]{:S(2)}, u32[]{:S(2)}) collective-permute-start(f32[288,896]{1,0:T(8,128)} %get-tuple-element.98), channel_id=1, source_target_pairs={{8,24},{16,0},{9,25},{17,1},{10,26},{18,2},{11,27},{19,3},{12,28},... | collective-permute-start | bytes 3096584 | tf_op jit(solution)/shard_map/ppermute | solution.py:626
  87.8 70.8 %collective-permute-start.20 = (f32[288,896]{1,0:T(8,128)}, f32[288,896]{1,0:T(8,128)S(1)}, u32[]{:S(2)}, u32[]{:S(2)}) collective-permute-start(f32[288,896]{1,0:T(8,128)} %get-tuple-element.99), channel_id=1, source_target_pairs={{8,16},{16,8},{9,17},{17,9},{10,18},{18,10},{11,19},{19,11},{12,20... | collective-permute-start | bytes 3096584 | tf_op jit(solution)/shard_map/ppermute | solution.py:626
  100.9 72.6 %collective-permute-start.18 = (f32[288,896]{1,0:T(8,128)}, f32[288,896]{1,0:T(8,128)S(1)}, u32[]{:S(2)}, u32[]{:S(2)}) collective-permute-start(f32[288,896]{1,0:T(8,128)} %get-tuple-element.94), channel_id=1, source_target_pairs={{8,24},{16,0},{9,25},{17,1},{10,26},{18,2},{11,27},{19,3},{12,28},... | collective-permute-start | bytes 3096584 | tf_op jit(solution)/shard_map/ppermute | solution.py:626
  102.2 92.9 %collective-permute-start.17 = (f32[288,896]{1,0:T(8,128)}, f32[288,896]{1,0:T(8,128)S(1)}, u32[]{:S(2)}, u32[]{:S(2)}) collective-permute-start(f32[288,896]{1,0:T(8,128)} %get-tuple-element.93), channel_id=1, source_target_pairs={{8,0},{16,24},{9,1},{17,25},{10,2},{18,26},{11,3},{19,27},{12,4},{... | collective-permute-start | bytes 3096584 | tf_op jit(solution)/shard_map/ppermute | solution.py:626
  144.4 52.3 %collective-permute-start.16 = (f32[288,896]{1,0:T(8,128)}, f32[288,896]{1,0:T(8,128)S(1)}, u32[]{:S(2)}, u32[]{:S(2)}) collective-permute-start(f32[288,896]{1,0:T(8,128)} %get-tuple-element.92), channel_id=1, source_target_pairs={{8,16},{16,8},{9,17},{17,9},{10,18},{18,10},{11,19},{19,11},{12,20... | collective-permute-start | bytes 3096584 | tf_op jit(solution)/shard_map/ppermute | solution.py:626
  150.9 7.7 %copy-start.8 = (s32[4]{0:T(128)S(1)}, s32[4]{0:T(128)}, u32[]{:S(2)}) copy-start(s32[4]{0:T(128)} %refs_0_.17) | copy-start | bytes 52
  150.9 0.7 copy-start.2

commit v11 on v10

--- a/solution.py
+++ b/solution.py
@@ -436,7 +436,7 @@
 def blend(first, tables, momentum, gradient, before):
     _, slots, columns = momentum.shape
     ranks = tables[1].shape[0]
-    chunks = 4 if slots % (4 * SUBLANES) == 0 else 1
+    chunks = 2 if slots % (2 * SUBLANES) == 0 else 1
     return pl.pallas_call(
         functools.partial(blend_kernel, first, chunks),
         out_shape=[floats(slots, columns)] * ranks + [floats(SUBLANES, 128)],
@@ -595,7 +595,7 @@
     )(owner_group, *blocks, shards)
 
 
-def sum_halves(keep, send, axis):
+def sum_halves(keep, send, axis, streams):
     size = lax.axis_size(axis)
 
     def exchange(piece, bits):
@@ -603,8 +603,10 @@
 
     chips = [1 << shift for shift in range(1, size.bit_length() - 1)]
     keep = keep + exchange(send, (1, 1))
+    pieces = jnp.split(keep, streams, axis=0)
     for bits in zip(chips, reversed(chips)):
-        keep = keep + exchange(keep, bits)
+        pieces = [piece + exchange(piece, bits[:: 1 - 2 * index]) for index, piece in enumerate(pieces)]
+    keep = jnp.concatenate(pieces, axis=0)
     return keep, exchange(keep, (1, 1))
 
 
@@ -643,7 +645,7 @@
     pair, keep, send = assemble_and_gram(True, tables, first_blocks, *[handed[step] for step in far[1:]])
 
     def first_update(pair, keep, send, after):
-        return apply_update(True, [0, *early], tables, *sum_halves(keep, send, "tensor"), pair, slots, after)
+        return apply_update(True, [0, *early], tables, *sum_halves(keep, send, "tensor", 1), pair, slots, after)
 
     def first_skip(*_):
         return nothing(update_shapes(True, [0, *early], slots, columns))
@@ -655,7 +657,7 @@
 
     def last_update(after, *blocks):
         pair, keep, send = assemble_and_gram(False, tables, blocks, after)
-        return apply_update(False, [0, *last], tables, *sum_halves(keep, send, "tensor"), pair, slots)
+        return apply_update(False, [0, *last], tables, *sum_halves(keep, send, "tensor", 2), pair, slots)
 
     def last_skip(*_):
         return nothing(update_shapes(False, [0, *last], slots, columns))

time: 198 us -> 197 us (level)
  no operation moved by 1% of the time
where the time goes in v11:
time: 197 us
  waiting for transfers between devices  132 us (67%)
  Pallas kernels  33.4 us (17%)
  starting transfers between devices  28.6 us (15%)
    ppermute x8, waiting for transfers between devices, from_inner(): return lax.ppermute(block, 'fsdp', pairs(step, False))  93.2 us
    ppermute x5, waiting for transfers between devices, to_inner(): return lax.ppermute(block, 'fsdp', pairs(step, True))  20.3 us
    ppermute x1, waiting for transfers between devices, on_device(): swapped = lax.ppermute(own, 'fsdp', [(i, i ^ near) for i in range(ranks)])  18.6 us
    ppermute x5, starting transfers between devices, to_inner(): return lax.ppermute(block, 'fsdp', pairs(step, True))  14.6 us
    pallas_call x2, Pallas kernels, blend(): pl.pallas_call(functools.partial(blend_kernel, first, chunks), out_shape=...  9.25 us
    ppermute x8, starting transfers between devices, from_inner(): return lax.ppermute(block, 'fsdp', pairs(step, False))  9.15 us
    pallas_call x1, Pallas kernels, finish(): pl.pallas_call(functools.partial(finish_kernel, tables[1].shape[0]), out_...  6.92 us
    pallas_call x4, Pallas kernels, place_blocks(): pl.pallas_call(functools.partial(place_kernel, first, ranks, steps), out_...  6.37 us
  transfers between devices with their start and end apart: 14, of which 7 were waited for; matrix products, arithmetic and copies ran while one was open for 0% of the time, Pallas kernels for 14%

profile of v11, /device:TPU:0, one launch (start us, length us, event | category | flops | bytes accessed | tf_op | source)
XLA Modules:
  0.0 196.8 jit_solution(16230122560774015121)
XLA Ops:
  0.7 4.8 %blend.2 = (f32[288,896]{1,0:T(8,128)}, f32[288,896]{1,0:T(8,128)}, f32[288,896]{1,0:T(8,128)}, f32[288,896]{1,0:T(8,128)}, f32[8,128]{1,0:T(8,128)}) custom-call(s32[4]{0:T(128)} %refs_0_.17, s32[4]{0:T(128)} %refs_1_.9, s32[4,4]{1,0:T(4,128)} %refs_2_.9, s32[4,4]{1,0:T(4,128)} %refs_3_.9, f32[4,288,896]{2,1,0:T(8,128)} %momentum.1, f32[4,288,896]{2,1,0:T(8,128)} %gradient.1), custom_call_target="tpu_custom_call" | custom-call | tf_op jit(solution)/shard_map/blend/pallas_call | solution.py:440
  5.5 1.7 collective-permute-start.16
  7.1 4.9 %collective-permute-start.10 = (f32[288,896]{1,0:T(8,128)}, f32[288,896]{1,0:T(8,128)S(1)}, u32[]{:S(2)}, u32[]{:S(2)}) collective-permute-start(f32[288,896]{1,0:T(8,128)} %get-tuple-element.83.refs_5_.refs_4_), channel_id=1, source_target_pairs={{0,8},{8,0},{16,24},{24,16},{1,9},{9,1},{17,25},{25,17},{2,10},{10... | collective-permute-start | bytes 3096584 | tf_op jit(solution)/shard_map/ppermute | solution.py:634
  12.1 3.7 %collective-permute-start.14 = (f32[288,896]{1,0:T(8,128)}, f32[288,896]{1,0:T(8,128)}, u32[]{:S(2)}, u32[]{:S(2)}) collective-permute-start(f32[288,896]{1,0:T(8,128)} %get-tuple-element.90), channel_id=1, source_target_pairs={{0,16},{24,8},{1,17},{25,9},{2,18},{26,10},{3,19},{27,11},{4,20},{... | collective-permute-start | bytes 3096584 | tf_op jit(solution)/shard_map/ppermute | solution.py:625
  15.7 1.3 collective-permute-start.17
  17.0 18.6 %collective-permute-done.10.refs_0_.refs_4_.refs_5_ = f32[288,896]{1,0:T(8,128)S(1)} collective-permute-done((f32[288,896]{1,0:T(8,128)}, f32[288,896]{1,0:T(8,128)S(1)}, u32[]{:S(2)}, u32[]{:S(2)}) %collective-permute-start.10) | collective-permute-done | bytes 1032224 | tf_op jit(solution)/shard_map/ppermute | solution.py:634
  36.2 4.5 %blend.3 = (f32[288,896]{1,0:T(8,128)}, f32[288,896]{1,0:T(8,128)}, f32[288,896]{1,0:T(8,128)}, f32[288,896]{1,0:T(8,128)}, f32[8,128]{1,0:T(8,128)}) custom-call(s32[4]{0:T(128)S(1)} %copy-done.7, s32[4]{0:T(128)S(1)} %copy-done.10, s32[4,4]{1,0:T(4,128)S(1)} %copy-done.3, s32[4,4]{1,0:T(4,128)S(1)} %copy-done.5, f32[4,288,896]{2,1,0:T(8,128)} %momentum.1, ...), custom_call_target="tpu_custom_call" | custom-call | tf_op jit(solution)/shard_map/blend/pallas_call | solution.py:440
  40.7 5.3 %collective-permute-start.11 = (f32[288,896]{1,0:T(8,128)}, f32[288,896]{1,0:T(8,128)}, u32[]{:S(2)}, u32[]{:S(2)}) collective-permute-start(f32[288,896]{1,0:T(8,128)} %get-tuple-element.87), channel_id=1, source_target_pairs={{0,8},{24,16},{1,9},{25,17},{2,10},{26,18},{3,11},{27,19},{4,12},{... | collective-permute-start | bytes 3096584 | tf_op jit(solution)/shard_map/ppermute | solution.py:625
  46.0 2.3 %collective-permute-start.12 = (f32[288,896]{1,0:T(8,128)}, f32[288,896]{1,0:T(8,128)}, u32[]{:S(2)}, u32[]{:S(2)}) collective-permute-start(f32[288,896]{1,0:T(8,128)} %get-tuple-element.88), channel_id=1, source_target_pairs={{0,16},{24,8},{1,17},{25,9},{2,18},{26,10},{3,19},{27,11},{4,20},{... | collective-permute-start | bytes 3096584 | tf_op jit(solution)/shard_map/ppermute | solution.py:625
  48.3 1.6 collective-permute-start.13
  49.9 7.8 %collective-permute-done.14.refs_6_ = f32[288,896]{1,0:T(8,128)} collective-permute-done((f32[288,896]{1,0:T(8,128)}, f32[288,896]{1,0:T(8,128)}, u32[]{:S(2)}, u32[]{:S(2)}) %collective-permute-start.14) | collective-permute-done | bytes 1032224 | tf_op jit(solution)/shard_map/ppermute | solution.py:625
  60.2 1.3 collective-permute-start.23
  61.5 20.3 %collective-permute-done.15.refs_6_ = f32[288,896]{1,0:T(8,128)} collective-permute-done((f32[288,896]{1,0:T(8,128)}, f32[288,896]{1,0:T(8,128)}, u32[]{:S(2)}, u32[]{:S(2)}) %collective-permute-start.15) | collective-permute-done | bytes 1032224 | tf_op jit(solution)/shard_map/ppermute | solution.py:628
  83.2 4.2 %assemble_outer.1.refs_5_ = f32[576,896]{1,0:T(8,128)} custom-call(s32[4]{0:T(128)S(1)} %copy-done.7, s32[4]{0:T(128)S(1)} %copy-done.10, s32[4,4]{1,0:T(4,128)S(1)} %copy-done.3, s32[4,4]{1,0:T(4,128)S(1)} %copy-done.5, f32[288,896]{1,0:T(8,128)S(1)} %collective-permute-done.10.refs_0_.refs_4_.refs_5_, f32[288,896]{1,0:T(8,128)S(1)} %copy-done, ...), custom_call_target="tpu_custom_call" | custom-call | tf_op jit(solution)/shard_map/assemble_outer/pallas_call | solution.py:497
  88.2 12.4 %collective-permute-done.12 = f32[288,896]{1,0:T(8,128)} collective-permute-done((f32[288,896]{1,0:T(8,128)}, f32[288,896]{1,0:T(8,128)}, u32[]{:S(2)}, u32[]{:S(2)}) %collective-permute-start.12) | collective-permute-done | bytes 1032224 | tf_op jit(solution)/shard_map/ppermute | solution.py:625
  101.9 1.3 collective-permute-start.19
  103.2 40.8 %collective-permute-done.23.refs_4_ = f32[576,384]{1,0:T(8,128)} collective-permute-done((f32[576,384]{1,0:T(8,128)}, f32[576,384]{1,0:T(8,128)}, u32[]{:S(2)}, u32[]{:S(2)}) %collective-permute-start.23) | collective-permute-done | bytes 884768 | tf_op jit(solution)/shard_map/ppermute | solution.py:628
  144.7 5.8 %fresh_momentum.1 = (f32[4,288,896]{2,1,0:T(8,128)}, f32[8,128]{1,0:T(8,128)}) custom-call(s32[4]{0:T(128)} %refs_1_.9, s32[4,4]{1,0:T(4,128)} %refs_2_.9, f32[4,288,896]{2,1,0:T(8,128)} %momentum.1, f32[4,288,896]{2,1,0:T(8,128)} %gradient.1, f32[8,128]{1,0:T(8,128)} %get-tuple-element.84._), custom_call_target="tpu_custom_call" | custom-call | tf_op jit(solution)/shard_map/fresh_momentum/pallas_call | solution.py:457
  151.2 6.9 %finish.1 = (f32[576,896]{1,0:T(8,128)}, f32[4,288,896]{2,1,0:T(8,128)}) custom-call(s32[4]{0:T(128)} %refs_0_.17, s32[4]{0:T(128)} %refs_1_.9, s32[4,4]{1,0:T(4,128)} %refs_2_.9, s32[4,4]{1,0:T(4,128)} %refs_3_.9, f32[576,384]{1,0:T(8,128)} %collective-permute-done.23.refs_4_, f32[576,896]{1,0:T(8,128)} %assemble_outer.1.refs_5_, ...), custom_call_target="tpu_custom_call" | custom-call | tf_op jit(solution)/shard_map/finish/pallas_call | solution.py:563
  158.2 2.8 %place_blocks.4.refs_2_ = f32[4,288,896]{2,1,0:T(8,128)} custom-call(s32[4]{0:T(128)S(1)} %copy-done.8, f32[288,896]{1,0:T(8,128)} %collective-permute-done.21.refs_1_, f32[288,896]{1,0:T(8,128)S(1)} %collective-permute-done.22.refs_2_, f32[4,288,896]{2,1,0:T(8,128)} %get-tuple-element.105.refs_3_), custom_call_target="tpu_custom_call", output_to_operand_aliasing={{}: (3, {})} | custom-call | tf_op jit(solution)/shard_map/place_blocks/pallas_call | solution.py:585
  160.9 11.7 %collective-permute-done.20.refs_1_ = f32[288,896]{1,0:T(8,128)S(1)} collective-permute-done((f32[288,896]{1,0:T(8,128)}, f32[288,896]{1,0:T(8,128)S(1)}, u32[]{:S(2)}, u32[]{:S(2)}) %collective-permute-start.20) | collective-permute-done | bytes 1032224 | tf_op jit(solution)/shard_map/ppermute | solution.py:628
  172.7 1.5 place_blocks.5.refs_2_
  174.2 20.2 %collective-permute-done.19.refs_1_ = f32[288,896]{1,0:T(8,128)S(1)} collective-permute-done((f32[288,896]{1,0:T(8,128)}, f32[288,896]{1,0:T(8,128)S(1)}, u32[]{:S(2)}, u32[]{:S(2)}) %collective-permute-start.19) | collective-permute-done | bytes 1032224 | tf_op jit(solution)/shard_map/ppermute | solution.py:628
  194.5 1.5 place_blocks.6.refs_2_
  (36 shorter events, 8.3 us)
Async XLA Ops:
  0.6 35.6 %copy-start.7 = (s32[4]{0:T(128)S(1)}, s32[4]{0:T(128)}, u32[]{:S(2)}) copy-start(s32[4]{0:T(128)} %refs_0_.17) | copy-start | bytes 52
  0.6 35.6 %copy-start.3 = (s32[4,4]{1,0:T(4,128)S(1)}, s32[4,4]{1,0:T(4,128)}, u32[]{:S(2)}) copy-start(s32[4,4]{1,0:T(4,128)} %refs_2_.9) | copy-start | bytes 196
  0.7 35.6 %copy-start.10 = (s32[4]{0:T(128)S(1)}, s32[4]{0:T(128)}, u32[]{:S(2)}) copy-start(s32[4]{0:T(128)} %refs_1_.9) | copy-start | bytes 52
  0.7 35.6 %copy-start.5 = (s32[4,4]{1,0:T(4,128)S(1)}, s32[4,4]{1,0:T(4,128)}, u32[]{:S(2)}) copy-start(s32[4,4]{1,0:T(4,128)} %refs_3_.9) | copy-start | bytes 196
  5.5 10.3 %collective-permute-start.16 = (f32[288,896]{1,0:T(8,128)}, f32[288,896]{1,0:T(8,128)}, u32[]{:S(2)}, u32[]{:S(2)}) collective-permute-start(f32[288,896]{1,0:T(8,128)} %get-tuple-element.91), channel_id=1, source_target_pairs={{8,16},{16,8},{9,17},{17,9},{10,18},{18,10},{11,19},{19,11},{12,20... | collective-permute-start | bytes 3096584 | tf_op jit(solution)/shard_map/ppermute | solution.py:625
  7.1 28.5 %collective-permute-start.10 = (f32[288,896]{1,0:T(8,128)}, f32[288,896]{1,0:T(8,128)S(1)}, u32[]{:S(2)}, u32[]{:S(2)}) collective-permute-start(f32[288,896]{1,0:T(8,128)} %get-tuple-element.83.refs_5_.refs_4_), channel_id=1, source_target_pairs={{0,8},{8,0},{16,24},{24,16},{1,9},{9,1},{17,25},{25,17},{2,10},{10... | collective-permute-start | bytes 3096584 | tf_op jit(solution)/shard_map/ppermute | solution.py:634
  12.1 45.7 %collective-permute-start.14 = (f32[288,896]{1,0:T(8,128)}, f32[288,896]{1,0:T(8,128)}, u32[]{:S(2)}, u32[]{:S(2)}) collective-permute-start(f32[288,896]{1,0:T(8,128)} %get-tuple-element.90), channel_id=1, source_target_pairs={{0,16},{24,8},{1,17},{25,9},{2,18},{26,10},{3,19},{27,11},{4,20},{... | collective-permute-start | bytes 3096584 | tf_op jit(solution)/shard_map/ppermute | solution.py:625
  15.7 43.3 %collective-permute-start.17 = (f32[288,896]{1,0:T(8,128)}, f32[288,896]{1,0:T(8,128)S(1)}, u32[]{:S(2)}, u32[]{:S(2)}) collective-permute-start(f32[288,896]{1,0:T(8,128)} %collective-permute-done.16.refs_7_), channel_id=1, source_target_pairs={{8,0},{16,24},{9,1},{17,25},{10,2},{18,26},{11,3},{19,27},{12,4},{... | collective-permute-start | bytes 3096584 | tf_op jit(solution)/shard_map/ppermute | solution.py:628
  35.6 0.6 copy-start.1
  36.2 22.9 %copy-start = (f32[288,896]{1,0:T(8,128)S(1)}, f32[288,896]{1,0:T(8,128)}, u32[]{:S(2)}) copy-start(f32[288,896]{1,0:T(8,128)} %get-tuple-element.83.refs_5_.refs_4_) | copy-start | bytes 3096580
  40.7 46.7 %collective-permute-start.11 = (f32[288,896]{1,0:T(8,128)}, f32[288,896]{1,0:T(8,128)}, u32[]{:S(2)}, u32[]{:S(2)}) collective-permute-start(f32[288,896]{1,0:T(8,128)} %get-tuple-element.87), channel_id=1, source_target_pairs={{0,8},{24,16},{1,9},{25,17},{2,10},{26,18},{3,11},{27,19},{4,12},{... | collective-permute-start | bytes 3096584 | tf_op jit(solution)/shard_map/ppermute | solution.py:625
  46.0 54.5 %collective-permute-start.12 = (f32[288,896]{1,0:T(8,128)}, f32[288,896]{1,0:T(8,128)}, u32[]{:S(2)}, u32[]{:S(2)}) collective-permute-start(f32[288,896]{1,0:T(8,128)} %get-tuple-element.88), channel_id=1, source_target_pairs={{0,16},{24,8},{1,17},{25,9},{2,18},{26,10},{3,19},{27,11},{4,20},{... | collective-permute-start | bytes 3096584 | tf_op jit(solution)/shard_map/ppermute | solution.py:625
  48.3 52.3 %collective-permute-start.13 = (f32[288,896]{1,0:T(8,128)}, f32[288,896]{1,0:T(8,128)}, u32[]{:S(2)}, u32[]{:S(2)}) collective-permute-start(f32[288,896]{1,0:T(8,128)} %get-tuple-element.89), channel_id=1, source_target_pairs={{8,16},{16,8},{9,17},{17,9},{10,18},{18,10},{11,19},{19,11},{12,20... | collective-permute-start | bytes 3096584 | tf_op jit(solution)/shard_map/ppermute | solution.py:625
  57.8 24.1 %collective-permute-start.15 = (f32[288,896]{1,0:T(8,128)}, f32[288,896]{1,0:T(8,128)}, u32[]{:S(2)}, u32[]{:S(2)}) collective-permute-start(f32[288,896]{1,0:T(8,128)} %collective-permute-done.14.refs_6_), channel_id=1, source_target_pairs={{8,0},{16,24},{9,1},{17,25},{10,2},{18,26},{11,3},{19,27},{12,4},{... | collective-permute-start | bytes 3096584 | tf_op jit(solution)/shard_map/ppermute | solution.py:628
  60.2 83.7 %collective-permute-start.23 = (f32[576,384]{1,0:T(8,128)}, f32[576,384]{1,0:T(8,128)}, u32[]{:S(2)}, u32[]{:S(2)}) collective-permute-start(f32[576,384]{1,0:T(8,128)} %get-tuple-element.100), channel_id=1, source_target_pairs={{8,0},{16,24},{9,1},{17,25},{10,2},{18,26},{11,3},{19,27},{12,4},{... | collective-permute-start | bytes 2654216 | tf_op jit(solution)/shard_map/ppermute | solution.py:628
  81.9 76.3 %collective-permute-start.21 = (f32[288,896]{1,0:T(8,128)}, f32[288,896]{1,0:T(8,128)}, u32[]{:S(2)}, u32[]{:S(2)}) collective-permute-start(f32[288,896]{1,0:T(8,128)} %get-tuple-element.98), channel_id=1, source_target_pairs={{8,24},{16,0},{9,25},{17,1},{10,26},{18,2},{11,27},{19,3},{12,28},... | collective-permute-start | bytes 3096584 | tf_op jit(solution)/shard_map/ppermute | solution.py:628
  87.4 70.7 %collective-permute-start.22 = (f32[288,896]{1,0:T(8,128)}, f32[288,896]{1,0:T(8,128)S(1)}, u32[]{:S(2)}, u32[]{:S(2)}) collective-permute-start(f32[288,896]{1,0:T(8,128)} %get-tuple-element.99), channel_id=1, source_target_pairs={{8,16},{16,8},{9,17},{17,9},{10,18},{18,10},{11,19},{19,11},{12,20... | collective-permute-start | bytes 3096584 | tf_op jit(solution)/shard_map/ppermute | solution.py:628
  100.6 72.1 %collective-permute-start.20 = (f32[288,896]{1,0:T(8,128)}, f32[288,896]{1,0:T(8,128)S(1)}, u32[]{:S(2)}, u32[]{:S(2)}) collective-permute-start(f32[288,896]{1,0:T(8,128)} %get-tuple-element.94), channel_id=1, source_target_pairs={{8,24},{16,0},{9,25},{17,1},{10,26},{18,2},{11,27},{19,3},{12,28},... | collective-permute-start | bytes 3096584 | tf_op jit(solution)/shard_map/ppermute | solution.py:628
  101.9 92.6 %collective-permute-start.19 = (f32[288,896]{1,0:T(8,128)}, f32[288,896]{1,0:T(8,128)S(1)}, u32[]{:S(2)}, u32[]{:S(2)}) collective-permute-start(f32[288,896]{1,0:T(8,128)} %get-tuple-element.93), channel_id=1, source_target_pairs={{8,0},{16,24},{9,1},{17,25},{10,2},{18,26},{11,3},{19,27},{12,4},{... | collective-permute-start | bytes 3096584 | tf_op jit(solution)/shard_map/ppermute | solution.py:628
  144.0 52.0 %collective-permute-start.18 = (f32[288,896]{1,0:T(8,128)}, f32[288,896]{1,0:T(8,128)S(1)}, u32[]{:S(2)}, u32[]{:S(2)}) collective-permute-start(f32[288,896]{1,0:T(8,128)} %get-tuple-element.92), channel_id=1, source_target_pairs={{8,16},{16,8},{9,17},{17,9},{10,18},{18,10},{11,19},{19,11},{12,20... | collective-permute-start | bytes 3096584 | tf_op jit(solution)/shard_map/ppermute | solution.py:628
  150.5 7.7 %copy-start.8 = (s32[4]{0:T(128)S(1)}, s32[4]{0:T(128)}, u32[]{:S(2)}) copy-start(s32[4]{0:T(128)} %refs_0_.17) | copy-start | bytes 52
  150.5 0.7 copy-start.2

commit v12 on v11

--- a/solution.py
+++ b/solution.py
@@ -115,7 +115,7 @@
 def blend_kernel(first, chunks, *refs):
     tables, (momentum, gradient) = refs[:4], refs[4:6]
     ranks = tables[1].shape[0]
-    *outs, token, olds, grads, arrive, leave = refs[-ranks - 10 : -5]
+    *outs, token, olds, grads, arrive, leave = refs[-ranks - 10 + first : -5]
     owner_group, live_ranks, row_counts, _ = fetch_tables(tables, refs[-5:])
     rank = lax.axis_index("fsdp")
     slots, columns = outs[0].shape
@@ -139,7 +139,7 @@
                 (wanted, momentum.at[matrix, part], olds.at[step, part], flags[0]),
                 (wanted, gradient.at[matrix, part], grads.at[step, part], flags[1]),
             )
-            outgoing = (wanted, olds.at[step, part], outs[step].at[part], leave.at[step, chunk])
+            outgoing = (wanted, olds.at[step, part], outs[step - first].at[part], leave.at[step, chunk])
             jobs.append((step, chunk, count, incoming, outgoing))
             each_copy(incoming, "start")
     token[...] = jnp.zeros_like(token)
@@ -307,6 +307,16 @@
     over_tiles(slots // SUBLANES, tile, window(0))
 
 
+def stack_copies(pair, stacked, arrive):
+    copies, begin = [], 0
+    for index, (side, (first_row, last_row)) in enumerate(PARTS):
+        size = last_row - first_row
+        source = pair.at[side, pl.ds(first_row, size)]
+        copies.append(pltpu.make_async_copy(source, stacked.at[pl.ds(begin, size)], arrive.at[index]))
+        begin += size
+    return copies
+
+
 def update_kernel(first, steps, *refs):
     tables, (keep, away, pair), refs = refs[:4], refs[4:7], refs[8 if first else 7 :]
     whole, refs = refs[0], refs[1:]
@@ -317,31 +327,22 @@
 
     @pl.when(is_inner(rank, ranks))
     def _():
-        incoming, begin = [], 0
-        for index, (side, (first_row, last_row)) in enumerate(PARTS):
-            size = last_row - first_row
-            source = pair.at[side, pl.ds(first_row, size)]
-            incoming.append(pltpu.make_async_copy(source, stacked.at[pl.ds(begin, size)], arrive.at[index]))
-            incoming[-1].start()
-            begin += size
+        incoming = stack_copies(pair, stacked, arrive)
+        for copy in incoming:
+            copy.start()
         owner_group, live_ranks, row_counts, row_offsets = fetch_tables(tables, refs[7:])
         matrix = matrix_of(owner_group, rank ^ mate(ranks) if first else rank)
         mine, other = core_rows()
         held[mine, :] = keep[...]
         held[other, :] = away[...]
         total = polynomial(unpack(held, gram), gram)
-        copies = []
-        if first:
-            for panel in range(3):
-                store_panel(held, panel, total[panel * PANEL :, panel * PANEL : (panel + 1) * PANEL])
-            copies = [pltpu.make_async_copy(held, whole, leave.at[len(steps)])]
-            copies[0].start()
+        for panel in range(3):
+            store_panel(held, panel, total[panel * PANEL :, panel * PANEL : (panel + 1) * PANEL])
+        copies = [pltpu.make_async_copy(held, whole, leave.at[len(steps)])]
+        copies[0].start()
         for copy in incoming:
             copy.wait()
         padded[:INNER, :] = dot(passes_left(total), stacked[...])
-        if not first:
-            copies = [pltpu.make_async_copy(padded.at[pl.ds(0, INNER)], whole, leave.at[len(steps)])]
-            copies[0].start()
         for index, step in enumerate(steps):
             target = rank ^ step
             count = row_counts[matrix, target] * live_ranks[target]
@@ -353,49 +354,42 @@
 
 
 def finish_kernel(ranks, *refs):
-    tables, (packed, iterate, inner_result, own_first, own_last), refs = refs[:4], refs[4:9], refs[10:]
-    (result, shards), refs = refs[:2], refs[2:]
-    gram, padded, staged, whole, held, arrive, leave = refs[:7]
+    tables, (first_there, iterate, first_packed, first_pair, last_packed, last_pair) = refs[:4], refs[4:10]
+    (result, shards, gram, padded, staged, whole, stacked, held, arrive, leave), refs = refs[11:21], refs[21:]
     rank = lax.axis_index("fsdp")
-    owner_group, live_ranks, row_counts, row_offsets = fetch_tables(tables, refs[7:])
-    matrix = matrix_of(owner_group, rank)
-
-    def run(jobs):
-        copies = [pltpu.make_async_copy(*job) for job in jobs]
+    owner_group, live_ranks, row_counts, row_offsets = fetch_tables(tables, refs)
+
+    def run(copies):
         for copy in copies:
             copy.start()
         for copy in copies:
             copy.wait()
 
+    def own_block(matrix, index):
+        extract(padded, row_offsets[matrix, rank], row_counts[matrix, rank] * live_ranks[rank], staged, index)
+        return pltpu.make_async_copy(staged.at[index], shards.at[matrix], leave.at[index])
+
+    def to_result():
+        return pltpu.make_async_copy(padded.at[pl.ds(0, INNER)], result, leave.at[2])
+
     @pl.when(is_inner(rank, ranks))
+    def _():
+        for index, (packed, pair) in enumerate(((last_packed, last_pair), (first_packed, first_pair))):
+            run([pltpu.make_async_copy(packed, held, leave.at[2]), *stack_copies(pair, stacked, arrive)])
+            padded[:INNER, :] = dot(passes_left(unpack(held, gram)), stacked[...])
+            matrix = matrix_of(owner_group, rank ^ (index * mate(ranks)))
+            run([own_block(matrix, index)] + [to_result()] * (index == 0))
+
+    @pl.when(jnp.logical_not(is_inner(rank, ranks)))
     def _():
         run(
             [
-                (inner_result, whole, arrive.at[0]),
-                (own_first, staged.at[0], arrive.at[1]),
-                (own_last, staged.at[1], arrive.at[2]),
+                pltpu.make_async_copy(iterate, whole, leave.at[0]),
+                pltpu.make_async_copy(first_there, held, leave.at[2]),
             ]
         )
-        other = matrix_of(owner_group, rank ^ mate(ranks))
-        run(
-            [
-                (whole, result, leave.at[0]),
-                (staged.at[0], shards.at[other], leave.at[1]),
-                (staged.at[1], shards.at[matrix], leave.at[2]),
-            ]
-        )
-
-    @pl.when(jnp.logical_not(is_inner(rank, ranks)))
-    def _():
-        run([(iterate, whole, arrive.at[0]), (packed, held, arrive.at[1])])
         padded[:INNER, :] = dot(passes_left(unpack(held, gram)), passes_right(whole[...]))
-        extract(padded, row_offsets[matrix, rank], row_counts[matrix, rank] * live_ranks[rank], staged, 0)
-        run(
-            [
-                (padded.at[pl.ds(0, INNER)], result, leave.at[0]),
-                (staged.at[0], shards.at[matrix], leave.at[1]),
-            ]
-        )
+        run([own_block(matrix_of(owner_group, rank), 0), to_result()])
 
 
 def place_kernel(first, ranks, steps, *refs):
@@ -439,9 +433,9 @@
     chunks = 2 if slots % (2 * SUBLANES) == 0 else 1
     return pl.pallas_call(
         functools.partial(blend_kernel, first, chunks),
-        out_shape=[floats(slots, columns)] * ranks + [floats(SUBLANES, 128)],
+        out_shape=[floats(slots, columns)] * (ranks - first) + [floats(SUBLANES, 128)],
         in_specs=[HBM] * 6 + [ANY] * len(before),
-        out_specs=[HBM] * ranks + [VMEM],
+        out_specs=[ANY] * (ranks - first) + [VMEM],
         scratch_shapes=[vmem(ranks, slots, columns)] * 2
         + [flags(ranks, chunks, 2), flags(ranks, chunks)]
         + table_scratch(*tables[2].shape),
@@ -512,9 +506,8 @@
     )(*tables, *blocks)
 
 
-def update_shapes(first, steps, slots, columns):
-    whole = floats(INNER, 2 * PANEL if first else columns)
-    return [whole] + [floats(slots, columns)] * len(steps)
+def update_shapes(steps, slots, columns):
+    return [floats(INNER, 2 * PANEL)] + [floats(slots, columns)] * len(steps)
 
 
 def nothing(shapes):
@@ -527,7 +520,7 @@
     columns = pair.shape[2]
     return pl.pallas_call(
         functools.partial(update_kernel, first, steps),
-        out_shape=update_shapes(first, steps, slots, columns),
+        out_shape=update_shapes(steps, slots, columns),
         in_specs=[HBM] * 4 + [VMEM] * 2 + [ANY] * (1 + len(after)),
         out_specs=[ANY] * (1 + len(steps)),
         scratch_shapes=[
@@ -558,27 +551,28 @@
     )(value)
 
 
-def finish(tables, packed, iterate, inner_result, own_first, own_last, shape, after):
-    slots, columns = own_first.shape
+def finish(tables, first_there, iterate, first_packed, first_pair, last_packed, last_pair, shape, after):
+    _, slots, columns = shape
     return pl.pallas_call(
         functools.partial(finish_kernel, tables[1].shape[0]),
         out_shape=[floats(INNER, columns), floats(*shape)],
-        in_specs=[HBM] * 4 + [ANY] * 6,
+        in_specs=[HBM] * 4 + [ANY] * 7,
         out_specs=[HBM] * 2,
         scratch_shapes=[
             vmem(INNER, INNER),
             vmem(INNER + slots + 2 * SUBLANES, columns),
             vmem(2, slots, columns),
             vmem(INNER, columns),
+            vmem(3 * INNER, columns, dtype=jnp.bfloat16),
             vmem(INNER, 2 * PANEL),
-            flags(3),
+            flags(len(PARTS)),
             flags(3),
         ]
         + table_scratch(*tables[2].shape),
         compiler_params=PARAMS,
         cost_estimate=FREE,
         name="finish",
-    )(*tables, packed, iterate, inner_result, own_first, own_last, after)
+    )(*tables, first_there, iterate, first_packed, first_pair, last_packed, last_pair, after)
 
 
 def place_blocks(first, owner_group, steps, blocks, shards, ranks):
@@ -630,9 +624,9 @@
     near = mate(ranks)
     far = [step for step in last if step != near]
     *blends, token = blend(True, tables, momentum, gradient, [])
-    own = blends[near]
+    own = blends[near - 1]
     swapped = lax.ppermute(own, "fsdp", [(i, i ^ near) for i in range(ranks)])
-    arrived = {step: to_inner(blends[step], step) for step in far}
+    arrived = {step: to_inner(blends[step - 1], step) for step in far}
     *blends, token = blend(False, tables, momentum, gradient, [token, touch(swapped)])
     last_blocks = [blends[0]] + [to_inner(blends[step], step) for step in range(1, ranks)]
     new_momentum, token = fresh_momentum(tables, momentum, gradient, token)
@@ -645,27 +639,29 @@
     pair, keep, send = assemble_and_gram(True, tables, first_blocks, *[handed[step] for step in far[1:]])
 
     def first_update(pair, keep, send, after):
-        return apply_update(True, [0, *early], tables, *sum_halves(keep, send, "tensor", 1), pair, slots, after)
+        return apply_update(True, early, tables, *sum_halves(keep, send, "tensor", 1), pair, slots, after)
 
     def first_skip(*_):
-        return nothing(update_shapes(True, [0, *early], slots, columns))
-
-    packed, own_first, *homes = lax.cond(inner, first_update, first_skip, pair, keep, send, touch(keep, 10**11))
+        return nothing(update_shapes(early, slots, columns))
+
+    packed, *homes = lax.cond(inner, first_update, first_skip, pair, keep, send, touch(keep, 10**11))
     packed_there = from_inner(packed, near)
     iterate = assemble_outer(tables, ordered(swapped, own, handed))
     first_home = [from_inner(block, step) for step, block in zip(early, homes)]
 
     def last_update(after, *blocks):
         pair, keep, send = assemble_and_gram(False, tables, blocks, after)
-        return apply_update(False, [0, *last], tables, *sum_halves(keep, send, "tensor", 2), pair, slots)
+        return (pair, *apply_update(False, last, tables, *sum_halves(keep, send, "tensor", 2), pair, slots))
 
     def last_skip(*_):
-        return nothing(update_shapes(False, [0, *last], slots, columns))
-
-    result, own_last, *homes = lax.cond(inner, last_update, last_skip, iterate, *last_blocks)
+        return tuple(nothing([jax.ShapeDtypeStruct(pair.shape, pair.dtype), *update_shapes(last, slots, columns)]))
+
+    last_pair, last_packed, *homes = lax.cond(inner, last_update, last_skip, iterate, *last_blocks)
     last_home = [from_inner(block, step) for step, block in zip(last, homes)]
 
-    result, shards = finish(tables, packed_there, iterate, result, own_first, own_last, momentum.shape, token)
+    result, shards = finish(
+        tables, packed_there, iterate, packed, pair, last_packed, last_pair, momentum.shape, token
+    )
     shards = place_blocks(True, owner_group, early, first_home, shards, ranks)
     for step, block in zip(last, last_home):
         shards = place_blocks(False, owner_group, [step], [block], shards, ranks)

time: 197 us -> 197 us (level)
  transfers between devices with their start and end apart: 14 -> 14, of which waited for: 7 -> 7; matrix products, arithmetic and copies ran while one was open for 0% -> 0% of each run, Pallas kernels for 14% -> 15%
where the time goes in v12:
time: 197 us; the launch traced here: 196 us
  waiting for transfers between devices  131 us (66%)
  Pallas kernels  33.9 us (17%)
  starting transfers between devices  28.6 us (15%)
    ppermute x8, waiting for transfers between devices, from_inner(): return lax.ppermute(block, 'fsdp', pairs(step, False))  92.2 us
    ppermute x5, waiting for transfers between devices, to_inner(): return lax.ppermute(block, 'fsdp', pairs(step, True))  20.3 us
    ppermute x1, waiting for transfers between devices, on_device(): swapped = lax.ppermute(own, 'fsdp', [(i, i ^ near) for i in range(ranks)])  18.6 us
    ppermute x5, starting transfers between devices, to_inner(): return lax.ppermute(block, 'fsdp', pairs(step, True))  14.5 us
    pallas_call x2, Pallas kernels, blend(): pl.pallas_call(functools.partial(blend_kernel, first, chunks), out_shape=...  9.2 us
    ppermute x8, starting transfers between devices, from_inner(): return lax.ppermute(block, 'fsdp', pairs(step, False))  9.15 us
    pallas_call x1, Pallas kernels, finish(): pl.pallas_call(functools.partial(finish_kernel, tables[1].shape[0]), out_...  7.36 us
    pallas_call x4, Pallas kernels, place_blocks(): pl.pallas_call(functools.partial(place_kernel, first, ranks, steps), out_...  6.37 us
  transfers between devices with their start and end apart: 14, of which 7 were waited for; matrix products, arithmetic and copies ran while one was open for 0% of the time, Pallas kernels for 15%

profile of v12, /device:TPU:0, one launch (start us, length us, event | category | flops | bytes accessed | tf_op | source)
XLA Modules:
  0.0 196.2 jit_solution(2000889634286415645)
XLA Ops:
  0.7 4.7 %blend.2 = (f32[288,896]{1,0:T(8,128)}, f32[288,896]{1,0:T(8,128)}, f32[288,896]{1,0:T(8,128)}, f32[8,128]{1,0:T(8,128)}) custom-call(s32[4]{0:T(128)} %refs_0_.17, s32[4]{0:T(128)} %refs_1_.9, s32[4,4]{1,0:T(4,128)} %refs_2_.9, s32[4,4]{1,0:T(4,128)} %refs_3_.9, f32[4,288,896]{2,1,0:T(8,128)} %momentum.1, f32[4,288,896]{2,1,0:T(8,128)} %gradient.1), custom_call_target="tpu_custom_call" | custom-call | tf_op jit(solution)/shard_map/blend/pallas_call | solution.py:434
  5.4 1.6 collective-permute-start.16
  7.1 4.9 %collective-permute-start.10 = (f32[288,896]{1,0:T(8,128)}, f32[288,896]{1,0:T(8,128)S(1)}, u32[]{:S(2)}, u32[]{:S(2)}) collective-permute-start(f32[288,896]{1,0:T(8,128)} %get-tuple-element.86.refs_5_.refs_4_), channel_id=1, source_target_pairs={{0,8},{8,0},{16,24},{24,16},{1,9},{9,1},{17,25},{25,17},{2,10},{10... | collective-permute-start | bytes 3096584 | tf_op jit(solution)/shard_map/ppermute | solution.py:628
  12.0 3.6 %collective-permute-start.14 = (f32[288,896]{1,0:T(8,128)}, f32[288,896]{1,0:T(8,128)}, u32[]{:S(2)}, u32[]{:S(2)}) collective-permute-start(f32[288,896]{1,0:T(8,128)} %get-tuple-element.93), channel_id=1, source_target_pairs={{0,16},{24,8},{1,17},{25,9},{2,18},{26,10},{3,19},{27,11},{4,20},{... | collective-permute-start | bytes 3096584 | tf_op jit(solution)/shard_map/ppermute | solution.py:619
  15.6 1.3 collective-permute-start.17
  16.9 18.6 %collective-permute-done.10.refs_0_.refs_4_.refs_5_ = f32[288,896]{1,0:T(8,128)S(1)} collective-permute-done((f32[288,896]{1,0:T(8,128)}, f32[288,896]{1,0:T(8,128)S(1)}, u32[]{:S(2)}, u32[]{:S(2)}) %collective-permute-start.10) | collective-permute-done | bytes 1032224 | tf_op jit(solution)/shard_map/ppermute | solution.py:628
  36.2 4.5 %blend.3 = (f32[288,896]{1,0:T(8,128)}, f32[288,896]{1,0:T(8,128)}, f32[288,896]{1,0:T(8,128)}, f32[288,896]{1,0:T(8,128)}, f32[8,128]{1,0:T(8,128)}) custom-call(s32[4]{0:T(128)S(1)} %copy-done.8, s32[4]{0:T(128)S(1)} %copy-done.11, s32[4,4]{1,0:T(4,128)S(1)} %copy-done.4, s32[4,4]{1,0:T(4,128)S(1)} %copy-done.6, f32[4,288,896]{2,1,0:T(8,128)} %momentum.1, ...), custom_call_target="tpu_custom_call" | custom-call | tf_op jit(solution)/shard_map/blend/pallas_call | solution.py:434
  40.7 5.3 %collective-permute-start.11 = (f32[288,896]{1,0:T(8,128)}, f32[288,896]{1,0:T(8,128)}, u32[]{:S(2)}, u32[]{:S(2)}) collective-permute-start(f32[288,896]{1,0:T(8,128)} %get-tuple-element.90), channel_id=1, source_target_pairs={{0,8},{24,16},{1,9},{25,17},{2,10},{26,18},{3,11},{27,19},{4,12},{... | collective-permute-start | bytes 3096584 | tf_op jit(solution)/shard_map/ppermute | solution.py:619
  45.9 2.3 %collective-permute-start.12 = (f32[288,896]{1,0:T(8,128)}, f32[288,896]{1,0:T(8,128)}, u32[]{:S(2)}, u32[]{:S(2)}) collective-permute-start(f32[288,896]{1,0:T(8,128)} %get-tuple-element.91), channel_id=1, source_target_pairs={{0,16},{24,8},{1,17},{25,9},{2,18},{26,10},{3,19},{27,11},{4,20},{... | collective-permute-start | bytes 3096584 | tf_op jit(solution)/shard_map/ppermute | solution.py:619
  48.2 1.6 collective-permute-start.13
  49.9 7.9 %collective-permute-done.14.refs_6_ = f32[288,896]{1,0:T(8,128)} collective-permute-done((f32[288,896]{1,0:T(8,128)}, f32[288,896]{1,0:T(8,128)}, u32[]{:S(2)}, u32[]{:S(2)}) %collective-permute-start.14) | collective-permute-done | bytes 1032224 | tf_op jit(solution)/shard_map/ppermute | solution.py:619
  60.2 1.3 collective-permute-start.23
  61.5 20.4 %collective-permute-done.15.refs_6_ = f32[288,896]{1,0:T(8,128)} collective-permute-done((f32[288,896]{1,0:T(8,128)}, f32[288,896]{1,0:T(8,128)}, u32[]{:S(2)}, u32[]{:S(2)}) %collective-permute-start.15) | collective-permute-done | bytes 1032224 | tf_op jit(solution)/shard_map/ppermute | solution.py:622
  83.1 4.2 %assemble_outer.1.refs_5_ = f32[576,896]{1,0:T(8,128)} custom-call(s32[4]{0:T(128)S(1)} %copy-done.8, s32[4]{0:T(128)S(1)} %copy-done.11, s32[4,4]{1,0:T(4,128)S(1)} %copy-done.4, s32[4,4]{1,0:T(4,128)S(1)} %copy-done.6, f32[288,896]{1,0:T(8,128)S(1)} %collective-permute-done.10.refs_0_.refs_4_.refs_5_, f32[288,896]{1,0:T(8,128)S(1)} %copy-done, ...), custom_call_target="tpu_custom_call" | custom-call | tf_op jit(solution)/shard_map/assemble_outer/pallas_call | solution.py:491
  88.1 12.4 %collective-permute-done.12 = f32[288,896]{1,0:T(8,128)} collective-permute-done((f32[288,896]{1,0:T(8,128)}, f32[288,896]{1,0:T(8,128)}, u32[]{:S(2)}, u32[]{:S(2)}) %collective-permute-start.12) | collective-permute-done | bytes 1032224 | tf_op jit(solution)/shard_map/ppermute | solution.py:619
  101.8 1.3 collective-permute-start.19
  103.1 40.5 %collective-permute-done.23.refs_4_ = f32[576,384]{1,0:T(8,128)} collective-permute-done((f32[576,384]{1,0:T(8,128)}, f32[576,384]{1,0:T(8,128)}, u32[]{:S(2)}, u32[]{:S(2)}) %collective-permute-start.23) | collective-permute-done | bytes 884768 | tf_op jit(solution)/shard_map/ppermute | solution.py:622
  144.3 5.8 %fresh_momentum.1 = (f32[4,288,896]{2,1,0:T(8,128)}, f32[8,128]{1,0:T(8,128)}) custom-call(s32[4]{0:T(128)} %refs_1_.9, s32[4,4]{1,0:T(4,128)} %refs_2_.9, f32[4,288,896]{2,1,0:T(8,128)} %momentum.1, f32[4,288,896]{2,1,0:T(8,128)} %gradient.1, f32[8,128]{1,0:T(8,128)} %get-tuple-element.87._), custom_call_target="tpu_custom_call" | custom-call | tf_op jit(solution)/shard_map/fresh_momentum/pallas_call | solution.py:451
  150.8 7.4 %finish.1 = (f32[576,896]{1,0:T(8,128)}, f32[4,288,896]{2,1,0:T(8,128)}) custom-call(s32[4]{0:T(128)} %refs_0_.17, s32[4]{0:T(128)} %refs_1_.9, s32[4,4]{1,0:T(4,128)} %refs_2_.9, s32[4,4]{1,0:T(4,128)} %refs_3_.9, f32[576,384]{1,0:T(8,128)} %collective-permute-done.23.refs_4_, f32[576,896]{1,0:T(8,128)} %assemble_outer.1.refs_5_, ...), custom_call_target="tpu_custom_call" | custom-call | tf_op jit(solution)/shard_map/finish/pallas_call | solution.py:556
  158.2 2.8 %place_blocks.4.refs_2_ = f32[4,288,896]{2,1,0:T(8,128)} custom-call(s32[4]{0:T(128)S(1)} %copy-done.9, f32[288,896]{1,0:T(8,128)} %collective-permute-done.21.refs_1_, f32[288,896]{1,0:T(8,128)S(1)} %collective-permute-done.22.refs_2_, f32[4,288,896]{2,1,0:T(8,128)} %get-tuple-element.107.refs_3_), custom_call_target="tpu_custom_call", output_to_operand_aliasing={{}: (3, {})} | custom-call | tf_op jit(solution)/shard_map/place_blocks/pallas_call | solution.py:579
  161.0 11.3 %collective-permute-done.20.refs_1_ = f32[288,896]{1,0:T(8,128)S(1)} collective-permute-done((f32[288,896]{1,0:T(8,128)}, f32[288,896]{1,0:T(8,128)S(1)}, u32[]{:S(2)}, u32[]{:S(2)}) %collective-permute-start.20) | collective-permute-done | bytes 1032224 | tf_op jit(solution)/shard_map/ppermute | solution.py:622
  172.3 1.5 place_blocks.5.refs_2_
  173.8 20.1 %collective-permute-done.19.refs_1_ = f32[288,896]{1,0:T(8,128)S(1)} collective-permute-done((f32[288,896]{1,0:T(8,128)}, f32[288,896]{1,0:T(8,128)S(1)}, u32[]{:S(2)}, u32[]{:S(2)}) %collective-permute-start.19) | collective-permute-done | bytes 1032224 | tf_op jit(solution)/shard_map/ppermute | solution.py:622
  193.9 1.5 place_blocks.6.refs_2_
  (36 shorter events, 8.3 us)
Async XLA Ops:
  0.6 35.5 %copy-start.8 = (s32[4]{0:T(128)S(1)}, s32[4]{0:T(128)}, u32[]{:S(2)}) copy-start(s32[4]{0:T(128)} %refs_0_.17) | copy-start | bytes 52
  0.6 35.5 %copy-start.4 = (s32[4,4]{1,0:T(4,128)S(1)}, s32[4,4]{1,0:T(4,128)}, u32[]{:S(2)}) copy-start(s32[4,4]{1,0:T(4,128)} %refs_2_.9) | copy-start | bytes 196
  0.7 35.5 %copy-start.11 = (s32[4]{0:T(128)S(1)}, s32[4]{0:T(128)}, u32[]{:S(2)}) copy-start(s32[4]{0:T(128)} %refs_1_.9) | copy-start | bytes 52
  0.7 35.5 %copy-start.6 = (s32[4,4]{1,0:T(4,128)S(1)}, s32[4,4]{1,0:T(4,128)}, u32[]{:S(2)}) copy-start(s32[4,4]{1,0:T(4,128)} %refs_3_.9) | copy-start | bytes 196
  5.4 10.2 %collective-permute-start.16 = (f32[288,896]{1,0:T(8,128)}, f32[288,896]{1,0:T(8,128)}, u32[]{:S(2)}, u32[]{:S(2)}) collective-permute-start(f32[288,896]{1,0:T(8,128)} %get-tuple-element.94), channel_id=1, source_target_pairs={{8,16},{16,8},{9,17},{17,9},{10,18},{18,10},{11,19},{19,11},{12,20... | collective-permute-start | bytes 3096584 | tf_op jit(solution)/shard_map/ppermute | solution.py:619
  7.1 28.5 %collective-permute-start.10 = (f32[288,896]{1,0:T(8,128)}, f32[288,896]{1,0:T(8,128)S(1)}, u32[]{:S(2)}, u32[]{:S(2)}) collective-permute-start(f32[288,896]{1,0:T(8,128)} %get-tuple-element.86.refs_5_.refs_4_), channel_id=1, source_target_pairs={{0,8},{8,0},{16,24},{24,16},{1,9},{9,1},{17,25},{25,17},{2,10},{10... | collective-permute-start | bytes 3096584 | tf_op jit(solution)/shard_map/ppermute | solution.py:628
  12.0 45.7 %collective-permute-start.14 = (f32[288,896]{1,0:T(8,128)}, f32[288,896]{1,0:T(8,128)}, u32[]{:S(2)}, u32[]{:S(2)}) collective-permute-start(f32[288,896]{1,0:T(8,128)} %get-tuple-element.93), channel_id=1, source_target_pairs={{0,16},{24,8},{1,17},{25,9},{2,18},{26,10},{3,19},{27,11},{4,20},{... | collective-permute-start | bytes 3096584 | tf_op jit(solution)/shard_map/ppermute | solution.py:619
  15.6 43.4 %collective-permute-start.17 = (f32[288,896]{1,0:T(8,128)}, f32[288,896]{1,0:T(8,128)S(1)}, u32[]{:S(2)}, u32[]{:S(2)}) collective-permute-start(f32[288,896]{1,0:T(8,128)} %collective-permute-done.16.refs_7_), channel_id=1, source_target_pairs={{8,0},{16,24},{9,1},{17,25},{10,2},{18,26},{11,3},{19,27},{12,4},{... | collective-permute-start | bytes 3096584 | tf_op jit(solution)/shard_map/ppermute | solution.py:622
  35.6 0.6 copy-start.1
  36.2 22.9 %copy-start = (f32[288,896]{1,0:T(8,128)S(1)}, f32[288,896]{1,0:T(8,128)}, u32[]{:S(2)}) copy-start(f32[288,896]{1,0:T(8,128)} %get-tuple-element.86.refs_5_.refs_4_) | copy-start | bytes 3096580
  40.7 46.7 %collective-permute-start.11 = (f32[288,896]{1,0:T(8,128)}, f32[288,896]{1,0:T(8,128)}, u32[]{:S(2)}, u32[]{:S(2)}) collective-permute-start(f32[288,896]{1,0:T(8,128)} %get-tuple-element.90), channel_id=1, source_target_pairs={{0,8},{24,16},{1,9},{25,17},{2,10},{26,18},{3,11},{27,19},{4,12},{... | collective-permute-start | bytes 3096584 | tf_op jit(solution)/shard_map/ppermute | solution.py:619
  45.9 54.6 %collective-permute-start.12 = (f32[288,896]{1,0:T(8,128)}, f32[288,896]{1,0:T(8,128)}, u32[]{:S(2)}, u32[]{:S(2)}) collective-permute-start(f32[288,896]{1,0:T(8,128)} %get-tuple-element.91), channel_id=1, source_target_pairs={{0,16},{24,8},{1,17},{25,9},{2,18},{26,10},{3,19},{27,11},{4,20},{... | collective-permute-start | bytes 3096584 | tf_op jit(solution)/shard_map/ppermute | solution.py:619
  48.2 52.3 %collective-permute-start.13 = (f32[288,896]{1,0:T(8,128)}, f32[288,896]{1,0:T(8,128)}, u32[]{:S(2)}, u32[]{:S(2)}) collective-permute-start(f32[288,896]{1,0:T(8,128)} %get-tuple-element.92), channel_id=1, source_target_pairs={{8,16},{16,8},{9,17},{17,9},{10,18},{18,10},{11,19},{19,11},{12,20... | collective-permute-start | bytes 3096584 | tf_op jit(solution)/shard_map/ppermute | solution.py:619
  57.7 24.1 %collective-permute-start.15 = (f32[288,896]{1,0:T(8,128)}, f32[288,896]{1,0:T(8,128)}, u32[]{:S(2)}, u32[]{:S(2)}) collective-permute-start(f32[288,896]{1,0:T(8,128)} %collective-permute-done.14.refs_6_), channel_id=1, source_target_pairs={{8,0},{16,24},{9,1},{17,25},{10,2},{18,26},{11,3},{19,27},{12,4},{... | collective-permute-start | bytes 3096584 | tf_op jit(solution)/shard_map/ppermute | solution.py:622
  60.2 83.4 %collective-permute-start.23 = (f32[576,384]{1,0:T(8,128)}, f32[576,384]{1,0:T(8,128)}, u32[]{:S(2)}, u32[]{:S(2)}) collective-permute-start(f32[576,384]{1,0:T(8,128)} %get-tuple-element.103.refs_6_), channel_id=1, source_target_pairs={{8,0},{16,24},{9,1},{17,25},{10,2},{18,26},{11,3},{19,27},{12,4},{... | collective-permute-start | bytes 2654216 | tf_op jit(solution)/shard_map/ppermute | solution.py:622
  81.8 76.4 %collective-permute-start.21 = (f32[288,896]{1,0:T(8,128)}, f32[288,896]{1,0:T(8,128)}, u32[]{:S(2)}, u32[]{:S(2)}) collective-permute-start(f32[288,896]{1,0:T(8,128)} %get-tuple-element.101), channel_id=1, source_target_pairs={{8,24},{16,0},{9,25},{17,1},{10,26},{18,2},{11,27},{19,3},{12,28},... | collective-permute-start | bytes 3096584 | tf_op jit(solution)/shard_map/ppermute | solution.py:622
  87.4 70.8 %collective-permute-start.22 = (f32[288,896]{1,0:T(8,128)}, f32[288,896]{1,0:T(8,128)S(1)}, u32[]{:S(2)}, u32[]{:S(2)}) collective-permute-start(f32[288,896]{1,0:T(8,128)} %get-tuple-element.102), channel_id=1, source_target_pairs={{8,16},{16,8},{9,17},{17,9},{10,18},{18,10},{11,19},{19,11},{12,20... | collective-permute-start | bytes 3096584 | tf_op jit(solution)/shard_map/ppermute | solution.py:622
  100.5 71.8 %collective-permute-start.20 = (f32[288,896]{1,0:T(8,128)}, f32[288,896]{1,0:T(8,128)S(1)}, u32[]{:S(2)}, u32[]{:S(2)}) collective-permute-start(f32[288,896]{1,0:T(8,128)} %get-tuple-element.97), channel_id=1, source_target_pairs={{8,24},{16,0},{9,25},{17,1},{10,26},{18,2},{11,27},{19,3},{12,28},... | collective-permute-start | bytes 3096584 | tf_op jit(solution)/shard_map/ppermute | solution.py:622
  101.8 92.1 %collective-permute-start.19 = (f32[288,896]{1,0:T(8,128)}, f32[288,896]{1,0:T(8,128)S(1)}, u32[]{:S(2)}, u32[]{:S(2)}) collective-permute-start(f32[288,896]{1,0:T(8,128)} %get-tuple-element.96), channel_id=1, source_target_pairs={{8,0},{16,24},{9,1},{17,25},{10,2},{18,26},{11,3},{19,27},{12,4},{... | collective-permute-start | bytes 3096584 | tf_op jit(solution)/shard_map/ppermute | solution.py:622
  143.6 51.8 %collective-permute-start.18 = (f32[288,896]{1,0:T(8,128)}, f32[288,896]{1,0:T(8,128)S(1)}, u32[]{:S(2)}, u32[]{:S(2)}) collective-permute-start(f32[288,896]{1,0:T(8,128)} %get-tuple-element.95), channel_id=1, source_target_pairs={{8,16},{16,8},{9,17},{17,9},{10,18},{18,10},{11,19},{19,11},{12,20... | collective-permute-start | bytes 3096584 | tf_op jit(solution)/shard_map/ppermute | solution.py:622
  150.1 0.7 copy-start.2
  150.8 7.4 %copy-start.9 = (s32[4]{0:T(128)S(1)}, s32[4]{0:T(128)}, u32[]{:S(2)}) copy-start(s32[4]{0:T(128)} %refs_0_.17) | copy-start | bytes 52
